TPU v7x, 512 devices: a whole 4x8x8 slice. The times are simulated.
512 devices in a mesh: ray: 16 (over z_lo, x), mp: 32 (over y, z_hi, core).
Axes of the slice: x: 4, y: 8, z: 8 (z_hi: 2, z_lo: 4; z = z_hi * 4 + z_lo), core: 2. Of those that a mesh axis runs over, the one named last changes fastest.
Arguments:
- slowness: float32 [128, 128, 128], P('mp', 'ray'), may hold values from 0.5 to 1.5
- accumulated: float32 [128, 128, 128], P('mp', 'ray'), may hold values from -3 to 3
- extrapolated: float32 [128, 128, 128], P('mp', 'ray'), may hold values from -3 to 3
- tv_dual: float32 [3, 128, 128, 128], P(None, 'mp', 'ray'), may hold values from -1.2 to 1.2
- ray_dual: float32 [256, 128], P('ray'), may hold values from -3 to 3
- traveltimes: float32 [256, 128], P('ray'), may hold values from -6 to 6
- tiles: bfloat16 [256, 256, 128, 128], P('ray', 'mp'), may hold values from -0.03125 to 0.03125
- pattern: int32 [256, 256], P('ray', 'mp'), may hold values from 0 to 511, as said below
- selected: int32 [2, 256], P(None, 'ray'), may hold values from 0 to 1, as said below
Outputs:
- slowness_out: float32 [128, 128, 128], P('mp', 'ray')
- ray_dual_out: float32 [256, 128], P('ray')
- tv_dual_out: float32 [3, 128, 128, 128], P(None, 'mp', 'ray')
- accumulated_out: float32 [128, 128, 128], P('mp', 'ray')
- extrapolated_out: float32 [128, 128, 128], P('mp', 'ray')
Inputs may be any that keep to these rules, and one draw needn't show every extreme that they name: In each iteration every aligned block of 16 ray blocks (those of one index of ray) has 1 to 8 selected ray blocks, and some block has exactly 8. Among the 128 tiles of one index of ray's ray blocks on one index of mp, at most 16 have model blocks whose grid rows lie on one index of ray (pattern % 128 // 8), and one index of ray has exactly 16.
All inputs are finite; a program needn't handle non-finite values.
Results may differ from a plain program's by a relative error of at most 0.0022.
Values may be sent and summed in bfloat16 or wider, within the bound.
No kernel may reach another device: no remote copies, remote signals or barrier semaphores. Data moves between devices by JAX's collectives and lax.ppermute only.
A program may use at most 64 MiB of HBM per device.

v0:
```python
import jax
import jax.numpy as jnp
from jax import lax
from jax.sharding import PartitionSpec as P

RB_DEV = 16
ITERS = 2
MAXSEL = 8


primal_step = 0.5
dual_step = 0.5
tv_step = 0.25
tv_weight = 0.3


def shifted(block, axis, distance):
    devices = range(lax.axis_size(axis))
    route = [(i - distance, i) for i in devices if i - distance in devices]
    return lax.ppermute(block, axis, route)


def ray_work(blocks, rays, traveltimes, tiles, pattern, flags):
    used, cols, y_rows, t_rows = (tiles, pattern, rays, traveltimes)
    taken = flags.astype(jnp.float32)[:, None]
    cells = blocks[cols]
    partial_value = jnp.einsum("rsij,rsj->ri", used, cells, preferred_element_type=jnp.float32)
    predicted = lax.psum(partial_value, "mp")
    fresh = (y_rows + dual_step * (predicted - t_rows)) / (1.0 + dual_step)
    change = taken * (fresh - y_rows)
    contrib = jnp.einsum(
        "rsij,ri->rsj", used, change.astype(jnp.bfloat16), preferred_element_type=jnp.float32
    )
    rays = rays + change
    return (rays, contrib, cols)


def total_variation(field, dual):
    plane_len, row_len, depth = field.shape
    full_x = plane_len * lax.axis_size("mp")
    xpos = lax.axis_index("mp") * plane_len + jnp.arange(plane_len)
    last_x = (xpos == full_x - 1)[:, None, None]
    full_y = row_len * lax.axis_size("ray")
    ypos = lax.axis_index("ray") * row_len + jnp.arange(row_len)
    last_y = (ypos == full_y - 1)[None, :, None]
    last_z = (jnp.arange(depth) == depth - 1)[None, None, :]
    after_x = shifted(field[0:1], "mp", -1)
    after_y = shifted(field[:, 0:1], "ray", -1)
    step_x = jnp.where(last_x, 0.0, jnp.concatenate([field[1:], after_x], 0) - field)
    step_y = jnp.where(last_y, 0.0, jnp.concatenate([field[:, 1:], after_y], 1) - field)
    step_z = jnp.where(
        last_z,
        0.0,
        jnp.concatenate([field[:, :, 1:], jnp.zeros((plane_len, row_len, 1), jnp.float32)], 2)
        - field,
    )
    moved = dual + tv_step * jnp.stack([step_x, step_y, step_z])
    length = jnp.sqrt(jnp.sum(moved * moved, axis=0))
    fresh = moved / jnp.maximum(1.0, length / tv_weight)
    delta = fresh - dual
    comp_x = jnp.where(last_x, 0.0, delta[0])
    before_x = shifted(comp_x[-1:], "mp", 1)
    back_x = jnp.concatenate([before_x, comp_x[:-1]], 0) - comp_x
    comp_y = jnp.where(last_y, 0.0, delta[1])
    before_y = shifted(comp_y[:, -1:], "ray", 1)
    back_y = jnp.concatenate([before_y, comp_y[:, :-1]], 1) - comp_y
    comp_z = jnp.where(last_z, 0.0, delta[2])
    back_z = (
        jnp.concatenate([jnp.zeros((plane_len, row_len, 1), jnp.float32), comp_z[:, :, :-1]], 2)
        - comp_z
    )
    return (fresh, back_x + back_y + back_z)


def on_device(
    slowness, accumulated, extrapolated, tv_dual, ray_dual, traveltimes, tiles, pattern, selected
):
    extrapolation = 2.0 * RB_DEV / (MAXSEL + 1)
    field, image, image_bar, dual = (slowness, accumulated, extrapolated, tv_dual)
    rays = ray_dual
    for step in range(ITERS):
        field = field - primal_step * image_bar
        rounded = field.astype(jnp.bfloat16)
        blocks = lax.all_gather(rounded, "ray", axis=1, tiled=True)
        blocks = blocks.reshape(-1, blocks.shape[2])
        rays, contrib, cols = ray_work(blocks, rays, traveltimes, tiles, pattern, selected[step])
        summed = jax.ops.segment_sum(
            contrib.reshape(-1, contrib.shape[2]), cols.reshape(-1), num_segments=blocks.shape[0]
        )
        wide = summed.reshape(field.shape[0], -1, field.shape[2])
        back = lax.psum_scatter(wide, "ray", scatter_dimension=1, tiled=True)
        dual, tv_back = total_variation(field, dual)
        image = image + back + tv_back
        image_bar = image + extrapolation * back + tv_back
    return (field, rays, dual, image, image_bar)


def solution(mesh):
    in_specs = (
        P("mp", "ray", None),
        P("mp", "ray", None),
        P("mp", "ray", None),
        P(None, "mp", "ray", None),
        P("ray", None),
        P("ray", None),
        P("ray", "mp", None, None),
        P("ray", "mp"),
        P(None, "ray"),
    )
    out_specs = (
        P("mp", "ray", None),
        P("ray", None),
        P(None, "mp", "ray", None),
        P("mp", "ray", None),
        P("mp", "ray", None),
    )
    return jax.shard_map(
        on_device, mesh=mesh, in_specs=in_specs, out_specs=out_specs, check_vma=False
    )
```

profile of v0, /device:TPU:16, one launch (start us, length us, event | category | flops | bytes accessed | tf_op | source)
XLA Modules:
  0.0 474.2 jit_solution(11973597249543037380)
XLA Ops:
  7.2 0.0 reduce-scatter.3.cloned.1.call-start
  7.2 0.7 fusion.35
  8.0 10.2 %collective-permute-start = (f32[1,8,128]{2,1,0:T(8,128)S(1)}, f32[1,8,128]{2,1,0:T(8,128)S(1)}, u32[]{:S(2)}, u32[]{:S(2)}) collective-permute-start(f32[1,8,128]{2,1,0:T(8,128)S(1)} %slice.117), channel_id=1, source_target_pairs={{1,0},{2,1},{3,2},{4,3},{5,4},{6,5},{7,6},{8,7},{9,8},{10,9},{11,1... | collective-permute-start | bytes 12296 | tf_op jit(solution)/shard_map/ppermute | solution.py:20
  18.2 1.3 collective-permute-start.1
  19.5 0.7 compare_select_fusion
  20.2 0.8 copy.16
  21.0 44.3 %all_gather.6 = bf16[4,128,128]{2,1,0:T(8,128)(2,1)S(1)} all-gather(bf16[4,8,128]{2,1,0:T(8,128)(2,1)S(1)} %get-tuple-element.12), channel_id=1, replica_groups=mesh['ray'=16,'mp'=32] {'ray'}, dimensions={1}, use_global_device_ids=true | all-gather | bytes 139264 | tf_op jit(solution)/shard_map/all_gather | solution.py:84
  65.3 0.1 copy.17
  65.4 0.1 reshape.72
  65.5 0.7 gather_fusion
  66.2 3.4 fusion.6
  69.6 75.6 %psum.14 = f32[16,128]{1,0:T(8,128)S(1)} all-reduce(f32[16,128]{1,0:T(8,128)S(1)} %bitcast.88), channel_id=1, replica_groups=mesh['ray'=16,'mp'=32] {'mp'}, use_global_device_ids=true, to_apply=%region_0.0 | all-reduce | flops 2048 | bytes 16384 | tf_op jit(solution)/shard_map/psum | solution.py:28
  145.2 0.1 convert_bitcast_fusion.1
  145.3 2.8 fusion.30
  148.1 0.1 reshape.88
  148.2 1.7 scatter_custom_fusion
  149.9 0.0 reduce-scatter.3.cloned.1.call-update
  149.9 0.0 reduce-scatter.5.cloned.1.call-start
  150.0 0.1 slice.120
  150.1 0.1 fusion.17
  150.3 0.1 fusion.15
  150.3 1.9 collective-permute-start.2
  152.3 1.3 collective-permute-start.3
  153.6 1.3 collective-permute-done.3
  154.9 5.2 %collective-permute-done.2 = f32[1,8,128]{2,1,0:T(8,128)S(1)} collective-permute-done((f32[1,8,128]{2,1,0:T(8,128)S(1)}, f32[1,8,128]{2,1,0:T(8,128)S(1)}, u32[]{:S(2)}, u32[]{:S(2)}) %collective-permute-start.2) | collective-permute-done | bytes 4128 | tf_op jit(solution)/shard_map/ppermute | solution.py:20
  160.1 80.2 %reduce-scatter.3.cloned.1.call-done = f32[4,8,128]{2,1,0:T(8,128)} async-done(((f32[4,128,128]{2,1,0:T(8,128)}), f32[4,8,128]{2,1,0:T(8,128)}) %reduce-scatter.3.cloned.1.call-update) | async-done | bytes 16400 | tf_op jit(solution)/shard_map/reduce_scatter | solution.py:91
  240.3 0.8 fusion.33
  241.1 0.0 copy-start
  241.1 38.2 %all_gather.7 = bf16[4,128,128]{2,1,0:T(8,128)(2,1)S(1)} all-gather(bf16[4,8,128]{2,1,0:T(8,128)(2,1)S(1)} %get-tuple-element.9), channel_id=1, replica_groups=mesh['ray'=16,'mp'=32] {'ray'}, dimensions={1}, use_global_device_ids=true | all-gather | bytes 139264 | tf_op jit(solution)/shard_map/all_gather | solution.py:84
  279.3 0.7 gather_fusion.1
  280.1 3.4 fusion.4
  283.4 75.6 %psum.15 = f32[16,128]{1,0:T(8,128)S(1)} all-reduce(f32[16,128]{1,0:T(8,128)S(1)} %bitcast.89), channel_id=1, replica_groups=mesh['ray'=16,'mp'=32] {'mp'}, use_global_device_ids=true, to_apply=%region_4.5 | all-reduce | flops 2048 | bytes 16384 | tf_op jit(solution)/shard_map/psum | solution.py:28
  359.1 1.9 collective-permute-start.4
  361.0 1.3 collective-permute-start.5
  362.3 0.7 convert_bitcast_fusion
  363.0 2.8 fusion.28
  365.8 0.1 slice.133
  365.9 1.7 scatter_custom_fusion.1
  367.6 0.0 reduce-scatter.5.cloned.1.call-update
  367.6 0.1 fusion.23
  367.7 0.6 fusion.32
  368.4 0.1 fusion.10
  368.4 2.4 collective-permute-start.6
  370.9 4.3 collective-permute-start.7
  375.1 1.3 collective-permute-done.7
  376.4 1.7 collective-permute-done.6
  378.2 87.7 %reduce-scatter.5.cloned.1.call-done = f32[4,8,128]{2,1,0:T(8,128)} async-done(((f32[4,128,128]{2,1,0:T(8,128)}), f32[4,8,128]{2,1,0:T(8,128)}) %reduce-scatter.5.cloned.1.call-update) | async-done | bytes 16400 | tf_op jit(solution)/shard_map/reduce_scatter | solution.py:91
  465.9 1.4 add_add_fusion
  (41 shorter events, 0.2 us)
Async XLA Ops:
  7.2 138.0 %copy-start.6 = (s32[2,16]{1,0:T(2,128)S(1)}, s32[2,16]{1,0:T(2,128)}, u32[]{:S(2)}) copy-start(s32[2,16]{1,0:T(2,128)} %param.17) | copy-start | bytes 388
  7.2 138.0 %copy-start.4 = (f32[16,128]{1,0:T(8,128)S(1)}, f32[16,128]{1,0:T(8,128)}, u32[]{:S(2)}) copy-start(f32[16,128]{1,0:T(8,128)} %param.13) | copy-start | bytes 24580
  7.2 138.0 %copy-start.5 = (f32[16,128]{1,0:T(8,128)S(1)}, f32[16,128]{1,0:T(8,128)}, u32[]{:S(2)}) copy-start(f32[16,128]{1,0:T(8,128)} %param.14) | copy-start | bytes 24580
  7.2 233.1 %reduce-scatter.3.cloned.1.call-start = ((), (), s32[]{:S(2)}) async-start(), calls=%async_computation.2 | async-start | bytes 278528 | tf_op jit(solution)/shard_map/reduce_scatter | solution.py:91
  8.0 142.1 %collective-permute-start = (f32[1,8,128]{2,1,0:T(8,128)S(1)}, f32[1,8,128]{2,1,0:T(8,128)S(1)}, u32[]{:S(2)}, u32[]{:S(2)}) collective-permute-start(f32[1,8,128]{2,1,0:T(8,128)S(1)} %slice.117), channel_id=1, source_target_pairs={{1,0},{2,1},{3,2},{4,3},{5,4},{6,5},{7,6},{8,7},{9,8},{10,9},{11,1... | collective-permute-start | bytes 12296 | tf_op jit(solution)/shard_map/ppermute | solution.py:20
  18.2 131.9 %collective-permute-start.1 = (f32[4,1,128]{2,1,0:T(1,128)S(1)}, f32[4,1,128]{2,1,0:T(1,128)S(1)}, u32[]{:S(2)}, u32[]{:S(2)}) collective-permute-start(f32[4,1,128]{2,1,0:T(1,128)S(1)} %slice.119), channel_id=1, source_target_pairs={{32,0},{64,32},{96,64},{128,96},{160,128},{192,160},{224,192},{256... | collective-permute-start | bytes 6152 | tf_op jit(solution)/shard_map/ppermute | solution.py:20
  66.2 84.0 %copy-start.1 = (f32[3,4,8,128]{3,2,1,0:T(8,128)S(1)}, f32[3,4,8,128]{3,2,1,0:T(8,128)}, u32[]{:S(2)}) copy-start(f32[3,4,8,128]{3,2,1,0:T(8,128)} %param.12) | copy-start | bytes 147460
  66.2 174.1 %copy-start.2 = (f32[4,8,128]{2,1,0:T(8,128)S(1)}, f32[4,8,128]{2,1,0:T(8,128)}, u32[]{:S(2)}) copy-start(f32[4,8,128]{2,1,0:T(8,128)} %param.10) | copy-start | bytes 49156
  149.9 316.0 %reduce-scatter.5.cloned.1.call-start = ((), (), s32[]{:S(2)}) async-start(), calls=%async_computation.3 | async-start | bytes 278528 | tf_op jit(solution)/shard_map/reduce_scatter | solution.py:91
  150.3 9.7 %collective-permute-start.2 = (f32[1,8,128]{2,1,0:T(8,128)S(1)}, f32[1,8,128]{2,1,0:T(8,128)S(1)}, u32[]{:S(2)}, u32[]{:S(2)}) collective-permute-start(f32[1,8,128]{2,1,0:T(8,128)S(1)} %slice.122), channel_id=1, source_target_pairs={{0,1},{1,2},{2,3},{3,4},{4,5},{5,6},{6,7},{7,8},{8,9},{9,10},{10,1... | collective-permute-start | bytes 12296 | tf_op jit(solution)/shard_map/ppermute | solution.py:20
  152.3 2.6 collective-permute-start.3
  241.1 126.5 %copy-start = (f32[4,8,128]{2,1,0:T(8,128)}, f32[4,8,128]{2,1,0:T(8,128)S(1)}, u32[]{:S(2)}) copy-start(f32[4,8,128]{2,1,0:T(8,128)S(1)} %get-tuple-element.10) | copy-start | bytes 49156
  280.1 185.9 %copy-start.3 = (f32[4,8,128]{2,1,0:T(8,128)S(1)}, f32[4,8,128]{2,1,0:T(8,128)}, u32[]{:S(2)}) copy-start(f32[4,8,128]{2,1,0:T(8,128)} %reduce-scatter.3.cloned.1.call-done) | copy-start | bytes 49156
  359.1 8.5 %collective-permute-start.4 = (f32[1,8,128]{2,1,0:T(8,128)S(1)}, f32[1,8,128]{2,1,0:T(8,128)S(1)}, u32[]{:S(2)}, u32[]{:S(2)}) collective-permute-start(f32[1,8,128]{2,1,0:T(8,128)S(1)} %slice.130), channel_id=1, source_target_pairs={{1,0},{2,1},{3,2},{4,3},{5,4},{6,5},{7,6},{8,7},{9,8},{10,9},{11,1... | collective-permute-start | bytes 12296 | tf_op jit(solution)/shard_map/ppermute | solution.py:20
  361.0 6.6 %collective-permute-start.5 = (f32[4,1,128]{2,1,0:T(1,128)S(1)}, f32[4,1,128]{2,1,0:T(1,128)S(1)}, u32[]{:S(2)}, u32[]{:S(2)}) collective-permute-start(f32[4,1,128]{2,1,0:T(1,128)S(1)} %slice.132), channel_id=1, source_target_pairs={{32,0},{64,32},{96,64},{128,96},{160,128},{192,160},{224,192},{256... | collective-permute-start | bytes 6152 | tf_op jit(solution)/shard_map/ppermute | solution.py:20
  368.4 9.7 %collective-permute-start.6 = (f32[1,8,128]{2,1,0:T(8,128)S(1)}, f32[1,8,128]{2,1,0:T(8,128)S(1)}, u32[]{:S(2)}, u32[]{:S(2)}) collective-permute-start(f32[1,8,128]{2,1,0:T(8,128)S(1)} %slice.135), channel_id=1, source_target_pairs={{0,1},{1,2},{2,3},{3,4},{4,5},{5,6},{6,7},{7,8},{8,9},{9,10},{10,1... | collective-permute-start | bytes 12296 | tf_op jit(solution)/shard_map/ppermute | solution.py:20
  370.9 5.6 %collective-permute-start.7 = (f32[4,1,128]{2,1,0:T(1,128)S(1)}, f32[4,1,128]{2,1,0:T(1,128)S(1)}, u32[]{:S(2)}, u32[]{:S(2)}) collective-permute-start(f32[4,1,128]{2,1,0:T(1,128)S(1)} %slice.138), channel_id=1, source_target_pairs={{0,32},{32,64},{64,96},{96,128},{128,160},{160,192},{192,224},{224... | collective-permute-start | bytes 6152 | tf_op jit(solution)/shard_map/ppermute | solution.py:20
Sparse Core Ops, SparseCore 0:
  150.0 90.2 reduce-scatter.2
  367.7 98.1 reduce-scatter.4
where the time goes:
time: 475 us; the launch traced here: 474 us
  blocking collectives  234 us (49%)
  waiting for transfers between devices  178 us (37%)
  starting transfers between devices  24.7 us (5%)
  between operations  14.4 us (3%)
  matrix products  12.4 us (3%)
  other arithmetic  8.79 us (2%)
    reduce_scatter x2, waiting for transfers between devices, on_device(): back = lax.psum_scatter(wide, 'ray', scatter_dimension=1, tiled=True)  168 us
    psum x2, blocking collectives, ray_work(): predicted = lax.psum(partial_value, 'mp')  151 us
    all_gather x2, blocking collectives, on_device(): blocks = lax.all_gather(rounded, 'ray', axis=1, tiled=True)  82.5 us
    ppermute x8, starting transfers between devices, shifted(): return lax.ppermute(block, axis, route)  24.6 us
    ppermute x8, waiting for transfers between devices, shifted(): return lax.ppermute(block, axis, route)  9.51 us
  transfers between devices with their start and end apart: 10, of which 6 were waited for; matrix products, arithmetic and copies ran while one was open for 4% of the time, Pallas kernels for 0%

commit v1 on v0

--- a/solution.py
+++ b/solution.py
@@ -20,19 +20,23 @@
     return lax.ppermute(block, axis, route)
 
 
-def ray_work(blocks, rays, traveltimes, tiles, pattern, flags):
-    used, cols, y_rows, t_rows = (tiles, pattern, rays, traveltimes)
+def to_all(block, axis):
+    count = lax.axis_size(axis)
+    copies = jnp.broadcast_to(block[None], (count,) + block.shape)
+    return lax.all_to_all(copies, axis, 0, 0, tiled=True)
+
+
+def ray_work(blocks, rays, traveltimes, tiles, cols, flags):
     taken = flags.astype(jnp.float32)[:, None]
     cells = blocks[cols]
-    partial_value = jnp.einsum("rsij,rsj->ri", used, cells, preferred_element_type=jnp.float32)
-    predicted = lax.psum(partial_value, "mp")
-    fresh = (y_rows + dual_step * (predicted - t_rows)) / (1.0 + dual_step)
-    change = taken * (fresh - y_rows)
+    partial_value = jnp.einsum("rsij,rsj->ri", tiles, cells, preferred_element_type=jnp.float32)
+    predicted = jnp.sum(to_all(partial_value, "mp"), axis=0)
+    fresh = (rays + dual_step * (predicted - traveltimes)) / (1.0 + dual_step)
+    change = taken * (fresh - rays)
     contrib = jnp.einsum(
-        "rsij,ri->rsj", used, change.astype(jnp.bfloat16), preferred_element_type=jnp.float32
+        "rsij,ri->rsj", tiles, change.astype(jnp.bfloat16), preferred_element_type=jnp.float32
     )
-    rays = rays + change
-    return (rays, contrib, cols)
+    return (rays + change, contrib)
 
 
 def total_variation(field, dual):
@@ -78,17 +82,22 @@
     extrapolation = 2.0 * RB_DEV / (MAXSEL + 1)
     field, image, image_bar, dual = (slowness, accumulated, extrapolated, tv_dual)
     rays = ray_dual
+    planes, rows, depth = field.shape
+    peers = lax.axis_size("ray")
+    row = pattern % (rows * peers)
+    cols = (row // rows) * (planes * rows) + (pattern // (rows * peers)) * rows + row % rows
     for step in range(ITERS):
         field = field - primal_step * image_bar
-        rounded = field.astype(jnp.bfloat16)
-        blocks = lax.all_gather(rounded, "ray", axis=1, tiled=True)
-        blocks = blocks.reshape(-1, blocks.shape[2])
-        rays, contrib, cols = ray_work(blocks, rays, traveltimes, tiles, pattern, selected[step])
+        rounded = field.astype(jnp.bfloat16).reshape(planes * rows, depth)
+        blocks = to_all(rounded, "ray").reshape(-1, depth)
+        rays, contrib = ray_work(blocks, rays, traveltimes, tiles, cols, selected[step])
         summed = jax.ops.segment_sum(
-            contrib.reshape(-1, contrib.shape[2]), cols.reshape(-1), num_segments=blocks.shape[0]
+            contrib.reshape(-1, depth), cols.reshape(-1), num_segments=blocks.shape[0]
         )
-        wide = summed.reshape(field.shape[0], -1, field.shape[2])
-        back = lax.psum_scatter(wide, "ray", scatter_dimension=1, tiled=True)
+        parts = lax.all_to_all(
+            summed.reshape(peers, planes * rows, depth), "ray", 0, 0, tiled=True
+        )
+        back = jnp.sum(parts, axis=0).reshape(field.shape)
         dual, tv_back = total_variation(field, dual)
         image = image + back + tv_back
         image_bar = image + extrapolation * back + tv_back

time: 475 us -> 140 us (0.29)
  the two profiles are of different devices: /device:TPU:16 before, /device:TPU:1 now
where the time goes in v1:
time: 140 us; the launch traced here: 139 us
  starting transfers between devices  61.2 us (44%)
  waiting for transfers between devices  37.5 us (27%)
  blocking collectives  14.6 us (10%)
  matrix products  12.4 us (9%)
  other arithmetic  8.3 us (6%)
  local copies, waits for them, and re-layouts  4.12 us (3%)
    ppermute x8, starting transfers between devices, shifted(): return lax.ppermute(block, axis, route)  28.7 us
    all_to_all x3, waiting for transfers between devices, to_all(): return lax.all_to_all(copies, axis, 0, 0, tiled=True)  27.6 us
    all_to_all x3, starting transfers between devices, to_all(): return lax.all_to_all(copies, axis, 0, 0, tiled=True)  25.5 us
    all_to_all x1, blocking collectives, to_all(): return lax.all_to_all(copies, axis, 0, 0, tiled=True)  14.6 us
    all_to_all x2, starting transfers between devices, on_device(): lax.all_to_all(summed.reshape(peers, planes * rows, depth), 'ray', 0, 0,...  7.06 us
    dot_general x2, matrix products, ray_work(): jnp.einsum('rsij,rsj->ri', tiles, cells, preferred_element_type=jnp.float32)  6.73 us
    ppermute x8, waiting for transfers between devices, shifted(): return lax.ppermute(block, axis, route)  5.91 us
    dot_general x2, matrix products, ray_work(): jnp.einsum('rsij,ri->rsj', tiles, change.astype(jnp.bfloat16), preferred_...  5.67 us
  transfers between devices with their start and end apart: 13, of which 7 were waited for; matrix products, arithmetic and copies ran while one was open for 6% of the time, Pallas kernels for 0%

profile of v1, /device:TPU:1, one launch (start us, length us, event | category | flops | bytes accessed | tf_op | source)
XLA Modules:
  0.0 139.2 jit_solution(14880136984453865089)
XLA Ops:
  0.7 0.8 convert_bitcast_fusion.1
  1.4 8.8 %collective-permute-start = (f32[1,8,128]{2,1,0:T(8,128)S(1)}, f32[1,8,128]{2,1,0:T(8,128)S(1)}, u32[]{:S(2)}, u32[]{:S(2)}) collective-permute-start(f32[1,8,128]{2,1,0:T(8,128)S(1)} %slice.117), channel_id=1, source_target_pairs={{1,0},{2,1},{3,2},{4,3},{5,4},{6,5},{7,6},{8,7},{9,8},{10,9},{11,1... | collective-permute-start | bytes 12296 | tf_op jit(solution)/shard_map/ppermute | solution.py:20
  10.2 1.3 collective-permute-start.1
  11.5 0.7 broadcast_in_dim.115
  12.2 5.1 %all-to-all-start = ((bf16[16,32,128]{2,1,0:T(8,128)(2,1)}), bf16[16,32,128]{2,1,0:T(8,128)(2,1)S(1)}, u32[]{:S(2)}, u32[]{:S(2)}) async-start(bf16[16,32,128]{2,1,0:T(8,128)(2,1)} %broadcast_in_dim.115), calls=%async_computation | async-start | bytes 262144 | tf_op jit(solution)/shard_map/all_to_all | solution.py:26
  17.3 0.7 compare_select_fusion
  18.0 0.1 copy.19
  18.0 0.1 reshape.84
  18.2 0.8 convert_bitcast_fusion.4
  18.9 6.8 %all-to-all-done = bf16[16,32,128]{2,1,0:T(8,128)(2,1)S(1)} async-done(((bf16[16,32,128]{2,1,0:T(8,128)(2,1)}), bf16[16,32,128]{2,1,0:T(8,128)(2,1)S(1)}, u32[]{:S(2)}, u32[]{:S(2)}) %all-to-all-start) | async-done | bytes 131104 | tf_op jit(solution)/shard_map/all_to_all | solution.py:26
  25.8 0.7 gather_fusion
  26.5 3.4 %fusion.6 = f32[16,1,128,1]{2,1,3,0:T(1,128)S(1)} fusion(bf16[16,8,128,128]{3,2,1,0:T(8,128)(2,1)} %param.15, bf16[16,8,128,1]{2,1,0,3:T(8,128)(2,1)S(1)} %bitcast.112), kind=kOutput, calls=%fused_computation.10 | convolution fusion | flops 4194304 | bytes 4235264 | tf_op jit(solution)/shard_map/rsij,rsj->ri/dot_general | solution.py:32
  29.9 0.7 broadcast_in_dim.117
  30.6 14.0 %all-to-all-start.1 = ((f32[32,16,128]{2,1,0:T(8,128)}), f32[32,16,128]{2,1,0:T(8,128)S(1)}, u32[]{:S(2)}, u32[]{:S(2)}) async-start(f32[32,16,128]{2,1,0:T(8,128)} %broadcast_in_dim.117), calls=%async_computation.1 | async-start | bytes 524288 | tf_op jit(solution)/shard_map/all_to_all | solution.py:26
  44.7 0.1 slice.120
  44.8 0.1 reshape.100
  44.9 0.1 fusion.17
  45.0 14.9 %all-to-all-done.1 = f32[32,16,128]{2,1,0:T(8,128)S(1)} async-done(((f32[32,16,128]{2,1,0:T(8,128)}), f32[32,16,128]{2,1,0:T(8,128)S(1)}, u32[]{:S(2)}, u32[]{:S(2)}) %all-to-all-start.1) | async-done | bytes 262176 | tf_op jit(solution)/shard_map/all_to_all | solution.py:26
  60.0 0.1 convert_bitcast_fusion.3
  60.1 2.8 %fusion.38 = f32[16,1,8,128]{3,1,2,0:T(1,128)S(1)} fusion(bf16[16,8,128,128]{3,2,1,0:T(8,128)(2,1)} %param.15, bf16[16,128,1,1]{1,0,2,3:T(8,128)(2,1)S(1)} %convert_bitcast_fusion.3), kind=kOutput, calls=%fused_computation.72 | convolution fusion | flops 4194304 | bytes 4263936 | tf_op jit(solution)/shard_map/rsij,ri->rsj/dot_general | solution.py:36
  62.9 1.7 %scatter_custom_fusion = f32[512,128]{1,0:T(8,128)} fusion(s32[128]{0:T(128)S(1)} %reshape.100, f32[128,128]{1,0:T(8,128)S(1)} %bitcast.118, f32[]{:T(128)} %constant.68.clone.1), kind=kCustom, calls=%fused_computation.6 | custom fusion | flops 16384 | bytes 262148 | tf_op jit(solution)/shard_map/scatter-add | solution.py:94
  64.6 3.5 %all-to-all-start.2 = ((f32[16,32,128]{2,1,0:T(8,128)}), f32[16,32,128]{2,1,0:T(8,128)S(1)}, u32[]{:S(2)}, u32[]{:S(2)}) async-start(f32[16,32,128]{2,1,0:T(8,128)} %bitcast.11), calls=%async_computation.2 | async-start | bytes 524288 | tf_op jit(solution)/shard_map/all_to_all | solution.py:97
  68.2 0.1 fusion.15
  68.3 4.2 %collective-permute-start.2 = (f32[1,8,128]{2,1,0:T(8,128)S(1)}, f32[1,8,128]{2,1,0:T(8,128)S(1)}, u32[]{:S(2)}, u32[]{:S(2)}) collective-permute-start(f32[1,8,128]{2,1,0:T(8,128)S(1)} %slice.122), channel_id=1, source_target_pairs={{0,1},{1,2},{2,3},{3,4},{4,5},{5,6},{6,7},{7,8},{8,9},{9,10},{10,1... | collective-permute-start | bytes 12296 | tf_op jit(solution)/shard_map/ppermute | solution.py:20
  72.5 3.4 %collective-permute-start.3 = (f32[4,1,128]{2,1,0:T(1,128)S(1)}, f32[4,1,128]{2,1,0:T(1,128)S(1)}, u32[]{:S(2)}, u32[]{:S(2)}) collective-permute-start(f32[4,1,128]{2,1,0:T(1,128)S(1)} %slice.125), channel_id=1, source_target_pairs={{0,32},{32,64},{64,96},{96,128},{128,160},{160,192},{192,224},{224... | collective-permute-start | bytes 6152 | tf_op jit(solution)/shard_map/ppermute | solution.py:20
  75.9 2.3 %all-to-all-done.2 = f32[16,32,128]{2,1,0:T(8,128)S(1)} async-done(((f32[16,32,128]{2,1,0:T(8,128)}), f32[16,32,128]{2,1,0:T(8,128)S(1)}, u32[]{:S(2)}, u32[]{:S(2)}) %all-to-all-start.2) | async-done | bytes 262176 | tf_op jit(solution)/shard_map/all_to_all | solution.py:97
  78.3 0.1 convert_bitcast_fusion
  78.4 14.6 %all_to_all.30 = bf16[16,32,128]{2,1,0:T(8,128)(2,1)S(1)} all-to-all(bf16[16,32,128]{2,1,0:T(8,128)(2,1)S(1)} %broadcast_in_dim.123), channel_id=1, replica_groups=mesh['ray'=16,'mp'=32] {'ray'}, dimensions={0} | all-to-all | bytes 262144 | tf_op jit(solution)/shard_map/all_to_all | solution.py:26
  93.0 0.7 gather_fusion.1
  93.8 3.4 %fusion.4 = f32[16,1,128,1]{2,1,3,0:T(1,128)S(1)} fusion(bf16[16,8,128,128]{3,2,1,0:T(8,128)(2,1)} %param.15, bf16[16,8,128,1]{2,1,0,3:T(8,128)(2,1)S(1)} %bitcast.111), kind=kOutput, calls=%fused_computation.8 | convolution fusion | flops 4194304 | bytes 4235264 | tf_op jit(solution)/shard_map/rsij,rsj->ri/dot_general | solution.py:32
  97.1 0.7 broadcast_in_dim.124
  97.9 6.4 %all-to-all-start.4 = ((f32[32,16,128]{2,1,0:T(8,128)}), f32[32,16,128]{2,1,0:T(8,128)S(1)}, u32[]{:S(2)}, u32[]{:S(2)}) async-start(f32[32,16,128]{2,1,0:T(8,128)} %broadcast_in_dim.124), calls=%async_computation.4 | async-start | bytes 524288 | tf_op jit(solution)/shard_map/all_to_all | solution.py:26
  104.3 2.1 %collective-permute-start.4 = (f32[1,8,128]{2,1,0:T(8,128)S(1)}, f32[1,8,128]{2,1,0:T(8,128)S(1)}, u32[]{:S(2)}, u32[]{:S(2)}) collective-permute-start(f32[1,8,128]{2,1,0:T(8,128)S(1)} %slice.130), channel_id=1, source_target_pairs={{1,0},{2,1},{3,2},{4,3},{5,4},{6,5},{7,6},{8,7},{9,8},{10,9},{11,1... | collective-permute-start | bytes 12296 | tf_op jit(solution)/shard_map/ppermute | solution.py:20
  106.4 1.3 collective-permute-start.5
  107.8 3.2 %collective-permute-done.5 = f32[4,1,128]{2,1,0:T(1,128)S(1)} collective-permute-done((f32[4,1,128]{2,1,0:T(1,128)S(1)}, f32[4,1,128]{2,1,0:T(1,128)S(1)}, u32[]{:S(2)}, u32[]{:S(2)}) %collective-permute-start.5) | collective-permute-done | bytes 2080 | tf_op jit(solution)/shard_map/ppermute | solution.py:20
  111.1 2.7 %collective-permute-done.4 = f32[1,8,128]{2,1,0:T(8,128)S(1)} collective-permute-done((f32[1,8,128]{2,1,0:T(8,128)S(1)}, f32[1,8,128]{2,1,0:T(8,128)S(1)}, u32[]{:S(2)}, u32[]{:S(2)}) %collective-permute-start.4) | collective-permute-done | bytes 4128 | tf_op jit(solution)/shard_map/ppermute | solution.py:20
  113.7 0.1 fusion.23
  113.8 5.8 %all-to-all-done.4 = f32[32,16,128]{2,1,0:T(8,128)S(1)} async-done(((f32[32,16,128]{2,1,0:T(8,128)}), f32[32,16,128]{2,1,0:T(8,128)S(1)}, u32[]{:S(2)}, u32[]{:S(2)}) %all-to-all-start.4) | async-done | bytes 262176 | tf_op jit(solution)/shard_map/all_to_all | solution.py:26
  119.6 0.7 convert_bitcast_fusion.2
  120.3 2.8 %fusion.36 = f32[16,1,8,128]{3,1,2,0:T(1,128)S(1)} fusion(bf16[16,8,128,128]{3,2,1,0:T(8,128)(2,1)} %param.15, bf16[16,128,1,1]{1,0,2,3:T(8,128)(2,1)S(1)} %get-tuple-element.24), kind=kOutput, calls=%fused_computation.70 | convolution fusion | flops 4194304 | bytes 4263936 | tf_op jit(solution)/shard_map/rsij,ri->rsj/dot_general | solution.py:36
  123.2 1.7 %scatter_custom_fusion.1 = f32[512,128]{1,0:T(8,128)} fusion(s32[128]{0:T(128)S(1)} %reshape.100, f32[128,128]{1,0:T(8,128)S(1)} %bitcast.117, f32[]{:T(128)} %constant.68.clone.1), kind=kCustom, calls=%fused_computation.4 | custom fusion | flops 16384 | bytes 262148 | tf_op jit(solution)/shard_map/scatter-add | solution.py:94
  124.8 3.5 %all-to-all-start.5 = ((f32[16,32,128]{2,1,0:T(8,128)}), f32[16,32,128]{2,1,0:T(8,128)S(1)}, u32[]{:S(2)}, u32[]{:S(2)}) async-start(f32[16,32,128]{2,1,0:T(8,128)} %bitcast.33), calls=%async_computation.5 | async-start | bytes 524288 | tf_op jit(solution)/shard_map/all_to_all | solution.py:97
  128.4 0.6 fusion.51
  129.0 0.1 fusion.10
  129.1 4.2 %collective-permute-start.6 = (f32[1,8,128]{2,1,0:T(8,128)S(1)}, f32[1,8,128]{2,1,0:T(8,128)S(1)}, u32[]{:S(2)}, u32[]{:S(2)}) collective-permute-start(f32[1,8,128]{2,1,0:T(8,128)S(1)} %slice.135), channel_id=1, source_target_pairs={{0,1},{1,2},{2,3},{3,4},{4,5},{5,6},{6,7},{7,8},{8,9},{9,10},{10,1... | collective-permute-start | bytes 12296 | tf_op jit(solution)/shard_map/ppermute | solution.py:20
  133.3 3.4 %collective-permute-start.7 = (f32[4,1,128]{2,1,0:T(1,128)S(1)}, f32[4,1,128]{2,1,0:T(1,128)S(1)}, u32[]{:S(2)}, u32[]{:S(2)}) collective-permute-start(f32[4,1,128]{2,1,0:T(1,128)S(1)} %slice.138), channel_id=1, source_target_pairs={{0,32},{32,64},{64,96},{96,128},{128,160},{160,192},{192,224},{224... | collective-permute-start | bytes 6152 | tf_op jit(solution)/shard_map/ppermute | solution.py:20
  136.8 1.7 %all-to-all-done.5 = f32[16,32,128]{2,1,0:T(8,128)S(1)} async-done(((f32[16,32,128]{2,1,0:T(8,128)}), f32[16,32,128]{2,1,0:T(8,128)S(1)}, u32[]{:S(2)}, u32[]{:S(2)}) %all-to-all-start.5) | async-done | bytes 262176 | tf_op jit(solution)/shard_map/all_to_all | solution.py:97
  138.5 0.7 fusion.30
  (46 shorter events, 0.5 us)
Async XLA Ops:
  0.6 44.4 %copy-start.1 = (f32[3,4,8,128]{3,2,1,0:T(8,128)S(1)}, f32[3,4,8,128]{3,2,1,0:T(8,128)}, u32[]{:S(2)}) copy-start(f32[3,4,8,128]{3,2,1,0:T(8,128)} %param.12) | copy-start | bytes 147460
  0.6 59.4 %copy-start.3 = (f32[16,128]{1,0:T(8,128)S(1)}, f32[16,128]{1,0:T(8,128)}, u32[]{:S(2)}) copy-start(f32[16,128]{1,0:T(8,128)} %param.13) | copy-start | bytes 24580
  0.7 59.4 %copy-start.4 = (f32[16,128]{1,0:T(8,128)S(1)}, f32[16,128]{1,0:T(8,128)}, u32[]{:S(2)}) copy-start(f32[16,128]{1,0:T(8,128)} %param.14) | copy-start | bytes 24580
  1.4 43.5 %collective-permute-start = (f32[1,8,128]{2,1,0:T(8,128)S(1)}, f32[1,8,128]{2,1,0:T(8,128)S(1)}, u32[]{:S(2)}, u32[]{:S(2)}) collective-permute-start(f32[1,8,128]{2,1,0:T(8,128)S(1)} %slice.117), channel_id=1, source_target_pairs={{1,0},{2,1},{3,2},{4,3},{5,4},{6,5},{7,6},{8,7},{9,8},{10,9},{11,1... | collective-permute-start | bytes 12296 | tf_op jit(solution)/shard_map/ppermute | solution.py:20
  10.2 34.7 %collective-permute-start.1 = (f32[4,1,128]{2,1,0:T(1,128)S(1)}, f32[4,1,128]{2,1,0:T(1,128)S(1)}, u32[]{:S(2)}, u32[]{:S(2)}) collective-permute-start(f32[4,1,128]{2,1,0:T(1,128)S(1)} %slice.119), channel_id=1, source_target_pairs={{32,0},{64,32},{96,64},{128,96},{160,128},{192,160},{224,192},{256... | collective-permute-start | bytes 6152 | tf_op jit(solution)/shard_map/ppermute | solution.py:20
  12.2 13.6 %all-to-all-start = ((bf16[16,32,128]{2,1,0:T(8,128)(2,1)}), bf16[16,32,128]{2,1,0:T(8,128)(2,1)S(1)}, u32[]{:S(2)}, u32[]{:S(2)}) async-start(bf16[16,32,128]{2,1,0:T(8,128)(2,1)} %broadcast_in_dim.115), calls=%async_computation | async-start | bytes 262144 | tf_op jit(solution)/shard_map/all_to_all | solution.py:26
  29.8 48.5 %copy-start.2 = (f32[4,8,128]{2,1,0:T(8,128)S(1)}, f32[4,8,128]{2,1,0:T(8,128)}, u32[]{:S(2)}) copy-start(f32[4,8,128]{2,1,0:T(8,128)} %param.10) | copy-start | bytes 49156
  30.6 29.4 %all-to-all-start.1 = ((f32[32,16,128]{2,1,0:T(8,128)}), f32[32,16,128]{2,1,0:T(8,128)S(1)}, u32[]{:S(2)}, u32[]{:S(2)}) async-start(f32[32,16,128]{2,1,0:T(8,128)} %broadcast_in_dim.117), calls=%async_computation.1 | async-start | bytes 524288 | tf_op jit(solution)/shard_map/all_to_all | solution.py:26
  64.6 13.6 %all-to-all-start.2 = ((f32[16,32,128]{2,1,0:T(8,128)}), f32[16,32,128]{2,1,0:T(8,128)S(1)}, u32[]{:S(2)}, u32[]{:S(2)}) async-start(f32[16,32,128]{2,1,0:T(8,128)} %bitcast.11), calls=%async_computation.2 | async-start | bytes 524288 | tf_op jit(solution)/shard_map/all_to_all | solution.py:97
  68.3 10.0 %collective-permute-start.2 = (f32[1,8,128]{2,1,0:T(8,128)S(1)}, f32[1,8,128]{2,1,0:T(8,128)S(1)}, u32[]{:S(2)}, u32[]{:S(2)}) collective-permute-start(f32[1,8,128]{2,1,0:T(8,128)S(1)} %slice.122), channel_id=1, source_target_pairs={{0,1},{1,2},{2,3},{3,4},{4,5},{5,6},{6,7},{7,8},{8,9},{9,10},{10,1... | collective-permute-start | bytes 12296 | tf_op jit(solution)/shard_map/ppermute | solution.py:20
  72.5 5.8 %collective-permute-start.3 = (f32[4,1,128]{2,1,0:T(1,128)S(1)}, f32[4,1,128]{2,1,0:T(1,128)S(1)}, u32[]{:S(2)}, u32[]{:S(2)}) collective-permute-start(f32[4,1,128]{2,1,0:T(1,128)S(1)} %slice.125), channel_id=1, source_target_pairs={{0,32},{32,64},{64,96},{96,128},{128,160},{160,192},{192,224},{224... | collective-permute-start | bytes 6152 | tf_op jit(solution)/shard_map/ppermute | solution.py:20
  78.4 44.7 %copy-start = (f32[4,8,128]{2,1,0:T(8,128)}, f32[4,8,128]{2,1,0:T(8,128)S(1)}, u32[]{:S(2)}) copy-start(f32[4,8,128]{2,1,0:T(8,128)S(1)} %get-tuple-element.10) | copy-start | bytes 49156
  97.9 21.7 %all-to-all-start.4 = ((f32[32,16,128]{2,1,0:T(8,128)}), f32[32,16,128]{2,1,0:T(8,128)S(1)}, u32[]{:S(2)}, u32[]{:S(2)}) async-start(f32[32,16,128]{2,1,0:T(8,128)} %broadcast_in_dim.124), calls=%async_computation.4 | async-start | bytes 524288 | tf_op jit(solution)/shard_map/all_to_all | solution.py:26
  104.3 9.4 %collective-permute-start.4 = (f32[1,8,128]{2,1,0:T(8,128)S(1)}, f32[1,8,128]{2,1,0:T(8,128)S(1)}, u32[]{:S(2)}, u32[]{:S(2)}) collective-permute-start(f32[1,8,128]{2,1,0:T(8,128)S(1)} %slice.130), channel_id=1, source_target_pairs={{1,0},{2,1},{3,2},{4,3},{5,4},{6,5},{7,6},{8,7},{9,8},{10,9},{11,1... | collective-permute-start | bytes 12296 | tf_op jit(solution)/shard_map/ppermute | solution.py:20
  106.4 4.6 %collective-permute-start.5 = (f32[4,1,128]{2,1,0:T(1,128)S(1)}, f32[4,1,128]{2,1,0:T(1,128)S(1)}, u32[]{:S(2)}, u32[]{:S(2)}) collective-permute-start(f32[4,1,128]{2,1,0:T(1,128)S(1)} %slice.132), channel_id=1, source_target_pairs={{32,0},{64,32},{96,64},{128,96},{160,128},{192,160},{224,192},{256... | collective-permute-start | bytes 6152 | tf_op jit(solution)/shard_map/ppermute | solution.py:20
  124.8 13.6 %all-to-all-start.5 = ((f32[16,32,128]{2,1,0:T(8,128)}), f32[16,32,128]{2,1,0:T(8,128)S(1)}, u32[]{:S(2)}, u32[]{:S(2)}) async-start(f32[16,32,128]{2,1,0:T(8,128)} %bitcast.33), calls=%async_computation.5 | async-start | bytes 524288 | tf_op jit(solution)/shard_map/all_to_all | solution.py:97
  129.1 9.4 %collective-permute-start.6 = (f32[1,8,128]{2,1,0:T(8,128)S(1)}, f32[1,8,128]{2,1,0:T(8,128)S(1)}, u32[]{:S(2)}, u32[]{:S(2)}) collective-permute-start(f32[1,8,128]{2,1,0:T(8,128)S(1)} %slice.135), channel_id=1, source_target_pairs={{0,1},{1,2},{2,3},{3,4},{4,5},{5,6},{6,7},{7,8},{8,9},{9,10},{10,1... | collective-permute-start | bytes 12296 | tf_op jit(solution)/shard_map/ppermute | solution.py:20
  133.3 5.2 %collective-permute-start.7 = (f32[4,1,128]{2,1,0:T(1,128)S(1)}, f32[4,1,128]{2,1,0:T(1,128)S(1)}, u32[]{:S(2)}, u32[]{:S(2)}) collective-permute-start(f32[4,1,128]{2,1,0:T(1,128)S(1)} %slice.138), channel_id=1, source_target_pairs={{0,32},{32,64},{64,96},{96,128},{128,160},{160,192},{192,224},{224... | collective-permute-start | bytes 6152 | tf_op jit(solution)/shard_map/ppermute | solution.py:20

commit v2 on v0

--- a/solution.py
+++ b/solution.py
@@ -1,17 +1,33 @@
+import functools
+
 import jax
 import jax.numpy as jnp
 from jax import lax
+from jax.experimental import pallas as pl
+from jax.experimental.pallas import tpu as pltpu
 from jax.sharding import PartitionSpec as P
 
+TILE = 128
+GX = 4
+GY = 8
 RB_DEV = 16
-ITERS = 2
+CAP = 8
 MAXSEL = 8
-
+N_RAY = 16
+N_MP = 32
+OWN = GX * GY
+ALL = N_RAY * OWN
+PRODUCTS = MAXSEL * CAP
+SENT = OWN + 16
 
 primal_step = 0.5
 dual_step = 0.5
 tv_step = 0.25
 tv_weight = 0.3
+extrapolation = 2.0 * RB_DEV / (MAXSEL + 1)
+
+F32 = jnp.float32
+BF16 = jnp.bfloat16
 
 
 def shifted(block, axis, distance):
@@ -20,19 +36,185 @@
     return lax.ppermute(block, axis, route)
 
 
-def ray_work(blocks, rays, traveltimes, tiles, pattern, flags):
-    used, cols, y_rows, t_rows = (tiles, pattern, rays, traveltimes)
-    taken = flags.astype(jnp.float32)[:, None]
-    cells = blocks[cols]
-    partial_value = jnp.einsum("rsij,rsj->ri", used, cells, preferred_element_type=jnp.float32)
-    predicted = lax.psum(partial_value, "mp")
-    fresh = (y_rows + dual_step * (predicted - t_rows)) / (1.0 + dual_step)
-    change = taken * (fresh - y_rows)
-    contrib = jnp.einsum(
-        "rsij,ri->rsj", used, change.astype(jnp.bfloat16), preferred_element_type=jnp.float32
-    )
-    rays = rays + change
-    return (rays, contrib, cols)
+def exchange(copies, axis):
+    return lax.all_to_all(copies, axis, 0, 0, tiled=True)
+
+
+def block_number(pattern):
+    row = pattern & (GY * N_RAY - 1)
+    plane = pattern // (GY * N_RAY)
+    return (row // GY) * OWN + plane * GY + (row & (GY - 1))
+
+
+def list_selected(selected_ref, step, list_ref):
+    for n in range(MAXSEL):
+        list_ref[n] = 0
+    count = jnp.int32(0)
+    for r in range(RB_DEV):
+        list_ref[count] = jnp.int32(r)
+        count = count + selected_ref[step, r]
+    return count
+
+
+def forward(table_ref, pattern_ref, tiles_ref, list_ref):
+    sub = lax.broadcasted_iota(jnp.int32, (MAXSEL, TILE), 0)
+    total = jnp.zeros((MAXSEL, TILE), F32)
+    for n in range(MAXSEL):
+        r = list_ref[n]
+        cells = []
+        for s in range(CAP):
+            b = block_number(pattern_ref[r, s])
+            row = table_ref[pl.ds(b, 1), :]
+            cells.append(jnp.where(sub == n, row, 0.0).astype(BF16))
+        for s in range(CAP):
+            total = total + lax.dot_general(
+                cells[s], tiles_ref[r, s], (((1,), (1,)), ((), ())), preferred_element_type=F32
+            )
+    return total
+
+
+def first_kernel(slowness_ref, bar_ref, pattern_ref, selected_ref, field_ref, sent_ref, list_ref):
+    field = slowness_ref[...] - primal_step * bar_ref[...]
+    field_ref[...] = field
+    rounded = field.reshape(OWN, TILE).astype(BF16)
+    list_selected(selected_ref, 0, list_ref)
+    lane = lax.broadcasted_iota(jnp.int32, (16, TILE), 1)
+    sub = lax.broadcasted_iota(jnp.int32, (16, TILE), 0)
+    numbers = jnp.zeros((16, TILE), jnp.int32)
+    for n in range(MAXSEL):
+        r = list_ref[n]
+        for s in range(CAP):
+            b = block_number(pattern_ref[r, s])
+            numbers = jnp.where((lane & (PRODUCTS - 1)) == n * CAP + s, b, numbers)
+    numbers = jnp.where(sub == 0, numbers // OWN, numbers & (OWN - 1))
+    numbers = numbers.astype(F32).astype(BF16)
+    for p in range(N_RAY):
+        sent_ref[p, 0:OWN, :] = rounded
+        sent_ref[p, OWN:SENT, :] = numbers
+
+
+def predict_kernel(gathered_ref, tiles_ref, pattern_ref, selected_ref, out_ref, table_ref, list_ref):
+    list_selected(selected_ref, 0, list_ref)
+    for p in range(N_RAY):
+        table_ref[p * OWN : (p + 1) * OWN, :] = gathered_ref[p, 0:OWN, :].astype(F32)
+    total = forward(table_ref, pattern_ref, tiles_ref, list_ref)
+    for m in range(N_MP):
+        out_ref[m] = total
+
+
+def dual_update(parts_ref, rays_ref, times_ref, new_rays_ref, list_ref, count):
+    predicted = parts_ref[0]
+    for m in range(1, N_MP):
+        predicted = predicted + parts_ref[m]
+    rays = jnp.concatenate([rays_ref[pl.ds(list_ref[n], 1), :] for n in range(MAXSEL)], axis=0)
+    times = jnp.concatenate([times_ref[pl.ds(list_ref[n], 1), :] for n in range(MAXSEL)], axis=0)
+    fresh = (rays + dual_step * (predicted - times)) / (1.0 + dual_step)
+    sub = lax.broadcasted_iota(jnp.int32, (MAXSEL, TILE), 0)
+    change = jnp.where(sub < count, fresh - rays, 0.0)
+    new_rays_ref[...] = rays_ref[...]
+    for n in range(MAXSEL):
+        r = list_ref[n]
+        new_rays_ref[pl.ds(r, 1), :] = new_rays_ref[pl.ds(r, 1), :] + change[n : n + 1]
+    return change
+
+
+def products(change, tiles_ref, list_ref, n):
+    sub = lax.broadcasted_iota(jnp.int32, (CAP, TILE), 0)
+    row = change[n : n + 1]
+    r = list_ref[n]
+    total = jnp.zeros((CAP, TILE), F32)
+    for s in range(CAP):
+        lhs = jnp.where(sub == s, row, 0.0).astype(BF16)
+        total = total + lax.dot_general(
+            lhs, tiles_ref[r, s], (((1,), (0,)), ((), ())), preferred_element_type=F32
+        )
+    return total
+
+
+def back_share_kernel(
+    parts_ref, rays_ref, times_ref, tiles_ref, selected_ref, rest_ref, new_rays_ref, out_ref, list_ref
+):
+    count = list_selected(selected_ref, 0, list_ref)
+    change = dual_update(parts_ref, rays_ref, times_ref, new_rays_ref, list_ref, count)
+    for n in range(0, MAXSEL, 2):
+        pair = jnp.concatenate(
+            [products(change, tiles_ref, list_ref, n), products(change, tiles_ref, list_ref, n + 1)]
+        ).astype(BF16)
+        for p in range(N_RAY):
+            out_ref[p, n * CAP : (n + 2) * CAP, :] = pair
+    rest = rest_ref[...]
+    for p in range(N_RAY):
+        out_ref[p, PRODUCTS : PRODUCTS + OWN, :] = rest
+
+
+def image_kernel(
+    shared_ref, gathered_ref, tiles_ref, pattern_ref, selected_ref, me_ref, back_ref, out_ref, table_ref, list_ref
+):
+    list_selected(selected_ref, 1, list_ref)
+    lane = lax.broadcasted_iota(jnp.int32, (1, TILE), 1)
+    pairs = []
+    for p in range(N_RAY):
+        rows = gathered_ref[p, OWN:SENT, :].astype(F32)
+        pairs.append(rows[0:1] * OWN + rows[1:2])
+    pairs = [jnp.where(lane < PRODUCTS, pairs[p], pairs[p + 1]) for p in range(0, N_RAY, 2)]
+    group = 4
+    numbers = []
+    terms = []
+    for g in range(0, N_RAY, group):
+        numbers.append(jnp.concatenate([pairs[g // 2], pairs[g // 2 + 1]], axis=1).astype(jnp.int32))
+        terms.append(jnp.concatenate([shared_ref[p, 0:PRODUCTS, :] for p in range(g, g + group)], axis=0))
+    chunk = group * OWN
+    me = me_ref[0]
+    place = lax.broadcasted_iota(jnp.int32, (chunk, group * PRODUCTS), 0)
+    for g in range(0, N_RAY, group):
+        back = jnp.zeros((chunk, TILE), F32)
+        for k in range(N_RAY // group):
+            hot = jnp.where(place + g * OWN == numbers[k], 1.0, 0.0).astype(BF16)
+            back = back + lax.dot_general(
+                hot, terms[k], (((1,), (0,)), ((), ())), preferred_element_type=F32
+            )
+        table_ref[g * OWN : g * OWN + chunk, :] = back
+    back_ref[...] = table_ref[pl.ds(pl.multiple_of(me * OWN, OWN), OWN), :]
+    for p in range(N_RAY):
+        rows = slice(p * OWN, (p + 1) * OWN)
+        before = gathered_ref[p, 0:OWN, :].astype(F32)
+        rest = shared_ref[p, PRODUCTS : PRODUCTS + OWN, :].astype(F32)
+        field = before + (rest - (primal_step * (1.0 + extrapolation)) * table_ref[rows, :])
+        table_ref[rows, :] = field.astype(BF16).astype(F32)
+    total = forward(table_ref, pattern_ref, tiles_ref, list_ref)
+    for m in range(N_MP):
+        out_ref[m] = total
+
+
+def back_kernel(
+    parts_ref, rays_ref, times_ref, tiles_ref, pattern_ref, selected_ref, new_rays_ref, out_ref, table_ref, list_ref
+):
+    count = list_selected(selected_ref, 1, list_ref)
+    change = dual_update(parts_ref, rays_ref, times_ref, new_rays_ref, list_ref, count)
+    table_ref[...] = jnp.zeros_like(table_ref)
+    for n in range(MAXSEL):
+        r = list_ref[n]
+        total = products(change, tiles_ref, list_ref, n)
+        for s in range(CAP):
+            b = block_number(pattern_ref[r, s])
+            table_ref[pl.ds(b, 1), :] = table_ref[pl.ds(b, 1), :] + total[s : s + 1]
+    for p in range(N_RAY):
+        out_ref[p] = table_ref[p * OWN : (p + 1) * OWN, :].astype(BF16)
+
+
+def call(kernel, outs, places, *args):
+    spaces = {"v": pltpu.VMEM, "s": pltpu.SMEM}
+    scratch = [pltpu.SMEM((RB_DEV,), jnp.int32)]
+    if kernel in (predict_kernel, image_kernel, back_kernel):
+        scratch = [pltpu.VMEM((ALL, TILE), F32)] + scratch
+    return pl.pallas_call(
+        kernel,
+        out_shape=[jax.ShapeDtypeStruct(shape, dtype) for shape, dtype in outs],
+        in_specs=[pl.BlockSpec(memory_space=spaces[c]) for c in places],
+        out_specs=[pl.BlockSpec(memory_space=pltpu.VMEM) for _ in outs],
+        scratch_shapes=scratch,
+        compiler_params=pltpu.CompilerParams(vmem_limit_bytes=24 * 1024 * 1024),
+    )(*args)
 
 
 def total_variation(field, dual):
@@ -75,23 +257,47 @@
 def on_device(
     slowness, accumulated, extrapolated, tv_dual, ray_dual, traveltimes, tiles, pattern, selected
 ):
-    extrapolation = 2.0 * RB_DEV / (MAXSEL + 1)
-    field, image, image_bar, dual = (slowness, accumulated, extrapolated, tv_dual)
-    rays = ray_dual
-    for step in range(ITERS):
-        field = field - primal_step * image_bar
-        rounded = field.astype(jnp.bfloat16)
-        blocks = lax.all_gather(rounded, "ray", axis=1, tiled=True)
-        blocks = blocks.reshape(-1, blocks.shape[2])
-        rays, contrib, cols = ray_work(blocks, rays, traveltimes, tiles, pattern, selected[step])
-        summed = jax.ops.segment_sum(
-            contrib.reshape(-1, contrib.shape[2]), cols.reshape(-1), num_segments=blocks.shape[0]
-        )
-        wide = summed.reshape(field.shape[0], -1, field.shape[2])
-        back = lax.psum_scatter(wide, "ray", scatter_dimension=1, tiled=True)
-        dual, tv_back = total_variation(field, dual)
-        image = image + back + tv_back
-        image_bar = image + extrapolation * back + tv_back
+    grid = slowness.shape
+    me = lax.axis_index("ray").astype(jnp.int32).reshape(1)
+    sums = ((N_MP, MAXSEL, TILE), F32)
+    rays_out = (ray_dual.shape, F32)
+
+    field, sent = call(
+        first_kernel, [(grid, F32), ((N_RAY, SENT, TILE), BF16)], "vvss",
+        slowness, extrapolated, pattern, selected,
+    )
+    gathered = exchange(sent, "ray")
+    (partial_value,) = call(predict_kernel, [sums], "vvss", gathered, tiles, pattern, selected)
+    parts = exchange(partial_value, "mp")
+
+    dual, tv_back = total_variation(field, tv_dual)
+    base = field - primal_step * (accumulated + 2.0 * tv_back)
+    rest = (base - field.astype(BF16).astype(F32)).astype(BF16).reshape(OWN, TILE)
+
+    rays, share = call(
+        back_share_kernel, [rays_out, ((N_RAY, PRODUCTS + OWN, TILE), BF16)], "vvvvsv",
+        parts, ray_dual, traveltimes, tiles, selected, rest,
+    )
+    shared = exchange(share, "ray")
+    back, partial_value = call(
+        image_kernel, [((OWN, TILE), F32), sums], "vvvsss",
+        shared, gathered, tiles, pattern, selected, me,
+    )
+    parts = exchange(partial_value, "mp")
+
+    back = back.reshape(grid)
+    field = base - (primal_step * (1.0 + extrapolation)) * back
+    image = accumulated + back + tv_back
+    dual, tv_back = total_variation(field, dual)
+    image = image + tv_back
+
+    rays, share = call(
+        back_kernel, [rays_out, ((N_RAY, OWN, TILE), BF16)], "vvvvss",
+        parts, rays, traveltimes, tiles, pattern, selected,
+    )
+    back = jnp.sum(exchange(share, "ray").astype(F32), axis=0).reshape(grid)
+    image = image + back
+    image_bar = image + extrapolation * back + tv_back
     return (field, rays, dual, image, image_bar)
 
 

time: 475 us -> 141 us (0.30)
  the two profiles are of different devices: /device:TPU:16 before, /device:TPU:8 now
where the time goes in v2:
time: 141 us; the launch traced here: 140 us
  starting transfers between devices  64 us (45%)
  waiting for transfers between devices  28.1 us (20%)
  blocking collectives  21.9 us (16%)
  Pallas kernels  11.4 us (8%)
  local copies, waits for them, and re-layouts  10.3 us (7%)
  other arithmetic  3.43 us (2%)
    all_to_all x4, starting transfers between devices, exchange(): return lax.all_to_all(copies, axis, 0, 0, tiled=True)  40.2 us
    ppermute x8, starting transfers between devices, shifted(): return lax.ppermute(block, axis, route)  23.8 us
    all_to_all x1, blocking collectives, exchange(): return lax.all_to_all(copies, axis, 0, 0, tiled=True)  21.9 us
    all_to_all x4, waiting for transfers between devices, exchange(): return lax.all_to_all(copies, axis, 0, 0, tiled=True)  18.1 us
    pallas_call x5, Pallas kernels, call(): pl.pallas_call(kernel, out_shape=[jax.ShapeDtypeStruct(shape, dtype) for...  11.4 us
    unnamed x27, local copies, waits for them, and re-layouts  10.1 us
    ppermute x8, waiting for transfers between devices, shifted(): return lax.ppermute(block, axis, route)  10 us
  transfers between devices with their start and end apart: 12, of which 7 were waited for; matrix products, arithmetic and copies ran while one was open for 2% of the time, Pallas kernels for 0%

profile of v2, /device:TPU:8, one launch (start us, length us, event | category | flops | bytes accessed | tf_op | source)
XLA Modules:
  0.0 140.2 jit_solution(12965462973715352957)
XLA Ops:
  0.6 0.0 copy-start.7
  0.7 0.8 copy.14.pattern_ref
  1.4 0.7 copy-done.5
  2.1 0.7 copy-done.8
  2.8 0.7 copy-done.9
  3.5 2.0 %shard_map.128 = (f32[4,8,128]{2,1,0:T(8,128)S(1)}, bf16[16,48,128]{2,1,0:T(8,128)(2,1)}) custom-call(f32[4,8,128]{2,1,0:T(8,128)S(1)} %copy-done.8, f32[4,8,128]{2,1,0:T(8,128)S(1)} %copy-done.9, s32[16,8]{1,0:T(8,128)S(1)} %copy.14.pattern_ref, s32[2,16]{1,0:T(2,128)S(1)} %copy-done.5), custom_call_target="tpu_custom_call" | custom-call | tf_op jit(solution)/shard_map/pallas_call | solution.py:210
  5.5 9.8 %all-to-all-start = ((bf16[16,48,128]{2,1,0:T(8,128)(2,1)}), bf16[16,48,128]{2,1,0:T(8,128)(2,1)S(1)}, u32[]{:S(2)}, u32[]{:S(2)}) async-start(bf16[16,48,128]{2,1,0:T(8,128)(2,1)} %get-tuple-element.14), calls=%async_computation | async-start | bytes 393216 | tf_op jit(solution)/shard_map/all_to_all | solution.py:40
  15.4 1.3 collective-permute-start.1
  16.7 7.3 %collective-permute-start = (f32[1,8,128]{2,1,0:T(8,128)S(1)}, f32[1,8,128]{2,1,0:T(8,128)S(1)}, u32[]{:S(2)}, u32[]{:S(2)}) collective-permute-start(f32[1,8,128]{2,1,0:T(8,128)S(1)} %slice.79), channel_id=1, source_target_pairs={{1,0},{2,1},{3,2},{4,3},{5,4},{6,5},{7,6},{8,7},{9,8},{10,9},{11,1... | collective-permute-start | bytes 12296 | tf_op jit(solution)/shard_map/ppermute | solution.py:36
  24.0 0.1 slice.82
  24.1 1.2 collective-permute-done
  25.3 0.1 fusion.9
  25.3 0.8 multiply_reduce_fusion.1
  26.2 0.8 fusion.28
  27.0 0.0 copy-start
  27.0 2.2 %copy-done = bf16[16,8,128,128]{3,2,1,0:T(8,128)(2,1)S(1)} copy-done((bf16[16,8,128,128]{3,2,1,0:T(8,128)(2,1)S(1)}, bf16[16,8,128,128]{3,2,1,0:T(8,128)(2,1)}, u32[]{:S(2)}) %copy-start) | copy-done | bytes 4194328
  29.2 0.7 copy-done.6
  29.9 2.6 %shard_map.129 = f32[32,8,128]{2,1,0:T(8,128)} custom-call(bf16[16,48,128]{2,1,0:T(8,128)(2,1)S(1)} %all-to-all-done.gathered_ref, bf16[16,8,128,128]{3,2,1,0:T(8,128)(2,1)S(1)} %copy-done, s32[16,8]{1,0:T(8,128)S(1)} %copy.14.pattern_ref, s32[2,16]{1,0:T(2,128)S(1)} %copy-done.6), custom_call_target="tpu_custom_call" | custom-call | tf_op jit(solution)/shard_map/pallas_call | solution.py:210
  32.4 13.8 %all-to-all-start.1 = ((f32[32,8,128]{2,1,0:T(8,128)}), f32[32,8,128]{2,1,0:T(8,128)S(1)}, u32[]{:S(2)}, u32[]{:S(2)}) async-start(f32[32,8,128]{2,1,0:T(8,128)} %shard_map.129), calls=%async_computation.1 | async-start | bytes 262144 | tf_op jit(solution)/shard_map/all_to_all | solution.py:40
  46.2 0.1 fusion.7
  46.3 2.0 %collective-permute-start.2 = (f32[1,8,128]{2,1,0:T(8,128)S(1)}, f32[1,8,128]{2,1,0:T(8,128)S(1)}, u32[]{:S(2)}, u32[]{:S(2)}) collective-permute-start(f32[1,8,128]{2,1,0:T(8,128)S(1)} %slice.105), channel_id=1, source_target_pairs={{0,1},{1,2},{2,3},{3,4},{4,5},{5,6},{6,7},{7,8},{8,9},{9,10},{10,1... | collective-permute-start | bytes 12296 | tf_op jit(solution)/shard_map/ppermute | solution.py:36
  48.4 4.3 %collective-permute-start.3 = (f32[4,1,128]{2,1,0:T(1,128)S(1)}, f32[4,1,128]{2,1,0:T(1,128)S(1)}, u32[]{:S(2)}, u32[]{:S(2)}) collective-permute-start(f32[4,1,128]{2,1,0:T(1,128)S(1)} %slice.108), channel_id=1, source_target_pairs={{0,32},{32,64},{64,96},{96,128},{128,160},{160,192},{192,224},{224... | collective-permute-start | bytes 6152 | tf_op jit(solution)/shard_map/ppermute | solution.py:36
  52.6 1.3 collective-permute-done.3
  53.9 2.2 %collective-permute-done.2 = f32[1,8,128]{2,1,0:T(8,128)S(1)} collective-permute-done((f32[1,8,128]{2,1,0:T(8,128)S(1)}, f32[1,8,128]{2,1,0:T(8,128)S(1)}, u32[]{:S(2)}, u32[]{:S(2)}) %collective-permute-start.2) | collective-permute-done | bytes 4128 | tf_op jit(solution)/shard_map/ppermute | solution.py:36
  56.1 0.1 fusion.25
  56.2 2.9 %all-to-all-done.1.parts_ref = f32[32,8,128]{2,1,0:T(8,128)S(1)} async-done(((f32[32,8,128]{2,1,0:T(8,128)}), f32[32,8,128]{2,1,0:T(8,128)S(1)}, u32[]{:S(2)}, u32[]{:S(2)}) %all-to-all-start.1) | async-done | bytes 131104 | tf_op jit(solution)/shard_map/all_to_all | solution.py:40
  59.1 0.0 copy-start.1
  59.2 2.2 %copy-done.1 = bf16[16,8,128,128]{3,2,1,0:T(8,128)(2,1)S(1)} copy-done((bf16[16,8,128,128]{3,2,1,0:T(8,128)(2,1)S(1)}, bf16[16,8,128,128]{3,2,1,0:T(8,128)(2,1)}, u32[]{:S(2)}) %copy-start.1) | copy-done | bytes 4194328
  61.3 1.2 shard_map.130
  62.6 21.9 %all_to_all.25.shared_ref = bf16[16,96,128]{2,1,0:T(8,128)(2,1)S(1)} all-to-all(bf16[16,96,128]{2,1,0:T(8,128)(2,1)S(1)} %get-tuple-element.15), channel_id=1, replica_groups=mesh['ray'=16,'mp'=32] {'ray'}, dimensions={0} | all-to-all | bytes 786432 | tf_op jit(solution)/shard_map/all_to_all | solution.py:40
  84.4 3.4 %shard_map.131 = (f32[32,128]{1,0:T(8,128)S(1)}, f32[32,8,128]{2,1,0:T(8,128)}) custom-call(bf16[16,96,128]{2,1,0:T(8,128)(2,1)S(1)} %all_to_all.25.shared_ref, bf16[16,48,128]{2,1,0:T(8,128)(2,1)S(1)} %all-to-all-done.gathered_ref, bf16[16,8,128,128]{3,2,1,0:T(8,128)(2,1)S(1)} %copy-done.2, s32[16,8]{1,0:T(8,128)S(1)} %copy.14.pattern_ref, ...), custom_call_target="tpu_custom_call" | custom-call | tf_op jit(solution)/shard_map/pallas_call | solution.py:210
  87.9 0.0 copy-start.11
  87.9 1.9 %collective-permute-start.4 = (f32[1,8,128]{2,1,0:T(8,128)S(1)}, f32[1,8,128]{2,1,0:T(8,128)S(1)}, u32[]{:S(2)}, u32[]{:S(2)}) collective-permute-start(f32[1,8,128]{2,1,0:T(8,128)S(1)} %slice.113), channel_id=1, source_target_pairs={{1,0},{2,1},{3,2},{4,3},{5,4},{6,5},{7,6},{8,7},{9,8},{10,9},{11,1... | collective-permute-start | bytes 12296 | tf_op jit(solution)/shard_map/ppermute | solution.py:36
  89.8 1.3 collective-permute-start.5
  91.1 0.1 slice.116
  91.2 11.1 %all-to-all-start.3 = ((f32[32,8,128]{2,1,0:T(8,128)}), f32[32,8,128]{2,1,0:T(8,128)S(1)}, u32[]{:S(2)}, u32[]{:S(2)}) async-start(f32[32,8,128]{2,1,0:T(8,128)} %get-tuple-element.17), calls=%async_computation.3 | async-start | bytes 262144 | tf_op jit(solution)/shard_map/all_to_all | solution.py:40
  102.4 0.1 fusion.15
  102.5 12.8 %all-to-all-done.3.parts_ref = f32[32,8,128]{2,1,0:T(8,128)S(1)} async-done(((f32[32,8,128]{2,1,0:T(8,128)}), f32[32,8,128]{2,1,0:T(8,128)S(1)}, u32[]{:S(2)}, u32[]{:S(2)}) %all-to-all-start.3) | async-done | bytes 131104 | tf_op jit(solution)/shard_map/all_to_all | solution.py:40
  115.3 2.2 %copy-done.3 = bf16[16,8,128,128]{3,2,1,0:T(8,128)(2,1)S(1)} copy-done((bf16[16,8,128,128]{3,2,1,0:T(8,128)(2,1)S(1)}, bf16[16,8,128,128]{3,2,1,0:T(8,128)(2,1)}, u32[]{:S(2)}) %copy-start.3) | copy-done | bytes 4194328
  117.5 2.2 %shard_map.132 = (f32[16,128]{1,0:T(8,128)}, bf16[16,32,128]{2,1,0:T(8,128)(2,1)}) custom-call(f32[32,8,128]{2,1,0:T(8,128)S(1)} %all-to-all-done.3.parts_ref, f32[16,128]{1,0:T(8,128)S(1)} %get-tuple-element.18.rays_ref, f32[16,128]{1,0:T(8,128)S(1)} %copy-done.4, bf16[16,8,128,128]{3,2,1,0:T(8,128)(2,1)S(1)} %copy-done.3, s32[16,8]{1,0:T(8,128)S(1)} %copy.14.pattern_ref, ...), custom_call_target="tpu_custom_call" | custom-call | tf_op jit(solution)/shard_map/pallas_call | solution.py:210
  119.7 5.4 %all-to-all-start.4 = ((bf16[16,32,128]{2,1,0:T(8,128)(2,1)}), bf16[16,32,128]{2,1,0:T(8,128)(2,1)S(1)}, u32[]{:S(2)}, u32[]{:S(2)}) async-start(bf16[16,32,128]{2,1,0:T(8,128)(2,1)} %get-tuple-element.20), calls=%async_computation.4 | async-start | bytes 262144 | tf_op jit(solution)/shard_map/all_to_all | solution.py:40
  125.1 0.6 fusion.26
  125.8 0.1 fusion.2
  125.9 3.8 %collective-permute-start.7 = (f32[4,1,128]{2,1,0:T(1,128)S(1)}, f32[4,1,128]{2,1,0:T(1,128)S(1)}, u32[]{:S(2)}, u32[]{:S(2)}) collective-permute-start(f32[4,1,128]{2,1,0:T(1,128)S(1)} %slice.121), channel_id=1, source_target_pairs={{0,32},{32,64},{64,96},{96,128},{128,160},{160,192},{192,224},{224... | collective-permute-start | bytes 6152 | tf_op jit(solution)/shard_map/ppermute | solution.py:36
  129.7 1.9 %collective-permute-start.6 = (f32[1,8,128]{2,1,0:T(8,128)S(1)}, f32[1,8,128]{2,1,0:T(8,128)S(1)}, u32[]{:S(2)}, u32[]{:S(2)}) collective-permute-start(f32[1,8,128]{2,1,0:T(8,128)S(1)} %slice.118), channel_id=1, source_target_pairs={{0,1},{1,2},{2,3},{3,4},{4,5},{5,6},{6,7},{7,8},{8,9},{9,10},{10,1... | collective-permute-start | bytes 12296 | tf_op jit(solution)/shard_map/ppermute | solution.py:36
  131.6 2.4 %all-to-all-done.4 = bf16[16,32,128]{2,1,0:T(8,128)(2,1)S(1)} async-done(((bf16[16,32,128]{2,1,0:T(8,128)(2,1)}), bf16[16,32,128]{2,1,0:T(8,128)(2,1)S(1)}, u32[]{:S(2)}, u32[]{:S(2)}) %all-to-all-start.4) | async-done | bytes 131104 | tf_op jit(solution)/shard_map/all_to_all | solution.py:40
  134.1 5.4 %collective-permute-done.6 = f32[1,8,128]{2,1,0:T(8,128)S(1)} collective-permute-done((f32[1,8,128]{2,1,0:T(8,128)S(1)}, f32[1,8,128]{2,1,0:T(8,128)S(1)}, u32[]{:S(2)}, u32[]{:S(2)}) %collective-permute-start.6) | collective-permute-done | bytes 4128 | tf_op jit(solution)/shard_map/ppermute | solution.py:36
  139.5 0.7 fusion.21
  (42 shorter events, 0.2 us)
Async XLA Ops:
  0.6 58.5 %copy-start.7 = (s32[2,16]{1,0:T(2,128)S(1)}, s32[2,16]{1,0:T(2,128)}, u32[]{:S(2)}) copy-start(s32[2,16]{1,0:T(2,128)} %selected_ref.9) | copy-start | bytes 388
  0.6 58.5 %copy-start.4 = (f32[16,128]{1,0:T(8,128)S(1)}, f32[16,128]{1,0:T(8,128)}, u32[]{:S(2)}) copy-start(f32[16,128]{1,0:T(8,128)} %times_ref.3) | copy-start | bytes 24580
  1.4 0.7 copy-start.5
  2.1 0.7 copy-start.8
  2.8 0.7 copy-start.9
  3.5 52.6 %copy-start.12 = (f32[4,8,128]{2,1,0:T(8,128)S(1)}, f32[4,8,128]{2,1,0:T(8,128)}, u32[]{:S(2)}) copy-start(f32[4,8,128]{2,1,0:T(8,128)} %param.10) | copy-start | bytes 49156
  3.5 55.6 %copy-start.10 = (f32[16,128]{1,0:T(8,128)S(1)}, f32[16,128]{1,0:T(8,128)}, u32[]{:S(2)}) copy-start(f32[16,128]{1,0:T(8,128)} %rays_ref.1) | copy-start | bytes 24580
  5.5 21.5 %all-to-all-start = ((bf16[16,48,128]{2,1,0:T(8,128)(2,1)}), bf16[16,48,128]{2,1,0:T(8,128)(2,1)S(1)}, u32[]{:S(2)}, u32[]{:S(2)}) async-start(bf16[16,48,128]{2,1,0:T(8,128)(2,1)} %get-tuple-element.14), calls=%async_computation | async-start | bytes 393216 | tf_op jit(solution)/shard_map/all_to_all | solution.py:40
  15.4 8.7 %collective-permute-start.1 = (f32[4,1,128]{2,1,0:T(1,128)S(1)}, f32[4,1,128]{2,1,0:T(1,128)S(1)}, u32[]{:S(2)}, u32[]{:S(2)}) collective-permute-start(f32[4,1,128]{2,1,0:T(1,128)S(1)} %slice.81), channel_id=1, source_target_pairs={{32,0},{64,32},{96,64},{128,96},{160,128},{192,160},{224,192},{256... | collective-permute-start | bytes 6152 | tf_op jit(solution)/shard_map/ppermute | solution.py:36
  16.7 8.6 %collective-permute-start = (f32[1,8,128]{2,1,0:T(8,128)S(1)}, f32[1,8,128]{2,1,0:T(8,128)S(1)}, u32[]{:S(2)}, u32[]{:S(2)}) collective-permute-start(f32[1,8,128]{2,1,0:T(8,128)S(1)} %slice.79), channel_id=1, source_target_pairs={{1,0},{2,1},{3,2},{4,3},{5,4},{6,5},{7,6},{8,7},{9,8},{10,9},{11,1... | collective-permute-start | bytes 12296 | tf_op jit(solution)/shard_map/ppermute | solution.py:36
  27.0 2.2 %copy-start = (bf16[16,8,128,128]{3,2,1,0:T(8,128)(2,1)S(1)}, bf16[16,8,128,128]{3,2,1,0:T(8,128)(2,1)}, u32[]{:S(2)}) copy-start(bf16[16,8,128,128]{3,2,1,0:T(8,128)(2,1)} %tiles_ref.7) | copy-start | bytes 12582916
  29.2 0.7 copy-start.6
  32.4 26.7 %all-to-all-start.1 = ((f32[32,8,128]{2,1,0:T(8,128)}), f32[32,8,128]{2,1,0:T(8,128)S(1)}, u32[]{:S(2)}, u32[]{:S(2)}) async-start(f32[32,8,128]{2,1,0:T(8,128)} %shard_map.129), calls=%async_computation.1 | async-start | bytes 262144 | tf_op jit(solution)/shard_map/all_to_all | solution.py:40
  46.3 9.8 %collective-permute-start.2 = (f32[1,8,128]{2,1,0:T(8,128)S(1)}, f32[1,8,128]{2,1,0:T(8,128)S(1)}, u32[]{:S(2)}, u32[]{:S(2)}) collective-permute-start(f32[1,8,128]{2,1,0:T(8,128)S(1)} %slice.105), channel_id=1, source_target_pairs={{0,1},{1,2},{2,3},{3,4},{4,5},{5,6},{6,7},{7,8},{8,9},{9,10},{10,1... | collective-permute-start | bytes 12296 | tf_op jit(solution)/shard_map/ppermute | solution.py:36
  48.4 5.6 %collective-permute-start.3 = (f32[4,1,128]{2,1,0:T(1,128)S(1)}, f32[4,1,128]{2,1,0:T(1,128)S(1)}, u32[]{:S(2)}, u32[]{:S(2)}) collective-permute-start(f32[4,1,128]{2,1,0:T(1,128)S(1)} %slice.108), channel_id=1, source_target_pairs={{0,32},{32,64},{64,96},{96,128},{128,160},{160,192},{192,224},{224... | collective-permute-start | bytes 6152 | tf_op jit(solution)/shard_map/ppermute | solution.py:36
  59.1 2.2 %copy-start.1 = (bf16[16,8,128,128]{3,2,1,0:T(8,128)(2,1)S(1)}, bf16[16,8,128,128]{3,2,1,0:T(8,128)(2,1)}, u32[]{:S(2)}) copy-start(bf16[16,8,128,128]{3,2,1,0:T(8,128)(2,1)} %tiles_ref.7) | copy-start | bytes 12582916
  61.3 23.1 %copy-start.2 = (bf16[16,8,128,128]{3,2,1,0:T(8,128)(2,1)S(1)}, bf16[16,8,128,128]{3,2,1,0:T(8,128)(2,1)}, u32[]{:S(2)}) copy-start(bf16[16,8,128,128]{3,2,1,0:T(8,128)(2,1)} %tiles_ref.7) | copy-start | bytes 12582916
  87.9 52.3 %copy-start.11 = (f32[4,8,128]{2,1,0:T(8,128)}, f32[4,8,128]{2,1,0:T(8,128)S(1)}, u32[]{:S(2)}) copy-start(f32[4,8,128]{2,1,0:T(8,128)S(1)} %fusion.22) | copy-start | bytes 49156
  87.9 14.5 %collective-permute-start.4 = (f32[1,8,128]{2,1,0:T(8,128)S(1)}, f32[1,8,128]{2,1,0:T(8,128)S(1)}, u32[]{:S(2)}, u32[]{:S(2)}) collective-permute-start(f32[1,8,128]{2,1,0:T(8,128)S(1)} %slice.113), channel_id=1, source_target_pairs={{1,0},{2,1},{3,2},{4,3},{5,4},{6,5},{7,6},{8,7},{9,8},{10,9},{11,1... | collective-permute-start | bytes 12296 | tf_op jit(solution)/shard_map/ppermute | solution.py:36
  89.8 12.5 %collective-permute-start.5 = (f32[4,1,128]{2,1,0:T(1,128)S(1)}, f32[4,1,128]{2,1,0:T(1,128)S(1)}, u32[]{:S(2)}, u32[]{:S(2)}) collective-permute-start(f32[4,1,128]{2,1,0:T(1,128)S(1)} %slice.115), channel_id=1, source_target_pairs={{32,0},{64,32},{96,64},{128,96},{160,128},{192,160},{224,192},{256... | collective-permute-start | bytes 6152 | tf_op jit(solution)/shard_map/ppermute | solution.py:36
  91.2 24.1 %all-to-all-start.3 = ((f32[32,8,128]{2,1,0:T(8,128)}), f32[32,8,128]{2,1,0:T(8,128)S(1)}, u32[]{:S(2)}, u32[]{:S(2)}) async-start(f32[32,8,128]{2,1,0:T(8,128)} %get-tuple-element.17), calls=%async_computation.3 | async-start | bytes 262144 | tf_op jit(solution)/shard_map/all_to_all | solution.py:40
  115.3 2.2 %copy-start.3 = (bf16[16,8,128,128]{3,2,1,0:T(8,128)(2,1)S(1)}, bf16[16,8,128,128]{3,2,1,0:T(8,128)(2,1)}, u32[]{:S(2)}) copy-start(bf16[16,8,128,128]{3,2,1,0:T(8,128)(2,1)} %tiles_ref.7) | copy-start | bytes 12582916
  119.7 14.4 %all-to-all-start.4 = ((bf16[16,32,128]{2,1,0:T(8,128)(2,1)}), bf16[16,32,128]{2,1,0:T(8,128)(2,1)S(1)}, u32[]{:S(2)}, u32[]{:S(2)}) async-start(bf16[16,32,128]{2,1,0:T(8,128)(2,1)} %get-tuple-element.20), calls=%async_computation.4 | async-start | bytes 262144 | tf_op jit(solution)/shard_map/all_to_all | solution.py:40
  125.9 8.2 %collective-permute-start.7 = (f32[4,1,128]{2,1,0:T(1,128)S(1)}, f32[4,1,128]{2,1,0:T(1,128)S(1)}, u32[]{:S(2)}, u32[]{:S(2)}) collective-permute-start(f32[4,1,128]{2,1,0:T(1,128)S(1)} %slice.121), channel_id=1, source_target_pairs={{0,32},{32,64},{64,96},{96,128},{128,160},{160,192},{192,224},{224... | collective-permute-start | bytes 6152 | tf_op jit(solution)/shard_map/ppermute | solution.py:36
  129.7 9.8 %collective-permute-start.6 = (f32[1,8,128]{2,1,0:T(8,128)S(1)}, f32[1,8,128]{2,1,0:T(8,128)S(1)}, u32[]{:S(2)}, u32[]{:S(2)}) collective-permute-start(f32[1,8,128]{2,1,0:T(8,128)S(1)} %slice.118), channel_id=1, source_target_pairs={{0,1},{1,2},{2,3},{3,4},{4,5},{5,6},{6,7},{7,8},{8,9},{9,10},{10,1... | collective-permute-start | bytes 12296 | tf_op jit(solution)/shard_map/ppermute | solution.py:36

commit v3 on v2

v3 whole, which is shorter than its diff:
```python
import jax
import jax.numpy as jnp
from jax import lax
from jax.experimental import pallas as pl
from jax.experimental.pallas import tpu as pltpu
from jax.sharding import PartitionSpec as P

TILE = 128
GX = 4
GY = 8
RB_DEV = 16
CAP = 8
MAXSEL = 8
N_RAY = 16
N_MP = 32
OWN = GX * GY
ALL = N_RAY * OWN
PRODUCTS = MAXSEL * CAP
SENT = OWN + 16

primal_step = 0.5
dual_step = 0.5
tv_step = 0.25
tv_weight = 0.3
extrapolation = 2.0 * RB_DEV / (MAXSEL + 1)
gain = primal_step * (1.0 + extrapolation)

F32 = jnp.float32
BF16 = jnp.bfloat16
GRID = (GX, GY, TILE)
SUMS = ((N_MP, MAXSEL, TILE), F32)
RAYS = ((RB_DEV, TILE), F32)


def exchange(copies, axis):
    return lax.all_to_all(copies, axis, 0, 0, tiled=True)


def call(kernel, outs, places, args, scratch=(), busy=0):
    spaces = {"v": pltpu.VMEM, "h": pltpu.HBM}
    cost = pl.CostEstimate(flops=0, bytes_accessed=busy, transcendentals=0) if busy else None
    return pl.pallas_call(
        kernel,
        out_shape=[jax.ShapeDtypeStruct(shape, dtype) for shape, dtype in outs],
        in_specs=[pl.BlockSpec(memory_space=spaces[c]) for c in places],
        out_specs=[pl.BlockSpec(memory_space=pltpu.VMEM) for _ in outs],
        scratch_shapes=list(scratch),
        cost_estimate=cost,
        compiler_params=pltpu.CompilerParams(vmem_limit_bytes=20 * 1024 * 1024),
    )(*args)


SCALARS = (
    pltpu.SMEM((CAP, RB_DEV), jnp.int32),
    pltpu.SMEM((2, RB_DEV), jnp.int32),
    pltpu.SMEM((RB_DEV,), jnp.int32),
    pltpu.SemaphoreType.DMA((2,)),
)


def scalar_copies(pattern_hbm, selected_hbm, pattern_ref, selected_ref, sems):
    return [
        pltpu.make_async_copy(pattern_hbm, pattern_ref, sems.at[0]),
        pltpu.make_async_copy(selected_hbm, selected_ref, sems.at[1]),
    ]


def block_number(pattern):
    row = pattern & (GY * N_RAY - 1)
    plane = lax.shift_right_logical(pattern, 7)
    return lax.shift_right_logical(row, 3) * OWN + plane * GY + (row & (GY - 1))


def list_selected(selected_ref, step, list_ref):
    for n in range(MAXSEL):
        list_ref[n] = jnp.int32(0)
    count = jnp.int32(0)
    for r in range(RB_DEV):
        list_ref[count] = jnp.int32(r)
        count = count + selected_ref[step, r]
    return count


def start_kernel(
    slowness_hbm, bar_hbm, pattern_hbm, selected_hbm, field_ref, sent_ref,
    slowness_ref, bar_ref, sems, pattern_ref, selected_ref, list_ref, scalar_sems,
):
    copies = scalar_copies(pattern_hbm, selected_hbm, pattern_ref, selected_ref, scalar_sems)
    copies.append(pltpu.make_async_copy(slowness_hbm, slowness_ref, sems.at[0]))
    copies.append(pltpu.make_async_copy(bar_hbm, bar_ref, sems.at[1]))
    for copy in copies:
        copy.start()
    copies[0].wait()
    copies[1].wait()
    list_selected(selected_ref, 0, list_ref)
    lane = lax.broadcasted_iota(jnp.int32, (16, TILE), 1) & (PRODUCTS - 1)
    sub = lax.broadcasted_iota(jnp.int32, (16, TILE), 0)
    numbers = jnp.zeros((16, TILE), jnp.int32)
    for n in range(MAXSEL):
        r = list_ref[n]
        for s in range(CAP):
            numbers = jnp.where(lane == n * CAP + s, block_number(pattern_ref[s, r]), numbers)
    numbers = jnp.where(sub == 0, lax.shift_right_logical(numbers, 5), numbers & (OWN - 1))
    numbers = numbers.astype(F32).astype(BF16)
    copies[2].wait()
    copies[3].wait()
    field = slowness_ref[...] - primal_step * bar_ref[...]
    field_ref[...] = field
    rounded = field.reshape(OWN, TILE).astype(BF16)
    for p in range(N_RAY):
        sent_ref[p, 0:OWN, :] = rounded
        sent_ref[p, OWN:SENT, :] = numbers


def fetch_kernel(step):
    def kernel(
        tiles_hbm, pattern_hbm, selected_hbm, after_ref, picked_ref, hot_ref, pick_ref,
        pattern_ref, selected_ref, list_ref, scalar_sems, sems,
    ):
        for copy in scalar_copies(pattern_hbm, selected_hbm, pattern_ref, selected_ref, scalar_sems):
            copy.start()
            copy.wait()
        count = list_selected(selected_ref, step, list_ref)
        copies = [
            pltpu.make_async_copy(tiles_hbm.at[list_ref[n]], picked_ref.at[n], sems.at[n])
            for n in range(MAXSEL)
        ]
        for copy in copies:
            copy.start()
        sub = lax.broadcasted_iota(jnp.int32, (MAXSEL, TILE), 0)
        lane = lax.broadcasted_iota(jnp.int32, (2 * CAP, TILE), 1)
        for n in range(0, MAXSEL, 2):
            halves = []
            for m in (n, n + 1):
                r = list_ref[m]
                numbers = jnp.zeros((CAP, TILE), jnp.int32)
                for s in range(CAP):
                    numbers = jnp.where(sub == s, block_number(pattern_ref[s, r]), numbers)
                halves.append(numbers)
            numbers = jnp.concatenate(halves, axis=0)
            for c in range(ALL // TILE):
                hot = jnp.where(numbers == lane + c * TILE, 1.0, 0.0).astype(BF16)
                hot_ref[n * CAP : (n + 2) * CAP, c * TILE : (c + 1) * TILE] = hot
        listed = jnp.full((MAXSEL, TILE), RB_DEV, jnp.int32)
        for n in range(MAXSEL):
            listed = jnp.where((sub == n) & (sub < count), list_ref[n], listed)
        for r in range(RB_DEV):
            pick_ref[r] = jnp.where(listed == r, 1.0, 0.0)
        for copy in copies:
            copy.wait()

    return kernel


def fetch(step, tiles, pattern, selected, after):
    outs = [
        ((MAXSEL, CAP, TILE, TILE), BF16),
        ((PRODUCTS, ALL), BF16),
        ((RB_DEV, MAXSEL, TILE), F32),
    ]
    scratch = SCALARS + (pltpu.SemaphoreType.DMA((MAXSEL,)),)
    return call(
        fetch_kernel(step), outs, "hhhh", (tiles, pattern, selected, after), scratch, 8 * 2**20
    )


def forward(hot_ref, blocks, picked_ref, out_ref):
    cells = jnp.dot(hot_ref[...], blocks, preferred_element_type=F32)
    sub = lax.broadcasted_iota(jnp.int32, (MAXSEL, TILE), 0)
    total = jnp.zeros((MAXSEL, TILE), F32)
    for n in range(MAXSEL):
        for s in range(CAP):
            row = cells[n * CAP + s : n * CAP + s + 1]
            lhs = jnp.where(sub == n, row, 0.0).astype(BF16)
            total = total + lax.dot_general(
                lhs, picked_ref[n, s], (((1,), (1,)), ((), ())), preferred_element_type=F32
            )
    for m in range(N_MP):
        out_ref[m] = total


def predict_kernel(gathered_ref, picked_ref, hot_ref, out_ref):
    blocks = jnp.concatenate([gathered_ref[p, 0:OWN, :] for p in range(N_RAY)], axis=0)
    forward(hot_ref, blocks, picked_ref, out_ref)


def dual_update(parts_ref, rays_ref, times_ref, pick_ref, new_rays_ref):
    predicted = parts_ref[0]
    for m in range(1, N_MP):
        predicted = predicted + parts_ref[m]
    rays = jnp.zeros((MAXSEL, TILE), F32)
    times = jnp.zeros((MAXSEL, TILE), F32)
    taken = jnp.zeros((MAXSEL, TILE), F32)
    for r in range(RB_DEV):
        pick = pick_ref[r]
        rays = rays + pick * rays_ref[r : r + 1, :]
        times = times + pick * times_ref[r : r + 1, :]
        taken = taken + pick
    fresh = (rays + dual_step * (predicted - times)) / (1.0 + dual_step)
    change = taken * (fresh - rays)
    for r in range(RB_DEV):
        new_rays_ref[r : r + 1, :] = rays_ref[r : r + 1, :] + jnp.sum(
            pick_ref[r] * change, axis=0, keepdims=True
        )
    return change


def products(change, picked_ref, n):
    sub = lax.broadcasted_iota(jnp.int32, (CAP, TILE), 0)
    row = change[n : n + 1]
    total = jnp.zeros((CAP, TILE), F32)
    for s in range(CAP):
        lhs = jnp.where(sub == s, row, 0.0).astype(BF16)
        total = total + jnp.dot(lhs, picked_ref[n, s], preferred_element_type=F32)
    return total


def share_kernel(
    parts_ref, rays_ref, times_ref, pick_ref, picked_ref, rest_ref, new_rays_ref, out_ref
):
    change = dual_update(parts_ref, rays_ref, times_ref, pick_ref, new_rays_ref)
    for n in range(0, MAXSEL, 2):
        pair = jnp.concatenate(
            [products(change, picked_ref, n), products(change, picked_ref, n + 1)], axis=0
        ).astype(BF16)
        for p in range(N_RAY):
            out_ref[p, n * CAP : (n + 2) * CAP, :] = pair
    rest = rest_ref[...]
    for p in range(N_RAY):
        out_ref[p, PRODUCTS : PRODUCTS + OWN, :] = rest


def image_kernel(
    shared_ref, gathered_ref, picked_ref, hot_ref, back_ref, edge_ref, out_ref, table_ref
):
    lane = lax.broadcasted_iota(jnp.int32, (1, TILE), 1)
    singles = []
    for p in range(N_RAY):
        rows = gathered_ref[p, OWN:SENT, :].astype(F32)
        singles.append(rows[0:1] * OWN + rows[1:2])
    pairs = [jnp.where(lane < PRODUCTS, singles[p], singles[p + 1]) for p in range(0, N_RAY, 2)]
    group = 4
    chunk = group * OWN
    numbers = []
    terms = []
    for g in range(0, N_RAY, group):
        numbers.append(jnp.concatenate(pairs[g // 2 : g // 2 + 2], axis=1).astype(jnp.int32))
        terms.append(
            jnp.concatenate([shared_ref[p, 0:PRODUCTS, :] for p in range(g, g + group)], axis=0)
        )
    place = lax.broadcasted_iota(jnp.int32, (chunk, group * PRODUCTS), 0)
    blocks = []
    for g in range(0, N_RAY, group):
        back = jnp.zeros((chunk, TILE), F32)
        for k in range(N_RAY // group):
            hot = jnp.where(place + g * OWN == numbers[k], 1.0, 0.0).astype(BF16)
            back = back + jnp.dot(hot, terms[k], preferred_element_type=F32)
        table_ref[g * OWN : g * OWN + chunk, :] = back
        before = jnp.concatenate([gathered_ref[p, 0:OWN, :] for p in range(g, g + group)], axis=0)
        rest = jnp.concatenate(
            [shared_ref[p, PRODUCTS : PRODUCTS + OWN, :] for p in range(g, g + group)], axis=0
        )
        blocks.append((before.astype(F32) + (rest.astype(F32) - gain * back)).astype(BF16))
    forward(hot_ref, jnp.concatenate(blocks, axis=0), picked_ref, out_ref)
    me = lax.axis_index("ray")
    back_ref[...] = table_ref[pl.ds(pl.multiple_of(me * OWN, OWN), OWN), :]
    for at, peer, row in ((0, jnp.maximum(me - 1, 0), GY - 1), (1, jnp.minimum(me + 1, N_RAY - 1), 0)):
        before = gathered_ref[peer, 0:OWN, :].astype(F32)
        rest = shared_ref[peer, PRODUCTS : PRODUCTS + OWN, :].astype(F32)
        back = table_ref[pl.ds(pl.multiple_of(peer * OWN, OWN), OWN), :]
        field = before + (rest - gain * back)
        for x in range(GX):
            edge_ref[at * GX + x : at * GX + x + 1, :] = field[x * GY + row : x * GY + row + 1]


def back_kernel(
    parts_ref, rays_ref, times_ref, pick_ref, picked_ref, hot_ref, new_rays_ref, out_ref
):
    change = dual_update(parts_ref, rays_ref, times_ref, pick_ref, new_rays_ref)
    terms = jnp.concatenate([products(change, picked_ref, n) for n in range(MAXSEL)], axis=0)
    high = terms.astype(BF16)
    low = (terms - high.astype(F32)).astype(BF16)
    turned = (((0,), (0,)), ((), ()))
    image = lax.dot_general(hot_ref[...], high, turned, preferred_element_type=F32)
    image = image + lax.dot_general(hot_ref[...], low, turned, preferred_element_type=F32)
    for p in range(N_RAY):
        out_ref[p] = image[p * OWN : (p + 1) * OWN].astype(BF16)


def x_swaps(far, near):
    far_route = [(m, m + 1) for m in range(1, N_MP - 1, 2)]
    near_route = [(m, m + 1) for m in range(0, N_MP - 1, 2)]
    far = lax.ppermute(far, "mp", far_route + [(b, a) for a, b in far_route])
    near = lax.ppermute(near, "mp", near_route + [(b, a) for a, b in near_route])
    return far, near


def first_edges_kernel(field_ref, dual_ref, far_ref, near_ref):
    odd = (lax.axis_index("mp") & 1) == 1
    first = field_ref[0]
    last = field_ref[GX - 1]
    far_ref[0:GY] = jnp.where(odd, last, first)
    near_ref[0:GY] = jnp.where(odd, first, last)
    for c in range(3):
        rows = slice((c + 1) * GY, (c + 2) * GY)
        far_ref[rows] = dual_ref[c, GX - 1]
        near_ref[rows] = dual_ref[c, GX - 1]


def x_halos(far_ref, near_ref):
    odd = (lax.axis_index("mp") & 1) == 1
    far, near = far_ref[...], near_ref[...]
    return jnp.where(odd, near, far), jnp.where(odd, far, near)


def row_edges_kernel(field_ref, dual_ref, far_ref, near_ref, after_ref, up_ref, down_ref):
    before, behind = x_halos(far_ref, near_ref)
    up_ref[...] = jnp.zeros_like(up_ref)
    down_ref[...] = jnp.zeros_like(down_ref)
    up_ref[GX : GX + 1] = before[0:1]
    down_ref[GX : GX + 1] = behind[GY - 1 : GY]
    for x in range(GX):
        up_ref[x : x + 1] = field_ref[x, 0:1]
        down_ref[x : x + 1] = field_ref[x, GY - 1 : GY]
        for c in range(3):
            at = 8 + c * GX + x
            down_ref[at : at + 1] = dual_ref[c, x, GY - 1 : GY]


def tv_cells(here, ahead_x, ahead_y, dual, no_x, no_y):
    lane = lax.broadcasted_iota(jnp.int32, here.shape, len(here.shape) - 1)
    ahead_z = pltpu.roll(here, TILE - 1, len(here.shape) - 1)
    steps = (
        jnp.where(no_x, 0.0, ahead_x - here),
        jnp.where(no_y, 0.0, ahead_y - here),
        jnp.where(lane == TILE - 1, 0.0, ahead_z - here),
    )
    moved = [d + tv_step * g for d, g in zip(dual, steps)]
    length = jnp.sqrt(moved[0] * moved[0] + moved[1] * moved[1] + moved[2] * moved[2])
    scale = jnp.maximum(1.0, length / tv_weight)
    fresh = [m / scale for m in moved]
    return fresh, [a - b for a, b in zip(fresh, dual)]


def up_one(plane, row):
    sub = lax.broadcasted_iota(jnp.int32, plane.shape, 0)
    return jnp.where(sub == GY - 1, row, pltpu.roll(plane, GY - 1, 0))


def tv_step_all(field, dual, before, before_next, dual_before, behind, corner, rows, dual_rows, next_rows):
    mp, ray = lax.axis_index("mp"), lax.axis_index("ray")
    sub = lax.broadcasted_iota(jnp.int32, (GY, TILE), 0)
    end_x = mp == N_MP - 1
    last_y = (sub == GY - 1) & (ray == N_RAY - 1)
    never = sub < 0
    lane = lax.broadcasted_iota(jnp.int32, (GY, TILE), 1)

    halo, halo_change = tv_cells(
        before, field[0], up_one(before, before_next), dual_before, never, last_y
    )
    from_x = jnp.where(mp == 0, 0.0, halo_change[0])
    fresh, backs, halo_rows = [], [], []
    for x in range(GX):
        ahead = field[x + 1] if x + 1 < GX else behind
        no_x = (end_x & (sub >= 0)) if x + 1 == GX else never
        new, change = tv_cells(
            field[x], ahead, up_one(field[x], next_rows[x]), [d[x] for d in dual], no_x, last_y
        )
        ahead_row = rows[x + 1] if x + 1 < GX else corner
        no_row = (end_x & (sub[0:1] >= 0)) if x + 1 == GX else never[0:1]
        new_row, row_change = tv_cells(
            rows[x], ahead_row, field[x][0:1], [d[x] for d in dual_rows], no_row, never[0:1]
        )
        from_y = jnp.where(ray == 0, 0.0, row_change[1])
        comp_x = jnp.where(no_x, 0.0, change[0])
        comp_y = jnp.where(last_y, 0.0, change[1])
        comp_z = jnp.where(lane == TILE - 1, 0.0, change[2])
        back = from_x - comp_x
        back = back + (jnp.where(sub == 0, from_y, pltpu.roll(comp_y, 1, 0)) - comp_y)
        back = back + (jnp.where(lane == 0, 0.0, pltpu.roll(comp_z, 1, 1)) - comp_z)
        from_x = comp_x
        fresh.append(new)
        backs.append(back)
        halo_rows.append(new_row)
    return fresh, backs, halo, halo_rows


def first_tv_kernel(
    field_ref, dual_ref, far_ref, near_ref, up_ref, down_ref, image_ref,
    new_dual_ref, plane_ref, row_ref, back_ref, base_ref, rest_ref,
):
    before, behind = x_halos(far_ref, near_ref)
    field = [field_ref[x] for x in range(GX)]
    dual = [[dual_ref[c, x] for x in range(GX)] for c in range(3)]
    up, down = up_ref[...], down_ref[...]
    rows = [down[x : x + 1] for x in range(GX)]
    dual_rows = [[down[8 + c * GX + x : 9 + c * GX + x] for x in range(GX)] for c in range(3)]
    fresh, backs, halo, halo_rows = tv_step_all(
        field, dual, before[0:GY], up[GX : GX + 1],
        [before[(c + 1) * GY : (c + 2) * GY] for c in range(3)],
        behind[0:GY], down[GX : GX + 1], rows, dual_rows, [up[x : x + 1] for x in range(GX)],
    )
    for x in range(GX):
        base = field[x] - primal_step * (image_ref[x] + 2.0 * backs[x])
        back_ref[x] = backs[x]
        base_ref[x] = base
        rest_ref[x] = base - field[x].astype(BF16).astype(F32)
        for c in range(3):
            new_dual_ref[c, x] = fresh[x][c]
            row_ref[c * GX + x : c * GX + x + 1] = halo_rows[x][c]
    for c in range(3):
        plane_ref[c] = halo[c]


def second_edges_kernel(base_ref, back_ref, edge_ref, image_ref, tv_ref, field_ref, new_image_ref, far_ref, near_ref):
    odd = (lax.axis_index("mp") & 1) == 1
    field = []
    for x in range(GX):
        back = back_ref[x * GY : (x + 1) * GY]
        field.append(base_ref[x] - gain * back)
        field_ref[x] = field[x]
        new_image_ref[x] = image_ref[x] + back + tv_ref[x]
    first = jnp.concatenate([field[0], edge_ref[...]], axis=0)
    last = jnp.concatenate([field[GX - 1], edge_ref[...]], axis=0)
    far_ref[...] = jnp.where(odd, last, first)
    near_ref[...] = jnp.where(odd, first, last)


def second_tv_kernel(
    field_ref, dual_ref, plane_ref, row_ref, far_ref, near_ref, edge_ref, new_dual_ref, back_ref
):
    before, behind = x_halos(far_ref, near_ref)
    edge = edge_ref[...]
    fresh, backs, _, _ = tv_step_all(
        [field_ref[x] for x in range(GX)],
        [[dual_ref[c, x] for x in range(GX)] for c in range(3)],
        before[0:GY], before[GY + 2 * GX - 1 : GY + 2 * GX],
        [plane_ref[c] for c in range(3)],
        behind[0:GY], behind[GY : GY + 1],
        [edge[x : x + 1] for x in range(GX)],
        [[row_ref[c * GX + x : c * GX + x + 1] for x in range(GX)] for c in range(3)],
        [edge[GX + x : GX + x + 1] for x in range(GX)],
    )
    for x in range(GX):
        back_ref[x] = backs[x]
        for c in range(3):
            new_dual_ref[c, x] = fresh[x][c]


def on_device(
    slowness, accumulated, extrapolated, tv_dual, ray_dual, traveltimes, tiles, pattern, selected
):
    pattern = pattern.T
    busy = 8 * 2**20
    grid = (GRID, F32)
    duals = ((3,) + GRID, F32)

    field, sent = call(
        start_kernel, [grid, ((N_RAY, SENT, TILE), BF16)], "hhhh",
        (slowness, extrapolated, pattern, selected),
        (pltpu.VMEM(GRID, F32), pltpu.VMEM(GRID, F32), pltpu.SemaphoreType.DMA((2,))) + SCALARS,
    )
    gathered = exchange(sent, "ray")
    far, near = call(
        first_edges_kernel, [((4 * GY, TILE), F32)] * 2, "vv", (field, tv_dual), busy=busy
    )
    far, near = x_swaps(far, near)
    picked, hot, pick = fetch(0, tiles, pattern, selected, field)
    (partial_value,) = call(predict_kernel, [SUMS], "vvv", (gathered, picked, hot))
    parts = exchange(partial_value, "mp")

    up, down = call(
        row_edges_kernel, [((8, TILE), F32), ((24, TILE), F32)], "vvvvh",
        (field, tv_dual, far, near, partial_value), busy=busy,
    )
    up = lax.ppermute(up, "ray", [(i + 1, i) for i in range(N_RAY - 1)])
    down = lax.ppermute(down, "ray", [(i, i + 1) for i in range(N_RAY - 1)])
    dual, dual_plane, dual_row, tv_back, base, rest = call(
        first_tv_kernel,
        [duals, ((3, GY, TILE), F32), ((3 * GX, TILE), F32), grid, grid, grid],
        "vvvvvvv", (field, tv_dual, far, near, up, down, accumulated), busy=busy,
    )
    picked_2, hot_2, pick_2 = fetch(1, tiles, pattern, selected, partial_value)

    rays, share = call(
        share_kernel, [RAYS, ((N_RAY, PRODUCTS + OWN, TILE), BF16)], "vvvvvv",
        (parts, ray_dual, traveltimes, pick, picked, rest.astype(BF16).reshape(OWN, TILE)),
    )
    shared = exchange(share, "ray")
    back, edge, partial_value = call(
        image_kernel, [((OWN, TILE), F32), ((2 * GX, TILE), F32), SUMS], "vvvv",
        (shared, gathered, picked_2, hot_2), (pltpu.VMEM((ALL, TILE), F32),),
    )
    parts = exchange(partial_value, "mp")

    field, image, far, near = call(
        second_edges_kernel, [grid, grid] + [((GY + 2 * GX, TILE), F32)] * 2, "vvvvv",
        (base, back, edge, accumulated, tv_back), busy=busy,
    )
    far, near = x_swaps(far, near)
    dual, tv_back = call(
        second_tv_kernel, [duals, grid], "vvvvvvv",
        (field, dual, dual_plane, dual_row, far, near, edge), busy=busy,
    )

    rays, share = call(
        back_kernel, [RAYS, ((N_RAY, OWN, TILE), BF16)], "vvvvvv",
        (parts, rays, traveltimes, pick_2, picked_2, hot_2),
    )
    back = jnp.sum(exchange(share, "ray").astype(F32), axis=0).reshape(GRID)
    image = image + back + tv_back
    image_bar = image + extrapolation * back + tv_back
    return (field, rays, dual, image, image_bar)


def solution(mesh):
    in_specs = (
        P("mp", "ray", None),
        P("mp", "ray", None),
        P("mp", "ray", None),
        P(None, "mp", "ray", None),
        P("ray", None),
        P("ray", None),
        P("ray", "mp", None, None),
        P("ray", "mp"),
        P(None, "ray"),
    )
    out_specs = (
        P("mp", "ray", None),
        P("ray", None),
        P(None, "mp", "ray", None),
        P("mp", "ray", None),
        P("mp", "ray", None),
    )
    return jax.shard_map(
        on_device, mesh=mesh, in_specs=in_specs, out_specs=out_specs, check_vma=False
    )
```

time: 141 us -> 125 us (0.89)
  the two profiles are of different devices: /device:TPU:8 before, /device:TPU:1 now
where the time goes in v3:
time: 125 us; the launch traced here: 124 us
  starting transfers between devices  54.4 us (44%)
  blocking collectives  27.7 us (22%)
  waiting for transfers between devices  17.3 us (14%)
  Pallas kernels  13.6 us (11%)
  local copies, waits for them, and re-layouts  9.28 us (7%)
    all_to_all x4, starting transfers between devices, exchange(): return lax.all_to_all(copies, axis, 0, 0, tiled=True)  35.8 us
    all_to_all x1, blocking collectives, exchange(): return lax.all_to_all(copies, axis, 0, 0, tiled=True)  27.7 us
    pallas_call x12, Pallas kernels, call(): pl.pallas_call(kernel, out_shape=[jax.ShapeDtypeStruct(shape, dtype) for...  13.6 us
    ppermute x2, starting transfers between devices, x_swaps(): far = lax.ppermute(far, 'mp', far_route + [(b, a) for a, b in far_route])  11.3 us
    all_to_all x4, waiting for transfers between devices, exchange(): return lax.all_to_all(copies, axis, 0, 0, tiled=True)  9.99 us
    unnamed x30, local copies, waits for them, and re-layouts  9.28 us
    ppermute x2, starting transfers between devices, x_swaps(): lax.ppermute(near, 'mp', near_route + [(b, a) for a, b in near_route])  3.84 us
    ppermute x2, waiting for transfers between devices, x_swaps(): far = lax.ppermute(far, 'mp', far_route + [(b, a) for a, b in far_route])  3.16 us
  transfers between devices with their start and end apart: 10, of which 6 were waited for; matrix products, arithmetic and copies ran while one was open for 0% of the time, Pallas kernels for 4%

profile of v3, /device:TPU:1, one launch (start us, length us, event | category | flops | bytes accessed | tf_op | source)
XLA Modules:
  0.0 123.7 jit_solution(9146020783517018566)
XLA Ops:
  0.6 0.0 copy-start.4
  0.6 0.7 copy-done.4
  1.3 0.7 copy-done.8
  2.0 0.7 copy-done.9
  2.8 0.7 copy-done.11
  3.4 1.6 %shard_map.128 = (f32[4,8,128]{2,1,0:T(8,128)S(1)}, bf16[16,48,128]{2,1,0:T(8,128)(2,1)}) custom-call(f32[4,8,128]{2,1,0:T(8,128)S(1)} %copy-done.8, f32[4,8,128]{2,1,0:T(8,128)S(1)} %copy-done.9, s32[8,16]{1,0:T(8,128)S(1)} %bitcast.13, s32[2,16]{1,0:T(2,128)S(1)} %copy-done.11), custom_call_target="tpu_custom_call" | custom-call | tf_op jit(solution)/shard_map/pallas_call | solution.py:42
  5.0 10.4 %all-to-all-start = ((bf16[16,48,128]{2,1,0:T(8,128)(2,1)}), bf16[16,48,128]{2,1,0:T(8,128)(2,1)S(1)}, u32[]{:S(2)}, u32[]{:S(2)}) async-start(bf16[16,48,128]{2,1,0:T(8,128)(2,1)} %get-tuple-element.39), calls=%async_computation | async-start | bytes 393216 | tf_op jit(solution)/shard_map/all_to_all | solution.py:36
  15.4 0.0 copy-start
  15.4 2.2 %copy-done = bf16[16,8,128,128]{3,2,1,0:T(8,128)(2,1)S(1)} copy-done((bf16[16,8,128,128]{3,2,1,0:T(8,128)(2,1)S(1)}, bf16[16,8,128,128]{3,2,1,0:T(8,128)(2,1)}, u32[]{:S(2)}) %copy-start) | copy-done | bytes 4194328
  17.6 0.7 copy-done.5
  18.3 0.7 copy-done.12
  19.0 1.6 %shard_map.130 = (bf16[8,8,128,128]{3,2,1,0:T(8,128)(2,1)S(1)}, bf16[64,512]{1,0:T(8,128)(2,1)S(1)}, f32[16,8,128]{2,1,0:T(8,128)S(1)}) custom-call(bf16[16,8,128,128]{3,2,1,0:T(8,128)(2,1)S(1)} %copy-done, s32[8,16]{1,0:T(8,128)S(1)} %bitcast.14, s32[2,16]{1,0:T(2,128)S(1)} %copy-done.12, f32[4,8,128]{2,1,0:T(8,128)S(1)} %get-tuple-element.36.field_ref.after_ref), custom_call_target="tpu_custom_call" | custom-call | bytes 8388608 | tf_op jit(solution)/shard_map/pallas_call | solution.py:42
  20.6 0.0 copy-start.2
  20.6 0.0 copy-start.3
  20.6 0.0 copy-start.7
  20.6 0.0 copy-start.14
  20.6 3.2 %all-to-all-done.gathered_ref = bf16[16,48,128]{2,1,0:T(8,128)(2,1)S(1)} async-done(((bf16[16,48,128]{2,1,0:T(8,128)(2,1)}), bf16[16,48,128]{2,1,0:T(8,128)(2,1)S(1)}, u32[]{:S(2)}, u32[]{:S(2)}) %all-to-all-start) | async-done | bytes 196640 | tf_op jit(solution)/shard_map/all_to_all | solution.py:36
  23.8 2.0 %shard_map.131.after_ref = f32[32,8,128]{2,1,0:T(8,128)} custom-call(bf16[16,48,128]{2,1,0:T(8,128)(2,1)S(1)} %all-to-all-done.gathered_ref, bf16[8,8,128,128]{3,2,1,0:T(8,128)(2,1)S(1)} %get-tuple-element.40.picked_ref, bf16[64,512]{1,0:T(8,128)(2,1)S(1)} %get-tuple-element.41.hot_ref), custom_call_target="tpu_custom_call" | custom-call | tf_op jit(solution)/shard_map/pallas_call | solution.py:42
  25.8 15.3 %all-to-all-start.1 = ((f32[32,8,128]{2,1,0:T(8,128)}), f32[32,8,128]{2,1,0:T(8,128)S(1)}, u32[]{:S(2)}, u32[]{:S(2)}) async-start(f32[32,8,128]{2,1,0:T(8,128)} %shard_map.131.after_ref), calls=%async_computation.1 | async-start | bytes 262144 | tf_op jit(solution)/shard_map/all_to_all | solution.py:36
  41.1 7.4 %collective-permute-start = (f32[32,128]{1,0:T(8,128)S(1)}, f32[32,128]{1,0:T(8,128)S(1)}, u32[]{:S(2)}, u32[]{:S(2)}) collective-permute-start(f32[32,128]{1,0:T(8,128)S(1)} %get-tuple-element.37), channel_id=1, source_target_pairs={{1,2},{3,4},{5,6},{7,8},{9,10},{11,12},{13,14},{15,16},{17,18},{19... | collective-permute-start | bytes 49160 | tf_op jit(solution)/shard_map/ppermute | solution.py:293
  48.6 1.9 %collective-permute-start.1 = (f32[32,128]{1,0:T(8,128)S(1)}, f32[32,128]{1,0:T(8,128)S(1)}, u32[]{:S(2)}, u32[]{:S(2)}) collective-permute-start(f32[32,128]{1,0:T(8,128)S(1)} %get-tuple-element.38), channel_id=1, source_target_pairs={{0,1},{2,3},{4,5},{6,7},{8,9},{10,11},{12,13},{14,15},{16,17},{18,... | collective-permute-start | bytes 49160 | tf_op jit(solution)/shard_map/ppermute | solution.py:294
  50.5 0.1 collective-permute-done.far_ref
  50.6 1.1 collective-permute-done.1.near_ref
  51.7 2.2 %collective-permute-start.3 = (f32[24,128]{1,0:T(8,128)S(1)}, f32[24,128]{1,0:T(8,128)S(1)}, u32[]{:S(2)}, u32[]{:S(2)}) collective-permute-start(f32[24,128]{1,0:T(8,128)S(1)} %get-tuple-element.43), channel_id=1, source_target_pairs={{0,32},{32,64},{64,96},{96,128},{128,160},{160,192},{192,224},{224... | collective-permute-start | bytes 36872 | tf_op jit(solution)/shard_map/ppermute | solution.py:477
  53.9 1.3 %collective-permute-start.2 = (f32[8,128]{1,0:T(8,128)S(1)}, f32[8,128]{1,0:T(8,128)S(1)}, u32[]{:S(2)}, u32[]{:S(2)}) collective-permute-start(f32[8,128]{1,0:T(8,128)S(1)} %get-tuple-element.42), channel_id=1, source_target_pairs={{32,0},{64,32},{96,64},{128,96},{160,128},{192,160},{224,192},{256... | collective-permute-start | bytes 12296 | tf_op jit(solution)/shard_map/ppermute | solution.py:476
  55.2 3.1 %collective-permute-done.2.up_ref = f32[8,128]{1,0:T(8,128)S(1)} collective-permute-done((f32[8,128]{1,0:T(8,128)S(1)}, f32[8,128]{1,0:T(8,128)S(1)}, u32[]{:S(2)}, u32[]{:S(2)}) %collective-permute-start.2) | collective-permute-done | bytes 4128 | tf_op jit(solution)/shard_map/ppermute | solution.py:476
  58.2 0.0 collective-permute-done.3.down_ref
  58.2 0.2 shard_map.133
  58.4 0.0 all-to-all-done.1.parts_ref
  58.5 1.5 %shard_map.134 = (f32[16,128]{1,0:T(8,128)S(1)}, bf16[16,96,128]{2,1,0:T(8,128)(2,1)}) custom-call(f32[32,8,128]{2,1,0:T(8,128)S(1)} %all-to-all-done.1.parts_ref, f32[16,128]{1,0:T(8,128)S(1)} %copy-done.14, f32[16,128]{1,0:T(8,128)S(1)} %copy-done.7, f32[16,8,128]{2,1,0:T(8,128)S(1)} %get-tuple-element.45.pick_ref, ...), custom_call_target="tpu_custom_call" | custom-call | tf_op jit(solution)/shard_map/pallas_call | solution.py:42
  59.9 6.4 %all-to-all-start.2 = ((bf16[16,96,128]{2,1,0:T(8,128)(2,1)}), bf16[16,96,128]{2,1,0:T(8,128)(2,1)S(1)}, u32[]{:S(2)}, u32[]{:S(2)}) async-start(bf16[16,96,128]{2,1,0:T(8,128)(2,1)} %get-tuple-element.47), calls=%async_computation.2 | async-start | bytes 786432 | tf_op jit(solution)/shard_map/all_to_all | solution.py:36
  66.3 0.0 copy-start.1
  66.3 2.2 %copy-done.1 = bf16[16,8,128,128]{3,2,1,0:T(8,128)(2,1)S(1)} copy-done((bf16[16,8,128,128]{3,2,1,0:T(8,128)(2,1)S(1)}, bf16[16,8,128,128]{3,2,1,0:T(8,128)(2,1)}, u32[]{:S(2)}) %copy-start.1) | copy-done | bytes 4194328
  68.5 1.6 %shard_map.135 = (bf16[8,8,128,128]{3,2,1,0:T(8,128)(2,1)S(1)}, bf16[64,512]{1,0:T(8,128)(2,1)S(1)}, f32[16,8,128]{2,1,0:T(8,128)S(1)}) custom-call(bf16[16,8,128,128]{3,2,1,0:T(8,128)(2,1)S(1)} %copy-done.1, s32[8,16]{1,0:T(8,128)S(1)} %bitcast.15, s32[2,16]{1,0:T(2,128)S(1)} %copy-done.13, f32[32,8,128]{2,1,0:T(8,128)} %shard_map.131.after_ref), custom_call_target="tpu_custom_call" | custom-call | bytes 8388608 | tf_op jit(solution)/shard_map/pallas_call | solution.py:42
  70.1 6.8 %all-to-all-done.2.shared_ref = bf16[16,96,128]{2,1,0:T(8,128)(2,1)S(1)} async-done(((bf16[16,96,128]{2,1,0:T(8,128)(2,1)}), bf16[16,96,128]{2,1,0:T(8,128)(2,1)S(1)}, u32[]{:S(2)}, u32[]{:S(2)}) %all-to-all-start.2) | async-done | bytes 393248 | tf_op jit(solution)/shard_map/all_to_all | solution.py:36
  77.0 2.2 %shard_map.136 = (f32[32,128]{1,0:T(8,128)S(1)}, f32[8,128]{1,0:T(8,128)S(1)}, f32[32,8,128]{2,1,0:T(8,128)S(1)}) custom-call(bf16[16,96,128]{2,1,0:T(8,128)(2,1)S(1)} %all-to-all-done.2.shared_ref, bf16[16,48,128]{2,1,0:T(8,128)(2,1)S(1)} %all-to-all-done.gathered_ref, bf16[8,8,128,128]{3,2,1,0:T(8,128)(2,1)S(1)} %get-tuple-element.48.picked_ref, ...), custom_call_target="tpu_custom_call" | custom-call | tf_op jit(solution)/shard_map/pallas_call | solution.py:42
  79.2 27.7 %all_to_all.25.parts_ref = f32[32,8,128]{2,1,0:T(8,128)S(1)} all-to-all(f32[32,8,128]{2,1,0:T(8,128)S(1)} %get-tuple-element.54), channel_id=1, replica_groups=mesh['ray'=16,'mp'=32] {'mp'}, dimensions={0} | all-to-all | bytes 262144 | tf_op jit(solution)/shard_map/all_to_all | solution.py:36
  106.9 1.5 %shard_map.138 = (f32[16,128]{1,0:T(8,128)}, bf16[16,32,128]{2,1,0:T(8,128)(2,1)}) custom-call(f32[32,8,128]{2,1,0:T(8,128)S(1)} %all_to_all.25.parts_ref, f32[16,128]{1,0:T(8,128)S(1)} %get-tuple-element.55.rays_ref, f32[16,128]{1,0:T(8,128)S(1)} %copy-done.7, f32[16,8,128]{2,1,0:T(8,128)S(1)} %get-tuple-element.56.pick_ref, ...), custom_call_target="tpu_custom_call" | custom-call | tf_op jit(solution)/shard_map/pallas_call | solution.py:42
  108.4 3.7 %all-to-all-start.4 = ((bf16[16,32,128]{2,1,0:T(8,128)(2,1)}), bf16[16,32,128]{2,1,0:T(8,128)(2,1)S(1)}, u32[]{:S(2)}, u32[]{:S(2)}) async-start(bf16[16,32,128]{2,1,0:T(8,128)(2,1)} %get-tuple-element.65), calls=%async_computation.4 | async-start | bytes 262144 | tf_op jit(solution)/shard_map/all_to_all | solution.py:36
  112.1 0.6 shard_map.137
  112.7 3.8 %collective-permute-start.4 = (f32[16,128]{1,0:T(8,128)S(1)}, f32[16,128]{1,0:T(8,128)S(1)}, u32[]{:S(2)}, u32[]{:S(2)}) collective-permute-start(f32[16,128]{1,0:T(8,128)S(1)} %get-tuple-element.61), channel_id=1, source_target_pairs={{1,2},{3,4},{5,6},{7,8},{9,10},{11,12},{13,14},{15,16},{17,18},{19... | collective-permute-start | bytes 24584 | tf_op jit(solution)/shard_map/ppermute | solution.py:293
  116.6 1.9 %collective-permute-start.5 = (f32[16,128]{1,0:T(8,128)S(1)}, f32[16,128]{1,0:T(8,128)S(1)}, u32[]{:S(2)}, u32[]{:S(2)}) collective-permute-start(f32[16,128]{1,0:T(8,128)S(1)} %get-tuple-element.62), channel_id=1, source_target_pairs={{0,1},{2,3},{4,5},{6,7},{8,9},{10,11},{12,13},{14,15},{16,17},{18,... | collective-permute-start | bytes 24584 | tf_op jit(solution)/shard_map/ppermute | solution.py:294
  118.5 3.1 %collective-permute-done.4.far_ref = f32[16,128]{1,0:T(8,128)S(1)} collective-permute-done((f32[16,128]{1,0:T(8,128)S(1)}, f32[16,128]{1,0:T(8,128)S(1)}, u32[]{:S(2)}, u32[]{:S(2)}) %collective-permute-start.4) | collective-permute-done | bytes 8224 | tf_op jit(solution)/shard_map/ppermute | solution.py:293
  121.6 0.0 collective-permute-done.5.near_ref
  121.6 0.7 copy-done.10
  122.3 0.7 shard_map.139
  123.0 0.0 all-to-all-done.4
  123.1 0.6 fusion.2
  (18 shorter events, 0.1 us)
Async XLA Ops:
  0.6 0.7 copy-start.4
  1.3 0.7 copy-start.8
  2.0 0.7 copy-start.9
  2.8 0.7 copy-start.11
  5.0 18.8 %all-to-all-start = ((bf16[16,48,128]{2,1,0:T(8,128)(2,1)}), bf16[16,48,128]{2,1,0:T(8,128)(2,1)S(1)}, u32[]{:S(2)}, u32[]{:S(2)}) async-start(bf16[16,48,128]{2,1,0:T(8,128)(2,1)} %get-tuple-element.39), calls=%async_computation | async-start | bytes 393216 | tf_op jit(solution)/shard_map/all_to_all | solution.py:36
  15.4 2.2 %copy-start = (bf16[16,8,128,128]{3,2,1,0:T(8,128)(2,1)S(1)}, bf16[16,8,128,128]{3,2,1,0:T(8,128)(2,1)}, u32[]{:S(2)}) copy-start(bf16[16,8,128,128]{3,2,1,0:T(8,128)(2,1)} %tiles_hbm.3) | copy-start | bytes 12582916
  17.6 0.7 copy-start.5
  18.3 0.7 copy-start.12
  20.6 20.5 %copy-start.2 = (f32[3,4,8,128]{3,2,1,0:T(8,128)S(1)}, f32[3,4,8,128]{3,2,1,0:T(8,128)}, u32[]{:S(2)}) copy-start(f32[3,4,8,128]{3,2,1,0:T(8,128)} %dual_ref.5) | copy-start | bytes 147460
  20.6 37.6 %copy-start.3 = (f32[4,8,128]{2,1,0:T(8,128)S(1)}, f32[4,8,128]{2,1,0:T(8,128)}, u32[]{:S(2)}) copy-start(f32[4,8,128]{2,1,0:T(8,128)} %image_ref.3) | copy-start | bytes 49156
  20.6 37.8 %copy-start.7 = (f32[16,128]{1,0:T(8,128)S(1)}, f32[16,128]{1,0:T(8,128)}, u32[]{:S(2)}) copy-start(f32[16,128]{1,0:T(8,128)} %times_ref.3) | copy-start | bytes 24580
  20.6 37.8 %copy-start.14 = (f32[16,128]{1,0:T(8,128)S(1)}, f32[16,128]{1,0:T(8,128)}, u32[]{:S(2)}) copy-start(f32[16,128]{1,0:T(8,128)} %rays_ref.1) | copy-start | bytes 24580
  25.8 40.5 %copy-start.6 = (s32[16,8]{0,1:T(8,128)S(1)}, s32[16,8]{0,1:T(8,128)}, u32[]{:S(2)}) copy-start(s32[16,8]{0,1:T(8,128)} %param.16) | copy-start | bytes 1540
  25.8 40.5 %copy-start.13 = (s32[2,16]{1,0:T(2,128)S(1)}, s32[2,16]{1,0:T(2,128)}, u32[]{:S(2)}) copy-start(s32[2,16]{1,0:T(2,128)} %selected_hbm.5) | copy-start | bytes 388
  25.8 32.6 %all-to-all-start.1 = ((f32[32,8,128]{2,1,0:T(8,128)}), f32[32,8,128]{2,1,0:T(8,128)S(1)}, u32[]{:S(2)}, u32[]{:S(2)}) async-start(f32[32,8,128]{2,1,0:T(8,128)} %shard_map.131.after_ref), calls=%async_computation.1 | async-start | bytes 262144 | tf_op jit(solution)/shard_map/all_to_all | solution.py:36
  41.1 9.4 %collective-permute-start = (f32[32,128]{1,0:T(8,128)S(1)}, f32[32,128]{1,0:T(8,128)S(1)}, u32[]{:S(2)}, u32[]{:S(2)}) collective-permute-start(f32[32,128]{1,0:T(8,128)S(1)} %get-tuple-element.37), channel_id=1, source_target_pairs={{1,2},{3,4},{5,6},{7,8},{9,10},{11,12},{13,14},{15,16},{17,18},{19... | collective-permute-start | bytes 49160 | tf_op jit(solution)/shard_map/ppermute | solution.py:293
  48.6 3.1 %collective-permute-start.1 = (f32[32,128]{1,0:T(8,128)S(1)}, f32[32,128]{1,0:T(8,128)S(1)}, u32[]{:S(2)}, u32[]{:S(2)}) collective-permute-start(f32[32,128]{1,0:T(8,128)S(1)} %get-tuple-element.38), channel_id=1, source_target_pairs={{0,1},{2,3},{4,5},{6,7},{8,9},{10,11},{12,13},{14,15},{16,17},{18,... | collective-permute-start | bytes 49160 | tf_op jit(solution)/shard_map/ppermute | solution.py:294
  51.7 6.6 %collective-permute-start.3 = (f32[24,128]{1,0:T(8,128)S(1)}, f32[24,128]{1,0:T(8,128)S(1)}, u32[]{:S(2)}, u32[]{:S(2)}) collective-permute-start(f32[24,128]{1,0:T(8,128)S(1)} %get-tuple-element.43), channel_id=1, source_target_pairs={{0,32},{32,64},{64,96},{96,128},{128,160},{160,192},{192,224},{224... | collective-permute-start | bytes 36872 | tf_op jit(solution)/shard_map/ppermute | solution.py:477
  53.9 4.4 %collective-permute-start.2 = (f32[8,128]{1,0:T(8,128)S(1)}, f32[8,128]{1,0:T(8,128)S(1)}, u32[]{:S(2)}, u32[]{:S(2)}) collective-permute-start(f32[8,128]{1,0:T(8,128)S(1)} %get-tuple-element.42), channel_id=1, source_target_pairs={{32,0},{64,32},{96,64},{128,96},{160,128},{192,160},{224,192},{256... | collective-permute-start | bytes 12296 | tf_op jit(solution)/shard_map/ppermute | solution.py:476
  59.9 17.0 %all-to-all-start.2 = ((bf16[16,96,128]{2,1,0:T(8,128)(2,1)}), bf16[16,96,128]{2,1,0:T(8,128)(2,1)S(1)}, u32[]{:S(2)}, u32[]{:S(2)}) async-start(bf16[16,96,128]{2,1,0:T(8,128)(2,1)} %get-tuple-element.47), calls=%async_computation.2 | async-start | bytes 786432 | tf_op jit(solution)/shard_map/all_to_all | solution.py:36
  66.3 2.2 %copy-start.1 = (bf16[16,8,128,128]{3,2,1,0:T(8,128)(2,1)S(1)}, bf16[16,8,128,128]{3,2,1,0:T(8,128)(2,1)}, u32[]{:S(2)}) copy-start(bf16[16,8,128,128]{3,2,1,0:T(8,128)(2,1)} %tiles_hbm.3) | copy-start | bytes 12582916
  108.4 14.6 %all-to-all-start.4 = ((bf16[16,32,128]{2,1,0:T(8,128)(2,1)}), bf16[16,32,128]{2,1,0:T(8,128)(2,1)S(1)}, u32[]{:S(2)}, u32[]{:S(2)}) async-start(bf16[16,32,128]{2,1,0:T(8,128)(2,1)} %get-tuple-element.65), calls=%async_computation.4 | async-start | bytes 262144 | tf_op jit(solution)/shard_map/all_to_all | solution.py:36
  112.7 8.9 %collective-permute-start.4 = (f32[16,128]{1,0:T(8,128)S(1)}, f32[16,128]{1,0:T(8,128)S(1)}, u32[]{:S(2)}, u32[]{:S(2)}) collective-permute-start(f32[16,128]{1,0:T(8,128)S(1)} %get-tuple-element.61), channel_id=1, source_target_pairs={{1,2},{3,4},{5,6},{7,8},{9,10},{11,12},{13,14},{15,16},{17,18},{19... | collective-permute-start | bytes 24584 | tf_op jit(solution)/shard_map/ppermute | solution.py:293
  116.6 5.0 %collective-permute-start.5 = (f32[16,128]{1,0:T(8,128)S(1)}, f32[16,128]{1,0:T(8,128)S(1)}, u32[]{:S(2)}, u32[]{:S(2)}) collective-permute-start(f32[16,128]{1,0:T(8,128)S(1)} %get-tuple-element.62), channel_id=1, source_target_pairs={{0,1},{2,3},{4,5},{6,7},{8,9},{10,11},{12,13},{14,15},{16,17},{18,... | collective-permute-start | bytes 24584 | tf_op jit(solution)/shard_map/ppermute | solution.py:294
  121.6 0.7 copy-start.10

commit v4 on v3

--- a/solution.py
+++ b/solution.py
@@ -36,12 +36,19 @@
     return lax.all_to_all(copies, axis, 0, 0, tiled=True)
 
 
-def call(kernel, outs, places, args, scratch=(), busy=0):
-    spaces = {"v": pltpu.VMEM, "h": pltpu.HBM}
+def call(kernel, outs, places, args, scratch=(), busy=0, keep=False):
+    spaces = {"v": pltpu.VMEM, "h": pltpu.HBM, "a": pl.ANY}
     cost = pl.CostEstimate(flops=0, bytes_accessed=busy, transcendentals=0) if busy else None
+    args = [
+        pltpu.with_memory_space_constraint(arg, pltpu.HBM) if place == "h" else arg
+        for arg, place in zip(args, places)
+    ]
     return pl.pallas_call(
         kernel,
-        out_shape=[jax.ShapeDtypeStruct(shape, dtype) for shape, dtype in outs],
+        out_shape=[
+            pltpu.VMEM(shape, dtype) if keep else jax.ShapeDtypeStruct(shape, dtype)
+            for shape, dtype in outs
+        ],
         in_specs=[pl.BlockSpec(memory_space=spaces[c]) for c in places],
         out_specs=[pl.BlockSpec(memory_space=pltpu.VMEM) for _ in outs],
         scratch_shapes=list(scratch),
@@ -82,12 +89,13 @@
 
 
 def start_kernel(
-    slowness_hbm, bar_hbm, pattern_hbm, selected_hbm, field_ref, sent_ref,
-    slowness_ref, bar_ref, sems, pattern_ref, selected_ref, list_ref, scalar_sems,
+    slowness_hbm, bar_hbm, dual_hbm, pattern_hbm, selected_hbm, field_ref, sent_ref, up_ref, down_ref,
+    slowness_ref, bar_ref, dual_ref, sems, pattern_ref, selected_ref, list_ref, scalar_sems,
 ):
     copies = scalar_copies(pattern_hbm, selected_hbm, pattern_ref, selected_ref, scalar_sems)
     copies.append(pltpu.make_async_copy(slowness_hbm, slowness_ref, sems.at[0]))
     copies.append(pltpu.make_async_copy(bar_hbm, bar_ref, sems.at[1]))
+    copies.append(pltpu.make_async_copy(dual_hbm, dual_ref, sems.at[2]))
     for copy in copies:
         copy.start()
     copies[0].wait()
@@ -110,6 +118,14 @@
     for p in range(N_RAY):
         sent_ref[p, 0:OWN, :] = rounded
         sent_ref[p, OWN:SENT, :] = numbers
+    up_ref[...] = jnp.zeros_like(up_ref)
+    copies[4].wait()
+    for x in range(GX):
+        up_ref[x : x + 1] = field_ref[x, 0:1]
+        down_ref[x : x + 1] = field_ref[x, GY - 1 : GY]
+        for c in range(3):
+            at = (c + 1) * GX + x
+            down_ref[at : at + 1] = dual_ref[c, x, GY - 1 : GY]
 
 
 def fetch_kernel(step):
@@ -160,7 +176,7 @@
     ]
     scratch = SCALARS + (pltpu.SemaphoreType.DMA((MAXSEL,)),)
     return call(
-        fetch_kernel(step), outs, "hhhh", (tiles, pattern, selected, after), scratch, 8 * 2**20
+        fetch_kernel(step), outs, "hhha", (tiles, pattern, selected, after), scratch, 8 * 2**20, True
     )
 
 
@@ -179,7 +195,7 @@
         out_ref[m] = total
 
 
-def predict_kernel(gathered_ref, picked_ref, hot_ref, out_ref):
+def predict_kernel(gathered_ref, picked_ref, hot_ref, up_any, down_any, out_ref):
     blocks = jnp.concatenate([gathered_ref[p, 0:OWN, :] for p in range(N_RAY)], axis=0)
     forward(hot_ref, blocks, picked_ref, out_ref)
 
@@ -274,7 +290,7 @@
 
 
 def back_kernel(
-    parts_ref, rays_ref, times_ref, pick_ref, picked_ref, hot_ref, new_rays_ref, out_ref
+    parts_ref, rays_ref, times_ref, pick_ref, picked_ref, hot_ref, far_any, near_any, new_rays_ref, out_ref
 ):
     change = dual_update(parts_ref, rays_ref, times_ref, pick_ref, new_rays_ref)
     terms = jnp.concatenate([products(change, picked_ref, n) for n in range(MAXSEL)], axis=0)
@@ -295,14 +311,16 @@
     return far, near
 
 
-def first_edges_kernel(field_ref, dual_ref, far_ref, near_ref):
+def first_edges_kernel(field_ref, dual_ref, up_ref, down_ref, after_any, far_ref, near_ref):
     odd = (lax.axis_index("mp") & 1) == 1
-    first = field_ref[0]
-    last = field_ref[GX - 1]
-    far_ref[0:GY] = jnp.where(odd, last, first)
-    near_ref[0:GY] = jnp.where(odd, first, last)
+    first = jnp.concatenate([field_ref[0], jnp.broadcast_to(down_ref[0:1], (8, TILE))], axis=0)
+    last = jnp.concatenate(
+        [field_ref[GX - 1], jnp.broadcast_to(up_ref[GX - 1 : GX], (8, TILE))], axis=0
+    )
+    far_ref[0 : 2 * GY] = jnp.where(odd, last, first)
+    near_ref[0 : 2 * GY] = jnp.where(odd, first, last)
     for c in range(3):
-        rows = slice((c + 1) * GY, (c + 2) * GY)
+        rows = slice((c + 2) * GY, (c + 3) * GY)
         far_ref[rows] = dual_ref[c, GX - 1]
         near_ref[rows] = dual_ref[c, GX - 1]
 
@@ -311,20 +329,6 @@
     odd = (lax.axis_index("mp") & 1) == 1
     far, near = far_ref[...], near_ref[...]
     return jnp.where(odd, near, far), jnp.where(odd, far, near)
-
-
-def row_edges_kernel(field_ref, dual_ref, far_ref, near_ref, after_ref, up_ref, down_ref):
-    before, behind = x_halos(far_ref, near_ref)
-    up_ref[...] = jnp.zeros_like(up_ref)
-    down_ref[...] = jnp.zeros_like(down_ref)
-    up_ref[GX : GX + 1] = before[0:1]
-    down_ref[GX : GX + 1] = behind[GY - 1 : GY]
-    for x in range(GX):
-        up_ref[x : x + 1] = field_ref[x, 0:1]
-        down_ref[x : x + 1] = field_ref[x, GY - 1 : GY]
-        for c in range(3):
-            at = 8 + c * GX + x
-            down_ref[at : at + 1] = dual_ref[c, x, GY - 1 : GY]
 
 
 def tv_cells(here, ahead_x, ahead_y, dual, no_x, no_y):
@@ -394,11 +398,13 @@
     dual = [[dual_ref[c, x] for x in range(GX)] for c in range(3)]
     up, down = up_ref[...], down_ref[...]
     rows = [down[x : x + 1] for x in range(GX)]
-    dual_rows = [[down[8 + c * GX + x : 9 + c * GX + x] for x in range(GX)] for c in range(3)]
+    dual_rows = [
+        [down[(c + 1) * GX + x : (c + 1) * GX + x + 1] for x in range(GX)] for c in range(3)
+    ]
     fresh, backs, halo, halo_rows = tv_step_all(
-        field, dual, before[0:GY], up[GX : GX + 1],
-        [before[(c + 1) * GY : (c + 2) * GY] for c in range(3)],
-        behind[0:GY], down[GX : GX + 1], rows, dual_rows, [up[x : x + 1] for x in range(GX)],
+        field, dual, before[0:GY], before[GY : GY + 1],
+        [before[(c + 2) * GY : (c + 3) * GY] for c in range(3)],
+        behind[0:GY], behind[GY : GY + 1], rows, dual_rows, [up[x : x + 1] for x in range(GX)],
     )
     for x in range(GX):
         base = field[x] - primal_step * (image_ref[x] + 2.0 * backs[x])
@@ -455,26 +461,29 @@
     grid = (GRID, F32)
     duals = ((3,) + GRID, F32)
 
-    field, sent = call(
-        start_kernel, [grid, ((N_RAY, SENT, TILE), BF16)], "hhhh",
-        (slowness, extrapolated, pattern, selected),
-        (pltpu.VMEM(GRID, F32), pltpu.VMEM(GRID, F32), pltpu.SemaphoreType.DMA((2,))) + SCALARS,
+    field, sent, up, down = call(
+        start_kernel,
+        [grid, ((N_RAY, SENT, TILE), BF16), ((8, TILE), F32), ((4 * GX, TILE), F32)], "hhhhh",
+        (slowness, extrapolated, tv_dual, pattern, selected),
+        (
+            pltpu.VMEM(GRID, F32), pltpu.VMEM(GRID, F32), pltpu.VMEM((3,) + GRID, F32),
+            pltpu.SemaphoreType.DMA((3,)),
+        ) + SCALARS,
     )
     gathered = exchange(sent, "ray")
-    far, near = call(
-        first_edges_kernel, [((4 * GY, TILE), F32)] * 2, "vv", (field, tv_dual), busy=busy
-    )
-    far, near = x_swaps(far, near)
-    picked, hot, pick = fetch(0, tiles, pattern, selected, field)
-    (partial_value,) = call(predict_kernel, [SUMS], "vvv", (gathered, picked, hot))
-    parts = exchange(partial_value, "mp")
-
-    up, down = call(
-        row_edges_kernel, [((8, TILE), F32), ((24, TILE), F32)], "vvvvh",
-        (field, tv_dual, far, near, partial_value), busy=busy,
-    )
     up = lax.ppermute(up, "ray", [(i + 1, i) for i in range(N_RAY - 1)])
     down = lax.ppermute(down, "ray", [(i, i + 1) for i in range(N_RAY - 1)])
+    picked, hot, pick = fetch(0, tiles, pattern, selected, field)
+    (partial_value,) = call(
+        predict_kernel, [SUMS], "vvvaa", (gathered, picked, hot, up, down)
+    )
+    parts = exchange(partial_value, "mp")
+
+    far, near = call(
+        first_edges_kernel, [((5 * GY, TILE), F32)] * 2, "vvvva",
+        (field, tv_dual, up, down, partial_value), busy=busy,
+    )
+    far, near = x_swaps(far, near)
     dual, dual_plane, dual_row, tv_back, base, rest = call(
         first_tv_kernel,
         [duals, ((3, GY, TILE), F32), ((3 * GX, TILE), F32), grid, grid, grid],
@@ -504,8 +513,8 @@
     )
 
     rays, share = call(
-        back_kernel, [RAYS, ((N_RAY, OWN, TILE), BF16)], "vvvvvv",
-        (parts, rays, traveltimes, pick_2, picked_2, hot_2),
+        back_kernel, [RAYS, ((N_RAY, OWN, TILE), BF16)], "vvvvvvaa",
+        (parts, rays, traveltimes, pick_2, picked_2, hot_2, far, near),
     )
     back = jnp.sum(exchange(share, "ray").astype(F32), axis=0).reshape(GRID)
     image = image + back + tv_back

time: 125 us -> 114 us (0.912)
  blocking collectives: 27.7 us -> 0 us
  starting transfers between devices: 54.4 us -> 71.1 us
  local copies, waits for them, and re-layouts: 9.28 us -> 0.03 us
  waiting for transfers between devices: 17.3 us -> 23.6 us
  Pallas kernels: 13.6 us -> 17.4 us
    all_to_all x1 -> x0, blocking collectives: 27.7 us -> none  [exchange(): return lax.all_to_all(copies, axis, 0, 0, tiled=True)]
    all_to_all x4 -> x5, starting transfers between devices: 35.8 us -> 47.7 us  [exchange(): return lax.all_to_all(copies, axis, 0, 0, tiled=True)]
    all_to_all x4 -> x5, waiting for transfers between devices: 9.99 us -> 20.9 us  [exchange(): return lax.all_to_all(copies, axis, 0, 0, tiled=True)]
    unnamed x30 -> x10, local copies, waits for them, and re-layouts: 9.28 us -> 0.03 us
    pallas_call x12 -> x11, Pallas kernels: 13.6 us -> 17.4 us  [call(): pl.pallas_call(kernel, out_shape=[pltpu.VMEM(shape, dtype) if keep else j...]
    ppermute x2, starting transfers between devices: 11.3 us -> 15 us  [x_swaps(): far = lax.ppermute(far, 'mp', far_route + [(b, a) for a, b in far_route])]
    ppermute x2, waiting for transfers between devices: 3.16 us -> 0.16 us  [x_swaps(): far = lax.ppermute(far, 'mp', far_route + [(b, a) for a, b in far_route])]
    ppermute x1, waiting for transfers between devices: 3.05 us -> 0.42 us  [on_device(): up = lax.ppermute(up, 'ray', [(i + 1, i) for i in range(N_RAY - 1)])]
  transfers between devices with their start and end apart: 10 -> 11, of which waited for: 6 -> 9; matrix products, arithmetic and copies ran while one was open for 0% -> 0% of each run, Pallas kernels for 4% -> 7%
where the time goes in v4:
time: 114 us; the launch traced here: 113 us
  starting transfers between devices  71.1 us (62%)
  waiting for transfers between devices  23.6 us (21%)
  Pallas kernels  17.4 us (15%)
    all_to_all x5, starting transfers between devices, exchange(): return lax.all_to_all(copies, axis, 0, 0, tiled=True)  47.7 us
    all_to_all x5, waiting for transfers between devices, exchange(): return lax.all_to_all(copies, axis, 0, 0, tiled=True)  20.9 us
    pallas_call x11, Pallas kernels, call(): pl.pallas_call(kernel, out_shape=[pltpu.VMEM(shape, dtype) if keep else j...  17.4 us
    ppermute x2, starting transfers between devices, x_swaps(): far = lax.ppermute(far, 'mp', far_route + [(b, a) for a, b in far_route])  15 us
    ppermute x2, starting transfers between devices, x_swaps(): lax.ppermute(near, 'mp', near_route + [(b, a) for a, b in near_route])  3.84 us
    ppermute x1, starting transfers between devices, on_device(): down = lax.ppermute(down, 'ray', [(i, i + 1) for i in range(N_RAY - 1)])  3.26 us
  transfers between devices with their start and end apart: 11, of which 9 were waited for; matrix products, arithmetic and copies ran while one was open for 0% of the time, Pallas kernels for 7%

profile of v4, /device:TPU:1, one launch (start us, length us, event | category | flops | bytes accessed | tf_op | source)
XLA Modules:
  0.0 113.5 jit_solution(7469515765834082564)
XLA Ops:
  0.6 1.9 %shard_map.128 = (f32[4,8,128]{2,1,0:T(8,128)S(1)}, bf16[16,48,128]{2,1,0:T(8,128)(2,1)}, f32[8,128]{1,0:T(8,128)S(1)}, f32[16,128]{1,0:T(8,128)S(1)}) custom-call(f32[4,8,128]{2,1,0:T(8,128)} %slowness_hbm.1, f32[4,8,128]{2,1,0:T(8,128)} %bar_hbm.1, f32[3,4,8,128]{3,2,1,0:T(8,128)} %dual_ref.3, s32[8,16]{1,0:T(8,128)} %bitcast.13, s32[2,16]{1,0:T(2,128)} %selected_hbm.5), custom_call_target="tpu_custom_call" | custom-call | tf_op jit(solution)/shard_map/pallas_call | solution.py:46
  2.5 10.4 %all-to-all-start = ((bf16[16,48,128]{2,1,0:T(8,128)(2,1)}), bf16[16,48,128]{2,1,0:T(8,128)(2,1)S(1)}, u32[]{:S(2)}, u32[]{:S(2)}) async-start(bf16[16,48,128]{2,1,0:T(8,128)(2,1)} %get-tuple-element.39), calls=%async_computation | async-start | bytes 393216 | tf_op jit(solution)/shard_map/all_to_all | solution.py:36
  12.9 3.3 %collective-permute-start.1 = (f32[16,128]{1,0:T(8,128)S(1)}, f32[16,128]{1,0:T(8,128)S(1)}, u32[]{:S(2)}, u32[]{:S(2)}) collective-permute-start(f32[16,128]{1,0:T(8,128)S(1)} %get-tuple-element.38), channel_id=1, source_target_pairs={{0,32},{32,64},{64,96},{96,128},{128,160},{160,192},{192,224},{224... | collective-permute-start | bytes 24584 | tf_op jit(solution)/shard_map/ppermute | solution.py:475
  16.2 1.3 %collective-permute-start = (f32[8,128]{1,0:T(8,128)S(1)}, f32[8,128]{1,0:T(8,128)S(1)}, u32[]{:S(2)}, u32[]{:S(2)}) collective-permute-start(f32[8,128]{1,0:T(8,128)S(1)} %get-tuple-element.37), channel_id=1, source_target_pairs={{32,0},{64,32},{96,64},{128,96},{160,128},{192,160},{224,192},{256... | collective-permute-start | bytes 12296 | tf_op jit(solution)/shard_map/ppermute | solution.py:474
  17.5 3.0 %shard_map.129 = (bf16[8,8,128,128]{3,2,1,0:T(8,128)(2,1)S(1)}, bf16[64,512]{1,0:T(8,128)(2,1)S(1)}, f32[16,8,128]{2,1,0:T(8,128)S(1)}) custom-call(bf16[16,8,128,128]{3,2,1,0:T(8,128)(2,1)} %tiles_hbm.3, s32[8,16]{1,0:T(8,128)} %bitcast.14, s32[2,16]{1,0:T(2,128)} %selected_hbm.5, f32[4,8,128]{2,1,0:T(8,128)S(1)} %get-tuple-element.36.after_ref.field_ref), custom_call_target="tpu_custom_call" | custom-call | bytes 8388608 | tf_op jit(solution)/shard_map/pallas_call | solution.py:46
  20.5 0.0 copy-start
  20.5 0.0 copy-start.1
  20.5 0.0 copy-start.2
  20.6 0.0 copy-start.4
  20.6 0.4 collective-permute-done.up_any.up_ref
  21.0 0.0 collective-permute-done.1.down_any.down_ref
  21.0 0.3 all-to-all-done.gathered_ref
  21.3 2.0 %shard_map.130.after_any.after_ref = f32[32,8,128]{2,1,0:T(8,128)} custom-call(bf16[16,48,128]{2,1,0:T(8,128)(2,1)S(1)} %all-to-all-done.gathered_ref, bf16[8,8,128,128]{3,2,1,0:T(8,128)(2,1)S(1)} %get-tuple-element.40.picked_ref, bf16[64,512]{1,0:T(8,128)(2,1)S(1)} %get-tuple-element.41.hot_ref, f32[8,128]{1,0:T(8,128)S(1)} %collective-permute-done.up_any.up_ref, ...), custom_call_target="tpu_custom_call" | custom-call | tf_op jit(solution)/shard_map/pallas_call | solution.py:46
  23.3 15.2 %all-to-all-start.1 = ((f32[32,8,128]{2,1,0:T(8,128)}), f32[32,8,128]{2,1,0:T(8,128)S(1)}, u32[]{:S(2)}, u32[]{:S(2)}) async-start(f32[32,8,128]{2,1,0:T(8,128)} %shard_map.130.after_any.after_ref), calls=%async_computation.1 | async-start | bytes 262144 | tf_op jit(solution)/shard_map/all_to_all | solution.py:36
  38.5 0.0 copy-done
  38.5 7.4 %collective-permute-start.2 = (f32[40,128]{1,0:T(8,128)S(1)}, f32[40,128]{1,0:T(8,128)S(1)}, u32[]{:S(2)}, u32[]{:S(2)}) collective-permute-start(f32[40,128]{1,0:T(8,128)S(1)} %get-tuple-element.42), channel_id=1, source_target_pairs={{1,2},{3,4},{5,6},{7,8},{9,10},{11,12},{13,14},{15,16},{17,18},{19... | collective-permute-start | bytes 61448 | tf_op jit(solution)/shard_map/ppermute | solution.py:309
  46.0 1.9 %collective-permute-start.3 = (f32[40,128]{1,0:T(8,128)S(1)}, f32[40,128]{1,0:T(8,128)S(1)}, u32[]{:S(2)}, u32[]{:S(2)}) collective-permute-start(f32[40,128]{1,0:T(8,128)S(1)} %get-tuple-element.43), channel_id=1, source_target_pairs={{0,1},{2,3},{4,5},{6,7},{8,9},{10,11},{12,13},{14,15},{16,17},{18,... | collective-permute-start | bytes 61448 | tf_op jit(solution)/shard_map/ppermute | solution.py:310
  47.9 0.2 collective-permute-done.2.far_ref
  48.1 1.0 collective-permute-done.3.near_ref
  49.1 0.0 copy-done.1
  49.1 0.2 shard_map.132
  49.2 2.4 %all-to-all-done.1.parts_ref = f32[32,8,128]{2,1,0:T(8,128)S(1)} async-done(((f32[32,8,128]{2,1,0:T(8,128)}), f32[32,8,128]{2,1,0:T(8,128)S(1)}, u32[]{:S(2)}, u32[]{:S(2)}) %all-to-all-start.1) | async-done | bytes 131104 | tf_op jit(solution)/shard_map/all_to_all | solution.py:36
  51.7 0.0 copy-done.2
  51.7 0.0 copy-done.4
  51.7 1.5 %shard_map.133 = (f32[16,128]{1,0:T(8,128)S(1)}, bf16[16,96,128]{2,1,0:T(8,128)(2,1)}) custom-call(f32[32,8,128]{2,1,0:T(8,128)S(1)} %all-to-all-done.1.parts_ref, f32[16,128]{1,0:T(8,128)S(1)} %copy-done.4, f32[16,128]{1,0:T(8,128)S(1)} %copy-done.2, f32[16,8,128]{2,1,0:T(8,128)S(1)} %get-tuple-element.45.pick_ref, ...), custom_call_target="tpu_custom_call" | custom-call | tf_op jit(solution)/shard_map/pallas_call | solution.py:46
  53.1 7.4 %all-to-all-start.2 = ((bf16[16,96,128]{2,1,0:T(8,128)(2,1)}), bf16[16,96,128]{2,1,0:T(8,128)(2,1)S(1)}, u32[]{:S(2)}, u32[]{:S(2)}) async-start(bf16[16,96,128]{2,1,0:T(8,128)(2,1)} %get-tuple-element.47), calls=%async_computation.2 | async-start | bytes 786432 | tf_op jit(solution)/shard_map/all_to_all | solution.py:36
  60.6 3.1 %shard_map.134 = (bf16[8,8,128,128]{3,2,1,0:T(8,128)(2,1)S(1)}, bf16[64,512]{1,0:T(8,128)(2,1)S(1)}, f32[16,8,128]{2,1,0:T(8,128)S(1)}) custom-call(bf16[16,8,128,128]{3,2,1,0:T(8,128)(2,1)} %tiles_hbm.3, s32[8,16]{1,0:T(8,128)} %bitcast.15, s32[2,16]{1,0:T(2,128)} %selected_hbm.5, f32[32,8,128]{2,1,0:T(8,128)} %shard_map.130.after_any.after_ref), custom_call_target="tpu_custom_call" | custom-call | bytes 8388608 | tf_op jit(solution)/shard_map/pallas_call | solution.py:46
  63.6 9.0 %all-to-all-done.2.shared_ref = bf16[16,96,128]{2,1,0:T(8,128)(2,1)S(1)} async-done(((bf16[16,96,128]{2,1,0:T(8,128)(2,1)}), bf16[16,96,128]{2,1,0:T(8,128)(2,1)S(1)}, u32[]{:S(2)}, u32[]{:S(2)}) %all-to-all-start.2) | async-done | bytes 393248 | tf_op jit(solution)/shard_map/all_to_all | solution.py:36
  72.6 2.9 %shard_map.135 = (f32[32,128]{1,0:T(8,128)S(1)}, f32[8,128]{1,0:T(8,128)S(1)}, f32[32,8,128]{2,1,0:T(8,128)}) custom-call(bf16[16,96,128]{2,1,0:T(8,128)(2,1)S(1)} %all-to-all-done.2.shared_ref, bf16[16,48,128]{2,1,0:T(8,128)(2,1)S(1)} %all-to-all-done.gathered_ref, bf16[8,8,128,128]{3,2,1,0:T(8,128)(2,1)S(1)} %get-tuple-element.48.picked_ref, ...), custom_call_target="tpu_custom_call" | custom-call | tf_op jit(solution)/shard_map/pallas_call | solution.py:46
  75.5 10.8 %all-to-all-start.3 = ((f32[32,8,128]{2,1,0:T(8,128)}), f32[32,8,128]{2,1,0:T(8,128)S(1)}, u32[]{:S(2)}, u32[]{:S(2)}) async-start(f32[32,8,128]{2,1,0:T(8,128)} %get-tuple-element.54), calls=%async_computation.3 | async-start | bytes 262144 | tf_op jit(solution)/shard_map/all_to_all | solution.py:36
  86.4 0.6 shard_map.136
  87.0 0.0 copy-start.3
  87.0 7.6 %collective-permute-start.4 = (f32[16,128]{1,0:T(8,128)S(1)}, f32[16,128]{1,0:T(8,128)S(1)}, u32[]{:S(2)}, u32[]{:S(2)}) collective-permute-start(f32[16,128]{1,0:T(8,128)S(1)} %get-tuple-element.57), channel_id=1, source_target_pairs={{1,2},{3,4},{5,6},{7,8},{9,10},{11,12},{13,14},{15,16},{17,18},{19... | collective-permute-start | bytes 24584 | tf_op jit(solution)/shard_map/ppermute | solution.py:309
  94.6 1.9 %collective-permute-start.5 = (f32[16,128]{1,0:T(8,128)S(1)}, f32[16,128]{1,0:T(8,128)S(1)}, u32[]{:S(2)}, u32[]{:S(2)}) collective-permute-start(f32[16,128]{1,0:T(8,128)S(1)} %get-tuple-element.58), channel_id=1, source_target_pairs={{0,1},{2,3},{4,5},{6,7},{8,9},{10,11},{12,13},{14,15},{16,17},{18,... | collective-permute-start | bytes 24584 | tf_op jit(solution)/shard_map/ppermute | solution.py:310
  96.5 0.0 collective-permute-done.4.far_any.far_ref
  96.5 1.1 collective-permute-done.5.near_any.near_ref
  97.6 1.9 %all-to-all-done.3.parts_ref = f32[32,8,128]{2,1,0:T(8,128)S(1)} async-done(((f32[32,8,128]{2,1,0:T(8,128)}), f32[32,8,128]{2,1,0:T(8,128)S(1)}, u32[]{:S(2)}, u32[]{:S(2)}) %all-to-all-start.3) | async-done | bytes 131104 | tf_op jit(solution)/shard_map/all_to_all | solution.py:36
  99.6 1.5 %shard_map.137 = (f32[16,128]{1,0:T(8,128)}, bf16[16,32,128]{2,1,0:T(8,128)(2,1)}) custom-call(f32[32,8,128]{2,1,0:T(8,128)S(1)} %all-to-all-done.3.parts_ref, f32[16,128]{1,0:T(8,128)S(1)} %get-tuple-element.55.rays_ref, f32[16,128]{1,0:T(8,128)S(1)} %copy-done.2, f32[16,8,128]{2,1,0:T(8,128)S(1)} %get-tuple-element.56.pick_ref, ...), custom_call_target="tpu_custom_call" | custom-call | tf_op jit(solution)/shard_map/pallas_call | solution.py:46
  101.1 3.9 %all-to-all-start.4 = ((bf16[16,32,128]{2,1,0:T(8,128)(2,1)}), bf16[16,32,128]{2,1,0:T(8,128)(2,1)S(1)}, u32[]{:S(2)}, u32[]{:S(2)}) async-start(bf16[16,32,128]{2,1,0:T(8,128)(2,1)} %get-tuple-element.65), calls=%async_computation.4 | async-start | bytes 262144 | tf_op jit(solution)/shard_map/all_to_all | solution.py:36
  105.0 0.0 copy-done.3
  105.0 0.7 shard_map.138
  105.7 7.2 %all-to-all-done.4 = bf16[16,32,128]{2,1,0:T(8,128)(2,1)S(1)} async-done(((bf16[16,32,128]{2,1,0:T(8,128)(2,1)}), bf16[16,32,128]{2,1,0:T(8,128)(2,1)S(1)}, u32[]{:S(2)}, u32[]{:S(2)}) %all-to-all-start.4) | async-done | bytes 131104 | tf_op jit(solution)/shard_map/all_to_all | solution.py:36
  112.9 0.6 fusion.2
  (3 shorter events, 0.0 us)
Async XLA Ops:
  2.5 18.8 %all-to-all-start = ((bf16[16,48,128]{2,1,0:T(8,128)(2,1)}), bf16[16,48,128]{2,1,0:T(8,128)(2,1)S(1)}, u32[]{:S(2)}, u32[]{:S(2)}) async-start(bf16[16,48,128]{2,1,0:T(8,128)(2,1)} %get-tuple-element.39), calls=%async_computation | async-start | bytes 393216 | tf_op jit(solution)/shard_map/all_to_all | solution.py:36
  12.9 8.1 %collective-permute-start.1 = (f32[16,128]{1,0:T(8,128)S(1)}, f32[16,128]{1,0:T(8,128)S(1)}, u32[]{:S(2)}, u32[]{:S(2)}) collective-permute-start(f32[16,128]{1,0:T(8,128)S(1)} %get-tuple-element.38), channel_id=1, source_target_pairs={{0,32},{32,64},{64,96},{96,128},{128,160},{160,192},{192,224},{224... | collective-permute-start | bytes 24584 | tf_op jit(solution)/shard_map/ppermute | solution.py:475
  16.2 4.8 %collective-permute-start = (f32[8,128]{1,0:T(8,128)S(1)}, f32[8,128]{1,0:T(8,128)S(1)}, u32[]{:S(2)}, u32[]{:S(2)}) collective-permute-start(f32[8,128]{1,0:T(8,128)S(1)} %get-tuple-element.37), channel_id=1, source_target_pairs={{32,0},{64,32},{96,64},{128,96},{160,128},{192,160},{224,192},{256... | collective-permute-start | bytes 12296 | tf_op jit(solution)/shard_map/ppermute | solution.py:474
  20.5 18.0 %copy-start = (f32[3,4,8,128]{3,2,1,0:T(8,128)S(1)}, f32[3,4,8,128]{3,2,1,0:T(8,128)}, u32[]{:S(2)}) copy-start(f32[3,4,8,128]{3,2,1,0:T(8,128)} %dual_ref.3) | copy-start | bytes 147460
  20.5 28.5 %copy-start.1 = (f32[4,8,128]{2,1,0:T(8,128)S(1)}, f32[4,8,128]{2,1,0:T(8,128)}, u32[]{:S(2)}) copy-start(f32[4,8,128]{2,1,0:T(8,128)} %image_ref.3) | copy-start | bytes 49156
  20.5 31.1 %copy-start.2 = (f32[16,128]{1,0:T(8,128)S(1)}, f32[16,128]{1,0:T(8,128)}, u32[]{:S(2)}) copy-start(f32[16,128]{1,0:T(8,128)} %times_ref.3) | copy-start | bytes 24580
  20.6 31.1 %copy-start.4 = (f32[16,128]{1,0:T(8,128)S(1)}, f32[16,128]{1,0:T(8,128)}, u32[]{:S(2)}) copy-start(f32[16,128]{1,0:T(8,128)} %rays_ref.1) | copy-start | bytes 24580
  23.3 28.3 %all-to-all-start.1 = ((f32[32,8,128]{2,1,0:T(8,128)}), f32[32,8,128]{2,1,0:T(8,128)S(1)}, u32[]{:S(2)}, u32[]{:S(2)}) async-start(f32[32,8,128]{2,1,0:T(8,128)} %shard_map.130.after_any.after_ref), calls=%async_computation.1 | async-start | bytes 262144 | tf_op jit(solution)/shard_map/all_to_all | solution.py:36
  38.5 9.5 %collective-permute-start.2 = (f32[40,128]{1,0:T(8,128)S(1)}, f32[40,128]{1,0:T(8,128)S(1)}, u32[]{:S(2)}, u32[]{:S(2)}) collective-permute-start(f32[40,128]{1,0:T(8,128)S(1)} %get-tuple-element.42), channel_id=1, source_target_pairs={{1,2},{3,4},{5,6},{7,8},{9,10},{11,12},{13,14},{15,16},{17,18},{19... | collective-permute-start | bytes 61448 | tf_op jit(solution)/shard_map/ppermute | solution.py:309
  46.0 3.1 %collective-permute-start.3 = (f32[40,128]{1,0:T(8,128)S(1)}, f32[40,128]{1,0:T(8,128)S(1)}, u32[]{:S(2)}, u32[]{:S(2)}) collective-permute-start(f32[40,128]{1,0:T(8,128)S(1)} %get-tuple-element.43), channel_id=1, source_target_pairs={{0,1},{2,3},{4,5},{6,7},{8,9},{10,11},{12,13},{14,15},{16,17},{18,... | collective-permute-start | bytes 61448 | tf_op jit(solution)/shard_map/ppermute | solution.py:310
  53.1 19.5 %all-to-all-start.2 = ((bf16[16,96,128]{2,1,0:T(8,128)(2,1)}), bf16[16,96,128]{2,1,0:T(8,128)(2,1)S(1)}, u32[]{:S(2)}, u32[]{:S(2)}) async-start(bf16[16,96,128]{2,1,0:T(8,128)(2,1)} %get-tuple-element.47), calls=%async_computation.2 | async-start | bytes 786432 | tf_op jit(solution)/shard_map/all_to_all | solution.py:36
  75.5 24.0 %all-to-all-start.3 = ((f32[32,8,128]{2,1,0:T(8,128)}), f32[32,8,128]{2,1,0:T(8,128)S(1)}, u32[]{:S(2)}, u32[]{:S(2)}) async-start(f32[32,8,128]{2,1,0:T(8,128)} %get-tuple-element.54), calls=%async_computation.3 | async-start | bytes 262144 | tf_op jit(solution)/shard_map/all_to_all | solution.py:36
  87.0 18.0 %copy-start.3 = (f32[4,8,128]{2,1,0:T(8,128)S(1)}, f32[4,8,128]{2,1,0:T(8,128)}, u32[]{:S(2)}) copy-start(f32[4,8,128]{2,1,0:T(8,128)} %get-tuple-element.31.field_ref) | copy-start | bytes 49156
  87.0 9.5 %collective-permute-start.4 = (f32[16,128]{1,0:T(8,128)S(1)}, f32[16,128]{1,0:T(8,128)S(1)}, u32[]{:S(2)}, u32[]{:S(2)}) collective-permute-start(f32[16,128]{1,0:T(8,128)S(1)} %get-tuple-element.57), channel_id=1, source_target_pairs={{1,2},{3,4},{5,6},{7,8},{9,10},{11,12},{13,14},{15,16},{17,18},{19... | collective-permute-start | bytes 24584 | tf_op jit(solution)/shard_map/ppermute | solution.py:309
  94.6 3.1 %collective-permute-start.5 = (f32[16,128]{1,0:T(8,128)S(1)}, f32[16,128]{1,0:T(8,128)S(1)}, u32[]{:S(2)}, u32[]{:S(2)}) collective-permute-start(f32[16,128]{1,0:T(8,128)S(1)} %get-tuple-element.58), channel_id=1, source_target_pairs={{0,1},{2,3},{4,5},{6,7},{8,9},{10,11},{12,13},{14,15},{16,17},{18,... | collective-permute-start | bytes 24584 | tf_op jit(solution)/shard_map/ppermute | solution.py:310
  101.1 11.8 %all-to-all-start.4 = ((bf16[16,32,128]{2,1,0:T(8,128)(2,1)}), bf16[16,32,128]{2,1,0:T(8,128)(2,1)S(1)}, u32[]{:S(2)}, u32[]{:S(2)}) async-start(bf16[16,32,128]{2,1,0:T(8,128)(2,1)} %get-tuple-element.65), calls=%async_computation.4 | async-start | bytes 262144 | tf_op jit(solution)/shard_map/all_to_all | solution.py:36

commit v5 on v3

--- a/solution.py
+++ b/solution.py
@@ -17,6 +17,9 @@
 ALL = N_RAY * OWN
 PRODUCTS = MAXSEL * CAP
 SENT = OWN + 16
+REST = OWN + 8
+EXTRA = PRODUCTS + OWN
+SHARED = EXTRA + 16
 
 primal_step = 0.5
 dual_step = 0.5
@@ -36,12 +39,19 @@
     return lax.all_to_all(copies, axis, 0, 0, tiled=True)
 
 
-def call(kernel, outs, places, args, scratch=(), busy=0):
-    spaces = {"v": pltpu.VMEM, "h": pltpu.HBM}
+def call(kernel, outs, places, args, scratch=(), busy=0, keep=False):
+    spaces = {"v": pltpu.VMEM, "h": pltpu.HBM, "a": pl.ANY}
     cost = pl.CostEstimate(flops=0, bytes_accessed=busy, transcendentals=0) if busy else None
+    args = [
+        pltpu.with_memory_space_constraint(arg, pltpu.HBM) if place == "h" else arg
+        for arg, place in zip(args, places)
+    ]
     return pl.pallas_call(
         kernel,
-        out_shape=[jax.ShapeDtypeStruct(shape, dtype) for shape, dtype in outs],
+        out_shape=[
+            pltpu.VMEM(shape, dtype) if keep else jax.ShapeDtypeStruct(shape, dtype)
+            for shape, dtype in outs
+        ],
         in_specs=[pl.BlockSpec(memory_space=spaces[c]) for c in places],
         out_specs=[pl.BlockSpec(memory_space=pltpu.VMEM) for _ in outs],
         scratch_shapes=list(scratch),
@@ -93,23 +103,28 @@
     copies[0].wait()
     copies[1].wait()
     list_selected(selected_ref, 0, list_ref)
-    lane = lax.broadcasted_iota(jnp.int32, (16, TILE), 1) & (PRODUCTS - 1)
-    sub = lax.broadcasted_iota(jnp.int32, (16, TILE), 0)
-    numbers = jnp.zeros((16, TILE), jnp.int32)
+    lane = lax.broadcasted_iota(jnp.int32, (8, TILE), 1) & (PRODUCTS - 1)
+    sub = lax.broadcasted_iota(jnp.int32, (8, TILE), 0)
+    numbers = jnp.zeros((8, TILE), jnp.int32)
     for n in range(MAXSEL):
         r = list_ref[n]
         for s in range(CAP):
             numbers = jnp.where(lane == n * CAP + s, block_number(pattern_ref[s, r]), numbers)
     numbers = jnp.where(sub == 0, lax.shift_right_logical(numbers, 5), numbers & (OWN - 1))
-    numbers = numbers.astype(F32).astype(BF16)
     copies[2].wait()
     copies[3].wait()
     field = slowness_ref[...] - primal_step * bar_ref[...]
     field_ref[...] = field
-    rounded = field.reshape(OWN, TILE).astype(BF16)
+    field = field.reshape(OWN, TILE)
+    rounded = field.astype(BF16)
+    low = field - rounded.astype(F32)
+    rest = jnp.zeros((8, TILE), F32)
+    for x in range(GX):
+        rest = jnp.where(sub == x, low[x * GY : x * GY + 1], rest)
+    tail = jnp.concatenate([numbers.astype(F32), rest], axis=0).astype(BF16)
     for p in range(N_RAY):
         sent_ref[p, 0:OWN, :] = rounded
-        sent_ref[p, OWN:SENT, :] = numbers
+        sent_ref[p, OWN:SENT, :] = tail
 
 
 def fetch_kernel(step):
@@ -117,8 +132,10 @@
         tiles_hbm, pattern_hbm, selected_hbm, after_ref, picked_ref, hot_ref, pick_ref,
         pattern_ref, selected_ref, list_ref, scalar_sems, sems,
     ):
-        for copy in scalar_copies(pattern_hbm, selected_hbm, pattern_ref, selected_ref, scalar_sems):
+        scalars = scalar_copies(pattern_hbm, selected_hbm, pattern_ref, selected_ref, scalar_sems)
+        for copy in scalars:
             copy.start()
+        for copy in scalars:
             copy.wait()
         count = list_selected(selected_ref, step, list_ref)
         copies = [
@@ -160,7 +177,7 @@
     ]
     scratch = SCALARS + (pltpu.SemaphoreType.DMA((MAXSEL,)),)
     return call(
-        fetch_kernel(step), outs, "hhhh", (tiles, pattern, selected, after), scratch, 8 * 2**20
+        fetch_kernel(step), outs, "hhha", (tiles, pattern, selected, after), scratch, 8 * 2**20, True
     )
 
 
@@ -216,7 +233,7 @@
 
 
 def share_kernel(
-    parts_ref, rays_ref, times_ref, pick_ref, picked_ref, rest_ref, new_rays_ref, out_ref
+    parts_ref, rays_ref, times_ref, pick_ref, picked_ref, rest_ref, extra_ref, new_rays_ref, out_ref
 ):
     change = dual_update(parts_ref, rays_ref, times_ref, pick_ref, new_rays_ref)
     for n in range(0, MAXSEL, 2):
@@ -225,9 +242,11 @@
         ).astype(BF16)
         for p in range(N_RAY):
             out_ref[p, n * CAP : (n + 2) * CAP, :] = pair
-    rest = rest_ref[...]
+    rest = rest_ref[...].reshape(OWN, TILE).astype(BF16)
+    extra = extra_ref[...].astype(BF16)
     for p in range(N_RAY):
-        out_ref[p, PRODUCTS : PRODUCTS + OWN, :] = rest
+        out_ref[p, PRODUCTS:EXTRA, :] = rest
+        out_ref[p, EXTRA:SHARED, :] = extra
 
 
 def image_kernel(
@@ -249,6 +268,7 @@
             jnp.concatenate([shared_ref[p, 0:PRODUCTS, :] for p in range(g, g + group)], axis=0)
         )
     place = lax.broadcasted_iota(jnp.int32, (chunk, group * PRODUCTS), 0)
+    sub = lax.broadcasted_iota(jnp.int32, (GY, TILE), 0)
     blocks = []
     for g in range(0, N_RAY, group):
         back = jnp.zeros((chunk, TILE), F32)
@@ -256,26 +276,35 @@
             hot = jnp.where(place + g * OWN == numbers[k], 1.0, 0.0).astype(BF16)
             back = back + jnp.dot(hot, terms[k], preferred_element_type=F32)
         table_ref[g * OWN : g * OWN + chunk, :] = back
-        before = jnp.concatenate([gathered_ref[p, 0:OWN, :] for p in range(g, g + group)], axis=0)
-        rest = jnp.concatenate(
-            [shared_ref[p, PRODUCTS : PRODUCTS + OWN, :] for p in range(g, g + group)], axis=0
-        )
-        blocks.append((before.astype(F32) + (rest.astype(F32) - gain * back)).astype(BF16))
-    forward(hot_ref, jnp.concatenate(blocks, axis=0), picked_ref, out_ref)
+        for p in range(g, g + group):
+            rows = slice(p * OWN, (p + 1) * OWN)
+            rest = shared_ref[p, PRODUCTS:EXTRA, :].astype(F32)
+            field = gathered_ref[p, 0:OWN, :].astype(F32) + (rest - gain * table_ref[rows, :])
+            if p > 0:
+                change = shared_ref[p - 1, EXTRA:SHARED, :].astype(F32)
+                field = field - (2.0 * primal_step) * jnp.concatenate(
+                    [jnp.where(sub == 0, change[x : x + 1], 0.0) for x in range(GX)], axis=0
+                )
+            blocks.append(field)
+    forward(
+        hot_ref, jnp.concatenate([field.astype(BF16) for field in blocks], axis=0), picked_ref, out_ref
+    )
     me = lax.axis_index("ray")
     back_ref[...] = table_ref[pl.ds(pl.multiple_of(me * OWN, OWN), OWN), :]
-    for at, peer, row in ((0, jnp.maximum(me - 1, 0), GY - 1), (1, jnp.minimum(me + 1, N_RAY - 1), 0)):
-        before = gathered_ref[peer, 0:OWN, :].astype(F32)
-        rest = shared_ref[peer, PRODUCTS : PRODUCTS + OWN, :].astype(F32)
-        back = table_ref[pl.ds(pl.multiple_of(peer * OWN, OWN), OWN), :]
-        field = before + (rest - gain * back)
+    for p in range(N_RAY):
+        table_ref[p * OWN : (p + 1) * OWN, :] = blocks[p]
+    before = jnp.maximum(me - 1, 0)
+    for at, peer, row in ((0, before, GY - 1), (1, jnp.minimum(me + 1, N_RAY - 1), 0)):
+        field = table_ref[pl.ds(pl.multiple_of(peer * OWN, OWN), OWN), :]
         for x in range(GX):
             edge_ref[at * GX + x : at * GX + x + 1, :] = field[x * GY + row : x * GY + row + 1]
+    edge_ref[2 * GX : 6 * GX] = shared_ref[before, EXTRA:SHARED, :].astype(F32)
 
 
 def back_kernel(
-    parts_ref, rays_ref, times_ref, pick_ref, picked_ref, hot_ref, new_rays_ref, out_ref
-):
+    parts_ref, rays_ref, times_ref, pick_ref, picked_ref, hot_ref, far_any, near_ref, new_rays_ref, out_ref, same_ref
+):
+    same_ref[...] = near_ref[...]
     change = dual_update(parts_ref, rays_ref, times_ref, pick_ref, new_rays_ref)
     terms = jnp.concatenate([products(change, picked_ref, n) for n in range(MAXSEL)], axis=0)
     high = terms.astype(BF16)
@@ -287,22 +316,39 @@
         out_ref[p] = image[p * OWN : (p + 1) * OWN].astype(BF16)
 
 
-def x_swaps(far, near):
-    far_route = [(m, m + 1) for m in range(1, N_MP - 1, 2)]
-    near_route = [(m, m + 1) for m in range(0, N_MP - 1, 2)]
-    far = lax.ppermute(far, "mp", far_route + [(b, a) for a, b in far_route])
-    near = lax.ppermute(near, "mp", near_route + [(b, a) for a, b in near_route])
-    return far, near
-
-
-def first_edges_kernel(field_ref, dual_ref, far_ref, near_ref):
+def swap(block, first):
+    route = [(m, m + 1) for m in range(first, N_MP - 1, 2)]
+    return lax.ppermute(block, "mp", route + [(b, a) for a, b in route])
+
+
+def swap_far(block):
+    return swap(block, 1)
+
+
+def swap_near(block):
+    return swap(block, 0)
+
+
+def next_rows(gathered_ref):
+    peer = jnp.minimum(lax.axis_index("ray") + 1, N_RAY - 1)
+    high = gathered_ref[peer, 0:OWN, :].astype(F32)
+    low = gathered_ref[peer, OWN:SENT, :].astype(F32)
+    return [
+        high[x * GY : x * GY + 1] + low[REST - OWN + x : REST - OWN + x + 1] for x in range(GX)
+    ]
+
+
+def first_edges_kernel(field_ref, dual_ref, gathered_ref, after_any, far_ref, near_ref):
     odd = (lax.axis_index("mp") & 1) == 1
     first = field_ref[0]
     last = field_ref[GX - 1]
     far_ref[0:GY] = jnp.where(odd, last, first)
     near_ref[0:GY] = jnp.where(odd, first, last)
+    corner = jnp.broadcast_to(next_rows(gathered_ref)[GX - 1], (GY, TILE))
+    far_ref[GY : 2 * GY] = corner
+    near_ref[GY : 2 * GY] = corner
     for c in range(3):
-        rows = slice((c + 1) * GY, (c + 2) * GY)
+        rows = slice((c + 2) * GY, (c + 3) * GY)
         far_ref[rows] = dual_ref[c, GX - 1]
         near_ref[rows] = dual_ref[c, GX - 1]
 
@@ -311,20 +357,6 @@
     odd = (lax.axis_index("mp") & 1) == 1
     far, near = far_ref[...], near_ref[...]
     return jnp.where(odd, near, far), jnp.where(odd, far, near)
-
-
-def row_edges_kernel(field_ref, dual_ref, far_ref, near_ref, after_ref, up_ref, down_ref):
-    before, behind = x_halos(far_ref, near_ref)
-    up_ref[...] = jnp.zeros_like(up_ref)
-    down_ref[...] = jnp.zeros_like(down_ref)
-    up_ref[GX : GX + 1] = before[0:1]
-    down_ref[GX : GX + 1] = behind[GY - 1 : GY]
-    for x in range(GX):
-        up_ref[x : x + 1] = field_ref[x, 0:1]
-        down_ref[x : x + 1] = field_ref[x, GY - 1 : GY]
-        for c in range(3):
-            at = 8 + c * GX + x
-            down_ref[at : at + 1] = dual_ref[c, x, GY - 1 : GY]
 
 
 def tv_cells(here, ahead_x, ahead_y, dual, no_x, no_y):
@@ -347,99 +379,112 @@
     return jnp.where(sub == GY - 1, row, pltpu.roll(plane, GY - 1, 0))
 
 
-def tv_step_all(field, dual, before, before_next, dual_before, behind, corner, rows, dual_rows, next_rows):
+def tv_step_all(field, dual, before, before_next, dual_before, behind, nexts, from_y):
     mp, ray = lax.axis_index("mp"), lax.axis_index("ray")
     sub = lax.broadcasted_iota(jnp.int32, (GY, TILE), 0)
-    end_x = mp == N_MP - 1
+    lane = lax.broadcasted_iota(jnp.int32, (GY, TILE), 1)
+    end_x = (mp == N_MP - 1) & (sub >= 0)
     last_y = (sub == GY - 1) & (ray == N_RAY - 1)
     never = sub < 0
-    lane = lax.broadcasted_iota(jnp.int32, (GY, TILE), 1)
 
     halo, halo_change = tv_cells(
         before, field[0], up_one(before, before_next), dual_before, never, last_y
     )
     from_x = jnp.where(mp == 0, 0.0, halo_change[0])
-    fresh, backs, halo_rows = [], [], []
+    fresh, backs, second = [], [], []
     for x in range(GX):
         ahead = field[x + 1] if x + 1 < GX else behind
-        no_x = (end_x & (sub >= 0)) if x + 1 == GX else never
+        no_x = end_x if x + 1 == GX else never
         new, change = tv_cells(
-            field[x], ahead, up_one(field[x], next_rows[x]), [d[x] for d in dual], no_x, last_y
+            field[x], ahead, up_one(field[x], nexts[x]), [d[x] for d in dual], no_x, last_y
         )
-        ahead_row = rows[x + 1] if x + 1 < GX else corner
-        no_row = (end_x & (sub[0:1] >= 0)) if x + 1 == GX else never[0:1]
-        new_row, row_change = tv_cells(
-            rows[x], ahead_row, field[x][0:1], [d[x] for d in dual_rows], no_row, never[0:1]
-        )
-        from_y = jnp.where(ray == 0, 0.0, row_change[1])
         comp_x = jnp.where(no_x, 0.0, change[0])
         comp_y = jnp.where(last_y, 0.0, change[1])
         comp_z = jnp.where(lane == TILE - 1, 0.0, change[2])
         back = from_x - comp_x
-        back = back + (jnp.where(sub == 0, from_y, pltpu.roll(comp_y, 1, 0)) - comp_y)
+        back = back + (jnp.where(sub == 0, from_y[x], pltpu.roll(comp_y, 1, 0)) - comp_y)
         back = back + (jnp.where(lane == 0, 0.0, pltpu.roll(comp_z, 1, 1)) - comp_z)
         from_x = comp_x
         fresh.append(new)
         backs.append(back)
-        halo_rows.append(new_row)
-    return fresh, backs, halo, halo_rows
+        second.append(comp_y)
+    return fresh, backs, halo, second
 
 
 def first_tv_kernel(
-    field_ref, dual_ref, far_ref, near_ref, up_ref, down_ref, image_ref,
-    new_dual_ref, plane_ref, row_ref, back_ref, base_ref, rest_ref,
+    field_ref, dual_ref, far_ref, near_ref, gathered_ref, image_ref,
+    new_dual_ref, plane_ref, back_ref, base_ref, rest_ref, extra_ref,
 ):
     before, behind = x_halos(far_ref, near_ref)
     field = [field_ref[x] for x in range(GX)]
-    dual = [[dual_ref[c, x] for x in range(GX)] for c in range(3)]
-    up, down = up_ref[...], down_ref[...]
-    rows = [down[x : x + 1] for x in range(GX)]
-    dual_rows = [[down[8 + c * GX + x : 9 + c * GX + x] for x in range(GX)] for c in range(3)]
-    fresh, backs, halo, halo_rows = tv_step_all(
-        field, dual, before[0:GY], up[GX : GX + 1],
-        [before[(c + 1) * GY : (c + 2) * GY] for c in range(3)],
-        behind[0:GY], down[GX : GX + 1], rows, dual_rows, [up[x : x + 1] for x in range(GX)],
+    fresh, backs, halo, second = tv_step_all(
+        field,
+        [[dual_ref[c, x] for x in range(GX)] for c in range(3)],
+        before[0:GY], before[GY : GY + 1],
+        [before[(c + 2) * GY : (c + 3) * GY] for c in range(3)],
+        behind[0:GY], next_rows(gathered_ref), [0.0] * GX,
     )
     for x in range(GX):
         base = field[x] - primal_step * (image_ref[x] + 2.0 * backs[x])
         back_ref[x] = backs[x]
         base_ref[x] = base
         rest_ref[x] = base - field[x].astype(BF16).astype(F32)
+        extra_ref[x : x + 1] = second[x][GY - 1 : GY]
         for c in range(3):
             new_dual_ref[c, x] = fresh[x][c]
-            row_ref[c * GX + x : c * GX + x + 1] = halo_rows[x][c]
+            at = (c + 1) * GX + x
+            extra_ref[at : at + 1] = fresh[x][c][GY - 1 : GY]
     for c in range(3):
         plane_ref[c] = halo[c]
 
 
-def second_edges_kernel(base_ref, back_ref, edge_ref, image_ref, tv_ref, field_ref, new_image_ref, far_ref, near_ref):
+def second_edges_kernel(
+    base_ref, back_ref, edge_ref, image_ref, tv_ref, field_ref, new_image_ref, far_ref, near_ref
+):
     odd = (lax.axis_index("mp") & 1) == 1
+    sub = lax.broadcasted_iota(jnp.int32, (GY, TILE), 0)
+    first_y = (sub == 0) & (lax.axis_index("ray") > 0)
     field = []
     for x in range(GX):
         back = back_ref[x * GY : (x + 1) * GY]
-        field.append(base_ref[x] - gain * back)
+        from_y = jnp.where(first_y, edge_ref[2 * GX + x : 2 * GX + x + 1], 0.0)
+        field.append(base_ref[x] - (gain * back + (2.0 * primal_step) * from_y))
         field_ref[x] = field[x]
-        new_image_ref[x] = image_ref[x] + back + tv_ref[x]
-    first = jnp.concatenate([field[0], edge_ref[...]], axis=0)
-    last = jnp.concatenate([field[GX - 1], edge_ref[...]], axis=0)
+        new_image_ref[x] = image_ref[x] + back + (tv_ref[x] + from_y)
+    edge = edge_ref[0 : 2 * GX]
+    first = jnp.concatenate([field[0], edge], axis=0)
+    last = jnp.concatenate([field[GX - 1], edge], axis=0)
     far_ref[...] = jnp.where(odd, last, first)
     near_ref[...] = jnp.where(odd, first, last)
 
 
 def second_tv_kernel(
-    field_ref, dual_ref, plane_ref, row_ref, far_ref, near_ref, edge_ref, new_dual_ref, back_ref
+    field_ref, dual_ref, plane_ref, far_ref, near_ref, edge_ref, new_dual_ref, back_ref
 ):
     before, behind = x_halos(far_ref, near_ref)
     edge = edge_ref[...]
+    ray = lax.axis_index("ray")
+    end_x = lax.axis_index("mp") == N_MP - 1
+    field = [field_ref[x] for x in range(GX)]
+    sub = lax.broadcasted_iota(jnp.int32, (2 * GX, TILE), 0)
+    rows = edge[0 : 2 * GX]
+    ahead_x = jnp.where(sub == GX - 1, behind[GY : GY + 1], pltpu.roll(rows, 2 * GX - 1, 0))
+    ahead_y = jnp.concatenate([field[x][0:1] for x in range(GX)] * 2, axis=0)
+    dual_rows = [
+        jnp.concatenate([edge[(c + 3) * GX : (c + 4) * GX]] * 2, axis=0) for c in range(3)
+    ]
+    _, change = tv_cells(
+        rows, ahead_x, ahead_y, dual_rows, (sub == GX - 1) & end_x, sub < 0
+    )
+    from_y = jnp.where(ray == 0, 0.0, change[1])
     fresh, backs, _, _ = tv_step_all(
-        [field_ref[x] for x in range(GX)],
+        field,
         [[dual_ref[c, x] for x in range(GX)] for c in range(3)],
         before[0:GY], before[GY + 2 * GX - 1 : GY + 2 * GX],
         [plane_ref[c] for c in range(3)],
-        behind[0:GY], behind[GY : GY + 1],
-        [edge[x : x + 1] for x in range(GX)],
-        [[row_ref[c * GX + x : c * GX + x + 1] for x in range(GX)] for c in range(3)],
+        behind[0:GY],
         [edge[GX + x : GX + x + 1] for x in range(GX)],
+        [from_y[x : x + 1] for x in range(GX)],
     )
     for x in range(GX):
         back_ref[x] = backs[x]
@@ -454,6 +499,7 @@
     busy = 8 * 2**20
     grid = (GRID, F32)
     duals = ((3,) + GRID, F32)
+    swapped = ((GY + 2 * GX, TILE), F32)
 
     field, sent = call(
         start_kernel, [grid, ((N_RAY, SENT, TILE), BF16)], "hhhh",
@@ -461,53 +507,49 @@
         (pltpu.VMEM(GRID, F32), pltpu.VMEM(GRID, F32), pltpu.SemaphoreType.DMA((2,))) + SCALARS,
     )
     gathered = exchange(sent, "ray")
-    far, near = call(
-        first_edges_kernel, [((4 * GY, TILE), F32)] * 2, "vv", (field, tv_dual), busy=busy
-    )
-    far, near = x_swaps(far, near)
     picked, hot, pick = fetch(0, tiles, pattern, selected, field)
     (partial_value,) = call(predict_kernel, [SUMS], "vvv", (gathered, picked, hot))
     parts = exchange(partial_value, "mp")
 
-    up, down = call(
-        row_edges_kernel, [((8, TILE), F32), ((24, TILE), F32)], "vvvvh",
-        (field, tv_dual, far, near, partial_value), busy=busy,
-    )
-    up = lax.ppermute(up, "ray", [(i + 1, i) for i in range(N_RAY - 1)])
-    down = lax.ppermute(down, "ray", [(i, i + 1) for i in range(N_RAY - 1)])
-    dual, dual_plane, dual_row, tv_back, base, rest = call(
+    far, near = call(
+        first_edges_kernel, [((5 * GY, TILE), F32)] * 2, "vvva",
+        (field, tv_dual, gathered, partial_value), busy=busy,
+    )
+    far, near = swap_far(far), swap_near(near)
+    dual, dual_plane, tv_back, base, rest, extra = call(
         first_tv_kernel,
-        [duals, ((3, GY, TILE), F32), ((3 * GX, TILE), F32), grid, grid, grid],
-        "vvvvvvv", (field, tv_dual, far, near, up, down, accumulated), busy=busy,
+        [duals, ((3, GY, TILE), F32), grid, grid, grid, ((4 * GX, TILE), F32)],
+        "vvvvvv", (field, tv_dual, far, near, gathered, accumulated), busy=busy,
     )
     picked_2, hot_2, pick_2 = fetch(1, tiles, pattern, selected, partial_value)
 
     rays, share = call(
-        share_kernel, [RAYS, ((N_RAY, PRODUCTS + OWN, TILE), BF16)], "vvvvvv",
-        (parts, ray_dual, traveltimes, pick, picked, rest.astype(BF16).reshape(OWN, TILE)),
+        share_kernel, [RAYS, ((N_RAY, SHARED, TILE), BF16)], "vvvvvvv",
+        (parts, ray_dual, traveltimes, pick, picked, rest, extra),
     )
     shared = exchange(share, "ray")
     back, edge, partial_value = call(
-        image_kernel, [((OWN, TILE), F32), ((2 * GX, TILE), F32), SUMS], "vvvv",
+        image_kernel, [((OWN, TILE), F32), ((6 * GX, TILE), F32), SUMS], "vvvv",
         (shared, gathered, picked_2, hot_2), (pltpu.VMEM((ALL, TILE), F32),),
     )
     parts = exchange(partial_value, "mp")
 
     field, image, far, near = call(
-        second_edges_kernel, [grid, grid] + [((GY + 2 * GX, TILE), F32)] * 2, "vvvvv",
+        second_edges_kernel, [grid, grid, swapped, swapped], "vvvvv",
         (base, back, edge, accumulated, tv_back), busy=busy,
     )
-    far, near = x_swaps(far, near)
+    far = swap_far(far)
+    rays, share, near = call(
+        back_kernel, [RAYS, ((N_RAY, OWN, TILE), BF16), swapped], "vvvvvvav",
+        (parts, rays, traveltimes, pick_2, picked_2, hot_2, far, near),
+    )
+    shared = exchange(share, "ray")
+    near = swap_near(near)
     dual, tv_back = call(
-        second_tv_kernel, [duals, grid], "vvvvvvv",
-        (field, dual, dual_plane, dual_row, far, near, edge), busy=busy,
-    )
-
-    rays, share = call(
-        back_kernel, [RAYS, ((N_RAY, OWN, TILE), BF16)], "vvvvvv",
-        (parts, rays, traveltimes, pick_2, picked_2, hot_2),
-    )
-    back = jnp.sum(exchange(share, "ray").astype(F32), axis=0).reshape(GRID)
+        second_tv_kernel, [duals, grid], "vvvvvv",
+        (field, dual, dual_plane, far, near, edge), busy=busy,
+    )
+    back = jnp.sum(shared.astype(F32), axis=0).reshape(GRID)
     image = image + back + tv_back
     image_bar = image + extrapolation * back + tv_back
     return (field, rays, dual, image, image_bar)

time: 125 us -> 111 us (0.89)
  blocking collectives: 27.7 us -> 0 us
  waiting for transfers between devices: 17.3 us -> 30.2 us
  local copies, waits for them, and re-layouts: 9.28 us -> 0.03 us
  starting transfers between devices: 54.4 us -> 62.4 us
  Pallas kernels: 13.6 us -> 16.3 us
    all_to_all x1 -> x0, blocking collectives: 27.7 us -> none  [exchange(): return lax.all_to_all(copies, axis, 0, 0, tiled=True)]
    all_to_all x4 -> x5, waiting for transfers between devices: 9.99 us -> 26.3 us  [exchange(): return lax.all_to_all(copies, axis, 0, 0, tiled=True)]
    unnamed x30 -> x10, local copies, waits for them, and re-layouts: 9.28 us -> 0.03 us
    all_to_all x4 -> x5, starting transfers between devices: 35.8 us -> 43.1 us  [exchange(): return lax.all_to_all(copies, axis, 0, 0, tiled=True)]
    ppermute x6 -> x4, waiting for transfers between devices: 7.31 us -> 3.9 us  [swap(): return lax.ppermute(block, 'mp', route + [(b, a) for a, b in route])]
    pallas_call x12 -> x11, Pallas kernels: 13.6 us -> 16.3 us  [call(): pl.pallas_call(kernel, out_shape=[pltpu.VMEM(shape, dtype) if keep else j...]
    ppermute x6 -> x4, starting transfers between devices: 18.6 us -> 19.3 us  [swap(): return lax.ppermute(block, 'mp', route + [(b, a) for a, b in route])]
  transfers between devices with their start and end apart: 10 -> 9, of which waited for: 6 -> 9; matrix products, arithmetic and copies ran while one was open for 0% -> 0% of each run, Pallas kernels for 4% -> 6%
where the time goes in v5:
time: 111 us; the launch traced here: 110 us
  starting transfers between devices  62.4 us (56%)
  waiting for transfers between devices  30.2 us (27%)
  Pallas kernels  16.3 us (15%)
    all_to_all x5, starting transfers between devices, exchange(): return lax.all_to_all(copies, axis, 0, 0, tiled=True)  43.1 us
    all_to_all x5, waiting for transfers between devices, exchange(): return lax.all_to_all(copies, axis, 0, 0, tiled=True)  26.3 us
    ppermute x4, starting transfers between devices, swap(): return lax.ppermute(block, 'mp', route + [(b, a) for a, b in route])  19.3 us
    pallas_call x11, Pallas kernels, call(): pl.pallas_call(kernel, out_shape=[pltpu.VMEM(shape, dtype) if keep else j...  16.3 us
    ppermute x4, waiting for transfers between devices, swap(): return lax.ppermute(block, 'mp', route + [(b, a) for a, b in route])  3.9 us
  transfers between devices with their start and end apart: 9, of which 9 were waited for; matrix products, arithmetic and copies ran while one was open for 0% of the time, Pallas kernels for 6%

profile of v5, /device:TPU:1, one launch (start us, length us, event | category | flops | bytes accessed | tf_op | source)
XLA Modules:
  0.0 110.4 jit_solution(14060593056911361112)
XLA Ops:
  0.6 1.9 %shard_map.128 = (f32[4,8,128]{2,1,0:T(8,128)S(1)}, bf16[16,48,128]{2,1,0:T(8,128)(2,1)}) custom-call(f32[4,8,128]{2,1,0:T(8,128)} %slowness_hbm.1, f32[4,8,128]{2,1,0:T(8,128)} %bar_hbm.1, s32[8,16]{1,0:T(8,128)} %bitcast.11, s32[2,16]{1,0:T(2,128)} %selected_hbm.5), custom_call_target="tpu_custom_call" | custom-call | tf_op jit(solution)/shard_map/pallas_call | solution.py:49
  2.5 10.4 %all-to-all-start = ((bf16[16,48,128]{2,1,0:T(8,128)(2,1)}), bf16[16,48,128]{2,1,0:T(8,128)(2,1)S(1)}, u32[]{:S(2)}, u32[]{:S(2)}) async-start(bf16[16,48,128]{2,1,0:T(8,128)(2,1)} %get-tuple-element.36), calls=%async_computation | async-start | bytes 393216 | tf_op jit(solution)/shard_map/all_to_all | solution.py:39
  12.9 2.6 %shard_map.129 = (bf16[8,8,128,128]{3,2,1,0:T(8,128)(2,1)S(1)}, bf16[64,512]{1,0:T(8,128)(2,1)S(1)}, f32[16,8,128]{2,1,0:T(8,128)S(1)}) custom-call(bf16[16,8,128,128]{3,2,1,0:T(8,128)(2,1)} %tiles_hbm.3, s32[8,16]{1,0:T(8,128)} %bitcast.12, s32[2,16]{1,0:T(2,128)} %selected_hbm.5, f32[4,8,128]{2,1,0:T(8,128)S(1)} %get-tuple-element.35.after_ref.field_ref), custom_call_target="tpu_custom_call" | custom-call | bytes 8388608 | tf_op jit(solution)/shard_map/pallas_call | solution.py:49
  15.5 0.0 copy-start
  15.5 0.0 copy-start.1
  15.5 0.0 copy-start.2
  15.6 0.0 copy-start.4
  15.6 5.7 %all-to-all-done.gathered_ref = bf16[16,48,128]{2,1,0:T(8,128)(2,1)S(1)} async-done(((bf16[16,48,128]{2,1,0:T(8,128)(2,1)}), bf16[16,48,128]{2,1,0:T(8,128)(2,1)S(1)}, u32[]{:S(2)}, u32[]{:S(2)}) %all-to-all-start) | async-done | bytes 196640 | tf_op jit(solution)/shard_map/all_to_all | solution.py:39
  21.3 2.0 %shard_map.130.after_any.after_ref = f32[32,8,128]{2,1,0:T(8,128)} custom-call(bf16[16,48,128]{2,1,0:T(8,128)(2,1)S(1)} %all-to-all-done.gathered_ref, bf16[8,8,128,128]{3,2,1,0:T(8,128)(2,1)S(1)} %get-tuple-element.37.picked_ref, bf16[64,512]{1,0:T(8,128)(2,1)S(1)} %get-tuple-element.38.hot_ref), custom_call_target="tpu_custom_call" | custom-call | tf_op jit(solution)/shard_map/pallas_call | solution.py:49
  23.3 15.2 %all-to-all-start.1 = ((f32[32,8,128]{2,1,0:T(8,128)}), f32[32,8,128]{2,1,0:T(8,128)S(1)}, u32[]{:S(2)}, u32[]{:S(2)}) async-start(f32[32,8,128]{2,1,0:T(8,128)} %shard_map.130.after_any.after_ref), calls=%async_computation.1 | async-start | bytes 262144 | tf_op jit(solution)/shard_map/all_to_all | solution.py:39
  38.5 0.0 copy-done
  38.5 7.4 %collective-permute-start = (f32[40,128]{1,0:T(8,128)S(1)}, f32[40,128]{1,0:T(8,128)S(1)}, u32[]{:S(2)}, u32[]{:S(2)}) collective-permute-start(f32[40,128]{1,0:T(8,128)S(1)} %get-tuple-element.39), channel_id=1, source_target_pairs={{1,2},{3,4},{5,6},{7,8},{9,10},{11,12},{13,14},{15,16},{17,18},{19... | collective-permute-start | bytes 61448 | tf_op jit(solution)/shard_map/ppermute | solution.py:321
  46.0 1.9 %collective-permute-start.1 = (f32[40,128]{1,0:T(8,128)S(1)}, f32[40,128]{1,0:T(8,128)S(1)}, u32[]{:S(2)}, u32[]{:S(2)}) collective-permute-start(f32[40,128]{1,0:T(8,128)S(1)} %get-tuple-element.40), channel_id=1, source_target_pairs={{0,1},{2,3},{4,5},{6,7},{8,9},{10,11},{12,13},{14,15},{16,17},{18,... | collective-permute-start | bytes 61448 | tf_op jit(solution)/shard_map/ppermute | solution.py:321
  47.9 0.1 collective-permute-done.far_ref
  48.0 1.0 collective-permute-done.1.near_ref
  49.0 0.0 copy-done.1
  49.0 0.2 shard_map.132
  49.2 2.4 %all-to-all-done.1.parts_ref = f32[32,8,128]{2,1,0:T(8,128)S(1)} async-done(((f32[32,8,128]{2,1,0:T(8,128)}), f32[32,8,128]{2,1,0:T(8,128)S(1)}, u32[]{:S(2)}, u32[]{:S(2)}) %all-to-all-start.1) | async-done | bytes 131104 | tf_op jit(solution)/shard_map/all_to_all | solution.py:39
  51.7 0.0 copy-done.2
  51.7 0.0 copy-done.4
  51.7 1.5 %shard_map.133 = (f32[16,128]{1,0:T(8,128)S(1)}, bf16[16,112,128]{2,1,0:T(8,128)(2,1)}) custom-call(f32[32,8,128]{2,1,0:T(8,128)S(1)} %all-to-all-done.1.parts_ref, f32[16,128]{1,0:T(8,128)S(1)} %copy-done.4, f32[16,128]{1,0:T(8,128)S(1)} %copy-done.2, f32[16,8,128]{2,1,0:T(8,128)S(1)} %get-tuple-element.42.pick_ref, ...), custom_call_target="tpu_custom_call" | custom-call | tf_op jit(solution)/shard_map/pallas_call | solution.py:49
  53.2 3.6 %all-to-all-start.2 = ((bf16[16,112,128]{2,1,0:T(8,128)(2,1)}), bf16[16,112,128]{2,1,0:T(8,128)(2,1)S(1)}, u32[]{:S(2)}, u32[]{:S(2)}) async-start(bf16[16,112,128]{2,1,0:T(8,128)(2,1)} %get-tuple-element.45), calls=%async_computation.2 | async-start | bytes 917504 | tf_op jit(solution)/shard_map/all_to_all | solution.py:39
  56.7 2.4 %shard_map.134 = (bf16[8,8,128,128]{3,2,1,0:T(8,128)(2,1)S(1)}, bf16[64,512]{1,0:T(8,128)(2,1)S(1)}, f32[16,8,128]{2,1,0:T(8,128)S(1)}) custom-call(bf16[16,8,128,128]{3,2,1,0:T(8,128)(2,1)} %tiles_hbm.3, s32[8,16]{1,0:T(8,128)} %bitcast.13, s32[2,16]{1,0:T(2,128)} %selected_hbm.5, f32[32,8,128]{2,1,0:T(8,128)} %shard_map.130.after_any.after_ref), custom_call_target="tpu_custom_call" | custom-call | bytes 8388608 | tf_op jit(solution)/shard_map/pallas_call | solution.py:49
  59.1 11.1 %all-to-all-done.2.shared_ref = bf16[16,112,128]{2,1,0:T(8,128)(2,1)S(1)} async-done(((bf16[16,112,128]{2,1,0:T(8,128)(2,1)}), bf16[16,112,128]{2,1,0:T(8,128)(2,1)S(1)}, u32[]{:S(2)}, u32[]{:S(2)}) %all-to-all-start.2) | async-done | bytes 458784 | tf_op jit(solution)/shard_map/all_to_all | solution.py:39
  70.2 2.9 %shard_map.135 = (f32[32,128]{1,0:T(8,128)S(1)}, f32[24,128]{1,0:T(8,128)S(1)}, f32[32,8,128]{2,1,0:T(8,128)}) custom-call(bf16[16,112,128]{2,1,0:T(8,128)(2,1)S(1)} %all-to-all-done.2.shared_ref, bf16[16,48,128]{2,1,0:T(8,128)(2,1)S(1)} %all-to-all-done.gathered_ref, bf16[8,8,128,128]{3,2,1,0:T(8,128)(2,1)S(1)} %get-tuple-element.46.picked_ref, ...), custom_call_target="tpu_custom_call" | custom-call | tf_op jit(solution)/shard_map/pallas_call | solution.py:49
  73.1 10.1 %all-to-all-start.3 = ((f32[32,8,128]{2,1,0:T(8,128)}), f32[32,8,128]{2,1,0:T(8,128)S(1)}, u32[]{:S(2)}, u32[]{:S(2)}) async-start(f32[32,8,128]{2,1,0:T(8,128)} %get-tuple-element.52), calls=%async_computation.3 | async-start | bytes 262144 | tf_op jit(solution)/shard_map/all_to_all | solution.py:39
  83.2 0.6 shard_map.136
  83.9 0.0 copy-start.3
  83.9 7.6 %collective-permute-start.2 = (f32[16,128]{1,0:T(8,128)S(1)}, f32[16,128]{1,0:T(8,128)S(1)}, u32[]{:S(2)}, u32[]{:S(2)}) collective-permute-start(f32[16,128]{1,0:T(8,128)S(1)} %get-tuple-element.55), channel_id=1, source_target_pairs={{1,2},{3,4},{5,6},{7,8},{9,10},{11,12},{13,14},{15,16},{17,18},{19... | collective-permute-start | bytes 24584 | tf_op jit(solution)/shard_map/ppermute | solution.py:321
  91.4 1.9 %collective-permute-done.2.far_any.far_ref = f32[16,128]{1,0:T(8,128)S(1)} collective-permute-done((f32[16,128]{1,0:T(8,128)S(1)}, f32[16,128]{1,0:T(8,128)S(1)}, u32[]{:S(2)}, u32[]{:S(2)}) %collective-permute-start.2) | collective-permute-done | bytes 8224 | tf_op jit(solution)/shard_map/ppermute | solution.py:321
  93.4 3.0 %all-to-all-done.3.parts_ref = f32[32,8,128]{2,1,0:T(8,128)S(1)} async-done(((f32[32,8,128]{2,1,0:T(8,128)}), f32[32,8,128]{2,1,0:T(8,128)S(1)}, u32[]{:S(2)}, u32[]{:S(2)}) %all-to-all-start.3) | async-done | bytes 131104 | tf_op jit(solution)/shard_map/all_to_all | solution.py:39
  96.4 1.5 %shard_map.137 = (f32[16,128]{1,0:T(8,128)}, bf16[16,32,128]{2,1,0:T(8,128)(2,1)}, f32[16,128]{1,0:T(8,128)S(1)}) custom-call(f32[32,8,128]{2,1,0:T(8,128)S(1)} %all-to-all-done.3.parts_ref, f32[16,128]{1,0:T(8,128)S(1)} %get-tuple-element.53.rays_ref, f32[16,128]{1,0:T(8,128)S(1)} %copy-done.2, f32[16,8,128]{2,1,0:T(8,128)S(1)} %get-tuple-element.54.pick_ref, ...), custom_call_target="tpu_custom_call" | custom-call | tf_op jit(solution)/shard_map/pallas_call | solution.py:49
  97.9 3.9 %all-to-all-start.4 = ((bf16[16,32,128]{2,1,0:T(8,128)(2,1)}), bf16[16,32,128]{2,1,0:T(8,128)(2,1)S(1)}, u32[]{:S(2)}, u32[]{:S(2)}) async-start(bf16[16,32,128]{2,1,0:T(8,128)(2,1)} %get-tuple-element.63), calls=%async_computation.4 | async-start | bytes 262144 | tf_op jit(solution)/shard_map/all_to_all | solution.py:39
  101.8 2.4 %collective-permute-start.3 = (f32[16,128]{1,0:T(8,128)S(1)}, f32[16,128]{1,0:T(8,128)S(1)}, u32[]{:S(2)}, u32[]{:S(2)}) collective-permute-start(f32[16,128]{1,0:T(8,128)S(1)} %get-tuple-element.60), channel_id=1, source_target_pairs={{0,1},{2,3},{4,5},{6,7},{8,9},{10,11},{12,13},{14,15},{16,17},{18,... | collective-permute-start | bytes 24584 | tf_op jit(solution)/shard_map/ppermute | solution.py:321
  104.3 0.8 collective-permute-done.3.near_ref
  105.1 0.0 copy-done.3
  105.1 0.7 shard_map.138
  105.8 4.0 %all-to-all-done.4 = bf16[16,32,128]{2,1,0:T(8,128)(2,1)S(1)} async-done(((bf16[16,32,128]{2,1,0:T(8,128)(2,1)}), bf16[16,32,128]{2,1,0:T(8,128)(2,1)S(1)}, u32[]{:S(2)}, u32[]{:S(2)}) %all-to-all-start.4) | async-done | bytes 131104 | tf_op jit(solution)/shard_map/all_to_all | solution.py:39
  109.8 0.6 fusion.2
  (2 shorter events, 0.0 us)
Async XLA Ops:
  2.5 18.8 %all-to-all-start = ((bf16[16,48,128]{2,1,0:T(8,128)(2,1)}), bf16[16,48,128]{2,1,0:T(8,128)(2,1)S(1)}, u32[]{:S(2)}, u32[]{:S(2)}) async-start(bf16[16,48,128]{2,1,0:T(8,128)(2,1)} %get-tuple-element.36), calls=%async_computation | async-start | bytes 393216 | tf_op jit(solution)/shard_map/all_to_all | solution.py:39
  15.5 22.9 %copy-start = (f32[3,4,8,128]{3,2,1,0:T(8,128)S(1)}, f32[3,4,8,128]{3,2,1,0:T(8,128)}, u32[]{:S(2)}) copy-start(f32[3,4,8,128]{3,2,1,0:T(8,128)} %dual_ref.3) | copy-start | bytes 147460
  15.5 33.5 %copy-start.1 = (f32[4,8,128]{2,1,0:T(8,128)S(1)}, f32[4,8,128]{2,1,0:T(8,128)}, u32[]{:S(2)}) copy-start(f32[4,8,128]{2,1,0:T(8,128)} %image_ref.3) | copy-start | bytes 49156
  15.5 36.1 %copy-start.2 = (f32[16,128]{1,0:T(8,128)S(1)}, f32[16,128]{1,0:T(8,128)}, u32[]{:S(2)}) copy-start(f32[16,128]{1,0:T(8,128)} %times_ref.3) | copy-start | bytes 24580
  15.6 36.1 %copy-start.4 = (f32[16,128]{1,0:T(8,128)S(1)}, f32[16,128]{1,0:T(8,128)}, u32[]{:S(2)}) copy-start(f32[16,128]{1,0:T(8,128)} %rays_ref.1) | copy-start | bytes 24580
  23.3 28.4 %all-to-all-start.1 = ((f32[32,8,128]{2,1,0:T(8,128)}), f32[32,8,128]{2,1,0:T(8,128)S(1)}, u32[]{:S(2)}, u32[]{:S(2)}) async-start(f32[32,8,128]{2,1,0:T(8,128)} %shard_map.130.after_any.after_ref), calls=%async_computation.1 | async-start | bytes 262144 | tf_op jit(solution)/shard_map/all_to_all | solution.py:39
  38.5 9.5 %collective-permute-start = (f32[40,128]{1,0:T(8,128)S(1)}, f32[40,128]{1,0:T(8,128)S(1)}, u32[]{:S(2)}, u32[]{:S(2)}) collective-permute-start(f32[40,128]{1,0:T(8,128)S(1)} %get-tuple-element.39), channel_id=1, source_target_pairs={{1,2},{3,4},{5,6},{7,8},{9,10},{11,12},{13,14},{15,16},{17,18},{19... | collective-permute-start | bytes 61448 | tf_op jit(solution)/shard_map/ppermute | solution.py:321
  46.0 3.1 %collective-permute-start.1 = (f32[40,128]{1,0:T(8,128)S(1)}, f32[40,128]{1,0:T(8,128)S(1)}, u32[]{:S(2)}, u32[]{:S(2)}) collective-permute-start(f32[40,128]{1,0:T(8,128)S(1)} %get-tuple-element.40), channel_id=1, source_target_pairs={{0,1},{2,3},{4,5},{6,7},{8,9},{10,11},{12,13},{14,15},{16,17},{18,... | collective-permute-start | bytes 61448 | tf_op jit(solution)/shard_map/ppermute | solution.py:321
  53.2 17.1 %all-to-all-start.2 = ((bf16[16,112,128]{2,1,0:T(8,128)(2,1)}), bf16[16,112,128]{2,1,0:T(8,128)(2,1)S(1)}, u32[]{:S(2)}, u32[]{:S(2)}) async-start(bf16[16,112,128]{2,1,0:T(8,128)(2,1)} %get-tuple-element.45), calls=%async_computation.2 | async-start | bytes 917504 | tf_op jit(solution)/shard_map/all_to_all | solution.py:39
  73.1 23.3 %all-to-all-start.3 = ((f32[32,8,128]{2,1,0:T(8,128)}), f32[32,8,128]{2,1,0:T(8,128)S(1)}, u32[]{:S(2)}, u32[]{:S(2)}) async-start(f32[32,8,128]{2,1,0:T(8,128)} %get-tuple-element.52), calls=%async_computation.3 | async-start | bytes 262144 | tf_op jit(solution)/shard_map/all_to_all | solution.py:39
  83.9 21.2 %copy-start.3 = (f32[4,8,128]{2,1,0:T(8,128)S(1)}, f32[4,8,128]{2,1,0:T(8,128)}, u32[]{:S(2)}) copy-start(f32[4,8,128]{2,1,0:T(8,128)} %get-tuple-element.30.field_ref) | copy-start | bytes 49156
  83.9 9.5 %collective-permute-start.2 = (f32[16,128]{1,0:T(8,128)S(1)}, f32[16,128]{1,0:T(8,128)S(1)}, u32[]{:S(2)}, u32[]{:S(2)}) collective-permute-start(f32[16,128]{1,0:T(8,128)S(1)} %get-tuple-element.55), channel_id=1, source_target_pairs={{1,2},{3,4},{5,6},{7,8},{9,10},{11,12},{13,14},{15,16},{17,18},{19... | collective-permute-start | bytes 24584 | tf_op jit(solution)/shard_map/ppermute | solution.py:321
  97.9 11.8 %all-to-all-start.4 = ((bf16[16,32,128]{2,1,0:T(8,128)(2,1)}), bf16[16,32,128]{2,1,0:T(8,128)(2,1)S(1)}, u32[]{:S(2)}, u32[]{:S(2)}) async-start(bf16[16,32,128]{2,1,0:T(8,128)(2,1)} %get-tuple-element.63), calls=%async_computation.4 | async-start | bytes 262144 | tf_op jit(solution)/shard_map/all_to_all | solution.py:39
  101.8 3.2 %collective-permute-start.3 = (f32[16,128]{1,0:T(8,128)S(1)}, f32[16,128]{1,0:T(8,128)S(1)}, u32[]{:S(2)}, u32[]{:S(2)}) collective-permute-start(f32[16,128]{1,0:T(8,128)S(1)} %get-tuple-element.60), channel_id=1, source_target_pairs={{0,1},{2,3},{4,5},{6,7},{8,9},{10,11},{12,13},{14,15},{16,17},{18,... | collective-permute-start | bytes 24584 | tf_op jit(solution)/shard_map/ppermute | solution.py:321

commit v6 on v5

--- a/solution.py
+++ b/solution.py
@@ -20,6 +20,7 @@
 REST = OWN + 8
 EXTRA = PRODUCTS + OWN
 SHARED = EXTRA + 16
+GATHER, SUM_1, SHARE, SUM_2, LAST = 15, 18, 15, 18, 15
 
 primal_step = 0.5
 dual_step = 0.5
@@ -35,8 +36,14 @@
 RAYS = ((RB_DEV, TILE), F32)
 
 
-def exchange(copies, axis):
-    return lax.all_to_all(copies, axis, 0, 0, tiled=True)
+def exchange(copies, axis, first):
+    size = N_RAY if axis == "ray" else N_MP
+    groups = [[(first + i) % size for i in range(size)]]
+    return lax.all_to_all(copies, axis, 0, 0, tiled=True, axis_index_groups=groups)
+
+
+def at(peer, first):
+    return (peer + (N_RAY - first)) & (N_RAY - 1)
 
 
 def call(kernel, outs, places, args, scratch=(), busy=0, keep=False):
@@ -197,7 +204,7 @@
 
 
 def predict_kernel(gathered_ref, picked_ref, hot_ref, out_ref):
-    blocks = jnp.concatenate([gathered_ref[p, 0:OWN, :] for p in range(N_RAY)], axis=0)
+    blocks = jnp.concatenate([gathered_ref[at(p, GATHER), 0:OWN, :] for p in range(N_RAY)], axis=0)
     forward(hot_ref, blocks, picked_ref, out_ref)
 
 
@@ -255,7 +262,7 @@
     lane = lax.broadcasted_iota(jnp.int32, (1, TILE), 1)
     singles = []
     for p in range(N_RAY):
-        rows = gathered_ref[p, OWN:SENT, :].astype(F32)
+        rows = gathered_ref[at(p, GATHER), OWN:SENT, :].astype(F32)
         singles.append(rows[0:1] * OWN + rows[1:2])
     pairs = [jnp.where(lane < PRODUCTS, singles[p], singles[p + 1]) for p in range(0, N_RAY, 2)]
     group = 4
@@ -265,7 +272,9 @@
     for g in range(0, N_RAY, group):
         numbers.append(jnp.concatenate(pairs[g // 2 : g // 2 + 2], axis=1).astype(jnp.int32))
         terms.append(
-            jnp.concatenate([shared_ref[p, 0:PRODUCTS, :] for p in range(g, g + group)], axis=0)
+            jnp.concatenate(
+                [shared_ref[at(p, SHARE), 0:PRODUCTS, :] for p in range(g, g + group)], axis=0
+            )
         )
     place = lax.broadcasted_iota(jnp.int32, (chunk, group * PRODUCTS), 0)
     sub = lax.broadcasted_iota(jnp.int32, (GY, TILE), 0)
@@ -278,10 +287,10 @@
         table_ref[g * OWN : g * OWN + chunk, :] = back
         for p in range(g, g + group):
             rows = slice(p * OWN, (p + 1) * OWN)
-            rest = shared_ref[p, PRODUCTS:EXTRA, :].astype(F32)
-            field = gathered_ref[p, 0:OWN, :].astype(F32) + (rest - gain * table_ref[rows, :])
+            rest = shared_ref[at(p, SHARE), PRODUCTS:EXTRA, :].astype(F32)
+            field = gathered_ref[at(p, GATHER), 0:OWN, :].astype(F32) + (rest - gain * table_ref[rows, :])
             if p > 0:
-                change = shared_ref[p - 1, EXTRA:SHARED, :].astype(F32)
+                change = shared_ref[at(p - 1, SHARE), EXTRA:SHARED, :].astype(F32)
                 field = field - (2.0 * primal_step) * jnp.concatenate(
                     [jnp.where(sub == 0, change[x : x + 1], 0.0) for x in range(GX)], axis=0
                 )
@@ -294,11 +303,11 @@
     for p in range(N_RAY):
         table_ref[p * OWN : (p + 1) * OWN, :] = blocks[p]
     before = jnp.maximum(me - 1, 0)
-    for at, peer, row in ((0, before, GY - 1), (1, jnp.minimum(me + 1, N_RAY - 1), 0)):
+    for side, peer, row in ((0, before, GY - 1), (1, jnp.minimum(me + 1, N_RAY - 1), 0)):
         field = table_ref[pl.ds(pl.multiple_of(peer * OWN, OWN), OWN), :]
         for x in range(GX):
-            edge_ref[at * GX + x : at * GX + x + 1, :] = field[x * GY + row : x * GY + row + 1]
-    edge_ref[2 * GX : 6 * GX] = shared_ref[before, EXTRA:SHARED, :].astype(F32)
+            edge_ref[side * GX + x : side * GX + x + 1, :] = field[x * GY + row : x * GY + row + 1]
+    edge_ref[2 * GX : 6 * GX] = shared_ref[at(before, SHARE), EXTRA:SHARED, :].astype(F32)
 
 
 def back_kernel(
@@ -313,7 +322,7 @@
     image = lax.dot_general(hot_ref[...], high, turned, preferred_element_type=F32)
     image = image + lax.dot_general(hot_ref[...], low, turned, preferred_element_type=F32)
     for p in range(N_RAY):
-        out_ref[p] = image[p * OWN : (p + 1) * OWN].astype(BF16)
+        out_ref[at(p, LAST)] = image[p * OWN : (p + 1) * OWN].astype(BF16)
 
 
 def swap(block, first):
@@ -331,8 +340,8 @@
 
 def next_rows(gathered_ref):
     peer = jnp.minimum(lax.axis_index("ray") + 1, N_RAY - 1)
-    high = gathered_ref[peer, 0:OWN, :].astype(F32)
-    low = gathered_ref[peer, OWN:SENT, :].astype(F32)
+    high = gathered_ref[at(peer, GATHER), 0:OWN, :].astype(F32)
+    low = gathered_ref[at(peer, GATHER), OWN:SENT, :].astype(F32)
     return [
         high[x * GY : x * GY + 1] + low[REST - OWN + x : REST - OWN + x + 1] for x in range(GX)
     ]
@@ -432,8 +441,8 @@
         extra_ref[x : x + 1] = second[x][GY - 1 : GY]
         for c in range(3):
             new_dual_ref[c, x] = fresh[x][c]
-            at = (c + 1) * GX + x
-            extra_ref[at : at + 1] = fresh[x][c][GY - 1 : GY]
+            row = (c + 1) * GX + x
+            extra_ref[row : row + 1] = fresh[x][c][GY - 1 : GY]
     for c in range(3):
         plane_ref[c] = halo[c]
 
@@ -506,10 +515,10 @@
         (slowness, extrapolated, pattern, selected),
         (pltpu.VMEM(GRID, F32), pltpu.VMEM(GRID, F32), pltpu.SemaphoreType.DMA((2,))) + SCALARS,
     )
-    gathered = exchange(sent, "ray")
+    gathered = exchange(sent, "ray", GATHER)
     picked, hot, pick = fetch(0, tiles, pattern, selected, field)
     (partial_value,) = call(predict_kernel, [SUMS], "vvv", (gathered, picked, hot))
-    parts = exchange(partial_value, "mp")
+    parts = exchange(partial_value, "mp", SUM_1)
 
     far, near = call(
         first_edges_kernel, [((5 * GY, TILE), F32)] * 2, "vvva",
@@ -527,12 +536,12 @@
         share_kernel, [RAYS, ((N_RAY, SHARED, TILE), BF16)], "vvvvvvv",
         (parts, ray_dual, traveltimes, pick, picked, rest, extra),
     )
-    shared = exchange(share, "ray")
+    shared = exchange(share, "ray", SHARE)
     back, edge, partial_value = call(
         image_kernel, [((OWN, TILE), F32), ((6 * GX, TILE), F32), SUMS], "vvvv",
         (shared, gathered, picked_2, hot_2), (pltpu.VMEM((ALL, TILE), F32),),
     )
-    parts = exchange(partial_value, "mp")
+    parts = exchange(partial_value, "mp", SUM_2)
 
     field, image, far, near = call(
         second_edges_kernel, [grid, grid, swapped, swapped], "vvvvv",
@@ -543,7 +552,7 @@
         back_kernel, [RAYS, ((N_RAY, OWN, TILE), BF16), swapped], "vvvvvvav",
         (parts, rays, traveltimes, pick_2, picked_2, hot_2, far, near),
     )
-    shared = exchange(share, "ray")
+    shared = exchange(share, "ray", LAST)
     near = swap_near(near)
     dual, tv_back = call(
         second_tv_kernel, [duals, grid], "vvvvvv",

time: 111 us -> 106 us (0.955)
  waiting for transfers between devices: 30.2 us -> 19.4 us
  starting transfers between devices: 62.4 us -> 68.1 us
    all_to_all x5, waiting for transfers between devices: 26.3 us -> 7.12 us  [exchange(): lax.all_to_all(copies, axis, 0, 0, tiled=True, axis_index_groups=groups)]
    all_to_all x5, starting transfers between devices: 43.1 us -> 59.2 us  [exchange(): lax.all_to_all(copies, axis, 0, 0, tiled=True, axis_index_groups=groups)]
    ppermute x4, starting transfers between devices: 19.3 us -> 8.84 us  [swap(): return lax.ppermute(block, 'mp', route + [(b, a) for a, b in route])]
    ppermute x4, waiting for transfers between devices: 3.9 us -> 12.3 us  [swap(): return lax.ppermute(block, 'mp', route + [(b, a) for a, b in route])]
  transfers between devices with their start and end apart: 9 -> 9, of which waited for: 9 -> 5; matrix products, arithmetic and copies ran while one was open for 0% -> 0% of each run, Pallas kernels for 6% -> 6%
where the time goes in v6:
time: 106 us; the launch traced here: 105 us
  starting transfers between devices  68.1 us (64%)
  waiting for transfers between devices  19.4 us (18%)
  Pallas kernels  16.1 us (15%)
    all_to_all x5, starting transfers between devices, exchange(): lax.all_to_all(copies, axis, 0, 0, tiled=True, axis_index_groups=groups)  59.2 us
    pallas_call x11, Pallas kernels, call(): pl.pallas_call(kernel, out_shape=[pltpu.VMEM(shape, dtype) if keep else j...  16.1 us
    ppermute x4, waiting for transfers between devices, swap(): return lax.ppermute(block, 'mp', route + [(b, a) for a, b in route])  12.3 us
    ppermute x4, starting transfers between devices, swap(): return lax.ppermute(block, 'mp', route + [(b, a) for a, b in route])  8.84 us
    all_to_all x5, waiting for transfers between devices, exchange(): lax.all_to_all(copies, axis, 0, 0, tiled=True, axis_index_groups=groups)  7.12 us
  transfers between devices with their start and end apart: 9, of which 5 were waited for; matrix products, arithmetic and copies ran while one was open for 0% of the time, Pallas kernels for 6%

profile of v6, /device:TPU:1, one launch (start us, length us, event | category | flops | bytes accessed | tf_op | source)
XLA Modules:
  0.0 105.0 jit_solution(12048606090675846119)
XLA Ops:
  0.6 1.9 %shard_map.128 = (f32[4,8,128]{2,1,0:T(8,128)S(1)}, bf16[16,48,128]{2,1,0:T(8,128)(2,1)}) custom-call(f32[4,8,128]{2,1,0:T(8,128)} %slowness_hbm.1, f32[4,8,128]{2,1,0:T(8,128)} %bar_hbm.1, s32[8,16]{1,0:T(8,128)} %bitcast.11, s32[2,16]{1,0:T(2,128)} %selected_hbm.5), custom_call_target="tpu_custom_call" | custom-call | tf_op jit(solution)/shard_map/pallas_call | solution.py:56
  2.5 12.1 %all-to-all-start = ((bf16[16,48,128]{2,1,0:T(8,128)(2,1)}), bf16[16,48,128]{2,1,0:T(8,128)(2,1)S(1)}, u32[]{:S(2)}, u32[]{:S(2)}) async-start(bf16[16,48,128]{2,1,0:T(8,128)(2,1)} %get-tuple-element.36), calls=%async_computation | async-start | bytes 393216 | tf_op jit(solution)/shard_map/all_to_all | solution.py:42
  14.5 2.4 %shard_map.129 = (bf16[8,8,128,128]{3,2,1,0:T(8,128)(2,1)S(1)}, bf16[64,512]{1,0:T(8,128)(2,1)S(1)}, f32[16,8,128]{2,1,0:T(8,128)S(1)}) custom-call(bf16[16,8,128,128]{3,2,1,0:T(8,128)(2,1)} %tiles_hbm.3, s32[8,16]{1,0:T(8,128)} %bitcast.12, s32[2,16]{1,0:T(2,128)} %selected_hbm.5, f32[4,8,128]{2,1,0:T(8,128)S(1)} %get-tuple-element.35.after_ref.field_ref), custom_call_target="tpu_custom_call" | custom-call | bytes 8388608 | tf_op jit(solution)/shard_map/pallas_call | solution.py:56
  16.9 0.0 copy-start
  16.9 0.0 copy-start.1
  16.9 0.0 copy-start.2
  17.0 0.0 copy-start.4
  17.0 1.7 %all-to-all-done.gathered_ref = bf16[16,48,128]{2,1,0:T(8,128)(2,1)S(1)} async-done(((bf16[16,48,128]{2,1,0:T(8,128)(2,1)}), bf16[16,48,128]{2,1,0:T(8,128)(2,1)S(1)}, u32[]{:S(2)}, u32[]{:S(2)}) %all-to-all-start) | async-done | bytes 196640 | tf_op jit(solution)/shard_map/all_to_all | solution.py:42
  18.7 2.0 %shard_map.130.after_any.after_ref = f32[32,8,128]{2,1,0:T(8,128)} custom-call(bf16[16,48,128]{2,1,0:T(8,128)(2,1)S(1)} %all-to-all-done.gathered_ref, bf16[8,8,128,128]{3,2,1,0:T(8,128)(2,1)S(1)} %get-tuple-element.37.picked_ref, bf16[64,512]{1,0:T(8,128)(2,1)S(1)} %get-tuple-element.38.hot_ref), custom_call_target="tpu_custom_call" | custom-call | tf_op jit(solution)/shard_map/pallas_call | solution.py:56
  20.7 16.9 %all-to-all-start.1 = ((f32[32,8,128]{2,1,0:T(8,128)}), f32[32,8,128]{2,1,0:T(8,128)S(1)}, u32[]{:S(2)}, u32[]{:S(2)}) async-start(f32[32,8,128]{2,1,0:T(8,128)} %shard_map.130.after_any.after_ref), calls=%async_computation.1 | async-start | bytes 262144 | tf_op jit(solution)/shard_map/all_to_all | solution.py:42
  37.6 0.0 copy-done
  37.7 2.5 %collective-permute-start = (f32[40,128]{1,0:T(8,128)S(1)}, f32[40,128]{1,0:T(8,128)S(1)}, u32[]{:S(2)}, u32[]{:S(2)}) collective-permute-start(f32[40,128]{1,0:T(8,128)S(1)} %get-tuple-element.39), channel_id=1, source_target_pairs={{1,2},{3,4},{5,6},{7,8},{9,10},{11,12},{13,14},{15,16},{17,18},{19... | collective-permute-start | bytes 61448 | tf_op jit(solution)/shard_map/ppermute | solution.py:330
  40.1 1.9 %collective-permute-start.1 = (f32[40,128]{1,0:T(8,128)S(1)}, f32[40,128]{1,0:T(8,128)S(1)}, u32[]{:S(2)}, u32[]{:S(2)}) collective-permute-start(f32[40,128]{1,0:T(8,128)S(1)} %get-tuple-element.40), channel_id=1, source_target_pairs={{0,1},{2,3},{4,5},{6,7},{8,9},{10,11},{12,13},{14,15},{16,17},{18,... | collective-permute-start | bytes 61448 | tf_op jit(solution)/shard_map/ppermute | solution.py:330
  42.0 4.7 %collective-permute-done.far_ref = f32[40,128]{1,0:T(8,128)S(1)} collective-permute-done((f32[40,128]{1,0:T(8,128)S(1)}, f32[40,128]{1,0:T(8,128)S(1)}, u32[]{:S(2)}, u32[]{:S(2)}) %collective-permute-start) | collective-permute-done | bytes 20512 | tf_op jit(solution)/shard_map/ppermute | solution.py:330
  46.7 0.0 collective-permute-done.1.near_ref
  46.7 0.0 copy-done.1
  46.7 0.2 shard_map.132
  46.9 0.0 all-to-all-done.1.parts_ref
  46.9 0.0 copy-done.2
  46.9 0.0 copy-done.4
  46.9 1.5 %shard_map.133 = (f32[16,128]{1,0:T(8,128)S(1)}, bf16[16,112,128]{2,1,0:T(8,128)(2,1)}) custom-call(f32[32,8,128]{2,1,0:T(8,128)S(1)} %all-to-all-done.1.parts_ref, f32[16,128]{1,0:T(8,128)S(1)} %copy-done.4, f32[16,128]{1,0:T(8,128)S(1)} %copy-done.2, f32[16,8,128]{2,1,0:T(8,128)S(1)} %get-tuple-element.42.pick_ref, ...), custom_call_target="tpu_custom_call" | custom-call | tf_op jit(solution)/shard_map/pallas_call | solution.py:56
  48.4 7.6 %all-to-all-start.2 = ((bf16[16,112,128]{2,1,0:T(8,128)(2,1)}), bf16[16,112,128]{2,1,0:T(8,128)(2,1)S(1)}, u32[]{:S(2)}, u32[]{:S(2)}) async-start(bf16[16,112,128]{2,1,0:T(8,128)(2,1)} %get-tuple-element.45), calls=%async_computation.2 | async-start | bytes 917504 | tf_op jit(solution)/shard_map/all_to_all | solution.py:42
  56.1 2.4 %shard_map.134 = (bf16[8,8,128,128]{3,2,1,0:T(8,128)(2,1)S(1)}, bf16[64,512]{1,0:T(8,128)(2,1)S(1)}, f32[16,8,128]{2,1,0:T(8,128)S(1)}) custom-call(bf16[16,8,128,128]{3,2,1,0:T(8,128)(2,1)} %tiles_hbm.3, s32[8,16]{1,0:T(8,128)} %bitcast.13, s32[2,16]{1,0:T(2,128)} %selected_hbm.5, f32[32,8,128]{2,1,0:T(8,128)} %shard_map.130.after_any.after_ref), custom_call_target="tpu_custom_call" | custom-call | bytes 8388608 | tf_op jit(solution)/shard_map/pallas_call | solution.py:56
  58.4 5.4 %all-to-all-done.2.shared_ref = bf16[16,112,128]{2,1,0:T(8,128)(2,1)S(1)} async-done(((bf16[16,112,128]{2,1,0:T(8,128)(2,1)}), bf16[16,112,128]{2,1,0:T(8,128)(2,1)S(1)}, u32[]{:S(2)}, u32[]{:S(2)}) %all-to-all-start.2) | async-done | bytes 458784 | tf_op jit(solution)/shard_map/all_to_all | solution.py:42
  63.9 2.9 %shard_map.135 = (f32[32,128]{1,0:T(8,128)S(1)}, f32[24,128]{1,0:T(8,128)S(1)}, f32[32,8,128]{2,1,0:T(8,128)}) custom-call(bf16[16,112,128]{2,1,0:T(8,128)(2,1)S(1)} %all-to-all-done.2.shared_ref, bf16[16,48,128]{2,1,0:T(8,128)(2,1)S(1)} %all-to-all-done.gathered_ref, bf16[8,8,128,128]{3,2,1,0:T(8,128)(2,1)S(1)} %get-tuple-element.46.picked_ref, ...), custom_call_target="tpu_custom_call" | custom-call | tf_op jit(solution)/shard_map/pallas_call | solution.py:56
  66.8 14.2 %all-to-all-start.3 = ((f32[32,8,128]{2,1,0:T(8,128)}), f32[32,8,128]{2,1,0:T(8,128)S(1)}, u32[]{:S(2)}, u32[]{:S(2)}) async-start(f32[32,8,128]{2,1,0:T(8,128)} %get-tuple-element.52), calls=%async_computation.3 | async-start | bytes 262144 | tf_op jit(solution)/shard_map/all_to_all | solution.py:42
  81.0 0.6 shard_map.136
  81.6 0.0 copy-start.3
  81.6 2.6 %collective-permute-start.2 = (f32[16,128]{1,0:T(8,128)S(1)}, f32[16,128]{1,0:T(8,128)S(1)}, u32[]{:S(2)}, u32[]{:S(2)}) collective-permute-start(f32[16,128]{1,0:T(8,128)S(1)} %get-tuple-element.55), channel_id=1, source_target_pairs={{1,2},{3,4},{5,6},{7,8},{9,10},{11,12},{13,14},{15,16},{17,18},{19... | collective-permute-start | bytes 24584 | tf_op jit(solution)/shard_map/ppermute | solution.py:330
  84.2 6.5 %collective-permute-done.2.far_any.far_ref = f32[16,128]{1,0:T(8,128)S(1)} collective-permute-done((f32[16,128]{1,0:T(8,128)S(1)}, f32[16,128]{1,0:T(8,128)S(1)}, u32[]{:S(2)}, u32[]{:S(2)}) %collective-permute-start.2) | collective-permute-done | bytes 8224 | tf_op jit(solution)/shard_map/ppermute | solution.py:330
  90.6 0.0 all-to-all-done.3.parts_ref
  90.6 1.5 %shard_map.137 = (f32[16,128]{1,0:T(8,128)}, bf16[16,32,128]{2,1,0:T(8,128)(2,1)}, f32[16,128]{1,0:T(8,128)S(1)}) custom-call(f32[32,8,128]{2,1,0:T(8,128)S(1)} %all-to-all-done.3.parts_ref, f32[16,128]{1,0:T(8,128)S(1)} %get-tuple-element.53.rays_ref, f32[16,128]{1,0:T(8,128)S(1)} %copy-done.2, f32[16,8,128]{2,1,0:T(8,128)S(1)} %get-tuple-element.54.pick_ref, ...), custom_call_target="tpu_custom_call" | custom-call | tf_op jit(solution)/shard_map/pallas_call | solution.py:56
  92.2 8.4 %all-to-all-start.4 = ((bf16[16,32,128]{2,1,0:T(8,128)(2,1)}), bf16[16,32,128]{2,1,0:T(8,128)(2,1)S(1)}, u32[]{:S(2)}, u32[]{:S(2)}) async-start(bf16[16,32,128]{2,1,0:T(8,128)(2,1)} %get-tuple-element.63), calls=%async_computation.4 | async-start | bytes 262144 | tf_op jit(solution)/shard_map/all_to_all | solution.py:42
  100.6 1.9 %collective-permute-start.3 = (f32[16,128]{1,0:T(8,128)S(1)}, f32[16,128]{1,0:T(8,128)S(1)}, u32[]{:S(2)}, u32[]{:S(2)}) collective-permute-start(f32[16,128]{1,0:T(8,128)S(1)} %get-tuple-element.60), channel_id=1, source_target_pairs={{0,1},{2,3},{4,5},{6,7},{8,9},{10,11},{12,13},{14,15},{16,17},{18,... | collective-permute-start | bytes 24584 | tf_op jit(solution)/shard_map/ppermute | solution.py:330
  102.5 1.1 %collective-permute-done.3.near_ref = f32[16,128]{1,0:T(8,128)S(1)} collective-permute-done((f32[16,128]{1,0:T(8,128)S(1)}, f32[16,128]{1,0:T(8,128)S(1)}, u32[]{:S(2)}, u32[]{:S(2)}) %collective-permute-start.3) | collective-permute-done | bytes 8224 | tf_op jit(solution)/shard_map/ppermute | solution.py:330
  103.6 0.0 copy-done.3
  103.6 0.7 shard_map.138
  104.3 0.0 all-to-all-done.4
  104.4 0.6 fusion.2
  (2 shorter events, 0.0 us)
Async XLA Ops:
  2.5 16.2 %all-to-all-start = ((bf16[16,48,128]{2,1,0:T(8,128)(2,1)}), bf16[16,48,128]{2,1,0:T(8,128)(2,1)S(1)}, u32[]{:S(2)}, u32[]{:S(2)}) async-start(bf16[16,48,128]{2,1,0:T(8,128)(2,1)} %get-tuple-element.36), calls=%async_computation | async-start | bytes 393216 | tf_op jit(solution)/shard_map/all_to_all | solution.py:42
  16.9 20.7 %copy-start = (f32[3,4,8,128]{3,2,1,0:T(8,128)S(1)}, f32[3,4,8,128]{3,2,1,0:T(8,128)}, u32[]{:S(2)}) copy-start(f32[3,4,8,128]{3,2,1,0:T(8,128)} %dual_ref.3) | copy-start | bytes 147460
  16.9 29.8 %copy-start.1 = (f32[4,8,128]{2,1,0:T(8,128)S(1)}, f32[4,8,128]{2,1,0:T(8,128)}, u32[]{:S(2)}) copy-start(f32[4,8,128]{2,1,0:T(8,128)} %image_ref.3) | copy-start | bytes 49156
  16.9 30.0 %copy-start.2 = (f32[16,128]{1,0:T(8,128)S(1)}, f32[16,128]{1,0:T(8,128)}, u32[]{:S(2)}) copy-start(f32[16,128]{1,0:T(8,128)} %times_ref.3) | copy-start | bytes 24580
  17.0 30.0 %copy-start.4 = (f32[16,128]{1,0:T(8,128)S(1)}, f32[16,128]{1,0:T(8,128)}, u32[]{:S(2)}) copy-start(f32[16,128]{1,0:T(8,128)} %rays_ref.1) | copy-start | bytes 24580
  20.7 26.3 %all-to-all-start.1 = ((f32[32,8,128]{2,1,0:T(8,128)}), f32[32,8,128]{2,1,0:T(8,128)S(1)}, u32[]{:S(2)}, u32[]{:S(2)}) async-start(f32[32,8,128]{2,1,0:T(8,128)} %shard_map.130.after_any.after_ref), calls=%async_computation.1 | async-start | bytes 262144 | tf_op jit(solution)/shard_map/all_to_all | solution.py:42
  37.7 9.1 %collective-permute-start = (f32[40,128]{1,0:T(8,128)S(1)}, f32[40,128]{1,0:T(8,128)S(1)}, u32[]{:S(2)}, u32[]{:S(2)}) collective-permute-start(f32[40,128]{1,0:T(8,128)S(1)} %get-tuple-element.39), channel_id=1, source_target_pairs={{1,2},{3,4},{5,6},{7,8},{9,10},{11,12},{13,14},{15,16},{17,18},{19... | collective-permute-start | bytes 61448 | tf_op jit(solution)/shard_map/ppermute | solution.py:330
  40.1 6.6 %collective-permute-start.1 = (f32[40,128]{1,0:T(8,128)S(1)}, f32[40,128]{1,0:T(8,128)S(1)}, u32[]{:S(2)}, u32[]{:S(2)}) collective-permute-start(f32[40,128]{1,0:T(8,128)S(1)} %get-tuple-element.40), channel_id=1, source_target_pairs={{0,1},{2,3},{4,5},{6,7},{8,9},{10,11},{12,13},{14,15},{16,17},{18,... | collective-permute-start | bytes 61448 | tf_op jit(solution)/shard_map/ppermute | solution.py:330
  48.4 15.4 %all-to-all-start.2 = ((bf16[16,112,128]{2,1,0:T(8,128)(2,1)}), bf16[16,112,128]{2,1,0:T(8,128)(2,1)S(1)}, u32[]{:S(2)}, u32[]{:S(2)}) async-start(bf16[16,112,128]{2,1,0:T(8,128)(2,1)} %get-tuple-element.45), calls=%async_computation.2 | async-start | bytes 917504 | tf_op jit(solution)/shard_map/all_to_all | solution.py:42
  66.8 23.9 %all-to-all-start.3 = ((f32[32,8,128]{2,1,0:T(8,128)}), f32[32,8,128]{2,1,0:T(8,128)S(1)}, u32[]{:S(2)}, u32[]{:S(2)}) async-start(f32[32,8,128]{2,1,0:T(8,128)} %get-tuple-element.52), calls=%async_computation.3 | async-start | bytes 262144 | tf_op jit(solution)/shard_map/all_to_all | solution.py:42
  81.6 22.1 %copy-start.3 = (f32[4,8,128]{2,1,0:T(8,128)S(1)}, f32[4,8,128]{2,1,0:T(8,128)}, u32[]{:S(2)}) copy-start(f32[4,8,128]{2,1,0:T(8,128)} %get-tuple-element.30.field_ref) | copy-start | bytes 49156
  81.6 9.0 %collective-permute-start.2 = (f32[16,128]{1,0:T(8,128)S(1)}, f32[16,128]{1,0:T(8,128)S(1)}, u32[]{:S(2)}, u32[]{:S(2)}) collective-permute-start(f32[16,128]{1,0:T(8,128)S(1)} %get-tuple-element.55), channel_id=1, source_target_pairs={{1,2},{3,4},{5,6},{7,8},{9,10},{11,12},{13,14},{15,16},{17,18},{19... | collective-permute-start | bytes 24584 | tf_op jit(solution)/shard_map/ppermute | solution.py:330
  92.2 12.2 %all-to-all-start.4 = ((bf16[16,32,128]{2,1,0:T(8,128)(2,1)}), bf16[16,32,128]{2,1,0:T(8,128)(2,1)S(1)}, u32[]{:S(2)}, u32[]{:S(2)}) async-start(bf16[16,32,128]{2,1,0:T(8,128)(2,1)} %get-tuple-element.63), calls=%async_computation.4 | async-start | bytes 262144 | tf_op jit(solution)/shard_map/all_to_all | solution.py:42
  100.6 3.1 %collective-permute-start.3 = (f32[16,128]{1,0:T(8,128)S(1)}, f32[16,128]{1,0:T(8,128)S(1)}, u32[]{:S(2)}, u32[]{:S(2)}) collective-permute-start(f32[16,128]{1,0:T(8,128)S(1)} %get-tuple-element.60), channel_id=1, source_target_pairs={{0,1},{2,3},{4,5},{6,7},{8,9},{10,11},{12,13},{14,15},{16,17},{18,... | collective-permute-start | bytes 24584 | tf_op jit(solution)/shard_map/ppermute | solution.py:330

commit v7 on v6

--- a/solution.py
+++ b/solution.py
@@ -20,7 +20,7 @@
 REST = OWN + 8
 EXTRA = PRODUCTS + OWN
 SHARED = EXTRA + 16
-GATHER, SUM_1, SHARE, SUM_2, LAST = 15, 18, 15, 18, 15
+GATHER, SUM_1, SHARE, SUM_2, LAST = 9, 19, 5, 3, 5
 
 primal_step = 0.5
 dual_step = 0.5
@@ -193,11 +193,12 @@
     sub = lax.broadcasted_iota(jnp.int32, (MAXSEL, TILE), 0)
     total = jnp.zeros((MAXSEL, TILE), F32)
     for n in range(MAXSEL):
-        for s in range(CAP):
-            row = cells[n * CAP + s : n * CAP + s + 1]
-            lhs = jnp.where(sub == n, row, 0.0).astype(BF16)
+        for s in range(0, CAP, 8):
+            rows = [cells[n * CAP + t : n * CAP + t + 1] for t in range(s, s + 8)]
+            lhs = jnp.concatenate([jnp.where(sub == n, row, 0.0) for row in rows], axis=1).astype(BF16)
+            rhs = jnp.concatenate([picked_ref[n, t] for t in range(s, s + 8)], axis=1)
             total = total + lax.dot_general(
-                lhs, picked_ref[n, s], (((1,), (1,)), ((), ())), preferred_element_type=F32
+                lhs, rhs, (((1,), (1,)), ((), ())), preferred_element_type=F32
             )
     for m in range(N_MP):
         out_ref[m] = total
@@ -233,9 +234,12 @@
     sub = lax.broadcasted_iota(jnp.int32, (CAP, TILE), 0)
     row = change[n : n + 1]
     total = jnp.zeros((CAP, TILE), F32)
-    for s in range(CAP):
-        lhs = jnp.where(sub == s, row, 0.0).astype(BF16)
-        total = total + jnp.dot(lhs, picked_ref[n, s], preferred_element_type=F32)
+    for s in range(0, CAP, 8):
+        lhs = jnp.concatenate(
+            [jnp.where(sub == t, row, 0.0) for t in range(s, s + 8)], axis=1
+        ).astype(BF16)
+        rhs = picked_ref[n, s : s + 8].reshape(8 * TILE, TILE)
+        total = total + jnp.dot(lhs, rhs, preferred_element_type=F32)
     return total
 
 

time: 106 us -> 98.8 us (0.932)
  the two profiles are of different devices: /device:TPU:1 before, /device:TPU:32 now
where the time goes in v7:
time: 98.8 us; the launch traced here: 98 us
  starting transfers between devices  51.3 us (52%)
  waiting for transfers between devices  30.4 us (31%)
  Pallas kernels  14.9 us (15%)
    all_to_all x5, starting transfers between devices, exchange(): lax.all_to_all(copies, axis, 0, 0, tiled=True, axis_index_groups=groups)  40.8 us
    all_to_all x5, waiting for transfers between devices, exchange(): lax.all_to_all(copies, axis, 0, 0, tiled=True, axis_index_groups=groups)  15.6 us
    pallas_call x11, Pallas kernels, call(): pl.pallas_call(kernel, out_shape=[pltpu.VMEM(shape, dtype) if keep else j...  14.9 us
    ppermute x4, waiting for transfers between devices, swap(): return lax.ppermute(block, 'mp', route + [(b, a) for a, b in route])  14.8 us
    ppermute x4, starting transfers between devices, swap(): return lax.ppermute(block, 'mp', route + [(b, a) for a, b in route])  10.5 us
  transfers between devices with their start and end apart: 9, of which 6 were waited for; matrix products, arithmetic and copies ran while one was open for 0% of the time, Pallas kernels for 7%

profile of v7, /device:TPU:32, one launch (start us, length us, event | category | flops | bytes accessed | tf_op | source)
XLA Modules:
  0.0 98.0 jit_solution(15391041618482070303)
XLA Ops:
  0.6 1.9 %shard_map.128 = (f32[4,8,128]{2,1,0:T(8,128)S(1)}, bf16[16,48,128]{2,1,0:T(8,128)(2,1)}) custom-call(f32[4,8,128]{2,1,0:T(8,128)} %slowness_hbm.1, f32[4,8,128]{2,1,0:T(8,128)} %bar_hbm.1, s32[8,16]{1,0:T(8,128)} %bitcast.11, s32[2,16]{1,0:T(2,128)} %selected_hbm.5), custom_call_target="tpu_custom_call" | custom-call | tf_op jit(solution)/shard_map/pallas_call | solution.py:56
  2.5 10.3 %all-to-all-start = ((bf16[16,48,128]{2,1,0:T(8,128)(2,1)}), bf16[16,48,128]{2,1,0:T(8,128)(2,1)S(1)}, u32[]{:S(2)}, u32[]{:S(2)}) async-start(bf16[16,48,128]{2,1,0:T(8,128)(2,1)} %get-tuple-element.36), calls=%async_computation | async-start | bytes 393216 | tf_op jit(solution)/shard_map/all_to_all | solution.py:42
  12.8 2.7 %shard_map.129 = (bf16[8,8,128,128]{3,2,1,0:T(8,128)(2,1)S(1)}, bf16[64,512]{1,0:T(8,128)(2,1)S(1)}, f32[16,8,128]{2,1,0:T(8,128)S(1)}) custom-call(bf16[16,8,128,128]{3,2,1,0:T(8,128)(2,1)} %tiles_hbm.3, s32[8,16]{1,0:T(8,128)} %bitcast.12, s32[2,16]{1,0:T(2,128)} %selected_hbm.5, f32[4,8,128]{2,1,0:T(8,128)S(1)} %get-tuple-element.35.after_ref.field_ref), custom_call_target="tpu_custom_call" | custom-call | bytes 8388608 | tf_op jit(solution)/shard_map/pallas_call | solution.py:56
  15.6 0.0 copy-start
  15.6 0.0 copy-start.1
  15.6 0.0 copy-start.2
  15.6 0.0 copy-start.4
  15.6 3.9 %all-to-all-done.gathered_ref = bf16[16,48,128]{2,1,0:T(8,128)(2,1)S(1)} async-done(((bf16[16,48,128]{2,1,0:T(8,128)(2,1)}), bf16[16,48,128]{2,1,0:T(8,128)(2,1)S(1)}, u32[]{:S(2)}, u32[]{:S(2)}) %all-to-all-start) | async-done | bytes 196640 | tf_op jit(solution)/shard_map/all_to_all | solution.py:42
  19.5 1.4 %shard_map.130.after_any.after_ref = f32[32,8,128]{2,1,0:T(8,128)} custom-call(bf16[16,48,128]{2,1,0:T(8,128)(2,1)S(1)} %all-to-all-done.gathered_ref, bf16[8,8,128,128]{3,2,1,0:T(8,128)(2,1)S(1)} %get-tuple-element.37.picked_ref, bf16[64,512]{1,0:T(8,128)(2,1)S(1)} %get-tuple-element.38.hot_ref), custom_call_target="tpu_custom_call" | custom-call | tf_op jit(solution)/shard_map/pallas_call | solution.py:56
  21.0 8.4 %all-to-all-start.1 = ((f32[32,8,128]{2,1,0:T(8,128)}), f32[32,8,128]{2,1,0:T(8,128)S(1)}, u32[]{:S(2)}, u32[]{:S(2)}) async-start(f32[32,8,128]{2,1,0:T(8,128)} %shard_map.130.after_any.after_ref), calls=%async_computation.1 | async-start | bytes 262144 | tf_op jit(solution)/shard_map/all_to_all | solution.py:42
  29.4 0.0 copy-done
  29.5 4.3 %collective-permute-start = (f32[40,128]{1,0:T(8,128)S(1)}, f32[40,128]{1,0:T(8,128)S(1)}, u32[]{:S(2)}, u32[]{:S(2)}) collective-permute-start(f32[40,128]{1,0:T(8,128)S(1)} %get-tuple-element.39), channel_id=1, source_target_pairs={{1,2},{3,4},{5,6},{7,8},{9,10},{11,12},{13,14},{15,16},{17,18},{19... | collective-permute-start | bytes 61448 | tf_op jit(solution)/shard_map/ppermute | solution.py:334
  33.8 1.9 %collective-permute-start.1 = (f32[40,128]{1,0:T(8,128)S(1)}, f32[40,128]{1,0:T(8,128)S(1)}, u32[]{:S(2)}, u32[]{:S(2)}) collective-permute-start(f32[40,128]{1,0:T(8,128)S(1)} %get-tuple-element.40), channel_id=1, source_target_pairs={{0,1},{2,3},{4,5},{6,7},{8,9},{10,11},{12,13},{14,15},{16,17},{18,... | collective-permute-start | bytes 61448 | tf_op jit(solution)/shard_map/ppermute | solution.py:334
  35.7 4.9 %collective-permute-done.far_ref = f32[40,128]{1,0:T(8,128)S(1)} collective-permute-done((f32[40,128]{1,0:T(8,128)S(1)}, f32[40,128]{1,0:T(8,128)S(1)}, u32[]{:S(2)}, u32[]{:S(2)}) %collective-permute-start) | collective-permute-done | bytes 20512 | tf_op jit(solution)/shard_map/ppermute | solution.py:334
  40.6 0.0 collective-permute-done.1.near_ref
  40.6 0.0 copy-done.1
  40.6 0.2 shard_map.132
  40.8 0.0 all-to-all-done.1.parts_ref
  40.8 0.0 copy-done.2
  40.8 0.0 copy-done.4
  40.8 1.2 %shard_map.133 = (f32[16,128]{1,0:T(8,128)S(1)}, bf16[16,112,128]{2,1,0:T(8,128)(2,1)}) custom-call(f32[32,8,128]{2,1,0:T(8,128)S(1)} %all-to-all-done.1.parts_ref, f32[16,128]{1,0:T(8,128)S(1)} %copy-done.4, f32[16,128]{1,0:T(8,128)S(1)} %copy-done.2, f32[16,8,128]{2,1,0:T(8,128)S(1)} %get-tuple-element.42.pick_ref, ...), custom_call_target="tpu_custom_call" | custom-call | tf_op jit(solution)/shard_map/pallas_call | solution.py:56
  42.0 5.4 %all-to-all-start.2 = ((bf16[16,112,128]{2,1,0:T(8,128)(2,1)}), bf16[16,112,128]{2,1,0:T(8,128)(2,1)S(1)}, u32[]{:S(2)}, u32[]{:S(2)}) async-start(bf16[16,112,128]{2,1,0:T(8,128)(2,1)} %get-tuple-element.45), calls=%async_computation.2 | async-start | bytes 917504 | tf_op jit(solution)/shard_map/all_to_all | solution.py:42
  47.4 2.5 %shard_map.134 = (bf16[8,8,128,128]{3,2,1,0:T(8,128)(2,1)S(1)}, bf16[64,512]{1,0:T(8,128)(2,1)S(1)}, f32[16,8,128]{2,1,0:T(8,128)S(1)}) custom-call(bf16[16,8,128,128]{3,2,1,0:T(8,128)(2,1)} %tiles_hbm.3, s32[8,16]{1,0:T(8,128)} %bitcast.13, s32[2,16]{1,0:T(2,128)} %selected_hbm.5, f32[32,8,128]{2,1,0:T(8,128)} %shard_map.130.after_any.after_ref), custom_call_target="tpu_custom_call" | custom-call | bytes 8388608 | tf_op jit(solution)/shard_map/pallas_call | solution.py:56
  49.9 8.7 %all-to-all-done.2.shared_ref = bf16[16,112,128]{2,1,0:T(8,128)(2,1)S(1)} async-done(((bf16[16,112,128]{2,1,0:T(8,128)(2,1)}), bf16[16,112,128]{2,1,0:T(8,128)(2,1)S(1)}, u32[]{:S(2)}, u32[]{:S(2)}) %all-to-all-start.2) | async-done | bytes 458784 | tf_op jit(solution)/shard_map/all_to_all | solution.py:42
  58.6 2.4 %shard_map.135 = (f32[32,128]{1,0:T(8,128)S(1)}, f32[24,128]{1,0:T(8,128)S(1)}, f32[32,8,128]{2,1,0:T(8,128)}) custom-call(bf16[16,112,128]{2,1,0:T(8,128)(2,1)S(1)} %all-to-all-done.2.shared_ref, bf16[16,48,128]{2,1,0:T(8,128)(2,1)S(1)} %all-to-all-done.gathered_ref, bf16[8,8,128,128]{3,2,1,0:T(8,128)(2,1)S(1)} %get-tuple-element.46.picked_ref, ...), custom_call_target="tpu_custom_call" | custom-call | tf_op jit(solution)/shard_map/pallas_call | solution.py:56
  61.0 12.1 %all-to-all-start.3 = ((f32[32,8,128]{2,1,0:T(8,128)}), f32[32,8,128]{2,1,0:T(8,128)S(1)}, u32[]{:S(2)}, u32[]{:S(2)}) async-start(f32[32,8,128]{2,1,0:T(8,128)} %get-tuple-element.52), calls=%async_computation.3 | async-start | bytes 262144 | tf_op jit(solution)/shard_map/all_to_all | solution.py:42
  73.1 0.6 shard_map.136
  73.7 0.0 copy-start.3
  73.7 2.3 %collective-permute-start.2 = (f32[16,128]{1,0:T(8,128)S(1)}, f32[16,128]{1,0:T(8,128)S(1)}, u32[]{:S(2)}, u32[]{:S(2)}) collective-permute-start(f32[16,128]{1,0:T(8,128)S(1)} %get-tuple-element.55), channel_id=1, source_target_pairs={{1,2},{3,4},{5,6},{7,8},{9,10},{11,12},{13,14},{15,16},{17,18},{19... | collective-permute-start | bytes 24584 | tf_op jit(solution)/shard_map/ppermute | solution.py:334
  76.0 8.8 %collective-permute-done.2.far_any.far_ref = f32[16,128]{1,0:T(8,128)S(1)} collective-permute-done((f32[16,128]{1,0:T(8,128)S(1)}, f32[16,128]{1,0:T(8,128)S(1)}, u32[]{:S(2)}, u32[]{:S(2)}) %collective-permute-start.2) | collective-permute-done | bytes 8224 | tf_op jit(solution)/shard_map/ppermute | solution.py:334
  84.8 0.0 all-to-all-done.3.parts_ref
  84.8 1.3 %shard_map.137 = (f32[16,128]{1,0:T(8,128)}, bf16[16,32,128]{2,1,0:T(8,128)(2,1)}, f32[16,128]{1,0:T(8,128)S(1)}) custom-call(f32[32,8,128]{2,1,0:T(8,128)S(1)} %all-to-all-done.3.parts_ref, f32[16,128]{1,0:T(8,128)S(1)} %get-tuple-element.53.rays_ref, f32[16,128]{1,0:T(8,128)S(1)} %copy-done.2, f32[16,8,128]{2,1,0:T(8,128)S(1)} %get-tuple-element.54.pick_ref, ...), custom_call_target="tpu_custom_call" | custom-call | tf_op jit(solution)/shard_map/pallas_call | solution.py:56
  86.1 4.5 %all-to-all-start.4 = ((bf16[16,32,128]{2,1,0:T(8,128)(2,1)}), bf16[16,32,128]{2,1,0:T(8,128)(2,1)S(1)}, u32[]{:S(2)}, u32[]{:S(2)}) async-start(bf16[16,32,128]{2,1,0:T(8,128)(2,1)} %get-tuple-element.63), calls=%async_computation.4 | async-start | bytes 262144 | tf_op jit(solution)/shard_map/all_to_all | solution.py:42
  90.6 1.9 %collective-permute-start.3 = (f32[16,128]{1,0:T(8,128)S(1)}, f32[16,128]{1,0:T(8,128)S(1)}, u32[]{:S(2)}, u32[]{:S(2)}) collective-permute-start(f32[16,128]{1,0:T(8,128)S(1)} %get-tuple-element.60), channel_id=1, source_target_pairs={{0,1},{2,3},{4,5},{6,7},{8,9},{10,11},{12,13},{14,15},{16,17},{18,... | collective-permute-start | bytes 24584 | tf_op jit(solution)/shard_map/ppermute | solution.py:334
  92.5 1.1 %collective-permute-done.3.near_ref = f32[16,128]{1,0:T(8,128)S(1)} collective-permute-done((f32[16,128]{1,0:T(8,128)S(1)}, f32[16,128]{1,0:T(8,128)S(1)}, u32[]{:S(2)}, u32[]{:S(2)}) %collective-permute-start.3) | collective-permute-done | bytes 8224 | tf_op jit(solution)/shard_map/ppermute | solution.py:334
  93.7 0.0 copy-done.3
  93.7 0.7 shard_map.138
  94.4 3.0 %all-to-all-done.4 = bf16[16,32,128]{2,1,0:T(8,128)(2,1)S(1)} async-done(((bf16[16,32,128]{2,1,0:T(8,128)(2,1)}), bf16[16,32,128]{2,1,0:T(8,128)(2,1)S(1)}, u32[]{:S(2)}, u32[]{:S(2)}) %all-to-all-start.4) | async-done | bytes 131104 | tf_op jit(solution)/shard_map/all_to_all | solution.py:42
  97.4 0.6 fusion.2
  (2 shorter events, 0.0 us)
Async XLA Ops:
  2.5 17.0 %all-to-all-start = ((bf16[16,48,128]{2,1,0:T(8,128)(2,1)}), bf16[16,48,128]{2,1,0:T(8,128)(2,1)S(1)}, u32[]{:S(2)}, u32[]{:S(2)}) async-start(bf16[16,48,128]{2,1,0:T(8,128)(2,1)} %get-tuple-element.36), calls=%async_computation | async-start | bytes 393216 | tf_op jit(solution)/shard_map/all_to_all | solution.py:42
  15.6 13.9 %copy-start = (f32[3,4,8,128]{3,2,1,0:T(8,128)S(1)}, f32[3,4,8,128]{3,2,1,0:T(8,128)}, u32[]{:S(2)}) copy-start(f32[3,4,8,128]{3,2,1,0:T(8,128)} %dual_ref.3) | copy-start | bytes 147460
  15.6 25.0 %copy-start.1 = (f32[4,8,128]{2,1,0:T(8,128)S(1)}, f32[4,8,128]{2,1,0:T(8,128)}, u32[]{:S(2)}) copy-start(f32[4,8,128]{2,1,0:T(8,128)} %image_ref.3) | copy-start | bytes 49156
  15.6 25.2 %copy-start.2 = (f32[16,128]{1,0:T(8,128)S(1)}, f32[16,128]{1,0:T(8,128)}, u32[]{:S(2)}) copy-start(f32[16,128]{1,0:T(8,128)} %times_ref.3) | copy-start | bytes 24580
  15.6 25.2 %copy-start.4 = (f32[16,128]{1,0:T(8,128)S(1)}, f32[16,128]{1,0:T(8,128)}, u32[]{:S(2)}) copy-start(f32[16,128]{1,0:T(8,128)} %rays_ref.1) | copy-start | bytes 24580
  21.0 19.8 %all-to-all-start.1 = ((f32[32,8,128]{2,1,0:T(8,128)}), f32[32,8,128]{2,1,0:T(8,128)S(1)}, u32[]{:S(2)}, u32[]{:S(2)}) async-start(f32[32,8,128]{2,1,0:T(8,128)} %shard_map.130.after_any.after_ref), calls=%async_computation.1 | async-start | bytes 262144 | tf_op jit(solution)/shard_map/all_to_all | solution.py:42
  29.5 11.1 %collective-permute-start = (f32[40,128]{1,0:T(8,128)S(1)}, f32[40,128]{1,0:T(8,128)S(1)}, u32[]{:S(2)}, u32[]{:S(2)}) collective-permute-start(f32[40,128]{1,0:T(8,128)S(1)} %get-tuple-element.39), channel_id=1, source_target_pairs={{1,2},{3,4},{5,6},{7,8},{9,10},{11,12},{13,14},{15,16},{17,18},{19... | collective-permute-start | bytes 61448 | tf_op jit(solution)/shard_map/ppermute | solution.py:334
  33.8 6.8 %collective-permute-start.1 = (f32[40,128]{1,0:T(8,128)S(1)}, f32[40,128]{1,0:T(8,128)S(1)}, u32[]{:S(2)}, u32[]{:S(2)}) collective-permute-start(f32[40,128]{1,0:T(8,128)S(1)} %get-tuple-element.40), channel_id=1, source_target_pairs={{0,1},{2,3},{4,5},{6,7},{8,9},{10,11},{12,13},{14,15},{16,17},{18,... | collective-permute-start | bytes 61448 | tf_op jit(solution)/shard_map/ppermute | solution.py:334
  42.0 16.6 %all-to-all-start.2 = ((bf16[16,112,128]{2,1,0:T(8,128)(2,1)}), bf16[16,112,128]{2,1,0:T(8,128)(2,1)S(1)}, u32[]{:S(2)}, u32[]{:S(2)}) async-start(bf16[16,112,128]{2,1,0:T(8,128)(2,1)} %get-tuple-element.45), calls=%async_computation.2 | async-start | bytes 917504 | tf_op jit(solution)/shard_map/all_to_all | solution.py:42
  61.0 23.8 %all-to-all-start.3 = ((f32[32,8,128]{2,1,0:T(8,128)}), f32[32,8,128]{2,1,0:T(8,128)S(1)}, u32[]{:S(2)}, u32[]{:S(2)}) async-start(f32[32,8,128]{2,1,0:T(8,128)} %get-tuple-element.52), calls=%async_computation.3 | async-start | bytes 262144 | tf_op jit(solution)/shard_map/all_to_all | solution.py:42
  73.7 20.0 %copy-start.3 = (f32[4,8,128]{2,1,0:T(8,128)S(1)}, f32[4,8,128]{2,1,0:T(8,128)}, u32[]{:S(2)}) copy-start(f32[4,8,128]{2,1,0:T(8,128)} %get-tuple-element.30.field_ref) | copy-start | bytes 49156
  73.7 11.1 %collective-permute-start.2 = (f32[16,128]{1,0:T(8,128)S(1)}, f32[16,128]{1,0:T(8,128)S(1)}, u32[]{:S(2)}, u32[]{:S(2)}) collective-permute-start(f32[16,128]{1,0:T(8,128)S(1)} %get-tuple-element.55), channel_id=1, source_target_pairs={{1,2},{3,4},{5,6},{7,8},{9,10},{11,12},{13,14},{15,16},{17,18},{19... | collective-permute-start | bytes 24584 | tf_op jit(solution)/shard_map/ppermute | solution.py:334
  86.1 11.3 %all-to-all-start.4 = ((bf16[16,32,128]{2,1,0:T(8,128)(2,1)}), bf16[16,32,128]{2,1,0:T(8,128)(2,1)S(1)}, u32[]{:S(2)}, u32[]{:S(2)}) async-start(bf16[16,32,128]{2,1,0:T(8,128)(2,1)} %get-tuple-element.63), calls=%async_computation.4 | async-start | bytes 262144 | tf_op jit(solution)/shard_map/all_to_all | solution.py:42
  90.6 3.1 %collective-permute-start.3 = (f32[16,128]{1,0:T(8,128)S(1)}, f32[16,128]{1,0:T(8,128)S(1)}, u32[]{:S(2)}, u32[]{:S(2)}) collective-permute-start(f32[16,128]{1,0:T(8,128)S(1)} %get-tuple-element.60), channel_id=1, source_target_pairs={{0,1},{2,3},{4,5},{6,7},{8,9},{10,11},{12,13},{14,15},{16,17},{18,... | collective-permute-start | bytes 24584 | tf_op jit(solution)/shard_map/ppermute | solution.py:334

commit v8 on v7

--- a/solution.py
+++ b/solution.py
@@ -20,7 +20,7 @@
 REST = OWN + 8
 EXTRA = PRODUCTS + OWN
 SHARED = EXTRA + 16
-GATHER, SUM_1, SHARE, SUM_2, LAST = 9, 19, 5, 3, 5
+GATHER, SUM_1, SHARE, SUM_2, LAST = 9, 19, 5, 19, 10
 
 primal_step = 0.5
 dual_step = 0.5
@@ -188,7 +188,7 @@
     )
 
 
-def forward(hot_ref, blocks, picked_ref, out_ref):
+def forward(hot_ref, blocks, picked_ref):
     cells = jnp.dot(hot_ref[...], blocks, preferred_element_type=F32)
     sub = lax.broadcasted_iota(jnp.int32, (MAXSEL, TILE), 0)
     total = jnp.zeros((MAXSEL, TILE), F32)
@@ -200,19 +200,17 @@
             total = total + lax.dot_general(
                 lhs, rhs, (((1,), (1,)), ((), ())), preferred_element_type=F32
             )
+    return total
+
+
+def predict_kernel(gathered_ref, picked_ref, hot_ref, out_ref):
+    blocks = jnp.concatenate([gathered_ref[at(p, GATHER), 0:OWN, :] for p in range(N_RAY)], axis=0)
+    total = forward(hot_ref, blocks, picked_ref)
     for m in range(N_MP):
         out_ref[m] = total
 
 
-def predict_kernel(gathered_ref, picked_ref, hot_ref, out_ref):
-    blocks = jnp.concatenate([gathered_ref[at(p, GATHER), 0:OWN, :] for p in range(N_RAY)], axis=0)
-    forward(hot_ref, blocks, picked_ref, out_ref)
-
-
-def dual_update(parts_ref, rays_ref, times_ref, pick_ref, new_rays_ref):
-    predicted = parts_ref[0]
-    for m in range(1, N_MP):
-        predicted = predicted + parts_ref[m]
+def dual_update(predicted, rays_ref, times_ref, pick_ref, new_rays_ref):
     rays = jnp.zeros((MAXSEL, TILE), F32)
     times = jnp.zeros((MAXSEL, TILE), F32)
     taken = jnp.zeros((MAXSEL, TILE), F32)
@@ -246,7 +244,10 @@
 def share_kernel(
     parts_ref, rays_ref, times_ref, pick_ref, picked_ref, rest_ref, extra_ref, new_rays_ref, out_ref
 ):
-    change = dual_update(parts_ref, rays_ref, times_ref, pick_ref, new_rays_ref)
+    predicted = parts_ref[0]
+    for m in range(1, N_MP):
+        predicted = predicted + parts_ref[m]
+    change = dual_update(predicted, rays_ref, times_ref, pick_ref, new_rays_ref)
     for n in range(0, MAXSEL, 2):
         pair = jnp.concatenate(
             [products(change, picked_ref, n), products(change, picked_ref, n + 1)], axis=0
@@ -261,7 +262,8 @@
 
 
 def image_kernel(
-    shared_ref, gathered_ref, picked_ref, hot_ref, back_ref, edge_ref, out_ref, table_ref
+    shared_ref, gathered_ref, picked_ref, hot_ref, first_ref, base_ref, image_ref, tv_ref,
+    field_ref, new_image_ref, edge_ref, out_ref, table_ref,
 ):
     lane = lax.broadcasted_iota(jnp.int32, (1, TILE), 1)
     singles = []
@@ -299,11 +301,11 @@
                     [jnp.where(sub == 0, change[x : x + 1], 0.0) for x in range(GX)], axis=0
                 )
             blocks.append(field)
-    forward(
-        hot_ref, jnp.concatenate([field.astype(BF16) for field in blocks], axis=0), picked_ref, out_ref
-    )
-    me = lax.axis_index("ray")
-    back_ref[...] = table_ref[pl.ds(pl.multiple_of(me * OWN, OWN), OWN), :]
+    total = forward(
+        hot_ref, jnp.concatenate([field.astype(BF16) for field in blocks], axis=0), picked_ref
+    )
+    me, mp = lax.axis_index("ray"), lax.axis_index("mp")
+    back = table_ref[pl.ds(pl.multiple_of(me * OWN, OWN), OWN), :]
     for p in range(N_RAY):
         table_ref[p * OWN : (p + 1) * OWN, :] = blocks[p]
     before = jnp.maximum(me - 1, 0)
@@ -311,14 +313,48 @@
         field = table_ref[pl.ds(pl.multiple_of(peer * OWN, OWN), OWN), :]
         for x in range(GX):
             edge_ref[side * GX + x : side * GX + x + 1, :] = field[x * GY + row : x * GY + row + 1]
-    edge_ref[2 * GX : 6 * GX] = shared_ref[at(before, SHARE), EXTRA:SHARED, :].astype(F32)
+    extra = shared_ref[at(before, SHARE), EXTRA:SHARED, :].astype(F32)
+    edge_ref[2 * GX : 6 * GX] = extra
+    first_y = (sub == 0) & (me > 0)
+    field = []
+    for x in range(GX):
+        own = back[x * GY : (x + 1) * GY]
+        from_y = jnp.where(first_y, extra[x : x + 1], 0.0)
+        field.append(base_ref[x] - (gain * own + (2.0 * primal_step) * from_y))
+        field_ref[x] = field[x]
+        new_image_ref[x] = image_ref[x] + own + (tv_ref[x] + from_y)
+    high = total.astype(BF16).astype(F32)
+    ends = [
+        jnp.concatenate([high, total - high, field[x] - first_ref[x]], axis=0) for x in (0, GX - 1)
+    ]
+    for j in range(N_MP):
+        out_ref[j] = jnp.where((SUM_2 + j) % N_MP == mp + 1, ends[1], ends[0]).astype(BF16)
 
 
 def back_kernel(
-    parts_ref, rays_ref, times_ref, pick_ref, picked_ref, hot_ref, far_any, near_ref, new_rays_ref, out_ref, same_ref
+    parts_ref, rays_ref, times_ref, pick_ref, picked_ref, hot_ref, far_ref, near_ref, new_rays_ref, out_ref, planes_ref
 ):
-    same_ref[...] = near_ref[...]
-    change = dual_update(parts_ref, rays_ref, times_ref, pick_ref, new_rays_ref)
+    mp = lax.axis_index("mp")
+    before, behind = x_halos(far_ref, near_ref)
+    step = parts_ref[(mp + (N_MP - 1 - SUM_2)) & (N_MP - 1)].astype(F32)
+    before = before[0:GY] + step[2 * MAXSEL :]
+    step = parts_ref[(mp + (N_MP + 1 - SUM_2)) & (N_MP - 1)].astype(F32)
+    behind = behind[0:GY] + step[2 * MAXSEL :]
+    planes_ref[0] = before
+    planes_ref[1] = behind
+    corners = [before[0:1], behind[GY - 1 : GY]]
+    highs = [corner.astype(BF16).astype(F32) for corner in corners]
+    sub = lax.broadcasted_iota(jnp.int32, (16, TILE), 0)
+    tail = jnp.zeros((16, TILE), F32)
+    for i in range(2):
+        tail = jnp.where(sub == 2 * i, highs[i], tail)
+        tail = jnp.where(sub == 2 * i + 1, corners[i] - highs[i], tail)
+    tail = tail.astype(BF16)
+    halves = parts_ref[0].astype(F32)
+    for m in range(1, N_MP):
+        halves = halves + parts_ref[m].astype(F32)
+    predicted = halves[0:MAXSEL] + halves[MAXSEL : 2 * MAXSEL]
+    change = dual_update(predicted, rays_ref, times_ref, pick_ref, new_rays_ref)
     terms = jnp.concatenate([products(change, picked_ref, n) for n in range(MAXSEL)], axis=0)
     high = terms.astype(BF16)
     low = (terms - high.astype(F32)).astype(BF16)
@@ -326,7 +362,8 @@
     image = lax.dot_general(hot_ref[...], high, turned, preferred_element_type=F32)
     image = image + lax.dot_general(hot_ref[...], low, turned, preferred_element_type=F32)
     for p in range(N_RAY):
-        out_ref[at(p, LAST)] = image[p * OWN : (p + 1) * OWN].astype(BF16)
+        out_ref[at(p, LAST), 0:OWN] = image[p * OWN : (p + 1) * OWN].astype(BF16)
+        out_ref[at(p, LAST), OWN:] = tail
 
 
 def swap(block, first):
@@ -392,18 +429,20 @@
     return jnp.where(sub == GY - 1, row, pltpu.roll(plane, GY - 1, 0))
 
 
-def tv_step_all(field, dual, before, before_next, dual_before, behind, nexts, from_y):
+def plane_before(before, before_next, dual, first):
+    sub = lax.broadcasted_iota(jnp.int32, (GY, TILE), 0)
+    last_y = (sub == GY - 1) & (lax.axis_index("ray") == N_RAY - 1)
+    fresh, change = tv_cells(before, first, up_one(before, before_next), dual, sub < 0, last_y)
+    return fresh, jnp.where(lax.axis_index("mp") == 0, 0.0, change[0])
+
+
+def tv_step_all(field, dual, behind, nexts, from_x):
     mp, ray = lax.axis_index("mp"), lax.axis_index("ray")
     sub = lax.broadcasted_iota(jnp.int32, (GY, TILE), 0)
     lane = lax.broadcasted_iota(jnp.int32, (GY, TILE), 1)
     end_x = (mp == N_MP - 1) & (sub >= 0)
     last_y = (sub == GY - 1) & (ray == N_RAY - 1)
     never = sub < 0
-
-    halo, halo_change = tv_cells(
-        before, field[0], up_one(before, before_next), dual_before, never, last_y
-    )
-    from_x = jnp.where(mp == 0, 0.0, halo_change[0])
     fresh, backs, second = [], [], []
     for x in range(GX):
         ahead = field[x + 1] if x + 1 < GX else behind
@@ -415,13 +454,13 @@
         comp_y = jnp.where(last_y, 0.0, change[1])
         comp_z = jnp.where(lane == TILE - 1, 0.0, change[2])
         back = from_x - comp_x
-        back = back + (jnp.where(sub == 0, from_y[x], pltpu.roll(comp_y, 1, 0)) - comp_y)
+        back = back + (jnp.where(sub == 0, 0.0, pltpu.roll(comp_y, 1, 0)) - comp_y)
         back = back + (jnp.where(lane == 0, 0.0, pltpu.roll(comp_z, 1, 1)) - comp_z)
         from_x = comp_x
         fresh.append(new)
         backs.append(back)
         second.append(comp_y)
-    return fresh, backs, halo, second
+    return fresh, backs, second
 
 
 def first_tv_kernel(
@@ -430,12 +469,14 @@
 ):
     before, behind = x_halos(far_ref, near_ref)
     field = [field_ref[x] for x in range(GX)]
-    fresh, backs, halo, second = tv_step_all(
+    halo, from_x = plane_before(
+        before[0:GY], before[GY : GY + 1],
+        [before[(c + 2) * GY : (c + 3) * GY] for c in range(3)], field[0],
+    )
+    fresh, backs, second = tv_step_all(
         field,
         [[dual_ref[c, x] for x in range(GX)] for c in range(3)],
-        before[0:GY], before[GY : GY + 1],
-        [before[(c + 2) * GY : (c + 3) * GY] for c in range(3)],
-        behind[0:GY], next_rows(gathered_ref), [0.0] * GX,
+        behind[0:GY], next_rows(gathered_ref), from_x,
     )
     for x in range(GX):
         base = field[x] - primal_step * (image_ref[x] + 2.0 * backs[x])
@@ -451,58 +492,52 @@
         plane_ref[c] = halo[c]
 
 
-def second_edges_kernel(
-    base_ref, back_ref, edge_ref, image_ref, tv_ref, field_ref, new_image_ref, far_ref, near_ref
+def second_tv_kernel(field_ref, dual_ref, planes_ref, edge_ref, new_dual_ref, back_ref):
+    edge = edge_ref[...]
+    fresh, backs, _ = tv_step_all(
+        [field_ref[x] for x in range(GX)],
+        [[dual_ref[c, x] for x in range(GX)] for c in range(3)],
+        planes_ref[1], [edge[GX + x : GX + x + 1] for x in range(GX)], 0.0,
+    )
+    for x in range(GX):
+        back_ref[x] = backs[x]
+        for c in range(3):
+            new_dual_ref[c, x] = fresh[x][c]
+
+
+def last_kernel(
+    shared_ref, field_ref, planes_ref, dual_plane_ref, edge_ref, image_ref, tv_ref, out_ref, bar_ref
 ):
-    odd = (lax.axis_index("mp") & 1) == 1
-    sub = lax.broadcasted_iota(jnp.int32, (GY, TILE), 0)
-    first_y = (sub == 0) & (lax.axis_index("ray") > 0)
-    field = []
-    for x in range(GX):
-        back = back_ref[x * GY : (x + 1) * GY]
-        from_y = jnp.where(first_y, edge_ref[2 * GX + x : 2 * GX + x + 1], 0.0)
-        field.append(base_ref[x] - (gain * back + (2.0 * primal_step) * from_y))
-        field_ref[x] = field[x]
-        new_image_ref[x] = image_ref[x] + back + (tv_ref[x] + from_y)
-    edge = edge_ref[0 : 2 * GX]
-    first = jnp.concatenate([field[0], edge], axis=0)
-    last = jnp.concatenate([field[GX - 1], edge], axis=0)
-    far_ref[...] = jnp.where(odd, last, first)
-    near_ref[...] = jnp.where(odd, first, last)
-
-
-def second_tv_kernel(
-    field_ref, dual_ref, plane_ref, far_ref, near_ref, edge_ref, new_dual_ref, back_ref
-):
-    before, behind = x_halos(far_ref, near_ref)
+    ray = lax.axis_index("ray")
+    above = shared_ref[at(jnp.minimum(ray + 1, N_RAY - 1), LAST), OWN:].astype(F32)
+    below = shared_ref[at(jnp.maximum(ray - 1, 0), LAST), OWN:].astype(F32)
+    field = [field_ref[x] for x in range(GX)]
+    _, from_x = plane_before(
+        planes_ref[0], above[0:1] + above[1:2], [dual_plane_ref[c] for c in range(3)], field[0]
+    )
     edge = edge_ref[...]
-    ray = lax.axis_index("ray")
-    end_x = lax.axis_index("mp") == N_MP - 1
-    field = [field_ref[x] for x in range(GX)]
     sub = lax.broadcasted_iota(jnp.int32, (2 * GX, TILE), 0)
     rows = edge[0 : 2 * GX]
-    ahead_x = jnp.where(sub == GX - 1, behind[GY : GY + 1], pltpu.roll(rows, 2 * GX - 1, 0))
+    ahead_x = jnp.where(sub == GX - 1, below[2:3] + below[3:4], pltpu.roll(rows, 2 * GX - 1, 0))
     ahead_y = jnp.concatenate([field[x][0:1] for x in range(GX)] * 2, axis=0)
     dual_rows = [
         jnp.concatenate([edge[(c + 3) * GX : (c + 4) * GX]] * 2, axis=0) for c in range(3)
     ]
-    _, change = tv_cells(
-        rows, ahead_x, ahead_y, dual_rows, (sub == GX - 1) & end_x, sub < 0
-    )
+    end_x = lax.axis_index("mp") == N_MP - 1
+    _, change = tv_cells(rows, ahead_x, ahead_y, dual_rows, (sub == GX - 1) & end_x, sub < 0)
     from_y = jnp.where(ray == 0, 0.0, change[1])
-    fresh, backs, _, _ = tv_step_all(
-        field,
-        [[dual_ref[c, x] for x in range(GX)] for c in range(3)],
-        before[0:GY], before[GY + 2 * GX - 1 : GY + 2 * GX],
-        [plane_ref[c] for c in range(3)],
-        behind[0:GY],
-        [edge[GX + x : GX + x + 1] for x in range(GX)],
-        [from_y[x : x + 1] for x in range(GX)],
-    )
+
+    back = shared_ref[0, 0:OWN].astype(F32)
+    for p in range(1, N_RAY):
+        back = back + shared_ref[p, 0:OWN].astype(F32)
     for x in range(GX):
-        back_ref[x] = backs[x]
-        for c in range(3):
-            new_dual_ref[c, x] = fresh[x][c]
+        tv_back = tv_ref[x] + jnp.where(sub == 0, from_y[x : x + 1], 0.0)
+        if x == 0:
+            tv_back = tv_back + from_x
+        own = back[x * GY : (x + 1) * GY]
+        image = image_ref[x] + own + tv_back
+        out_ref[x] = image
+        bar_ref[x] = image + extrapolation * own + tv_back
 
 
 def on_device(
@@ -512,7 +547,6 @@
     busy = 8 * 2**20
     grid = (GRID, F32)
     duals = ((3,) + GRID, F32)
-    swapped = ((GY + 2 * GX, TILE), F32)
 
     field, sent = call(
         start_kernel, [grid, ((N_RAY, SENT, TILE), BF16)], "hhhh",
@@ -541,30 +575,25 @@
         (parts, ray_dual, traveltimes, pick, picked, rest, extra),
     )
     shared = exchange(share, "ray", SHARE)
-    back, edge, partial_value = call(
-        image_kernel, [((OWN, TILE), F32), ((6 * GX, TILE), F32), SUMS], "vvvv",
-        (shared, gathered, picked_2, hot_2), (pltpu.VMEM((ALL, TILE), F32),),
+    field, image, edge, partial_value = call(
+        image_kernel,
+        [grid, grid, ((6 * GX, TILE), F32), ((N_MP, 2 * MAXSEL + GY, TILE), BF16)], "vvvvvvvv",
+        (shared, gathered, picked_2, hot_2, field, base, accumulated, tv_back),
+        (pltpu.VMEM((ALL, TILE), F32),),
     )
     parts = exchange(partial_value, "mp", SUM_2)
-
-    field, image, far, near = call(
-        second_edges_kernel, [grid, grid, swapped, swapped], "vvvvv",
-        (base, back, edge, accumulated, tv_back), busy=busy,
-    )
-    far = swap_far(far)
-    rays, share, near = call(
-        back_kernel, [RAYS, ((N_RAY, OWN, TILE), BF16), swapped], "vvvvvvav",
+    rays, share, planes = call(
+        back_kernel, [RAYS, ((N_RAY, OWN + 16, TILE), BF16), ((2, GY, TILE), F32)], "vvvvvvvv",
         (parts, rays, traveltimes, pick_2, picked_2, hot_2, far, near),
     )
     shared = exchange(share, "ray", LAST)
-    near = swap_near(near)
     dual, tv_back = call(
-        second_tv_kernel, [duals, grid], "vvvvvv",
-        (field, dual, dual_plane, far, near, edge), busy=busy,
-    )
-    back = jnp.sum(shared.astype(F32), axis=0).reshape(GRID)
-    image = image + back + tv_back
-    image_bar = image + extrapolation * back + tv_back
+        second_tv_kernel, [duals, grid], "vvvv", (field, dual, planes, edge), busy=busy
+    )
+    image, image_bar = call(
+        last_kernel, [grid, grid], "vvvvvvv",
+        (shared, field, planes, dual_plane, edge, image, tv_back),
+    )
     return (field, rays, dual, image, image_bar)
 
 

time: 98.8 us -> 96.4 us (0.976)
  the two profiles are of different devices: /device:TPU:32 before, /device:TPU:1 now
where the time goes in v8:
time: 96.4 us; the launch traced here: 95.4 us
  starting transfers between devices  41.4 us (43%)
  blocking collectives  19.5 us (20%)
  waiting for transfers between devices  19.2 us (20%)
  Pallas kernels  14.5 us (15%)
    all_to_all x4, starting transfers between devices, exchange(): lax.all_to_all(copies, axis, 0, 0, tiled=True, axis_index_groups=groups)  37 us
    all_to_all x1, blocking collectives, exchange(): lax.all_to_all(copies, axis, 0, 0, tiled=True, axis_index_groups=groups)  19.5 us
    pallas_call x11, Pallas kernels, call(): pl.pallas_call(kernel, out_shape=[pltpu.VMEM(shape, dtype) if keep else j...  14.5 us
    all_to_all x4, waiting for transfers between devices, exchange(): lax.all_to_all(copies, axis, 0, 0, tiled=True, axis_index_groups=groups)  14.4 us
    ppermute x2, waiting for transfers between devices, swap(): return lax.ppermute(block, 'mp', route + [(b, a) for a, b in route])  4.85 us
    ppermute x2, starting transfers between devices, swap(): return lax.ppermute(block, 'mp', route + [(b, a) for a, b in route])  4.36 us
  transfers between devices with their start and end apart: 6, of which 4 were waited for; matrix products, arithmetic and copies ran while one was open for 0% of the time, Pallas kernels for 7%

profile of v8, /device:TPU:1, one launch (start us, length us, event | category | flops | bytes accessed | tf_op | source)
XLA Modules:
  0.0 95.4 jit_solution(10739212628480304626)
XLA Ops:
  0.6 1.9 %shard_map.128 = (f32[4,8,128]{2,1,0:T(8,128)S(1)}, bf16[16,48,128]{2,1,0:T(8,128)(2,1)}) custom-call(f32[4,8,128]{2,1,0:T(8,128)} %slowness_hbm.1, f32[4,8,128]{2,1,0:T(8,128)} %bar_hbm.1, s32[8,16]{1,0:T(8,128)} %bitcast.1, s32[2,16]{1,0:T(2,128)} %selected_hbm.5), custom_call_target="tpu_custom_call" | custom-call | tf_op jit(solution)/shard_map/pallas_call | solution.py:56
  2.5 10.6 %all-to-all-start = ((bf16[16,48,128]{2,1,0:T(8,128)(2,1)}), bf16[16,48,128]{2,1,0:T(8,128)(2,1)S(1)}, u32[]{:S(2)}, u32[]{:S(2)}) async-start(bf16[16,48,128]{2,1,0:T(8,128)(2,1)} %get-tuple-element.34), calls=%async_computation | async-start | bytes 393216 | tf_op jit(solution)/shard_map/all_to_all | solution.py:42
  13.1 2.5 %shard_map.129 = (bf16[8,8,128,128]{3,2,1,0:T(8,128)(2,1)S(1)}, bf16[64,512]{1,0:T(8,128)(2,1)S(1)}, f32[16,8,128]{2,1,0:T(8,128)S(1)}) custom-call(bf16[16,8,128,128]{3,2,1,0:T(8,128)(2,1)} %tiles_hbm.3, s32[8,16]{1,0:T(8,128)} %bitcast.2, s32[2,16]{1,0:T(2,128)} %selected_hbm.5, f32[4,8,128]{2,1,0:T(8,128)S(1)} %get-tuple-element.35.after_ref.field_ref.first_ref), custom_call_target="tpu_custom_call" | custom-call | bytes 8388608 | tf_op jit(solution)/shard_map/pallas_call | solution.py:56
  15.7 0.0 copy-start
  15.7 0.0 copy-start.1
  15.7 0.0 copy-start.3
  15.7 0.0 copy-start.4
  15.7 2.8 %all-to-all-done.gathered_ref = bf16[16,48,128]{2,1,0:T(8,128)(2,1)S(1)} async-done(((bf16[16,48,128]{2,1,0:T(8,128)(2,1)}), bf16[16,48,128]{2,1,0:T(8,128)(2,1)S(1)}, u32[]{:S(2)}, u32[]{:S(2)}) %all-to-all-start) | async-done | bytes 196640 | tf_op jit(solution)/shard_map/all_to_all | solution.py:42
  18.6 1.4 %shard_map.130.after_any.after_ref = f32[32,8,128]{2,1,0:T(8,128)} custom-call(bf16[16,48,128]{2,1,0:T(8,128)(2,1)S(1)} %all-to-all-done.gathered_ref, bf16[8,8,128,128]{3,2,1,0:T(8,128)(2,1)S(1)} %get-tuple-element.36.picked_ref, bf16[64,512]{1,0:T(8,128)(2,1)S(1)} %get-tuple-element.37.hot_ref), custom_call_target="tpu_custom_call" | custom-call | tf_op jit(solution)/shard_map/pallas_call | solution.py:56
  20.0 15.7 %all-to-all-start.1 = ((f32[32,8,128]{2,1,0:T(8,128)}), f32[32,8,128]{2,1,0:T(8,128)S(1)}, u32[]{:S(2)}, u32[]{:S(2)}) async-start(f32[32,8,128]{2,1,0:T(8,128)} %shard_map.130.after_any.after_ref), calls=%async_computation.1 | async-start | bytes 262144 | tf_op jit(solution)/shard_map/all_to_all | solution.py:42
  35.8 0.0 copy-done
  35.8 2.4 %collective-permute-start = (f32[40,128]{1,0:T(8,128)S(1)}, f32[40,128]{1,0:T(8,128)S(1)}, u32[]{:S(2)}, u32[]{:S(2)}) collective-permute-start(f32[40,128]{1,0:T(8,128)S(1)} %get-tuple-element.39), channel_id=1, source_target_pairs={{1,2},{3,4},{5,6},{7,8},{9,10},{11,12},{13,14},{15,16},{17,18},{19... | collective-permute-start | bytes 61448 | tf_op jit(solution)/shard_map/ppermute | solution.py:371
  38.2 1.9 %collective-permute-start.1 = (f32[40,128]{1,0:T(8,128)S(1)}, f32[40,128]{1,0:T(8,128)S(1)}, u32[]{:S(2)}, u32[]{:S(2)}) collective-permute-start(f32[40,128]{1,0:T(8,128)S(1)} %get-tuple-element.40), channel_id=1, source_target_pairs={{0,1},{2,3},{4,5},{6,7},{8,9},{10,11},{12,13},{14,15},{16,17},{18,... | collective-permute-start | bytes 61448 | tf_op jit(solution)/shard_map/ppermute | solution.py:371
  40.2 4.8 %collective-permute-done.far_ref = f32[40,128]{1,0:T(8,128)S(1)} collective-permute-done((f32[40,128]{1,0:T(8,128)S(1)}, f32[40,128]{1,0:T(8,128)S(1)}, u32[]{:S(2)}, u32[]{:S(2)}) %collective-permute-start) | collective-permute-done | bytes 20512 | tf_op jit(solution)/shard_map/ppermute | solution.py:371
  45.0 0.0 collective-permute-done.1.near_ref
  45.0 0.0 copy-done.1
  45.0 0.2 shard_map.132
  45.2 0.0 all-to-all-done.1.parts_ref
  45.2 0.0 copy-done.3
  45.2 0.0 copy-done.4
  45.2 1.2 %shard_map.133 = (f32[16,128]{1,0:T(8,128)S(1)}, bf16[16,112,128]{2,1,0:T(8,128)(2,1)}) custom-call(f32[32,8,128]{2,1,0:T(8,128)S(1)} %all-to-all-done.1.parts_ref, f32[16,128]{1,0:T(8,128)S(1)} %copy-done.4, f32[16,128]{1,0:T(8,128)S(1)} %copy-done.3, f32[16,8,128]{2,1,0:T(8,128)S(1)} %get-tuple-element.38.pick_ref, ...), custom_call_target="tpu_custom_call" | custom-call | tf_op jit(solution)/shard_map/pallas_call | solution.py:56
  46.4 4.6 %all-to-all-start.2 = ((bf16[16,112,128]{2,1,0:T(8,128)(2,1)}), bf16[16,112,128]{2,1,0:T(8,128)(2,1)S(1)}, u32[]{:S(2)}, u32[]{:S(2)}) async-start(bf16[16,112,128]{2,1,0:T(8,128)(2,1)} %get-tuple-element.43), calls=%async_computation.2 | async-start | bytes 917504 | tf_op jit(solution)/shard_map/all_to_all | solution.py:42
  51.1 2.8 %shard_map.134 = (bf16[8,8,128,128]{3,2,1,0:T(8,128)(2,1)S(1)}, bf16[64,512]{1,0:T(8,128)(2,1)S(1)}, f32[16,8,128]{2,1,0:T(8,128)S(1)}) custom-call(bf16[16,8,128,128]{3,2,1,0:T(8,128)(2,1)} %tiles_hbm.3, s32[8,16]{1,0:T(8,128)} %bitcast.3, s32[2,16]{1,0:T(2,128)} %selected_hbm.5, f32[32,8,128]{2,1,0:T(8,128)} %shard_map.130.after_any.after_ref), custom_call_target="tpu_custom_call" | custom-call | bytes 8388608 | tf_op jit(solution)/shard_map/pallas_call | solution.py:56
  53.8 8.0 %all-to-all-done.2.shared_ref = bf16[16,112,128]{2,1,0:T(8,128)(2,1)S(1)} async-done(((bf16[16,112,128]{2,1,0:T(8,128)(2,1)}), bf16[16,112,128]{2,1,0:T(8,128)(2,1)S(1)}, u32[]{:S(2)}, u32[]{:S(2)}) %all-to-all-start.2) | async-done | bytes 458784 | tf_op jit(solution)/shard_map/all_to_all | solution.py:42
  61.9 1.7 %shard_map.135 = (f32[4,8,128]{2,1,0:T(8,128)}, f32[4,8,128]{2,1,0:T(8,128)S(1)}, f32[24,128]{1,0:T(8,128)S(1)}, bf16[32,24,128]{2,1,0:T(8,128)(2,1)S(1)}) custom-call(bf16[16,112,128]{2,1,0:T(8,128)(2,1)S(1)} %all-to-all-done.2.shared_ref, bf16[16,48,128]{2,1,0:T(8,128)(2,1)S(1)} %all-to-all-done.gathered_ref, ...), custom_call_target="tpu_custom_call" | custom-call | tf_op jit(solution)/shard_map/pallas_call | solution.py:56
  63.6 0.0 copy-start.2
  63.6 19.5 %all_to_all.25.parts_ref = bf16[32,24,128]{2,1,0:T(8,128)(2,1)S(1)} all-to-all(bf16[32,24,128]{2,1,0:T(8,128)(2,1)S(1)} %get-tuple-element.49), channel_id=1, replica_groups={{19,20,21,22,23,24,25,26,27,28,29,30,31,0,1,2,3,4,5,6,7,8,9,10,11,12,13..., dimensions={0} | all-to-all | bytes 393216 | tf_op jit(solution)/shard_map/all_to_all | solution.py:42
  83.1 1.3 %shard_map.136 = (f32[16,128]{1,0:T(8,128)}, bf16[16,48,128]{2,1,0:T(8,128)(2,1)}, f32[2,8,128]{2,1,0:T(8,128)S(1)}) custom-call(bf16[32,24,128]{2,1,0:T(8,128)(2,1)S(1)} %all_to_all.25.parts_ref, f32[16,128]{1,0:T(8,128)S(1)} %get-tuple-element.50.rays_ref, f32[16,128]{1,0:T(8,128)S(1)} %copy-done.3, f32[16,8,128]{2,1,0:T(8,128)S(1)} %get-tuple-element.51.pick_ref, ...), custom_call_target="tpu_custom_call" | custom-call | tf_op jit(solution)/shard_map/pallas_call | solution.py:56
  84.4 6.1 %all-to-all-start.4 = ((bf16[16,48,128]{2,1,0:T(8,128)(2,1)}), bf16[16,48,128]{2,1,0:T(8,128)(2,1)S(1)}, u32[]{:S(2)}, u32[]{:S(2)}) async-start(bf16[16,48,128]{2,1,0:T(8,128)(2,1)} %get-tuple-element.57), calls=%async_computation.4 | async-start | bytes 393216 | tf_op jit(solution)/shard_map/all_to_all | solution.py:42
  90.5 0.0 copy-done.2
  90.5 0.7 shard_map.137
  91.2 3.5 %all-to-all-done.4.shared_ref = bf16[16,48,128]{2,1,0:T(8,128)(2,1)S(1)} async-done(((bf16[16,48,128]{2,1,0:T(8,128)(2,1)}), bf16[16,48,128]{2,1,0:T(8,128)(2,1)S(1)}, u32[]{:S(2)}, u32[]{:S(2)}) %all-to-all-start.4) | async-done | bytes 196640 | tf_op jit(solution)/shard_map/all_to_all | solution.py:42
  94.7 0.7 shard_map.138
  (1 shorter events, 0.0 us)
Async XLA Ops:
  2.5 16.1 %all-to-all-start = ((bf16[16,48,128]{2,1,0:T(8,128)(2,1)}), bf16[16,48,128]{2,1,0:T(8,128)(2,1)S(1)}, u32[]{:S(2)}, u32[]{:S(2)}) async-start(bf16[16,48,128]{2,1,0:T(8,128)(2,1)} %get-tuple-element.34), calls=%async_computation | async-start | bytes 393216 | tf_op jit(solution)/shard_map/all_to_all | solution.py:42
  15.7 20.1 %copy-start = (f32[3,4,8,128]{3,2,1,0:T(8,128)S(1)}, f32[3,4,8,128]{3,2,1,0:T(8,128)}, u32[]{:S(2)}) copy-start(f32[3,4,8,128]{3,2,1,0:T(8,128)} %dual_ref.3) | copy-start | bytes 147460
  15.7 29.3 %copy-start.1 = (f32[4,8,128]{2,1,0:T(8,128)S(1)}, f32[4,8,128]{2,1,0:T(8,128)}, u32[]{:S(2)}) copy-start(f32[4,8,128]{2,1,0:T(8,128)} %image_ref.3) | copy-start | bytes 49156
  15.7 29.5 %copy-start.3 = (f32[16,128]{1,0:T(8,128)S(1)}, f32[16,128]{1,0:T(8,128)}, u32[]{:S(2)}) copy-start(f32[16,128]{1,0:T(8,128)} %times_ref.3) | copy-start | bytes 24580
  15.7 29.5 %copy-start.4 = (f32[16,128]{1,0:T(8,128)S(1)}, f32[16,128]{1,0:T(8,128)}, u32[]{:S(2)}) copy-start(f32[16,128]{1,0:T(8,128)} %rays_ref.1) | copy-start | bytes 24580
  20.0 25.2 %all-to-all-start.1 = ((f32[32,8,128]{2,1,0:T(8,128)}), f32[32,8,128]{2,1,0:T(8,128)S(1)}, u32[]{:S(2)}, u32[]{:S(2)}) async-start(f32[32,8,128]{2,1,0:T(8,128)} %shard_map.130.after_any.after_ref), calls=%async_computation.1 | async-start | bytes 262144 | tf_op jit(solution)/shard_map/all_to_all | solution.py:42
  35.8 9.2 %collective-permute-start = (f32[40,128]{1,0:T(8,128)S(1)}, f32[40,128]{1,0:T(8,128)S(1)}, u32[]{:S(2)}, u32[]{:S(2)}) collective-permute-start(f32[40,128]{1,0:T(8,128)S(1)} %get-tuple-element.39), channel_id=1, source_target_pairs={{1,2},{3,4},{5,6},{7,8},{9,10},{11,12},{13,14},{15,16},{17,18},{19... | collective-permute-start | bytes 61448 | tf_op jit(solution)/shard_map/ppermute | solution.py:371
  38.2 6.8 %collective-permute-start.1 = (f32[40,128]{1,0:T(8,128)S(1)}, f32[40,128]{1,0:T(8,128)S(1)}, u32[]{:S(2)}, u32[]{:S(2)}) collective-permute-start(f32[40,128]{1,0:T(8,128)S(1)} %get-tuple-element.40), channel_id=1, source_target_pairs={{0,1},{2,3},{4,5},{6,7},{8,9},{10,11},{12,13},{14,15},{16,17},{18,... | collective-permute-start | bytes 61448 | tf_op jit(solution)/shard_map/ppermute | solution.py:371
  46.4 15.4 %all-to-all-start.2 = ((bf16[16,112,128]{2,1,0:T(8,128)(2,1)}), bf16[16,112,128]{2,1,0:T(8,128)(2,1)S(1)}, u32[]{:S(2)}, u32[]{:S(2)}) async-start(bf16[16,112,128]{2,1,0:T(8,128)(2,1)} %get-tuple-element.43), calls=%async_computation.2 | async-start | bytes 917504 | tf_op jit(solution)/shard_map/all_to_all | solution.py:42
  63.6 26.9 %copy-start.2 = (f32[4,8,128]{2,1,0:T(8,128)S(1)}, f32[4,8,128]{2,1,0:T(8,128)}, u32[]{:S(2)}) copy-start(f32[4,8,128]{2,1,0:T(8,128)} %get-tuple-element.29.field_ref) | copy-start | bytes 49156
  84.4 10.3 %all-to-all-start.4 = ((bf16[16,48,128]{2,1,0:T(8,128)(2,1)}), bf16[16,48,128]{2,1,0:T(8,128)(2,1)S(1)}, u32[]{:S(2)}, u32[]{:S(2)}) async-start(bf16[16,48,128]{2,1,0:T(8,128)(2,1)} %get-tuple-element.57), calls=%async_computation.4 | async-start | bytes 393216 | tf_op jit(solution)/shard_map/all_to_all | solution.py:42

commit v9 on v8

--- a/solution.py
+++ b/solution.py
@@ -16,10 +16,10 @@
 OWN = GX * GY
 ALL = N_RAY * OWN
 PRODUCTS = MAXSEL * CAP
-SENT = OWN + 16
-REST = OWN + 8
+SENT = OWN + 8
+REST = OWN + 4
 EXTRA = PRODUCTS + OWN
-SHARED = EXTRA + 16
+SHARED = EXTRA + 8
 GATHER, SUM_1, SHARE, SUM_2, LAST = 9, 19, 5, 19, 10
 
 primal_step = 0.5
@@ -125,13 +125,12 @@
     field = field.reshape(OWN, TILE)
     rounded = field.astype(BF16)
     low = field - rounded.astype(F32)
-    rest = jnp.zeros((8, TILE), F32)
+    tail = numbers.astype(F32)
     for x in range(GX):
-        rest = jnp.where(sub == x, low[x * GY : x * GY + 1], rest)
-    tail = jnp.concatenate([numbers.astype(F32), rest], axis=0).astype(BF16)
+        tail = jnp.where(sub == REST - OWN + x, low[x * GY : x * GY + 1], tail)
+    sent = jnp.concatenate([rounded.astype(F32), tail], axis=0).astype(BF16)
     for p in range(N_RAY):
-        sent_ref[p, 0:OWN, :] = rounded
-        sent_ref[p, OWN:SENT, :] = tail
+        sent_ref[p] = sent
 
 
 def fetch_kernel(step):
@@ -254,11 +253,9 @@
         ).astype(BF16)
         for p in range(N_RAY):
             out_ref[p, n * CAP : (n + 2) * CAP, :] = pair
-    rest = rest_ref[...].reshape(OWN, TILE).astype(BF16)
-    extra = extra_ref[...].astype(BF16)
+    rest = jnp.concatenate([rest_ref[...].reshape(OWN, TILE), extra_ref[...]], axis=0).astype(BF16)
     for p in range(N_RAY):
-        out_ref[p, PRODUCTS:EXTRA, :] = rest
-        out_ref[p, EXTRA:SHARED, :] = extra
+        out_ref[p, PRODUCTS:SHARED, :] = rest
 
 
 def image_kernel(
@@ -268,7 +265,7 @@
     lane = lax.broadcasted_iota(jnp.int32, (1, TILE), 1)
     singles = []
     for p in range(N_RAY):
-        rows = gathered_ref[at(p, GATHER), OWN:SENT, :].astype(F32)
+        rows = gathered_ref[at(p, GATHER)].astype(F32)[OWN:SENT]
         singles.append(rows[0:1] * OWN + rows[1:2])
     pairs = [jnp.where(lane < PRODUCTS, singles[p], singles[p + 1]) for p in range(0, N_RAY, 2)]
     group = 4
@@ -296,7 +293,7 @@
             rest = shared_ref[at(p, SHARE), PRODUCTS:EXTRA, :].astype(F32)
             field = gathered_ref[at(p, GATHER), 0:OWN, :].astype(F32) + (rest - gain * table_ref[rows, :])
             if p > 0:
-                change = shared_ref[at(p - 1, SHARE), EXTRA:SHARED, :].astype(F32)
+                change = shared_ref[at(p - 1, SHARE), PRODUCTS:SHARED, :].astype(F32)[OWN:]
                 field = field - (2.0 * primal_step) * jnp.concatenate(
                     [jnp.where(sub == 0, change[x : x + 1], 0.0) for x in range(GX)], axis=0
                 )
@@ -313,15 +310,16 @@
         field = table_ref[pl.ds(pl.multiple_of(peer * OWN, OWN), OWN), :]
         for x in range(GX):
             edge_ref[side * GX + x : side * GX + x + 1, :] = field[x * GY + row : x * GY + row + 1]
-    extra = shared_ref[at(before, SHARE), EXTRA:SHARED, :].astype(F32)
-    edge_ref[2 * GX : 6 * GX] = extra
+    extra = shared_ref[at(before, SHARE), PRODUCTS:SHARED, :].astype(F32)[OWN:]
     first_y = (sub == 0) & (me > 0)
+    edge_ref[2 * GX :] = jnp.zeros((2 * GX, TILE), F32)
     field = []
     for x in range(GX):
         own = back[x * GY : (x + 1) * GY]
         from_y = jnp.where(first_y, extra[x : x + 1], 0.0)
         field.append(base_ref[x] - (gain * own + (2.0 * primal_step) * from_y))
         field_ref[x] = field[x]
+        edge_ref[2 * GX + x : 2 * GX + x + 1] = field[x][GY - 1 : GY]
         new_image_ref[x] = image_ref[x] + own + (tv_ref[x] + from_y)
     high = total.astype(BF16).astype(F32)
     ends = [
@@ -332,7 +330,8 @@
 
 
 def back_kernel(
-    parts_ref, rays_ref, times_ref, pick_ref, picked_ref, hot_ref, far_ref, near_ref, new_rays_ref, out_ref, planes_ref
+    parts_ref, rays_ref, times_ref, pick_ref, picked_ref, hot_ref, far_ref, near_ref, dual_ref, edge_ref,
+    new_rays_ref, out_ref, planes_ref,
 ):
     mp = lax.axis_index("mp")
     before, behind = x_halos(far_ref, near_ref)
@@ -342,14 +341,23 @@
     behind = behind[0:GY] + step[2 * MAXSEL :]
     planes_ref[0] = before
     planes_ref[1] = behind
-    corners = [before[0:1], behind[GY - 1 : GY]]
-    highs = [corner.astype(BF16).astype(F32) for corner in corners]
-    sub = lax.broadcasted_iota(jnp.int32, (16, TILE), 0)
-    tail = jnp.zeros((16, TILE), F32)
-    for i in range(2):
-        tail = jnp.where(sub == 2 * i, highs[i], tail)
-        tail = jnp.where(sub == 2 * i + 1, corners[i] - highs[i], tail)
-    tail = tail.astype(BF16)
+    sub = lax.broadcasted_iota(jnp.int32, (2 * GX, TILE), 0)
+
+    own = [edge_ref[2 * GX + x : 2 * GX + x + 1] for x in range(GX)]
+    last_ray = lax.axis_index("ray") == N_RAY - 1
+    _, change = tv_cells(
+        jnp.concatenate(own * 2, axis=0),
+        jnp.concatenate((own[1:] + [behind[GY - 1 : GY]]) * 2, axis=0),
+        jnp.concatenate([edge_ref[GX : 2 * GX]] * 2, axis=0),
+        [
+            jnp.concatenate([dual_ref[c, x][GY - 1 : GY] for x in range(GX)] * 2, axis=0)
+            for c in range(3)
+        ],
+        ((sub & (GX - 1)) == GX - 1) & (mp == N_MP - 1), (sub >= 0) & last_ray,
+    )
+    high = before[0:1].astype(BF16).astype(F32)
+    tail = jnp.where(last_ray, 0.0, change[1])
+    tail = jnp.where(sub == 0, high, jnp.where(sub == 1, before[0:1] - high, tail))
     halves = parts_ref[0].astype(F32)
     for m in range(1, N_MP):
         halves = halves + parts_ref[m].astype(F32)
@@ -362,8 +370,9 @@
     image = lax.dot_general(hot_ref[...], high, turned, preferred_element_type=F32)
     image = image + lax.dot_general(hot_ref[...], low, turned, preferred_element_type=F32)
     for p in range(N_RAY):
-        out_ref[at(p, LAST), 0:OWN] = image[p * OWN : (p + 1) * OWN].astype(BF16)
-        out_ref[at(p, LAST), OWN:] = tail
+        out_ref[at(p, LAST)] = jnp.concatenate(
+            [image[p * OWN : (p + 1) * OWN], tail], axis=0
+        ).astype(BF16)
 
 
 def swap(block, first):
@@ -381,10 +390,9 @@
 
 def next_rows(gathered_ref):
     peer = jnp.minimum(lax.axis_index("ray") + 1, N_RAY - 1)
-    high = gathered_ref[at(peer, GATHER), 0:OWN, :].astype(F32)
-    low = gathered_ref[at(peer, GATHER), OWN:SENT, :].astype(F32)
+    rows = gathered_ref[at(peer, GATHER)].astype(F32)
     return [
-        high[x * GY : x * GY + 1] + low[REST - OWN + x : REST - OWN + x + 1] for x in range(GX)
+        rows[x * GY : x * GY + 1] + rows[REST + x : REST + x + 1] for x in range(GX)
     ]
 
 
@@ -478,6 +486,7 @@
         [[dual_ref[c, x] for x in range(GX)] for c in range(3)],
         behind[0:GY], next_rows(gathered_ref), from_x,
     )
+    extra_ref[...] = jnp.zeros_like(extra_ref)
     for x in range(GX):
         base = field[x] - primal_step * (image_ref[x] + 2.0 * backs[x])
         back_ref[x] = backs[x]
@@ -486,8 +495,6 @@
         extra_ref[x : x + 1] = second[x][GY - 1 : GY]
         for c in range(3):
             new_dual_ref[c, x] = fresh[x][c]
-            row = (c + 1) * GX + x
-            extra_ref[row : row + 1] = fresh[x][c][GY - 1 : GY]
     for c in range(3):
         plane_ref[c] = halo[c]
 
@@ -506,32 +513,21 @@
 
 
 def last_kernel(
-    shared_ref, field_ref, planes_ref, dual_plane_ref, edge_ref, image_ref, tv_ref, out_ref, bar_ref
+    shared_ref, field_ref, planes_ref, dual_plane_ref, image_ref, tv_ref, out_ref, bar_ref
 ):
     ray = lax.axis_index("ray")
-    above = shared_ref[at(jnp.minimum(ray + 1, N_RAY - 1), LAST), OWN:].astype(F32)
-    below = shared_ref[at(jnp.maximum(ray - 1, 0), LAST), OWN:].astype(F32)
-    field = [field_ref[x] for x in range(GX)]
+    above = shared_ref[at(jnp.minimum(ray + 1, N_RAY - 1), LAST)].astype(F32)[OWN:]
+    below = shared_ref[at(jnp.maximum(ray - 1, 0), LAST)].astype(F32)[OWN:]
     _, from_x = plane_before(
-        planes_ref[0], above[0:1] + above[1:2], [dual_plane_ref[c] for c in range(3)], field[0]
-    )
-    edge = edge_ref[...]
-    sub = lax.broadcasted_iota(jnp.int32, (2 * GX, TILE), 0)
-    rows = edge[0 : 2 * GX]
-    ahead_x = jnp.where(sub == GX - 1, below[2:3] + below[3:4], pltpu.roll(rows, 2 * GX - 1, 0))
-    ahead_y = jnp.concatenate([field[x][0:1] for x in range(GX)] * 2, axis=0)
-    dual_rows = [
-        jnp.concatenate([edge[(c + 3) * GX : (c + 4) * GX]] * 2, axis=0) for c in range(3)
-    ]
-    end_x = lax.axis_index("mp") == N_MP - 1
-    _, change = tv_cells(rows, ahead_x, ahead_y, dual_rows, (sub == GX - 1) & end_x, sub < 0)
-    from_y = jnp.where(ray == 0, 0.0, change[1])
-
-    back = shared_ref[0, 0:OWN].astype(F32)
+        planes_ref[0], above[0:1] + above[1:2], [dual_plane_ref[c] for c in range(3)], field_ref[0]
+    )
+    sub = lax.broadcasted_iota(jnp.int32, (GY, TILE), 0)
+    first_y = (sub == 0) & (ray > 0)
+    back = shared_ref[0].astype(F32)
     for p in range(1, N_RAY):
-        back = back + shared_ref[p, 0:OWN].astype(F32)
+        back = back + shared_ref[p].astype(F32)
     for x in range(GX):
-        tv_back = tv_ref[x] + jnp.where(sub == 0, from_y[x : x + 1], 0.0)
+        tv_back = tv_ref[x] + jnp.where(first_y, below[GX + x : GX + x + 1], 0.0)
         if x == 0:
             tv_back = tv_back + from_x
         own = back[x * GY : (x + 1) * GY]
@@ -565,7 +561,7 @@
     far, near = swap_far(far), swap_near(near)
     dual, dual_plane, tv_back, base, rest, extra = call(
         first_tv_kernel,
-        [duals, ((3, GY, TILE), F32), grid, grid, grid, ((4 * GX, TILE), F32)],
+        [duals, ((3, GY, TILE), F32), grid, grid, grid, ((8, TILE), F32)],
         "vvvvvv", (field, tv_dual, far, near, gathered, accumulated), busy=busy,
     )
     picked_2, hot_2, pick_2 = fetch(1, tiles, pattern, selected, partial_value)
@@ -577,22 +573,22 @@
     shared = exchange(share, "ray", SHARE)
     field, image, edge, partial_value = call(
         image_kernel,
-        [grid, grid, ((6 * GX, TILE), F32), ((N_MP, 2 * MAXSEL + GY, TILE), BF16)], "vvvvvvvv",
+        [grid, grid, ((4 * GX, TILE), F32), ((N_MP, 2 * MAXSEL + GY, TILE), BF16)], "vvvvvvvv",
         (shared, gathered, picked_2, hot_2, field, base, accumulated, tv_back),
         (pltpu.VMEM((ALL, TILE), F32),),
     )
     parts = exchange(partial_value, "mp", SUM_2)
     rays, share, planes = call(
-        back_kernel, [RAYS, ((N_RAY, OWN + 16, TILE), BF16), ((2, GY, TILE), F32)], "vvvvvvvv",
-        (parts, rays, traveltimes, pick_2, picked_2, hot_2, far, near),
+        back_kernel, [RAYS, ((N_RAY, OWN + 8, TILE), BF16), ((2, GY, TILE), F32)], "vvvvvvvvvv",
+        (parts, rays, traveltimes, pick_2, picked_2, hot_2, far, near, dual, edge),
     )
     shared = exchange(share, "ray", LAST)
     dual, tv_back = call(
         second_tv_kernel, [duals, grid], "vvvv", (field, dual, planes, edge), busy=busy
     )
     image, image_bar = call(
-        last_kernel, [grid, grid], "vvvvvvv",
-        (shared, field, planes, dual_plane, edge, image, tv_back),
+        last_kernel, [grid, grid], "vvvvvv",
+        (shared, field, planes, dual_plane, image, tv_back),
     )
     return (field, rays, dual, image, image_bar)
 

time: 96.4 us -> 94.6 us (0.981)
  waiting for transfers between devices: 19.2 us -> 17.8 us
    all_to_all x4, waiting for transfers between devices: 14.4 us -> 12.9 us  [exchange(): lax.all_to_all(copies, axis, 0, 0, tiled=True, axis_index_groups=groups)]
where the time goes in v9:
time: 94.6 us; the launch traced here: 93.7 us
  starting transfers between devices  41.1 us (43%)
  blocking collectives  19.5 us (21%)
  waiting for transfers between devices  17.8 us (19%)
  Pallas kernels  14.5 us (15%)
    all_to_all x4, starting transfers between devices, exchange(): lax.all_to_all(copies, axis, 0, 0, tiled=True, axis_index_groups=groups)  36.7 us
    all_to_all x1, blocking collectives, exchange(): lax.all_to_all(copies, axis, 0, 0, tiled=True, axis_index_groups=groups)  19.5 us
    pallas_call x11, Pallas kernels, call(): pl.pallas_call(kernel, out_shape=[pltpu.VMEM(shape, dtype) if keep else j...  14.5 us
    all_to_all x4, waiting for transfers between devices, exchange(): lax.all_to_all(copies, axis, 0, 0, tiled=True, axis_index_groups=groups)  12.9 us
    ppermute x2, waiting for transfers between devices, swap(): return lax.ppermute(block, 'mp', route + [(b, a) for a, b in route])  4.86 us
    ppermute x2, starting transfers between devices, swap(): return lax.ppermute(block, 'mp', route + [(b, a) for a, b in route])  4.36 us
  transfers between devices with their start and end apart: 6, of which 4 were waited for; matrix products, arithmetic and copies ran while one was open for 0% of the time, Pallas kernels for 7%

profile of v9, /device:TPU:1, one launch (start us, length us, event | category | flops | bytes accessed | tf_op | source)
XLA Modules:
  0.0 93.7 jit_solution(1771796815106421973)
XLA Ops:
  0.6 1.8 %shard_map.128 = (f32[4,8,128]{2,1,0:T(8,128)S(1)}, bf16[16,40,128]{2,1,0:T(8,128)(2,1)}) custom-call(f32[4,8,128]{2,1,0:T(8,128)} %slowness_hbm.1, f32[4,8,128]{2,1,0:T(8,128)} %bar_hbm.1, s32[8,16]{1,0:T(8,128)} %bitcast.1, s32[2,16]{1,0:T(2,128)} %selected_hbm.5), custom_call_target="tpu_custom_call" | custom-call | tf_op jit(solution)/shard_map/pallas_call | solution.py:56
  2.5 10.6 %all-to-all-start = ((bf16[16,40,128]{2,1,0:T(8,128)(2,1)}), bf16[16,40,128]{2,1,0:T(8,128)(2,1)S(1)}, u32[]{:S(2)}, u32[]{:S(2)}) async-start(bf16[16,40,128]{2,1,0:T(8,128)(2,1)} %get-tuple-element.34), calls=%async_computation | async-start | bytes 327680 | tf_op jit(solution)/shard_map/all_to_all | solution.py:42
  13.1 2.5 %shard_map.129 = (bf16[8,8,128,128]{3,2,1,0:T(8,128)(2,1)S(1)}, bf16[64,512]{1,0:T(8,128)(2,1)S(1)}, f32[16,8,128]{2,1,0:T(8,128)S(1)}) custom-call(bf16[16,8,128,128]{3,2,1,0:T(8,128)(2,1)} %tiles_hbm.3, s32[8,16]{1,0:T(8,128)} %bitcast.2, s32[2,16]{1,0:T(2,128)} %selected_hbm.5, f32[4,8,128]{2,1,0:T(8,128)S(1)} %get-tuple-element.35.after_ref.field_ref.first_ref), custom_call_target="tpu_custom_call" | custom-call | bytes 8388608 | tf_op jit(solution)/shard_map/pallas_call | solution.py:56
  15.6 0.0 copy-start
  15.6 0.0 copy-start.1
  15.6 0.0 copy-start.3
  15.6 0.0 copy-start.4
  15.6 2.7 %all-to-all-done.gathered_ref = bf16[16,40,128]{2,1,0:T(8,128)(2,1)S(1)} async-done(((bf16[16,40,128]{2,1,0:T(8,128)(2,1)}), bf16[16,40,128]{2,1,0:T(8,128)(2,1)S(1)}, u32[]{:S(2)}, u32[]{:S(2)}) %all-to-all-start) | async-done | bytes 163872 | tf_op jit(solution)/shard_map/all_to_all | solution.py:42
  18.3 1.4 %shard_map.130.after_any.after_ref = f32[32,8,128]{2,1,0:T(8,128)} custom-call(bf16[16,40,128]{2,1,0:T(8,128)(2,1)S(1)} %all-to-all-done.gathered_ref, bf16[8,8,128,128]{3,2,1,0:T(8,128)(2,1)S(1)} %get-tuple-element.36.picked_ref, bf16[64,512]{1,0:T(8,128)(2,1)S(1)} %get-tuple-element.37.hot_ref), custom_call_target="tpu_custom_call" | custom-call | tf_op jit(solution)/shard_map/pallas_call | solution.py:56
  19.8 15.4 %all-to-all-start.1 = ((f32[32,8,128]{2,1,0:T(8,128)}), f32[32,8,128]{2,1,0:T(8,128)S(1)}, u32[]{:S(2)}, u32[]{:S(2)}) async-start(f32[32,8,128]{2,1,0:T(8,128)} %shard_map.130.after_any.after_ref), calls=%async_computation.1 | async-start | bytes 262144 | tf_op jit(solution)/shard_map/all_to_all | solution.py:42
  35.1 0.0 copy-done
  35.2 2.4 %collective-permute-start = (f32[40,128]{1,0:T(8,128)S(1)}, f32[40,128]{1,0:T(8,128)S(1)}, u32[]{:S(2)}, u32[]{:S(2)}) collective-permute-start(f32[40,128]{1,0:T(8,128)S(1)} %get-tuple-element.39), channel_id=1, source_target_pairs={{1,2},{3,4},{5,6},{7,8},{9,10},{11,12},{13,14},{15,16},{17,18},{19... | collective-permute-start | bytes 61448 | tf_op jit(solution)/shard_map/ppermute | solution.py:380
  37.6 1.9 %collective-permute-start.1 = (f32[40,128]{1,0:T(8,128)S(1)}, f32[40,128]{1,0:T(8,128)S(1)}, u32[]{:S(2)}, u32[]{:S(2)}) collective-permute-start(f32[40,128]{1,0:T(8,128)S(1)} %get-tuple-element.40), channel_id=1, source_target_pairs={{0,1},{2,3},{4,5},{6,7},{8,9},{10,11},{12,13},{14,15},{16,17},{18,... | collective-permute-start | bytes 61448 | tf_op jit(solution)/shard_map/ppermute | solution.py:380
  39.5 4.9 %collective-permute-done.far_ref = f32[40,128]{1,0:T(8,128)S(1)} collective-permute-done((f32[40,128]{1,0:T(8,128)S(1)}, f32[40,128]{1,0:T(8,128)S(1)}, u32[]{:S(2)}, u32[]{:S(2)}) %collective-permute-start) | collective-permute-done | bytes 20512 | tf_op jit(solution)/shard_map/ppermute | solution.py:380
  44.4 0.0 collective-permute-done.1.near_ref
  44.4 0.0 copy-done.1
  44.4 0.2 shard_map.132
  44.6 0.0 all-to-all-done.1.parts_ref
  44.6 0.0 copy-done.3
  44.6 0.0 copy-done.4
  44.6 1.2 %shard_map.133 = (f32[16,128]{1,0:T(8,128)S(1)}, bf16[16,104,128]{2,1,0:T(8,128)(2,1)}) custom-call(f32[32,8,128]{2,1,0:T(8,128)S(1)} %all-to-all-done.1.parts_ref, f32[16,128]{1,0:T(8,128)S(1)} %copy-done.4, f32[16,128]{1,0:T(8,128)S(1)} %copy-done.3, f32[16,8,128]{2,1,0:T(8,128)S(1)} %get-tuple-element.38.pick_ref, ...), custom_call_target="tpu_custom_call" | custom-call | tf_op jit(solution)/shard_map/pallas_call | solution.py:56
  45.8 4.7 %all-to-all-start.2 = ((bf16[16,104,128]{2,1,0:T(8,128)(2,1)}), bf16[16,104,128]{2,1,0:T(8,128)(2,1)S(1)}, u32[]{:S(2)}, u32[]{:S(2)}) async-start(bf16[16,104,128]{2,1,0:T(8,128)(2,1)} %get-tuple-element.43), calls=%async_computation.2 | async-start | bytes 851968 | tf_op jit(solution)/shard_map/all_to_all | solution.py:42
  50.5 2.9 %shard_map.134 = (bf16[8,8,128,128]{3,2,1,0:T(8,128)(2,1)S(1)}, bf16[64,512]{1,0:T(8,128)(2,1)S(1)}, f32[16,8,128]{2,1,0:T(8,128)S(1)}) custom-call(bf16[16,8,128,128]{3,2,1,0:T(8,128)(2,1)} %tiles_hbm.3, s32[8,16]{1,0:T(8,128)} %bitcast.3, s32[2,16]{1,0:T(2,128)} %selected_hbm.5, f32[32,8,128]{2,1,0:T(8,128)} %shard_map.130.after_any.after_ref), custom_call_target="tpu_custom_call" | custom-call | bytes 8388608 | tf_op jit(solution)/shard_map/pallas_call | solution.py:56
  53.4 7.2 %all-to-all-done.2.shared_ref = bf16[16,104,128]{2,1,0:T(8,128)(2,1)S(1)} async-done(((bf16[16,104,128]{2,1,0:T(8,128)(2,1)}), bf16[16,104,128]{2,1,0:T(8,128)(2,1)S(1)}, u32[]{:S(2)}, u32[]{:S(2)}) %all-to-all-start.2) | async-done | bytes 426016 | tf_op jit(solution)/shard_map/all_to_all | solution.py:42
  60.7 1.7 %shard_map.135 = (f32[4,8,128]{2,1,0:T(8,128)}, f32[4,8,128]{2,1,0:T(8,128)S(1)}, f32[16,128]{1,0:T(8,128)S(1)}, bf16[32,24,128]{2,1,0:T(8,128)(2,1)S(1)}) custom-call(bf16[16,104,128]{2,1,0:T(8,128)(2,1)S(1)} %all-to-all-done.2.shared_ref, bf16[16,40,128]{2,1,0:T(8,128)(2,1)S(1)} %all-to-all-done.gathered_ref, ...), custom_call_target="tpu_custom_call" | custom-call | tf_op jit(solution)/shard_map/pallas_call | solution.py:56
  62.4 0.0 copy-start.2
  62.4 19.5 %all_to_all.25.parts_ref = bf16[32,24,128]{2,1,0:T(8,128)(2,1)S(1)} all-to-all(bf16[32,24,128]{2,1,0:T(8,128)(2,1)S(1)} %get-tuple-element.49), channel_id=1, replica_groups={{19,20,21,22,23,24,25,26,27,28,29,30,31,0,1,2,3,4,5,6,7,8,9,10,11,12,13..., dimensions={0} | all-to-all | bytes 393216 | tf_op jit(solution)/shard_map/all_to_all | solution.py:42
  81.9 1.3 %shard_map.136 = (f32[16,128]{1,0:T(8,128)}, bf16[16,40,128]{2,1,0:T(8,128)(2,1)}, f32[2,8,128]{2,1,0:T(8,128)S(1)}) custom-call(bf16[32,24,128]{2,1,0:T(8,128)(2,1)S(1)} %all_to_all.25.parts_ref, f32[16,128]{1,0:T(8,128)S(1)} %get-tuple-element.50.rays_ref, f32[16,128]{1,0:T(8,128)S(1)} %copy-done.3, f32[16,8,128]{2,1,0:T(8,128)S(1)} %get-tuple-element.51.pick_ref, ...), custom_call_target="tpu_custom_call" | custom-call | tf_op jit(solution)/shard_map/pallas_call | solution.py:56
  83.2 6.1 %all-to-all-start.4 = ((bf16[16,40,128]{2,1,0:T(8,128)(2,1)}), bf16[16,40,128]{2,1,0:T(8,128)(2,1)S(1)}, u32[]{:S(2)}, u32[]{:S(2)}) async-start(bf16[16,40,128]{2,1,0:T(8,128)(2,1)} %get-tuple-element.57), calls=%async_computation.4 | async-start | bytes 327680 | tf_op jit(solution)/shard_map/all_to_all | solution.py:42
  89.3 0.0 copy-done.2
  89.3 0.7 shard_map.137
  90.0 3.0 %all-to-all-done.4.shared_ref = bf16[16,40,128]{2,1,0:T(8,128)(2,1)S(1)} async-done(((bf16[16,40,128]{2,1,0:T(8,128)(2,1)}), bf16[16,40,128]{2,1,0:T(8,128)(2,1)S(1)}, u32[]{:S(2)}, u32[]{:S(2)}) %all-to-all-start.4) | async-done | bytes 163872 | tf_op jit(solution)/shard_map/all_to_all | solution.py:42
  93.0 0.7 shard_map.138
  (1 shorter events, 0.0 us)
Async XLA Ops:
  2.5 15.8 %all-to-all-start = ((bf16[16,40,128]{2,1,0:T(8,128)(2,1)}), bf16[16,40,128]{2,1,0:T(8,128)(2,1)S(1)}, u32[]{:S(2)}, u32[]{:S(2)}) async-start(bf16[16,40,128]{2,1,0:T(8,128)(2,1)} %get-tuple-element.34), calls=%async_computation | async-start | bytes 327680 | tf_op jit(solution)/shard_map/all_to_all | solution.py:42
  15.6 19.6 %copy-start = (f32[3,4,8,128]{3,2,1,0:T(8,128)S(1)}, f32[3,4,8,128]{3,2,1,0:T(8,128)}, u32[]{:S(2)}) copy-start(f32[3,4,8,128]{3,2,1,0:T(8,128)} %dual_ref.3) | copy-start | bytes 147460
  15.6 28.8 %copy-start.1 = (f32[4,8,128]{2,1,0:T(8,128)S(1)}, f32[4,8,128]{2,1,0:T(8,128)}, u32[]{:S(2)}) copy-start(f32[4,8,128]{2,1,0:T(8,128)} %image_ref.3) | copy-start | bytes 49156
  15.6 29.0 %copy-start.3 = (f32[16,128]{1,0:T(8,128)S(1)}, f32[16,128]{1,0:T(8,128)}, u32[]{:S(2)}) copy-start(f32[16,128]{1,0:T(8,128)} %times_ref.3) | copy-start | bytes 24580
  15.6 29.0 %copy-start.4 = (f32[16,128]{1,0:T(8,128)S(1)}, f32[16,128]{1,0:T(8,128)}, u32[]{:S(2)}) copy-start(f32[16,128]{1,0:T(8,128)} %rays_ref.1) | copy-start | bytes 24580
  19.8 24.8 %all-to-all-start.1 = ((f32[32,8,128]{2,1,0:T(8,128)}), f32[32,8,128]{2,1,0:T(8,128)S(1)}, u32[]{:S(2)}, u32[]{:S(2)}) async-start(f32[32,8,128]{2,1,0:T(8,128)} %shard_map.130.after_any.after_ref), calls=%async_computation.1 | async-start | bytes 262144 | tf_op jit(solution)/shard_map/all_to_all | solution.py:42
  35.2 9.2 %collective-permute-start = (f32[40,128]{1,0:T(8,128)S(1)}, f32[40,128]{1,0:T(8,128)S(1)}, u32[]{:S(2)}, u32[]{:S(2)}) collective-permute-start(f32[40,128]{1,0:T(8,128)S(1)} %get-tuple-element.39), channel_id=1, source_target_pairs={{1,2},{3,4},{5,6},{7,8},{9,10},{11,12},{13,14},{15,16},{17,18},{19... | collective-permute-start | bytes 61448 | tf_op jit(solution)/shard_map/ppermute | solution.py:380
  37.6 6.8 %collective-permute-start.1 = (f32[40,128]{1,0:T(8,128)S(1)}, f32[40,128]{1,0:T(8,128)S(1)}, u32[]{:S(2)}, u32[]{:S(2)}) collective-permute-start(f32[40,128]{1,0:T(8,128)S(1)} %get-tuple-element.40), channel_id=1, source_target_pairs={{0,1},{2,3},{4,5},{6,7},{8,9},{10,11},{12,13},{14,15},{16,17},{18,... | collective-permute-start | bytes 61448 | tf_op jit(solution)/shard_map/ppermute | solution.py:380
  45.8 14.8 %all-to-all-start.2 = ((bf16[16,104,128]{2,1,0:T(8,128)(2,1)}), bf16[16,104,128]{2,1,0:T(8,128)(2,1)S(1)}, u32[]{:S(2)}, u32[]{:S(2)}) async-start(bf16[16,104,128]{2,1,0:T(8,128)(2,1)} %get-tuple-element.43), calls=%async_computation.2 | async-start | bytes 851968 | tf_op jit(solution)/shard_map/all_to_all | solution.py:42
  62.4 26.9 %copy-start.2 = (f32[4,8,128]{2,1,0:T(8,128)S(1)}, f32[4,8,128]{2,1,0:T(8,128)}, u32[]{:S(2)}) copy-start(f32[4,8,128]{2,1,0:T(8,128)} %get-tuple-element.29.field_ref) | copy-start | bytes 49156
  83.2 9.8 %all-to-all-start.4 = ((bf16[16,40,128]{2,1,0:T(8,128)(2,1)}), bf16[16,40,128]{2,1,0:T(8,128)(2,1)S(1)}, u32[]{:S(2)}, u32[]{:S(2)}) async-start(bf16[16,40,128]{2,1,0:T(8,128)(2,1)} %get-tuple-element.57), calls=%async_computation.4 | async-start | bytes 327680 | tf_op jit(solution)/shard_map/all_to_all | solution.py:42

commit v10 on v9

--- a/solution.py
+++ b/solution.py
@@ -17,7 +17,6 @@
 ALL = N_RAY * OWN
 PRODUCTS = MAXSEL * CAP
 SENT = OWN + 8
-REST = OWN + 4
 EXTRA = PRODUCTS + OWN
 SHARED = EXTRA + 8
 GATHER, SUM_1, SHARE, SUM_2, LAST = 9, 19, 5, 19, 10
@@ -98,44 +97,32 @@
     return count
 
 
-def start_kernel(
-    slowness_hbm, bar_hbm, pattern_hbm, selected_hbm, field_ref, sent_ref,
-    slowness_ref, bar_ref, sems, pattern_ref, selected_ref, list_ref, scalar_sems,
-):
-    copies = scalar_copies(pattern_hbm, selected_hbm, pattern_ref, selected_ref, scalar_sems)
-    copies.append(pltpu.make_async_copy(slowness_hbm, slowness_ref, sems.at[0]))
-    copies.append(pltpu.make_async_copy(bar_hbm, bar_ref, sems.at[1]))
+def start_kernel(slowness_hbm, bar_hbm, field_ref, sent_ref, slowness_ref, bar_ref, sems):
+    copies = [
+        pltpu.make_async_copy(slowness_hbm, slowness_ref, sems.at[0]),
+        pltpu.make_async_copy(bar_hbm, bar_ref, sems.at[1]),
+    ]
     for copy in copies:
         copy.start()
-    copies[0].wait()
-    copies[1].wait()
-    list_selected(selected_ref, 0, list_ref)
-    lane = lax.broadcasted_iota(jnp.int32, (8, TILE), 1) & (PRODUCTS - 1)
-    sub = lax.broadcasted_iota(jnp.int32, (8, TILE), 0)
-    numbers = jnp.zeros((8, TILE), jnp.int32)
-    for n in range(MAXSEL):
-        r = list_ref[n]
-        for s in range(CAP):
-            numbers = jnp.where(lane == n * CAP + s, block_number(pattern_ref[s, r]), numbers)
-    numbers = jnp.where(sub == 0, lax.shift_right_logical(numbers, 5), numbers & (OWN - 1))
-    copies[2].wait()
-    copies[3].wait()
+    for copy in copies:
+        copy.wait()
     field = slowness_ref[...] - primal_step * bar_ref[...]
     field_ref[...] = field
     field = field.reshape(OWN, TILE)
-    rounded = field.astype(BF16)
-    low = field - rounded.astype(F32)
-    tail = numbers.astype(F32)
+    rounded = field.astype(BF16).astype(F32)
+    low = field - rounded
+    sub = lax.broadcasted_iota(jnp.int32, (8, TILE), 0)
+    tail = jnp.zeros((8, TILE), F32)
     for x in range(GX):
-        tail = jnp.where(sub == REST - OWN + x, low[x * GY : x * GY + 1], tail)
-    sent = jnp.concatenate([rounded.astype(F32), tail], axis=0).astype(BF16)
+        tail = jnp.where(sub == x, low[x * GY : x * GY + 1], tail)
+    sent = jnp.concatenate([rounded, tail], axis=0).astype(BF16)
     for p in range(N_RAY):
         sent_ref[p] = sent
 
 
 def fetch_kernel(step):
     def kernel(
-        tiles_hbm, pattern_hbm, selected_hbm, after_ref, picked_ref, hot_ref, pick_ref,
+        tiles_hbm, pattern_hbm, selected_hbm, after_ref, picked_ref, hot_ref, pick_ref, numbers_ref,
         pattern_ref, selected_ref, list_ref, scalar_sems, sems,
     ):
         scalars = scalar_copies(pattern_hbm, selected_hbm, pattern_ref, selected_ref, scalar_sems)
@@ -152,18 +139,24 @@
             copy.start()
         sub = lax.broadcasted_iota(jnp.int32, (MAXSEL, TILE), 0)
         lane = lax.broadcasted_iota(jnp.int32, (2 * CAP, TILE), 1)
+        slot = lax.broadcasted_iota(jnp.int32, (8, TILE), 1) & (PRODUCTS - 1)
+        line = jnp.zeros((8, TILE), jnp.int32)
         for n in range(0, MAXSEL, 2):
             halves = []
             for m in (n, n + 1):
                 r = list_ref[m]
                 numbers = jnp.zeros((CAP, TILE), jnp.int32)
                 for s in range(CAP):
-                    numbers = jnp.where(sub == s, block_number(pattern_ref[s, r]), numbers)
+                    number = block_number(pattern_ref[s, r])
+                    numbers = jnp.where(sub == s, number, numbers)
+                    line = jnp.where(slot == m * CAP + s, number, line)
                 halves.append(numbers)
             numbers = jnp.concatenate(halves, axis=0)
             for c in range(ALL // TILE):
                 hot = jnp.where(numbers == lane + c * TILE, 1.0, 0.0).astype(BF16)
                 hot_ref[n * CAP : (n + 2) * CAP, c * TILE : (c + 1) * TILE] = hot
+        line = jnp.where(sub == 4, lax.shift_right_logical(line, 5), line & (OWN - 1))
+        numbers_ref[...] = jnp.where((sub == 4) | (sub == 5), line.astype(F32), 0.0)
         listed = jnp.full((MAXSEL, TILE), RB_DEV, jnp.int32)
         for n in range(MAXSEL):
             listed = jnp.where((sub == n) & (sub < count), list_ref[n], listed)
@@ -180,6 +173,7 @@
         ((MAXSEL, CAP, TILE, TILE), BF16),
         ((PRODUCTS, ALL), BF16),
         ((RB_DEV, MAXSEL, TILE), F32),
+        ((8, TILE), F32),
     ]
     scratch = SCALARS + (pltpu.SemaphoreType.DMA((MAXSEL,)),)
     return call(
@@ -241,7 +235,8 @@
 
 
 def share_kernel(
-    parts_ref, rays_ref, times_ref, pick_ref, picked_ref, rest_ref, extra_ref, new_rays_ref, out_ref
+    parts_ref, rays_ref, times_ref, pick_ref, picked_ref, rest_ref, extra_ref, numbers_ref,
+    new_rays_ref, out_ref,
 ):
     predicted = parts_ref[0]
     for m in range(1, N_MP):
@@ -253,7 +248,8 @@
         ).astype(BF16)
         for p in range(N_RAY):
             out_ref[p, n * CAP : (n + 2) * CAP, :] = pair
-    rest = jnp.concatenate([rest_ref[...].reshape(OWN, TILE), extra_ref[...]], axis=0).astype(BF16)
+    extra = extra_ref[...] + numbers_ref[...]
+    rest = jnp.concatenate([rest_ref[...].reshape(OWN, TILE), extra], axis=0).astype(BF16)
     for p in range(N_RAY):
         out_ref[p, PRODUCTS:SHARED, :] = rest
 
@@ -265,8 +261,8 @@
     lane = lax.broadcasted_iota(jnp.int32, (1, TILE), 1)
     singles = []
     for p in range(N_RAY):
-        rows = gathered_ref[at(p, GATHER)].astype(F32)[OWN:SENT]
-        singles.append(rows[0:1] * OWN + rows[1:2])
+        rows = shared_ref[at(p, SHARE), PRODUCTS:SHARED, :].astype(F32)[OWN:]
+        singles.append(rows[4:5] * OWN + rows[5:6])
     pairs = [jnp.where(lane < PRODUCTS, singles[p], singles[p + 1]) for p in range(0, N_RAY, 2)]
     group = 4
     chunk = group * OWN
@@ -392,7 +388,7 @@
     peer = jnp.minimum(lax.axis_index("ray") + 1, N_RAY - 1)
     rows = gathered_ref[at(peer, GATHER)].astype(F32)
     return [
-        rows[x * GY : x * GY + 1] + rows[REST + x : REST + x + 1] for x in range(GX)
+        rows[x * GY : x * GY + 1] + rows[OWN + x : OWN + x + 1] for x in range(GX)
     ]
 
 
@@ -545,12 +541,11 @@
     duals = ((3,) + GRID, F32)
 
     field, sent = call(
-        start_kernel, [grid, ((N_RAY, SENT, TILE), BF16)], "hhhh",
-        (slowness, extrapolated, pattern, selected),
-        (pltpu.VMEM(GRID, F32), pltpu.VMEM(GRID, F32), pltpu.SemaphoreType.DMA((2,))) + SCALARS,
+        start_kernel, [grid, ((N_RAY, SENT, TILE), BF16)], "hh", (slowness, extrapolated),
+        (pltpu.VMEM(GRID, F32), pltpu.VMEM(GRID, F32), pltpu.SemaphoreType.DMA((2,))),
     )
     gathered = exchange(sent, "ray", GATHER)
-    picked, hot, pick = fetch(0, tiles, pattern, selected, field)
+    picked, hot, pick, numbers = fetch(0, tiles, pattern, selected, field)
     (partial_value,) = call(predict_kernel, [SUMS], "vvv", (gathered, picked, hot))
     parts = exchange(partial_value, "mp", SUM_1)
 
@@ -564,11 +559,11 @@
         [duals, ((3, GY, TILE), F32), grid, grid, grid, ((8, TILE), F32)],
         "vvvvvv", (field, tv_dual, far, near, gathered, accumulated), busy=busy,
     )
-    picked_2, hot_2, pick_2 = fetch(1, tiles, pattern, selected, partial_value)
+    picked_2, hot_2, pick_2, _ = fetch(1, tiles, pattern, selected, partial_value)
 
     rays, share = call(
-        share_kernel, [RAYS, ((N_RAY, SHARED, TILE), BF16)], "vvvvvvv",
-        (parts, ray_dual, traveltimes, pick, picked, rest, extra),
+        share_kernel, [RAYS, ((N_RAY, SHARED, TILE), BF16)], "vvvvvvvv",
+        (parts, ray_dual, traveltimes, pick, picked, rest, extra, numbers),
     )
     shared = exchange(share, "ray", SHARE)
     field, image, edge, partial_value = call(

time: 94.6 us -> 94.3 us (level)
  no operation moved by 1% of the time
where the time goes in v10:
time: 94.3 us; the launch traced here: 93.2 us
  starting transfers between devices  41.1 us (44%)
  blocking collectives  19.5 us (21%)
  waiting for transfers between devices  17.8 us (19%)
  Pallas kernels  14 us (15%)
    all_to_all x4, starting transfers between devices, exchange(): lax.all_to_all(copies, axis, 0, 0, tiled=True, axis_index_groups=groups)  36.7 us
    all_to_all x1, blocking collectives, exchange(): lax.all_to_all(copies, axis, 0, 0, tiled=True, axis_index_groups=groups)  19.5 us
    pallas_call x11, Pallas kernels, call(): pl.pallas_call(kernel, out_shape=[pltpu.VMEM(shape, dtype) if keep else j...  14 us
    all_to_all x4, waiting for transfers between devices, exchange(): lax.all_to_all(copies, axis, 0, 0, tiled=True, axis_index_groups=groups)  13 us
    ppermute x2, waiting for transfers between devices, swap(): return lax.ppermute(block, 'mp', route + [(b, a) for a, b in route])  4.86 us
    ppermute x2, starting transfers between devices, swap(): return lax.ppermute(block, 'mp', route + [(b, a) for a, b in route])  4.36 us
  transfers between devices with their start and end apart: 6, of which 4 were waited for; matrix products, arithmetic and copies ran while one was open for 0% of the time, Pallas kernels for 7%

profile of v10, /device:TPU:1, one launch (start us, length us, event | category | flops | bytes accessed | tf_op | source)
XLA Modules:
  0.0 93.2 jit_solution(3867242542661295613)
XLA Ops:
  0.6 1.4 %shard_map.128 = (f32[4,8,128]{2,1,0:T(8,128)S(1)}, bf16[16,40,128]{2,1,0:T(8,128)(2,1)}) custom-call(f32[4,8,128]{2,1,0:T(8,128)} %slowness_hbm.1, f32[4,8,128]{2,1,0:T(8,128)} %bar_hbm.1), custom_call_target="tpu_custom_call" | custom-call | tf_op jit(solution)/shard_map/pallas_call | solution.py:55
  2.1 10.6 %all-to-all-start = ((bf16[16,40,128]{2,1,0:T(8,128)(2,1)}), bf16[16,40,128]{2,1,0:T(8,128)(2,1)S(1)}, u32[]{:S(2)}, u32[]{:S(2)}) async-start(bf16[16,40,128]{2,1,0:T(8,128)(2,1)} %get-tuple-element.35), calls=%async_computation | async-start | bytes 327680 | tf_op jit(solution)/shard_map/all_to_all | solution.py:41
  12.7 2.4 %shard_map.129 = (bf16[8,8,128,128]{3,2,1,0:T(8,128)(2,1)S(1)}, bf16[64,512]{1,0:T(8,128)(2,1)S(1)}, f32[16,8,128]{2,1,0:T(8,128)S(1)}, f32[8,128]{1,0:T(8,128)S(1)}) custom-call(bf16[16,8,128,128]{3,2,1,0:T(8,128)(2,1)} %tiles_hbm.3, s32[8,16]{1,0:T(8,128)} %bitcast.1, s32[2,16]{1,0:T(2,128)} %selected_hbm.3, ...), custom_call_target="tpu_custom_call" | custom-call | bytes 8388608 | tf_op jit(solution)/shard_map/pallas_call | solution.py:55
  15.1 0.0 copy-start
  15.1 0.0 copy-start.1
  15.1 0.0 copy-start.3
  15.1 0.0 copy-start.4
  15.1 2.8 %all-to-all-done.gathered_ref = bf16[16,40,128]{2,1,0:T(8,128)(2,1)S(1)} async-done(((bf16[16,40,128]{2,1,0:T(8,128)(2,1)}), bf16[16,40,128]{2,1,0:T(8,128)(2,1)S(1)}, u32[]{:S(2)}, u32[]{:S(2)}) %all-to-all-start) | async-done | bytes 163872 | tf_op jit(solution)/shard_map/all_to_all | solution.py:41
  17.9 1.4 %shard_map.130.after_any.after_ref = f32[32,8,128]{2,1,0:T(8,128)} custom-call(bf16[16,40,128]{2,1,0:T(8,128)(2,1)S(1)} %all-to-all-done.gathered_ref, bf16[8,8,128,128]{3,2,1,0:T(8,128)(2,1)S(1)} %get-tuple-element.37.picked_ref, bf16[64,512]{1,0:T(8,128)(2,1)S(1)} %get-tuple-element.38.hot_ref), custom_call_target="tpu_custom_call" | custom-call | tf_op jit(solution)/shard_map/pallas_call | solution.py:55
  19.3 15.4 %all-to-all-start.1 = ((f32[32,8,128]{2,1,0:T(8,128)}), f32[32,8,128]{2,1,0:T(8,128)S(1)}, u32[]{:S(2)}, u32[]{:S(2)}) async-start(f32[32,8,128]{2,1,0:T(8,128)} %shard_map.130.after_any.after_ref), calls=%async_computation.1 | async-start | bytes 262144 | tf_op jit(solution)/shard_map/all_to_all | solution.py:41
  34.7 0.0 copy-done
  34.7 2.4 %collective-permute-start = (f32[40,128]{1,0:T(8,128)S(1)}, f32[40,128]{1,0:T(8,128)S(1)}, u32[]{:S(2)}, u32[]{:S(2)}) collective-permute-start(f32[40,128]{1,0:T(8,128)S(1)} %get-tuple-element.40), channel_id=1, source_target_pairs={{1,2},{3,4},{5,6},{7,8},{9,10},{11,12},{13,14},{15,16},{17,18},{19... | collective-permute-start | bytes 61448 | tf_op jit(solution)/shard_map/ppermute | solution.py:376
  37.2 1.9 %collective-permute-start.1 = (f32[40,128]{1,0:T(8,128)S(1)}, f32[40,128]{1,0:T(8,128)S(1)}, u32[]{:S(2)}, u32[]{:S(2)}) collective-permute-start(f32[40,128]{1,0:T(8,128)S(1)} %get-tuple-element.41), channel_id=1, source_target_pairs={{0,1},{2,3},{4,5},{6,7},{8,9},{10,11},{12,13},{14,15},{16,17},{18,... | collective-permute-start | bytes 61448 | tf_op jit(solution)/shard_map/ppermute | solution.py:376
  39.1 4.9 %collective-permute-done.far_ref = f32[40,128]{1,0:T(8,128)S(1)} collective-permute-done((f32[40,128]{1,0:T(8,128)S(1)}, f32[40,128]{1,0:T(8,128)S(1)}, u32[]{:S(2)}, u32[]{:S(2)}) %collective-permute-start) | collective-permute-done | bytes 20512 | tf_op jit(solution)/shard_map/ppermute | solution.py:376
  44.0 0.0 collective-permute-done.1.near_ref
  44.0 0.0 copy-done.1
  44.0 0.2 shard_map.132
  44.2 0.0 all-to-all-done.1.parts_ref
  44.2 0.0 copy-done.3
  44.2 0.0 copy-done.4
  44.2 1.2 %shard_map.133 = (f32[16,128]{1,0:T(8,128)S(1)}, bf16[16,104,128]{2,1,0:T(8,128)(2,1)}) custom-call(f32[32,8,128]{2,1,0:T(8,128)S(1)} %all-to-all-done.1.parts_ref, f32[16,128]{1,0:T(8,128)S(1)} %copy-done.4, f32[16,128]{1,0:T(8,128)S(1)} %copy-done.3, f32[16,8,128]{2,1,0:T(8,128)S(1)} %get-tuple-element.39.pick_ref, ...), custom_call_target="tpu_custom_call" | custom-call | tf_op jit(solution)/shard_map/pallas_call | solution.py:55
  45.4 4.7 %all-to-all-start.2 = ((bf16[16,104,128]{2,1,0:T(8,128)(2,1)}), bf16[16,104,128]{2,1,0:T(8,128)(2,1)S(1)}, u32[]{:S(2)}, u32[]{:S(2)}) async-start(bf16[16,104,128]{2,1,0:T(8,128)(2,1)} %get-tuple-element.45), calls=%async_computation.2 | async-start | bytes 851968 | tf_op jit(solution)/shard_map/all_to_all | solution.py:41
  50.1 3.0 %shard_map.134 = (bf16[8,8,128,128]{3,2,1,0:T(8,128)(2,1)S(1)}, bf16[64,512]{1,0:T(8,128)(2,1)S(1)}, f32[16,8,128]{2,1,0:T(8,128)S(1)}, f32[8,128]{1,0:T(8,128)}) custom-call(bf16[16,8,128,128]{3,2,1,0:T(8,128)(2,1)} %tiles_hbm.3, s32[8,16]{1,0:T(8,128)} %bitcast.2, s32[2,16]{1,0:T(2,128)} %selected_hbm.3, f32[32,8,128]{2,1,0:T(8,128)} %shard_map.130.after_any.after_ref), custom_call_target="tpu_custom_call" | custom-call | bytes 8388608 | tf_op jit(solution)/shard_map/pallas_call | solution.py:55
  53.0 7.2 %all-to-all-done.2.shared_ref = bf16[16,104,128]{2,1,0:T(8,128)(2,1)S(1)} async-done(((bf16[16,104,128]{2,1,0:T(8,128)(2,1)}), bf16[16,104,128]{2,1,0:T(8,128)(2,1)S(1)}, u32[]{:S(2)}, u32[]{:S(2)}) %all-to-all-start.2) | async-done | bytes 426016 | tf_op jit(solution)/shard_map/all_to_all | solution.py:41
  60.2 1.7 %shard_map.135 = (f32[4,8,128]{2,1,0:T(8,128)}, f32[4,8,128]{2,1,0:T(8,128)S(1)}, f32[16,128]{1,0:T(8,128)S(1)}, bf16[32,24,128]{2,1,0:T(8,128)(2,1)S(1)}) custom-call(bf16[16,104,128]{2,1,0:T(8,128)(2,1)S(1)} %all-to-all-done.2.shared_ref, bf16[16,40,128]{2,1,0:T(8,128)(2,1)S(1)} %all-to-all-done.gathered_ref, ...), custom_call_target="tpu_custom_call" | custom-call | tf_op jit(solution)/shard_map/pallas_call | solution.py:55
  62.0 0.0 copy-start.2
  62.0 19.5 %all_to_all.25.parts_ref = bf16[32,24,128]{2,1,0:T(8,128)(2,1)S(1)} all-to-all(bf16[32,24,128]{2,1,0:T(8,128)(2,1)S(1)} %get-tuple-element.51), channel_id=1, replica_groups={{19,20,21,22,23,24,25,26,27,28,29,30,31,0,1,2,3,4,5,6,7,8,9,10,11,12,13..., dimensions={0} | all-to-all | bytes 393216 | tf_op jit(solution)/shard_map/all_to_all | solution.py:41
  81.5 1.3 %shard_map.136 = (f32[16,128]{1,0:T(8,128)}, bf16[16,40,128]{2,1,0:T(8,128)(2,1)}, f32[2,8,128]{2,1,0:T(8,128)S(1)}) custom-call(bf16[32,24,128]{2,1,0:T(8,128)(2,1)S(1)} %all_to_all.25.parts_ref, f32[16,128]{1,0:T(8,128)S(1)} %get-tuple-element.52.rays_ref, f32[16,128]{1,0:T(8,128)S(1)} %copy-done.3, f32[16,8,128]{2,1,0:T(8,128)S(1)} %get-tuple-element.53.pick_ref, ...), custom_call_target="tpu_custom_call" | custom-call | tf_op jit(solution)/shard_map/pallas_call | solution.py:55
  82.8 6.1 %all-to-all-start.4 = ((bf16[16,40,128]{2,1,0:T(8,128)(2,1)}), bf16[16,40,128]{2,1,0:T(8,128)(2,1)S(1)}, u32[]{:S(2)}, u32[]{:S(2)}) async-start(bf16[16,40,128]{2,1,0:T(8,128)(2,1)} %get-tuple-element.59), calls=%async_computation.4 | async-start | bytes 327680 | tf_op jit(solution)/shard_map/all_to_all | solution.py:41
  88.8 0.0 copy-done.2
  88.8 0.7 shard_map.137
  89.6 3.0 %all-to-all-done.4.shared_ref = bf16[16,40,128]{2,1,0:T(8,128)(2,1)S(1)} async-done(((bf16[16,40,128]{2,1,0:T(8,128)(2,1)}), bf16[16,40,128]{2,1,0:T(8,128)(2,1)S(1)}, u32[]{:S(2)}, u32[]{:S(2)}) %all-to-all-start.4) | async-done | bytes 163872 | tf_op jit(solution)/shard_map/all_to_all | solution.py:41
  92.5 0.7 shard_map.138
  (1 shorter events, 0.0 us)
Async XLA Ops:
  2.1 15.8 %all-to-all-start = ((bf16[16,40,128]{2,1,0:T(8,128)(2,1)}), bf16[16,40,128]{2,1,0:T(8,128)(2,1)S(1)}, u32[]{:S(2)}, u32[]{:S(2)}) async-start(bf16[16,40,128]{2,1,0:T(8,128)(2,1)} %get-tuple-element.35), calls=%async_computation | async-start | bytes 327680 | tf_op jit(solution)/shard_map/all_to_all | solution.py:41
  15.1 19.7 %copy-start = (f32[3,4,8,128]{3,2,1,0:T(8,128)S(1)}, f32[3,4,8,128]{3,2,1,0:T(8,128)}, u32[]{:S(2)}) copy-start(f32[3,4,8,128]{3,2,1,0:T(8,128)} %dual_ref.3) | copy-start | bytes 147460
  15.1 28.9 %copy-start.1 = (f32[4,8,128]{2,1,0:T(8,128)S(1)}, f32[4,8,128]{2,1,0:T(8,128)}, u32[]{:S(2)}) copy-start(f32[4,8,128]{2,1,0:T(8,128)} %image_ref.3) | copy-start | bytes 49156
  15.1 29.1 %copy-start.3 = (f32[16,128]{1,0:T(8,128)S(1)}, f32[16,128]{1,0:T(8,128)}, u32[]{:S(2)}) copy-start(f32[16,128]{1,0:T(8,128)} %times_ref.3) | copy-start | bytes 24580
  15.1 29.1 %copy-start.4 = (f32[16,128]{1,0:T(8,128)S(1)}, f32[16,128]{1,0:T(8,128)}, u32[]{:S(2)}) copy-start(f32[16,128]{1,0:T(8,128)} %rays_ref.1) | copy-start | bytes 24580
  19.3 24.8 %all-to-all-start.1 = ((f32[32,8,128]{2,1,0:T(8,128)}), f32[32,8,128]{2,1,0:T(8,128)S(1)}, u32[]{:S(2)}, u32[]{:S(2)}) async-start(f32[32,8,128]{2,1,0:T(8,128)} %shard_map.130.after_any.after_ref), calls=%async_computation.1 | async-start | bytes 262144 | tf_op jit(solution)/shard_map/all_to_all | solution.py:41
  34.7 9.2 %collective-permute-start = (f32[40,128]{1,0:T(8,128)S(1)}, f32[40,128]{1,0:T(8,128)S(1)}, u32[]{:S(2)}, u32[]{:S(2)}) collective-permute-start(f32[40,128]{1,0:T(8,128)S(1)} %get-tuple-element.40), channel_id=1, source_target_pairs={{1,2},{3,4},{5,6},{7,8},{9,10},{11,12},{13,14},{15,16},{17,18},{19... | collective-permute-start | bytes 61448 | tf_op jit(solution)/shard_map/ppermute | solution.py:376
  37.2 6.8 %collective-permute-start.1 = (f32[40,128]{1,0:T(8,128)S(1)}, f32[40,128]{1,0:T(8,128)S(1)}, u32[]{:S(2)}, u32[]{:S(2)}) collective-permute-start(f32[40,128]{1,0:T(8,128)S(1)} %get-tuple-element.41), channel_id=1, source_target_pairs={{0,1},{2,3},{4,5},{6,7},{8,9},{10,11},{12,13},{14,15},{16,17},{18,... | collective-permute-start | bytes 61448 | tf_op jit(solution)/shard_map/ppermute | solution.py:376
  45.4 14.8 %all-to-all-start.2 = ((bf16[16,104,128]{2,1,0:T(8,128)(2,1)}), bf16[16,104,128]{2,1,0:T(8,128)(2,1)S(1)}, u32[]{:S(2)}, u32[]{:S(2)}) async-start(bf16[16,104,128]{2,1,0:T(8,128)(2,1)} %get-tuple-element.45), calls=%async_computation.2 | async-start | bytes 851968 | tf_op jit(solution)/shard_map/all_to_all | solution.py:41
  62.0 26.8 %copy-start.2 = (f32[4,8,128]{2,1,0:T(8,128)S(1)}, f32[4,8,128]{2,1,0:T(8,128)}, u32[]{:S(2)}) copy-start(f32[4,8,128]{2,1,0:T(8,128)} %get-tuple-element.30.field_ref) | copy-start | bytes 49156
  82.8 9.7 %all-to-all-start.4 = ((bf16[16,40,128]{2,1,0:T(8,128)(2,1)}), bf16[16,40,128]{2,1,0:T(8,128)(2,1)S(1)}, u32[]{:S(2)}, u32[]{:S(2)}) async-start(bf16[16,40,128]{2,1,0:T(8,128)(2,1)} %get-tuple-element.59), calls=%async_computation.4 | async-start | bytes 327680 | tf_op jit(solution)/shard_map/all_to_all | solution.py:41

commit v11 on v10

--- a/solution.py
+++ b/solution.py
@@ -19,7 +19,7 @@
 SENT = OWN + 8
 EXTRA = PRODUCTS + OWN
 SHARED = EXTRA + 8
-GATHER, SUM_1, SHARE, SUM_2, LAST = 9, 19, 5, 19, 10
+GATHER, SUM_1, SHARE, SUM_2, LAST = 9, 19, 9, 19, 10
 
 primal_step = 0.5
 dual_step = 0.5

time: 94.3 us -> 94.2 us (level)
  waiting for transfers between devices: 17.8 us -> 16.3 us
  starting transfers between devices: 41.1 us -> 42.1 us
    all_to_all x4, waiting for transfers between devices: 13 us -> 11.5 us  [exchange(): lax.all_to_all(copies, axis, 0, 0, tiled=True, axis_index_groups=groups)]
    all_to_all x4, starting transfers between devices: 36.7 us -> 37.8 us  [exchange(): lax.all_to_all(copies, axis, 0, 0, tiled=True, axis_index_groups=groups)]
where the time goes in v11:
time: 94.2 us; the launch traced here: 93.2 us
  starting transfers between devices  42.1 us (45%)
  blocking collectives  19.6 us (21%)
  waiting for transfers between devices  16.3 us (17%)
  Pallas kernels  14.3 us (15%)
    all_to_all x4, starting transfers between devices, exchange(): lax.all_to_all(copies, axis, 0, 0, tiled=True, axis_index_groups=groups)  37.8 us
    all_to_all x1, blocking collectives, exchange(): lax.all_to_all(copies, axis, 0, 0, tiled=True, axis_index_groups=groups)  19.6 us
    pallas_call x11, Pallas kernels, call(): pl.pallas_call(kernel, out_shape=[pltpu.VMEM(shape, dtype) if keep else j...  14.3 us
    all_to_all x4, waiting for transfers between devices, exchange(): lax.all_to_all(copies, axis, 0, 0, tiled=True, axis_index_groups=groups)  11.5 us
    ppermute x2, waiting for transfers between devices, swap(): return lax.ppermute(block, 'mp', route + [(b, a) for a, b in route])  4.86 us
    ppermute x2, starting transfers between devices, swap(): return lax.ppermute(block, 'mp', route + [(b, a) for a, b in route])  4.36 us
  transfers between devices with their start and end apart: 6, of which 4 were waited for; matrix products, arithmetic and copies ran while one was open for 0% of the time, Pallas kernels for 7%

profile of v11, /device:TPU:1, one launch (start us, length us, event | category | flops | bytes accessed | tf_op | source)
XLA Modules:
  0.0 93.2 jit_solution(5724941102676796714)
XLA Ops:
  0.6 1.4 %shard_map.128 = (f32[4,8,128]{2,1,0:T(8,128)S(1)}, bf16[16,40,128]{2,1,0:T(8,128)(2,1)}) custom-call(f32[4,8,128]{2,1,0:T(8,128)} %slowness_hbm.1, f32[4,8,128]{2,1,0:T(8,128)} %bar_hbm.1), custom_call_target="tpu_custom_call" | custom-call | tf_op jit(solution)/shard_map/pallas_call | solution.py:55
  2.1 10.6 %all-to-all-start = ((bf16[16,40,128]{2,1,0:T(8,128)(2,1)}), bf16[16,40,128]{2,1,0:T(8,128)(2,1)S(1)}, u32[]{:S(2)}, u32[]{:S(2)}) async-start(bf16[16,40,128]{2,1,0:T(8,128)(2,1)} %get-tuple-element.35), calls=%async_computation | async-start | bytes 327680 | tf_op jit(solution)/shard_map/all_to_all | solution.py:41
  12.7 2.4 %shard_map.129 = (bf16[8,8,128,128]{3,2,1,0:T(8,128)(2,1)S(1)}, bf16[64,512]{1,0:T(8,128)(2,1)S(1)}, f32[16,8,128]{2,1,0:T(8,128)S(1)}, f32[8,128]{1,0:T(8,128)S(1)}) custom-call(bf16[16,8,128,128]{3,2,1,0:T(8,128)(2,1)} %tiles_hbm.3, s32[8,16]{1,0:T(8,128)} %bitcast.1, s32[2,16]{1,0:T(2,128)} %selected_hbm.3, ...), custom_call_target="tpu_custom_call" | custom-call | bytes 8388608 | tf_op jit(solution)/shard_map/pallas_call | solution.py:55
  15.1 0.0 copy-start
  15.1 0.0 copy-start.1
  15.1 0.0 copy-start.3
  15.1 0.0 copy-start.4
  15.1 2.8 %all-to-all-done.gathered_ref = bf16[16,40,128]{2,1,0:T(8,128)(2,1)S(1)} async-done(((bf16[16,40,128]{2,1,0:T(8,128)(2,1)}), bf16[16,40,128]{2,1,0:T(8,128)(2,1)S(1)}, u32[]{:S(2)}, u32[]{:S(2)}) %all-to-all-start) | async-done | bytes 163872 | tf_op jit(solution)/shard_map/all_to_all | solution.py:41
  17.9 1.4 %shard_map.130.after_any.after_ref = f32[32,8,128]{2,1,0:T(8,128)} custom-call(bf16[16,40,128]{2,1,0:T(8,128)(2,1)S(1)} %all-to-all-done.gathered_ref, bf16[8,8,128,128]{3,2,1,0:T(8,128)(2,1)S(1)} %get-tuple-element.37.picked_ref, bf16[64,512]{1,0:T(8,128)(2,1)S(1)} %get-tuple-element.38.hot_ref), custom_call_target="tpu_custom_call" | custom-call | tf_op jit(solution)/shard_map/pallas_call | solution.py:55
  19.3 15.4 %all-to-all-start.1 = ((f32[32,8,128]{2,1,0:T(8,128)}), f32[32,8,128]{2,1,0:T(8,128)S(1)}, u32[]{:S(2)}, u32[]{:S(2)}) async-start(f32[32,8,128]{2,1,0:T(8,128)} %shard_map.130.after_any.after_ref), calls=%async_computation.1 | async-start | bytes 262144 | tf_op jit(solution)/shard_map/all_to_all | solution.py:41
  34.7 0.0 copy-done
  34.7 2.4 %collective-permute-start = (f32[40,128]{1,0:T(8,128)S(1)}, f32[40,128]{1,0:T(8,128)S(1)}, u32[]{:S(2)}, u32[]{:S(2)}) collective-permute-start(f32[40,128]{1,0:T(8,128)S(1)} %get-tuple-element.40), channel_id=1, source_target_pairs={{1,2},{3,4},{5,6},{7,8},{9,10},{11,12},{13,14},{15,16},{17,18},{19... | collective-permute-start | bytes 61448 | tf_op jit(solution)/shard_map/ppermute | solution.py:376
  37.2 1.9 %collective-permute-start.1 = (f32[40,128]{1,0:T(8,128)S(1)}, f32[40,128]{1,0:T(8,128)S(1)}, u32[]{:S(2)}, u32[]{:S(2)}) collective-permute-start(f32[40,128]{1,0:T(8,128)S(1)} %get-tuple-element.41), channel_id=1, source_target_pairs={{0,1},{2,3},{4,5},{6,7},{8,9},{10,11},{12,13},{14,15},{16,17},{18,... | collective-permute-start | bytes 61448 | tf_op jit(solution)/shard_map/ppermute | solution.py:376
  39.1 4.9 %collective-permute-done.far_ref = f32[40,128]{1,0:T(8,128)S(1)} collective-permute-done((f32[40,128]{1,0:T(8,128)S(1)}, f32[40,128]{1,0:T(8,128)S(1)}, u32[]{:S(2)}, u32[]{:S(2)}) %collective-permute-start) | collective-permute-done | bytes 20512 | tf_op jit(solution)/shard_map/ppermute | solution.py:376
  44.0 0.0 collective-permute-done.1.near_ref
  44.0 0.0 copy-done.1
  44.0 0.2 shard_map.132
  44.2 0.0 all-to-all-done.1.parts_ref
  44.2 0.0 copy-done.3
  44.2 0.0 copy-done.4
  44.2 1.2 %shard_map.133 = (f32[16,128]{1,0:T(8,128)S(1)}, bf16[16,104,128]{2,1,0:T(8,128)(2,1)}) custom-call(f32[32,8,128]{2,1,0:T(8,128)S(1)} %all-to-all-done.1.parts_ref, f32[16,128]{1,0:T(8,128)S(1)} %copy-done.4, f32[16,128]{1,0:T(8,128)S(1)} %copy-done.3, f32[16,8,128]{2,1,0:T(8,128)S(1)} %get-tuple-element.39.pick_ref, ...), custom_call_target="tpu_custom_call" | custom-call | tf_op jit(solution)/shard_map/pallas_call | solution.py:55
  45.4 5.2 %all-to-all-start.2 = ((bf16[16,104,128]{2,1,0:T(8,128)(2,1)}), bf16[16,104,128]{2,1,0:T(8,128)(2,1)S(1)}, u32[]{:S(2)}, u32[]{:S(2)}) async-start(bf16[16,104,128]{2,1,0:T(8,128)(2,1)} %get-tuple-element.45), calls=%async_computation.2 | async-start | bytes 851968 | tf_op jit(solution)/shard_map/all_to_all | solution.py:41
  50.6 3.2 %shard_map.134 = (bf16[8,8,128,128]{3,2,1,0:T(8,128)(2,1)S(1)}, bf16[64,512]{1,0:T(8,128)(2,1)S(1)}, f32[16,8,128]{2,1,0:T(8,128)S(1)}, f32[8,128]{1,0:T(8,128)}) custom-call(bf16[16,8,128,128]{3,2,1,0:T(8,128)(2,1)} %tiles_hbm.3, s32[8,16]{1,0:T(8,128)} %bitcast.2, s32[2,16]{1,0:T(2,128)} %selected_hbm.3, f32[32,8,128]{2,1,0:T(8,128)} %shard_map.130.after_any.after_ref), custom_call_target="tpu_custom_call" | custom-call | bytes 8388608 | tf_op jit(solution)/shard_map/pallas_call | solution.py:55
  53.8 5.7 %all-to-all-done.2.shared_ref = bf16[16,104,128]{2,1,0:T(8,128)(2,1)S(1)} async-done(((bf16[16,104,128]{2,1,0:T(8,128)(2,1)}), bf16[16,104,128]{2,1,0:T(8,128)(2,1)S(1)}, u32[]{:S(2)}, u32[]{:S(2)}) %all-to-all-start.2) | async-done | bytes 426016 | tf_op jit(solution)/shard_map/all_to_all | solution.py:41
  59.5 1.7 %shard_map.135 = (f32[4,8,128]{2,1,0:T(8,128)}, f32[4,8,128]{2,1,0:T(8,128)S(1)}, f32[16,128]{1,0:T(8,128)S(1)}, bf16[32,24,128]{2,1,0:T(8,128)(2,1)S(1)}) custom-call(bf16[16,104,128]{2,1,0:T(8,128)(2,1)S(1)} %all-to-all-done.2.shared_ref, bf16[16,40,128]{2,1,0:T(8,128)(2,1)S(1)} %all-to-all-done.gathered_ref, ...), custom_call_target="tpu_custom_call" | custom-call | tf_op jit(solution)/shard_map/pallas_call | solution.py:55
  61.3 0.0 copy-start.2
  61.3 19.6 %all_to_all.25.parts_ref = bf16[32,24,128]{2,1,0:T(8,128)(2,1)S(1)} all-to-all(bf16[32,24,128]{2,1,0:T(8,128)(2,1)S(1)} %get-tuple-element.51), channel_id=1, replica_groups={{19,20,21,22,23,24,25,26,27,28,29,30,31,0,1,2,3,4,5,6,7,8,9,10,11,12,13..., dimensions={0} | all-to-all | bytes 393216 | tf_op jit(solution)/shard_map/all_to_all | solution.py:41
  80.8 1.3 %shard_map.136 = (f32[16,128]{1,0:T(8,128)}, bf16[16,40,128]{2,1,0:T(8,128)(2,1)}, f32[2,8,128]{2,1,0:T(8,128)S(1)}) custom-call(bf16[32,24,128]{2,1,0:T(8,128)(2,1)S(1)} %all_to_all.25.parts_ref, f32[16,128]{1,0:T(8,128)S(1)} %get-tuple-element.52.rays_ref, f32[16,128]{1,0:T(8,128)S(1)} %copy-done.3, f32[16,8,128]{2,1,0:T(8,128)S(1)} %get-tuple-element.53.pick_ref, ...), custom_call_target="tpu_custom_call" | custom-call | tf_op jit(solution)/shard_map/pallas_call | solution.py:55
  82.1 6.6 %all-to-all-start.4 = ((bf16[16,40,128]{2,1,0:T(8,128)(2,1)}), bf16[16,40,128]{2,1,0:T(8,128)(2,1)S(1)}, u32[]{:S(2)}, u32[]{:S(2)}) async-start(bf16[16,40,128]{2,1,0:T(8,128)(2,1)} %get-tuple-element.59), calls=%async_computation.4 | async-start | bytes 327680 | tf_op jit(solution)/shard_map/all_to_all | solution.py:41
  88.8 0.0 copy-done.2
  88.8 0.7 shard_map.137
  89.5 3.0 %all-to-all-done.4.shared_ref = bf16[16,40,128]{2,1,0:T(8,128)(2,1)S(1)} async-done(((bf16[16,40,128]{2,1,0:T(8,128)(2,1)}), bf16[16,40,128]{2,1,0:T(8,128)(2,1)S(1)}, u32[]{:S(2)}, u32[]{:S(2)}) %all-to-all-start.4) | async-done | bytes 163872 | tf_op jit(solution)/shard_map/all_to_all | solution.py:41
  92.5 0.7 shard_map.138
  (1 shorter events, 0.0 us)
Async XLA Ops:
  2.1 15.8 %all-to-all-start = ((bf16[16,40,128]{2,1,0:T(8,128)(2,1)}), bf16[16,40,128]{2,1,0:T(8,128)(2,1)S(1)}, u32[]{:S(2)}, u32[]{:S(2)}) async-start(bf16[16,40,128]{2,1,0:T(8,128)(2,1)} %get-tuple-element.35), calls=%async_computation | async-start | bytes 327680 | tf_op jit(solution)/shard_map/all_to_all | solution.py:41
  15.1 19.7 %copy-start = (f32[3,4,8,128]{3,2,1,0:T(8,128)S(1)}, f32[3,4,8,128]{3,2,1,0:T(8,128)}, u32[]{:S(2)}) copy-start(f32[3,4,8,128]{3,2,1,0:T(8,128)} %dual_ref.3) | copy-start | bytes 147460
  15.1 28.9 %copy-start.1 = (f32[4,8,128]{2,1,0:T(8,128)S(1)}, f32[4,8,128]{2,1,0:T(8,128)}, u32[]{:S(2)}) copy-start(f32[4,8,128]{2,1,0:T(8,128)} %image_ref.3) | copy-start | bytes 49156
  15.1 29.1 %copy-start.3 = (f32[16,128]{1,0:T(8,128)S(1)}, f32[16,128]{1,0:T(8,128)}, u32[]{:S(2)}) copy-start(f32[16,128]{1,0:T(8,128)} %times_ref.3) | copy-start | bytes 24580
  15.1 29.1 %copy-start.4 = (f32[16,128]{1,0:T(8,128)S(1)}, f32[16,128]{1,0:T(8,128)}, u32[]{:S(2)}) copy-start(f32[16,128]{1,0:T(8,128)} %rays_ref.1) | copy-start | bytes 24580
  19.3 24.8 %all-to-all-start.1 = ((f32[32,8,128]{2,1,0:T(8,128)}), f32[32,8,128]{2,1,0:T(8,128)S(1)}, u32[]{:S(2)}, u32[]{:S(2)}) async-start(f32[32,8,128]{2,1,0:T(8,128)} %shard_map.130.after_any.after_ref), calls=%async_computation.1 | async-start | bytes 262144 | tf_op jit(solution)/shard_map/all_to_all | solution.py:41
  34.7 9.2 %collective-permute-start = (f32[40,128]{1,0:T(8,128)S(1)}, f32[40,128]{1,0:T(8,128)S(1)}, u32[]{:S(2)}, u32[]{:S(2)}) collective-permute-start(f32[40,128]{1,0:T(8,128)S(1)} %get-tuple-element.40), channel_id=1, source_target_pairs={{1,2},{3,4},{5,6},{7,8},{9,10},{11,12},{13,14},{15,16},{17,18},{19... | collective-permute-start | bytes 61448 | tf_op jit(solution)/shard_map/ppermute | solution.py:376
  37.2 6.8 %collective-permute-start.1 = (f32[40,128]{1,0:T(8,128)S(1)}, f32[40,128]{1,0:T(8,128)S(1)}, u32[]{:S(2)}, u32[]{:S(2)}) collective-permute-start(f32[40,128]{1,0:T(8,128)S(1)} %get-tuple-element.41), channel_id=1, source_target_pairs={{0,1},{2,3},{4,5},{6,7},{8,9},{10,11},{12,13},{14,15},{16,17},{18,... | collective-permute-start | bytes 61448 | tf_op jit(solution)/shard_map/ppermute | solution.py:376
  45.4 14.1 %all-to-all-start.2 = ((bf16[16,104,128]{2,1,0:T(8,128)(2,1)}), bf16[16,104,128]{2,1,0:T(8,128)(2,1)S(1)}, u32[]{:S(2)}, u32[]{:S(2)}) async-start(bf16[16,104,128]{2,1,0:T(8,128)(2,1)} %get-tuple-element.45), calls=%async_computation.2 | async-start | bytes 851968 | tf_op jit(solution)/shard_map/all_to_all | solution.py:41
  61.3 27.5 %copy-start.2 = (f32[4,8,128]{2,1,0:T(8,128)S(1)}, f32[4,8,128]{2,1,0:T(8,128)}, u32[]{:S(2)}) copy-start(f32[4,8,128]{2,1,0:T(8,128)} %get-tuple-element.30.field_ref) | copy-start | bytes 49156
  82.1 10.3 %all-to-all-start.4 = ((bf16[16,40,128]{2,1,0:T(8,128)(2,1)}), bf16[16,40,128]{2,1,0:T(8,128)(2,1)S(1)}, u32[]{:S(2)}, u32[]{:S(2)}) async-start(bf16[16,40,128]{2,1,0:T(8,128)(2,1)} %get-tuple-element.59), calls=%async_computation.4 | async-start | bytes 327680 | tf_op jit(solution)/shard_map/all_to_all | solution.py:41

commit v12 on v11

--- a/solution.py
+++ b/solution.py
@@ -203,6 +203,12 @@
         out_ref[m] = total
 
 
+def added(terms):
+    while len(terms) > 1:
+        terms = [a + b for a, b in zip(terms[::2], terms[1::2])]
+    return terms[0]
+
+
 def dual_update(predicted, rays_ref, times_ref, pick_ref, new_rays_ref):
     rays = jnp.zeros((MAXSEL, TILE), F32)
     times = jnp.zeros((MAXSEL, TILE), F32)
@@ -238,9 +244,7 @@
     parts_ref, rays_ref, times_ref, pick_ref, picked_ref, rest_ref, extra_ref, numbers_ref,
     new_rays_ref, out_ref,
 ):
-    predicted = parts_ref[0]
-    for m in range(1, N_MP):
-        predicted = predicted + parts_ref[m]
+    predicted = added([parts_ref[m] for m in range(N_MP)])
     change = dual_update(predicted, rays_ref, times_ref, pick_ref, new_rays_ref)
     for n in range(0, MAXSEL, 2):
         pair = jnp.concatenate(
@@ -354,9 +358,7 @@
     high = before[0:1].astype(BF16).astype(F32)
     tail = jnp.where(last_ray, 0.0, change[1])
     tail = jnp.where(sub == 0, high, jnp.where(sub == 1, before[0:1] - high, tail))
-    halves = parts_ref[0].astype(F32)
-    for m in range(1, N_MP):
-        halves = halves + parts_ref[m].astype(F32)
+    halves = added([parts_ref[m].astype(F32) for m in range(N_MP)])
     predicted = halves[0:MAXSEL] + halves[MAXSEL : 2 * MAXSEL]
     change = dual_update(predicted, rays_ref, times_ref, pick_ref, new_rays_ref)
     terms = jnp.concatenate([products(change, picked_ref, n) for n in range(MAXSEL)], axis=0)
@@ -519,9 +521,7 @@
     )
     sub = lax.broadcasted_iota(jnp.int32, (GY, TILE), 0)
     first_y = (sub == 0) & (ray > 0)
-    back = shared_ref[0].astype(F32)
-    for p in range(1, N_RAY):
-        back = back + shared_ref[p].astype(F32)
+    back = added([shared_ref[p].astype(F32) for p in range(N_RAY)])
     for x in range(GX):
         tv_back = tv_ref[x] + jnp.where(first_y, below[GX + x : GX + x + 1], 0.0)
         if x == 0:

time: 94.2 us -> 94.2 us (level)
  no operation moved by 1% of the time
where the time goes in v12:
time: 94.2 us; the launch traced here: 93.1 us
  starting transfers between devices  42.1 us (45%)
  blocking collectives  19.6 us (21%)
  waiting for transfers between devices  16.2 us (17%)
  Pallas kernels  14.4 us (15%)
    all_to_all x4, starting transfers between devices, exchange(): lax.all_to_all(copies, axis, 0, 0, tiled=True, axis_index_groups=groups)  37.8 us
    all_to_all x1, blocking collectives, exchange(): lax.all_to_all(copies, axis, 0, 0, tiled=True, axis_index_groups=groups)  19.6 us
    pallas_call x11, Pallas kernels, call(): pl.pallas_call(kernel, out_shape=[pltpu.VMEM(shape, dtype) if keep else j...  14.4 us
    all_to_all x4, waiting for transfers between devices, exchange(): lax.all_to_all(copies, axis, 0, 0, tiled=True, axis_index_groups=groups)  11.4 us
    ppermute x2, waiting for transfers between devices, swap(): return lax.ppermute(block, 'mp', route + [(b, a) for a, b in route])  4.86 us
    ppermute x2, starting transfers between devices, swap(): return lax.ppermute(block, 'mp', route + [(b, a) for a, b in route])  4.36 us
  transfers between devices with their start and end apart: 6, of which 4 were waited for; matrix products, arithmetic and copies ran while one was open for 0% of the time, Pallas kernels for 7%

profile of v12, /device:TPU:1, one launch (start us, length us, event | category | flops | bytes accessed | tf_op | source)
XLA Modules:
  0.0 93.1 jit_solution(2167517291029517239)
XLA Ops:
  0.6 1.4 %shard_map.128 = (f32[4,8,128]{2,1,0:T(8,128)S(1)}, bf16[16,40,128]{2,1,0:T(8,128)(2,1)}) custom-call(f32[4,8,128]{2,1,0:T(8,128)} %slowness_hbm.1, f32[4,8,128]{2,1,0:T(8,128)} %bar_hbm.1), custom_call_target="tpu_custom_call" | custom-call | tf_op jit(solution)/shard_map/pallas_call | solution.py:55
  2.1 10.6 %all-to-all-start = ((bf16[16,40,128]{2,1,0:T(8,128)(2,1)}), bf16[16,40,128]{2,1,0:T(8,128)(2,1)S(1)}, u32[]{:S(2)}, u32[]{:S(2)}) async-start(bf16[16,40,128]{2,1,0:T(8,128)(2,1)} %get-tuple-element.35), calls=%async_computation | async-start | bytes 327680 | tf_op jit(solution)/shard_map/all_to_all | solution.py:41
  12.7 2.4 %shard_map.129 = (bf16[8,8,128,128]{3,2,1,0:T(8,128)(2,1)S(1)}, bf16[64,512]{1,0:T(8,128)(2,1)S(1)}, f32[16,8,128]{2,1,0:T(8,128)S(1)}, f32[8,128]{1,0:T(8,128)S(1)}) custom-call(bf16[16,8,128,128]{3,2,1,0:T(8,128)(2,1)} %tiles_hbm.3, s32[8,16]{1,0:T(8,128)} %bitcast.1, s32[2,16]{1,0:T(2,128)} %selected_hbm.3, ...), custom_call_target="tpu_custom_call" | custom-call | bytes 8388608 | tf_op jit(solution)/shard_map/pallas_call | solution.py:55
  15.1 0.0 copy-start
  15.1 0.0 copy-start.1
  15.1 0.0 copy-start.3
  15.1 0.0 copy-start.4
  15.1 2.8 %all-to-all-done.gathered_ref = bf16[16,40,128]{2,1,0:T(8,128)(2,1)S(1)} async-done(((bf16[16,40,128]{2,1,0:T(8,128)(2,1)}), bf16[16,40,128]{2,1,0:T(8,128)(2,1)S(1)}, u32[]{:S(2)}, u32[]{:S(2)}) %all-to-all-start) | async-done | bytes 163872 | tf_op jit(solution)/shard_map/all_to_all | solution.py:41
  17.9 1.4 %shard_map.130.after_any.after_ref = f32[32,8,128]{2,1,0:T(8,128)} custom-call(bf16[16,40,128]{2,1,0:T(8,128)(2,1)S(1)} %all-to-all-done.gathered_ref, bf16[8,8,128,128]{3,2,1,0:T(8,128)(2,1)S(1)} %get-tuple-element.37.picked_ref, bf16[64,512]{1,0:T(8,128)(2,1)S(1)} %get-tuple-element.38.hot_ref), custom_call_target="tpu_custom_call" | custom-call | tf_op jit(solution)/shard_map/pallas_call | solution.py:55
  19.3 15.4 %all-to-all-start.1 = ((f32[32,8,128]{2,1,0:T(8,128)}), f32[32,8,128]{2,1,0:T(8,128)S(1)}, u32[]{:S(2)}, u32[]{:S(2)}) async-start(f32[32,8,128]{2,1,0:T(8,128)} %shard_map.130.after_any.after_ref), calls=%async_computation.1 | async-start | bytes 262144 | tf_op jit(solution)/shard_map/all_to_all | solution.py:41
  34.7 0.0 copy-done
  34.7 2.4 %collective-permute-start = (f32[40,128]{1,0:T(8,128)S(1)}, f32[40,128]{1,0:T(8,128)S(1)}, u32[]{:S(2)}, u32[]{:S(2)}) collective-permute-start(f32[40,128]{1,0:T(8,128)S(1)} %get-tuple-element.40), channel_id=1, source_target_pairs={{1,2},{3,4},{5,6},{7,8},{9,10},{11,12},{13,14},{15,16},{17,18},{19... | collective-permute-start | bytes 61448 | tf_op jit(solution)/shard_map/ppermute | solution.py:378
  37.2 1.9 %collective-permute-start.1 = (f32[40,128]{1,0:T(8,128)S(1)}, f32[40,128]{1,0:T(8,128)S(1)}, u32[]{:S(2)}, u32[]{:S(2)}) collective-permute-start(f32[40,128]{1,0:T(8,128)S(1)} %get-tuple-element.41), channel_id=1, source_target_pairs={{0,1},{2,3},{4,5},{6,7},{8,9},{10,11},{12,13},{14,15},{16,17},{18,... | collective-permute-start | bytes 61448 | tf_op jit(solution)/shard_map/ppermute | solution.py:378
  39.1 4.9 %collective-permute-done.far_ref = f32[40,128]{1,0:T(8,128)S(1)} collective-permute-done((f32[40,128]{1,0:T(8,128)S(1)}, f32[40,128]{1,0:T(8,128)S(1)}, u32[]{:S(2)}, u32[]{:S(2)}) %collective-permute-start) | collective-permute-done | bytes 20512 | tf_op jit(solution)/shard_map/ppermute | solution.py:378
  44.0 0.0 collective-permute-done.1.near_ref
  44.0 0.0 copy-done.1
  44.0 0.2 shard_map.132
  44.2 0.0 all-to-all-done.1.parts_ref
  44.2 0.0 copy-done.3
  44.2 0.0 copy-done.4
  44.2 1.2 %shard_map.133 = (f32[16,128]{1,0:T(8,128)S(1)}, bf16[16,104,128]{2,1,0:T(8,128)(2,1)}) custom-call(f32[32,8,128]{2,1,0:T(8,128)S(1)} %all-to-all-done.1.parts_ref, f32[16,128]{1,0:T(8,128)S(1)} %copy-done.4, f32[16,128]{1,0:T(8,128)S(1)} %copy-done.3, f32[16,8,128]{2,1,0:T(8,128)S(1)} %get-tuple-element.39.pick_ref, ...), custom_call_target="tpu_custom_call" | custom-call | tf_op jit(solution)/shard_map/pallas_call | solution.py:55
  45.4 5.2 %all-to-all-start.2 = ((bf16[16,104,128]{2,1,0:T(8,128)(2,1)}), bf16[16,104,128]{2,1,0:T(8,128)(2,1)S(1)}, u32[]{:S(2)}, u32[]{:S(2)}) async-start(bf16[16,104,128]{2,1,0:T(8,128)(2,1)} %get-tuple-element.45), calls=%async_computation.2 | async-start | bytes 851968 | tf_op jit(solution)/shard_map/all_to_all | solution.py:41
  50.6 3.3 %shard_map.134 = (bf16[8,8,128,128]{3,2,1,0:T(8,128)(2,1)S(1)}, bf16[64,512]{1,0:T(8,128)(2,1)S(1)}, f32[16,8,128]{2,1,0:T(8,128)S(1)}, f32[8,128]{1,0:T(8,128)}) custom-call(bf16[16,8,128,128]{3,2,1,0:T(8,128)(2,1)} %tiles_hbm.3, s32[8,16]{1,0:T(8,128)} %bitcast.2, s32[2,16]{1,0:T(2,128)} %selected_hbm.3, f32[32,8,128]{2,1,0:T(8,128)} %shard_map.130.after_any.after_ref), custom_call_target="tpu_custom_call" | custom-call | bytes 8388608 | tf_op jit(solution)/shard_map/pallas_call | solution.py:55
  53.9 5.6 %all-to-all-done.2.shared_ref = bf16[16,104,128]{2,1,0:T(8,128)(2,1)S(1)} async-done(((bf16[16,104,128]{2,1,0:T(8,128)(2,1)}), bf16[16,104,128]{2,1,0:T(8,128)(2,1)S(1)}, u32[]{:S(2)}, u32[]{:S(2)}) %all-to-all-start.2) | async-done | bytes 426016 | tf_op jit(solution)/shard_map/all_to_all | solution.py:41
  59.5 1.7 %shard_map.135 = (f32[4,8,128]{2,1,0:T(8,128)}, f32[4,8,128]{2,1,0:T(8,128)S(1)}, f32[16,128]{1,0:T(8,128)S(1)}, bf16[32,24,128]{2,1,0:T(8,128)(2,1)S(1)}) custom-call(bf16[16,104,128]{2,1,0:T(8,128)(2,1)S(1)} %all-to-all-done.2.shared_ref, bf16[16,40,128]{2,1,0:T(8,128)(2,1)S(1)} %all-to-all-done.gathered_ref, ...), custom_call_target="tpu_custom_call" | custom-call | tf_op jit(solution)/shard_map/pallas_call | solution.py:55
  61.3 0.0 copy-start.2
  61.3 19.6 %all_to_all.25.parts_ref = bf16[32,24,128]{2,1,0:T(8,128)(2,1)S(1)} all-to-all(bf16[32,24,128]{2,1,0:T(8,128)(2,1)S(1)} %get-tuple-element.51), channel_id=1, replica_groups={{19,20,21,22,23,24,25,26,27,28,29,30,31,0,1,2,3,4,5,6,7,8,9,10,11,12,13..., dimensions={0} | all-to-all | bytes 393216 | tf_op jit(solution)/shard_map/all_to_all | solution.py:41
  80.8 1.3 %shard_map.136 = (f32[16,128]{1,0:T(8,128)}, bf16[16,40,128]{2,1,0:T(8,128)(2,1)}, f32[2,8,128]{2,1,0:T(8,128)S(1)}) custom-call(bf16[32,24,128]{2,1,0:T(8,128)(2,1)S(1)} %all_to_all.25.parts_ref, f32[16,128]{1,0:T(8,128)S(1)} %get-tuple-element.52.rays_ref, f32[16,128]{1,0:T(8,128)S(1)} %copy-done.3, f32[16,8,128]{2,1,0:T(8,128)S(1)} %get-tuple-element.53.pick_ref, ...), custom_call_target="tpu_custom_call" | custom-call | tf_op jit(solution)/shard_map/pallas_call | solution.py:55
  82.1 6.6 %all-to-all-start.4 = ((bf16[16,40,128]{2,1,0:T(8,128)(2,1)}), bf16[16,40,128]{2,1,0:T(8,128)(2,1)S(1)}, u32[]{:S(2)}, u32[]{:S(2)}) async-start(bf16[16,40,128]{2,1,0:T(8,128)(2,1)} %get-tuple-element.59), calls=%async_computation.4 | async-start | bytes 327680 | tf_op jit(solution)/shard_map/all_to_all | solution.py:41
  88.7 0.0 copy-done.2
  88.7 0.7 shard_map.137
  89.5 3.0 %all-to-all-done.4.shared_ref = bf16[16,40,128]{2,1,0:T(8,128)(2,1)S(1)} async-done(((bf16[16,40,128]{2,1,0:T(8,128)(2,1)}), bf16[16,40,128]{2,1,0:T(8,128)(2,1)S(1)}, u32[]{:S(2)}, u32[]{:S(2)}) %all-to-all-start.4) | async-done | bytes 163872 | tf_op jit(solution)/shard_map/all_to_all | solution.py:41
  92.4 0.7 shard_map.138
  (1 shorter events, 0.0 us)
Async XLA Ops:
  2.1 15.8 %all-to-all-start = ((bf16[16,40,128]{2,1,0:T(8,128)(2,1)}), bf16[16,40,128]{2,1,0:T(8,128)(2,1)S(1)}, u32[]{:S(2)}, u32[]{:S(2)}) async-start(bf16[16,40,128]{2,1,0:T(8,128)(2,1)} %get-tuple-element.35), calls=%async_computation | async-start | bytes 327680 | tf_op jit(solution)/shard_map/all_to_all | solution.py:41
  15.1 19.7 %copy-start = (f32[3,4,8,128]{3,2,1,0:T(8,128)S(1)}, f32[3,4,8,128]{3,2,1,0:T(8,128)}, u32[]{:S(2)}) copy-start(f32[3,4,8,128]{3,2,1,0:T(8,128)} %dual_ref.3) | copy-start | bytes 147460
  15.1 28.9 %copy-start.1 = (f32[4,8,128]{2,1,0:T(8,128)S(1)}, f32[4,8,128]{2,1,0:T(8,128)}, u32[]{:S(2)}) copy-start(f32[4,8,128]{2,1,0:T(8,128)} %image_ref.3) | copy-start | bytes 49156
  15.1 29.1 %copy-start.3 = (f32[16,128]{1,0:T(8,128)S(1)}, f32[16,128]{1,0:T(8,128)}, u32[]{:S(2)}) copy-start(f32[16,128]{1,0:T(8,128)} %times_ref.3) | copy-start | bytes 24580
  15.1 29.1 %copy-start.4 = (f32[16,128]{1,0:T(8,128)S(1)}, f32[16,128]{1,0:T(8,128)}, u32[]{:S(2)}) copy-start(f32[16,128]{1,0:T(8,128)} %rays_ref.1) | copy-start | bytes 24580
  19.3 24.8 %all-to-all-start.1 = ((f32[32,8,128]{2,1,0:T(8,128)}), f32[32,8,128]{2,1,0:T(8,128)S(1)}, u32[]{:S(2)}, u32[]{:S(2)}) async-start(f32[32,8,128]{2,1,0:T(8,128)} %shard_map.130.after_any.after_ref), calls=%async_computation.1 | async-start | bytes 262144 | tf_op jit(solution)/shard_map/all_to_all | solution.py:41
  34.7 9.2 %collective-permute-start = (f32[40,128]{1,0:T(8,128)S(1)}, f32[40,128]{1,0:T(8,128)S(1)}, u32[]{:S(2)}, u32[]{:S(2)}) collective-permute-start(f32[40,128]{1,0:T(8,128)S(1)} %get-tuple-element.40), channel_id=1, source_target_pairs={{1,2},{3,4},{5,6},{7,8},{9,10},{11,12},{13,14},{15,16},{17,18},{19... | collective-permute-start | bytes 61448 | tf_op jit(solution)/shard_map/ppermute | solution.py:378
  37.2 6.8 %collective-permute-start.1 = (f32[40,128]{1,0:T(8,128)S(1)}, f32[40,128]{1,0:T(8,128)S(1)}, u32[]{:S(2)}, u32[]{:S(2)}) collective-permute-start(f32[40,128]{1,0:T(8,128)S(1)} %get-tuple-element.41), channel_id=1, source_target_pairs={{0,1},{2,3},{4,5},{6,7},{8,9},{10,11},{12,13},{14,15},{16,17},{18,... | collective-permute-start | bytes 61448 | tf_op jit(solution)/shard_map/ppermute | solution.py:378
  45.4 14.1 %all-to-all-start.2 = ((bf16[16,104,128]{2,1,0:T(8,128)(2,1)}), bf16[16,104,128]{2,1,0:T(8,128)(2,1)S(1)}, u32[]{:S(2)}, u32[]{:S(2)}) async-start(bf16[16,104,128]{2,1,0:T(8,128)(2,1)} %get-tuple-element.45), calls=%async_computation.2 | async-start | bytes 851968 | tf_op jit(solution)/shard_map/all_to_all | solution.py:41
  61.3 27.5 %copy-start.2 = (f32[4,8,128]{2,1,0:T(8,128)S(1)}, f32[4,8,128]{2,1,0:T(8,128)}, u32[]{:S(2)}) copy-start(f32[4,8,128]{2,1,0:T(8,128)} %get-tuple-element.30.field_ref) | copy-start | bytes 49156
  82.1 10.3 %all-to-all-start.4 = ((bf16[16,40,128]{2,1,0:T(8,128)(2,1)}), bf16[16,40,128]{2,1,0:T(8,128)(2,1)S(1)}, u32[]{:S(2)}, u32[]{:S(2)}) async-start(bf16[16,40,128]{2,1,0:T(8,128)(2,1)} %get-tuple-element.59), calls=%async_computation.4 | async-start | bytes 327680 | tf_op jit(solution)/shard_map/all_to_all | solution.py:41
